TPU v7x, 32 devices: a whole 2x2x4 slice. The times are simulated.
32 devices in a mesh: pts: 8 (over z, y), mdl: 4 (over x, core).
Axes of the slice: x: 2, y: 2, z: 4, core: 2. Of those that a mesh axis runs over, the one named last changes fastest.
Arguments:
- points: bfloat16 [8192, 512], P('pts', 'mdl'), may hold values from -6 to 6
- cotangent: bfloat16 [8192, 512], P('pts', 'mdl'), may hold values from -6 to 6
- neighbours: int32 [8192, 27], P('pts'), may hold values from -1 to 8191, as said below
- scan_lengths: int32 [2], replicated, may hold values from 3584 to 4608, as said below
- to_patch: int32 [8192], P('pts'), may hold values from 0 to 16383, as said below
- from_patch: int32 [16384], P('pts'), may hold values from -1 to 8191, as said below
- owner_slot: int32 [40], replicated, may hold values from 0 to 39, as said below
- weights: float32 [40, 512, 512], P('mdl', 'pts')
- row_eigen_basis: float32 [40, 512, 512], P('mdl', 'pts'), may hold values from -1 to 1
- right_basis: float32 [40, 512, 512], P('mdl', 'pts'), may hold values from -1 to 1
- first_moment: float32 [40, 512, 512], P('mdl', 'pts'), may hold values from -64 to 64
- second_moment: float32 [40, 512, 512], P('mdl', 'pts'), may hold values from 4.096 to 65.536
- vectors: float32 [16, 512], P(None, 'mdl')
- vector_first: float32 [16, 512], P(None, 'mdl'), may hold values from -64 to 64
- vector_second: float32 [16, 512], P(None, 'mdl'), may hold values from 4.096 to 65.536
Outputs:
- out_points: bfloat16 [8192, 512], P('pts', 'mdl')
- point_grad: float32 [8192, 512], P('pts', 'mdl')
- weight_grad: float32 [40, 512, 512], P('mdl', 'pts')
- new_first: float32 [40, 512, 512], P('mdl', 'pts')
- new_second: float32 [40, 512, 512], P('mdl', 'pts')
- new_weights: float32 [40, 512, 512], P('mdl', 'pts')
- weights_bf16: bfloat16 [40, 512, 512], P('mdl', 'pts')
- vector_grad: float32 [16, 512], P(None, 'mdl')
- new_vector_first: float32 [16, 512], P(None, 'mdl')
- new_vector_second: float32 [16, 512], P(None, 'mdl')
- new_vectors: float32 [16, 512], P(None, 'mdl')
Inputs may be any that keep to these rules, and one draw needn't show every extreme that they name: neighbours[p, t] = q >= 0 exactly when neighbours[q, 26 - t] = p; column (26) / 2 is p itself; |q - p| <= 256. `scan_lengths`: the lengths sum to 8192. `to_patch`: one to one; slots d * 2048 to (d + 1) * 2048 - 1 belong to index d of pts, which receives 1024 rows; of the rows of one index of pts at most 256 go to one index, exactly that many to some; in every patch the used slots come first and at least one is used. `from_patch`: the inverse of to_patch, -1 at unused slots. `owner_slot`: a permutation.
All inputs are finite; a program needn't handle non-finite values.
Results may differ from a plain program's by a relative error of at most 0.034.
Values may be sent and summed in bfloat16 or wider, within the bound.
A program may use at most 256 MiB of HBM per device.

v0:
```python
import jax
import jax.numpy as jnp
from jax import lax
from jax.sharding import PartitionSpec as P

C = 512
HD = 16
FF = 2048
TAPS = 27
HALO = 256
PATCH = 1024
STEP = 5


EXACT_PRECISION = lax.Precision.HIGHEST
NORM_EPS = 1e-05
BETA_ONE = 0.9
BETA_TWO = 0.999
ADAM_EPS = 1e-08
VECTOR_RATE = 0.5
MATRIX_DECAY = 0.05
MASKED = -1e30


def with_halo(block, sides, width):
    for axis, dim in sides:
        count = lax.axis_size(axis)
        forward = [(i, i + 1) for i in range(count - 1)]
        backward = [(target, source) for source, target in forward]
        low = lax.ppermute(
            lax.slice_in_dim(block, block.shape[dim] - width, None, axis=dim), axis, forward
        )
        high = lax.ppermute(lax.slice_in_dim(block, 0, width, axis=dim), axis, backward)
        block = jnp.concatenate([low, block, high], axis=dim)
    return block


def spread_columns(owned_rows):
    return lax.all_to_all(owned_rows, "mdl", split_axis=2, concat_axis=0, tiled=True)


def collect_rows(owned_rows):
    return lax.all_gather(owned_rows, "pts", axis=1, tiled=True)


def merge_columns(grad_blocks):
    return lax.all_to_all(
        grad_blocks.astype(jnp.bfloat16), "mdl", split_axis=0, concat_axis=2, tiled=True
    ).astype(grad_blocks.dtype)


def reduce_rows(grad_blocks):
    return lax.psum_scatter(
        grad_blocks.astype(jnp.bfloat16), "pts", scatter_dimension=1, tiled=True
    ).astype(jnp.float32)


def widen(shard_rows):
    return lax.all_gather(shard_rows, "mdl", axis=1, tiled=True)


def add_parts(partial_value):
    return lax.psum_scatter(
        partial_value.astype(jnp.bfloat16), "mdl", scatter_dimension=1, tiled=True
    ).astype(jnp.float32)


def whole_sum(partial_value):
    return lax.psum(partial_value.astype(jnp.bfloat16), "mdl").astype(jnp.float32)


def row_sums(first_sum, second_sum):
    return lax.psum((first_sum, second_sum), "mdl")


def border(shard_rows):
    return with_halo(shard_rows, (("pts", 0),), HALO)


def trade(buffer):
    return lax.all_to_all(buffer, "pts", split_axis=0, concat_axis=0, tiled=True)


def scan_index(row_ids, scan_lengths):
    bounds = jnp.cumsum(scan_lengths)
    return jnp.sum((row_ids[..., None] >= bounds[:-1]).astype(jnp.int32), -1)


def normalize(values):
    total_sum, square_sum = row_sums(jnp.sum(values, 1), jnp.sum(values * values, 1))
    row_mean = total_sum / C
    inv_std = lax.rsqrt(square_sum / C - row_mean * row_mean + NORM_EPS)
    return ((values - row_mean[:, None]) * inv_std[:, None], inv_std)


def normalize_back(grad_unit, unit_rows, inv_std):
    total_sum, cross_sum = row_sums(jnp.sum(grad_unit, 1), jnp.sum(grad_unit * unit_rows, 1))
    return inv_std[:, None] * (
        grad_unit - total_sum[:, None] / C - unit_rows * cross_sum[:, None] / C
    )


def gelu_slope(pre_act):
    return (
        0.5 * (1.0 + lax.erf(pre_act * 0.7071067811865476))
        + pre_act * jnp.exp(-0.5 * pre_act * pre_act) * 0.3989422804014327
    )


def masked_scores(queries, keys_in, key_valid, scan_group):
    scores = jnp.einsum(
        "qhd,khd->hqk", queries, keys_in, preferred_element_type=jnp.float32
    ) * HD ** (-0.5)
    allowed = key_valid[None, :] & (
        (scan_group[:, None] == scan_group[None, :]) | ~key_valid[:, None]
    )
    return jnp.where(allowed[None], scores, MASKED)


def attend(items):
    queries, keys_in, values_in, key_valid, scan_group = items
    scores = masked_scores(queries, keys_in, key_valid, scan_group)
    row_max = jnp.max(scores, -1, keepdims=True)
    exp_scores = jnp.exp(scores - row_max)
    row_total = jnp.sum(exp_scores, -1, keepdims=True)
    soft_weights = (exp_scores / row_total).astype(jnp.bfloat16)
    attended = jnp.einsum(
        "hqk,khd->qhd", soft_weights, values_in, preferred_element_type=jnp.float32
    )
    return (attended.astype(jnp.bfloat16), (row_max + jnp.log(row_total))[..., 0])


def attend_back(items):
    queries, keys_in, values_in, grad_out, log_total, key_valid, scan_group = items
    scores = masked_scores(queries, keys_in, key_valid, scan_group)
    soft_weights = jnp.exp(scores - log_total[..., None])
    grad_soft = jnp.einsum("qhd,khd->hqk", grad_out, values_in, preferred_element_type=jnp.float32)
    grad_values = jnp.einsum(
        "hqk,qhd->khd",
        soft_weights.astype(jnp.bfloat16),
        grad_out,
        preferred_element_type=jnp.float32,
    )
    row_inner = jnp.sum(grad_soft * soft_weights, -1, keepdims=True)
    grad_scores = (soft_weights * (grad_soft - row_inner)).astype(jnp.bfloat16)
    grad_queries = jnp.einsum(
        "hqk,khd->qhd", grad_scores, keys_in, preferred_element_type=jnp.float32
    ) * HD ** (-0.5)
    grad_keys = jnp.einsum(
        "hqk,qhd->khd", grad_scores, queries, preferred_element_type=jnp.float32
    ) * HD ** (-0.5)
    return (grad_queries, grad_keys, grad_values)


def local(
    points,
    cotangent,
    neighbours,
    scan_lengths,
    to_patch,
    from_patch,
    owner_slot,
    weights,
    row_eigen_basis,
    right_basis,
    first_moment,
    second_moment,
    vectors,
    vector_first,
    vector_second,
):
    row_count, col_count = points.shape
    slot_count = from_patch.shape[0]
    pts_count = lax.axis_size("pts")
    pts_index = lax.axis_index("pts")
    mdl_index = lax.axis_index("mdl")
    local_heads = col_count // HD
    ff_blocks = FF // C
    patch_count = slot_count // PATCH
    capacity = 2 * row_count // pts_count
    dump_row = pts_count * capacity
    matrix_rate = 1.6 * C ** (-0.5)
    owned_rows = weights.astype(jnp.bfloat16)
    owned_rows = collect_rows(owned_rows)
    owned_rows = spread_columns(owned_rows)
    blocks = owned_rows[owner_slot]
    tap_maps = blocks[:TAPS]
    linear_map = blocks[TAPS]
    query_map = blocks[TAPS + 1]
    key_map = blocks[TAPS + 2]
    value_map = blocks[TAPS + 3]
    projection = blocks[TAPS + 4]
    first_mlp = (
        blocks[TAPS + 5 : TAPS + 5 + ff_blocks].transpose(1, 0, 2).reshape(C, ff_blocks * col_count)
    )
    second_mlp = (
        blocks[TAPS + 5 + ff_blocks : TAPS + 5 + 2 * ff_blocks]
        .transpose(0, 2, 1)
        .reshape(ff_blocks * col_count, C)
    )
    tap_stack = tap_maps.transpose(0, 2, 1).reshape(TAPS * col_count, C)
    first_bias = vectors[11 : 11 + ff_blocks].reshape(ff_blocks * col_count)
    extended = border(points)
    row_ids = pts_index * row_count + jnp.arange(row_count, dtype=jnp.int32)
    own_scan = scan_index(row_ids, scan_lengths)
    safe_ids = jnp.where(neighbours >= 0, neighbours, 0)
    usable = (neighbours >= 0) & (scan_index(safe_ids, scan_lengths) == own_scan[:, None])
    local_ids = jnp.where(usable, neighbours - (pts_index * row_count - HALO), row_count + 2 * HALO)
    extended = jnp.concatenate([extended, jnp.zeros((1, col_count), jnp.bfloat16)], 0)
    gathered = extended[local_ids].reshape(row_count, TAPS * col_count)
    conv_part = jnp.dot(gathered, tap_stack, preferred_element_type=jnp.float32)
    own_block = (
        lax.dynamic_slice_in_dim(conv_part, mdl_index * col_count, col_count, 1) + vectors[0]
    )
    conv_part = lax.dynamic_update_slice_in_dim(conv_part, own_block, mdl_index * col_count, 1)
    hidden_full = whole_sum(conv_part).astype(jnp.bfloat16)
    mixed_rows = jnp.dot(hidden_full, linear_map, preferred_element_type=jnp.float32) + vectors[1]
    mixed_unit, mixed_std = normalize(mixed_rows)
    stream_one = points.astype(jnp.float32) + mixed_unit * vectors[2] + vectors[3]
    one_unit, one_std = normalize(stream_one)
    normed = (one_unit * vectors[4] + vectors[5]).astype(jnp.bfloat16)
    target = to_patch // slot_count
    target_hits = (target[:, None] == jnp.arange(pts_count, dtype=jnp.int32)[None, :]).astype(
        jnp.int32
    )
    send_pos = target * capacity + jnp.sum((jnp.cumsum(target_hits, 0) - 1) * target_hits, 1)
    filled = from_patch >= 0
    source_row = jnp.where(filled, from_patch, pts_count * row_count)
    sort_order = jnp.argsort(source_row)
    source_dev = source_row // row_count
    sorted_dev = source_dev[sort_order]
    source_hits = (
        sorted_dev[:, None] == jnp.arange(pts_count + 1, dtype=jnp.int32)[None, :]
    ).astype(jnp.int32)
    sorted_rank = jnp.sum((jnp.cumsum(source_hits, 0) - 1) * source_hits, 1)
    slot_rank = jnp.zeros_like(sorted_rank).at[sort_order].set(sorted_rank)
    take_pos = jnp.where(filled, source_dev * capacity + slot_rank, dump_row)

    def to_slots(values):
        buffer = (
            jnp.zeros((dump_row + 1, values.shape[1]), values.dtype)
            .at[send_pos]
            .set(values)[:dump_row]
        )
        arrived = jnp.concatenate([trade(buffer), jnp.zeros((1, values.shape[1]), values.dtype)], 0)
        return arrived[take_pos]

    def from_slots(values):
        buffer = (
            jnp.zeros((dump_row + 1, values.shape[1]), values.dtype)
            .at[take_pos]
            .set(values)[:dump_row]
        )
        return trade(buffer)[send_pos]

    slot_in = widen(to_slots(normed))
    queries = (jnp.dot(slot_in, query_map, preferred_element_type=jnp.float32) + vectors[6]).astype(
        jnp.bfloat16
    )
    keys_all = jnp.dot(slot_in, key_map, preferred_element_type=jnp.float32).astype(jnp.bfloat16)
    values_all = (
        jnp.dot(slot_in, value_map, preferred_element_type=jnp.float32) + vectors[7]
    ).astype(jnp.bfloat16)
    slot_scan = jnp.where(filled, scan_index(jnp.where(filled, from_patch, 0), scan_lengths), -1)
    head_shape = (patch_count, PATCH, local_heads, HD)
    patch_valid = filled.reshape(patch_count, PATCH)
    patch_scan = slot_scan.reshape(patch_count, PATCH)
    attended, log_total = lax.map(
        attend,
        (
            queries.reshape(head_shape),
            keys_all.reshape(head_shape),
            values_all.reshape(head_shape),
            patch_valid,
            patch_scan,
        ),
    )
    attended = attended.reshape(slot_count, col_count)
    branch_part = lax.dot_general(
        attended, projection, (((1,), (1,)), ((), ())), preferred_element_type=jnp.float32
    )
    branch = (add_parts(branch_part) + vectors[8]).astype(jnp.bfloat16)
    stream_two = stream_one + from_slots(branch).astype(jnp.float32)
    two_unit, two_std = normalize(stream_two)
    normed_two = widen((two_unit * vectors[9] + vectors[10]).astype(jnp.bfloat16))
    pre_act = jnp.dot(normed_two, first_mlp, preferred_element_type=jnp.float32) + first_bias
    activ = jax.nn.gelu(pre_act, approximate=False).astype(jnp.bfloat16)
    out_part = jnp.dot(activ, second_mlp, preferred_element_type=jnp.float32)
    result = (stream_two + add_parts(out_part) + vectors[11 + ff_blocks]).astype(jnp.bfloat16)
    grad_out_full = widen(cotangent)
    grad_out_bias = jnp.sum(cotangent.astype(jnp.float32), 0)
    grad_activ = lax.dot_general(
        grad_out_full, second_mlp, (((1,), (1,)), ((), ())), preferred_element_type=jnp.float32
    )
    grad_pre = (grad_activ * gelu_slope(pre_act)).astype(jnp.bfloat16)
    grad_first_bias = jnp.sum(grad_pre.astype(jnp.float32), 0)
    grad_second_mlp = lax.dot_general(
        activ, grad_out_full, (((0,), (0,)), ((), ())), preferred_element_type=jnp.float32
    )
    grad_second_mlp = grad_second_mlp.reshape(ff_blocks, col_count, C).transpose(0, 2, 1)
    grad_first_mlp = lax.dot_general(
        normed_two, grad_pre, (((0,), (0,)), ((), ())), preferred_element_type=jnp.float32
    )
    grad_first_mlp = grad_first_mlp.reshape(C, ff_blocks, col_count).transpose(1, 0, 2)
    grad_normed_two = add_parts(
        lax.dot_general(
            grad_pre, first_mlp, (((1,), (1,)), ((), ())), preferred_element_type=jnp.float32
        )
    )
    grad_gain_two = jnp.sum(grad_normed_two * two_unit, 0)
    grad_shift_two = jnp.sum(grad_normed_two, 0)
    grad_two = cotangent.astype(jnp.float32) + normalize_back(
        grad_normed_two * vectors[9], two_unit, two_std
    )
    grad_branch = grad_two.astype(jnp.bfloat16)
    grad_proj_bias = jnp.sum(grad_branch.astype(jnp.float32), 0)
    grad_slot = widen(to_slots(grad_branch))
    grad_projection = lax.dot_general(
        grad_slot, attended, (((0,), (0,)), ((), ())), preferred_element_type=jnp.float32
    )
    grad_attended = jnp.dot(grad_slot, projection, preferred_element_type=jnp.float32).astype(
        jnp.bfloat16
    )
    grad_queries, grad_keys, grad_values = lax.map(
        attend_back,
        (
            queries.reshape(head_shape),
            keys_all.reshape(head_shape),
            values_all.reshape(head_shape),
            grad_attended.reshape(head_shape),
            log_total,
            patch_valid,
            patch_scan,
        ),
    )
    grad_queries = grad_queries.reshape(slot_count, col_count).astype(jnp.bfloat16)
    grad_keys = grad_keys.reshape(slot_count, col_count).astype(jnp.bfloat16)
    grad_values = grad_values.reshape(slot_count, col_count).astype(jnp.bfloat16)
    grad_query_bias = jnp.sum(grad_queries.astype(jnp.float32), 0)
    grad_value_bias = jnp.sum(grad_values.astype(jnp.float32), 0)
    grad_query_map = lax.dot_general(
        slot_in, grad_queries, (((0,), (0,)), ((), ())), preferred_element_type=jnp.float32
    )
    grad_key_map = lax.dot_general(
        slot_in, grad_keys, (((0,), (0,)), ((), ())), preferred_element_type=jnp.float32
    )
    grad_value_map = lax.dot_general(
        slot_in, grad_values, (((0,), (0,)), ((), ())), preferred_element_type=jnp.float32
    )
    slot_back = lax.dot_general(
        grad_queries, query_map, (((1,), (1,)), ((), ())), preferred_element_type=jnp.float32
    )
    slot_back = slot_back + lax.dot_general(
        grad_keys, key_map, (((1,), (1,)), ((), ())), preferred_element_type=jnp.float32
    )
    slot_back = slot_back + lax.dot_general(
        grad_values, value_map, (((1,), (1,)), ((), ())), preferred_element_type=jnp.float32
    )
    grad_normed = from_slots(add_parts(slot_back).astype(jnp.bfloat16)).astype(jnp.float32)
    grad_gain_one = jnp.sum(grad_normed * one_unit, 0)
    grad_shift_one = jnp.sum(grad_normed, 0)
    grad_one = grad_two + normalize_back(grad_normed * vectors[4], one_unit, one_std)
    grad_gain_zero = jnp.sum(grad_one * mixed_unit, 0)
    grad_shift_zero = jnp.sum(grad_one, 0)
    grad_mixed = normalize_back(grad_one * vectors[2], mixed_unit, mixed_std).astype(jnp.bfloat16)
    grad_linear_bias = jnp.sum(grad_mixed.astype(jnp.float32), 0)
    grad_linear = lax.dot_general(
        hidden_full, grad_mixed, (((0,), (0,)), ((), ())), preferred_element_type=jnp.float32
    )
    hidden_back = lax.dot_general(
        grad_mixed, linear_map, (((1,), (1,)), ((), ())), preferred_element_type=jnp.float32
    )
    grad_hidden_full = whole_sum(hidden_back).astype(jnp.bfloat16)
    own_grad = lax.dynamic_slice_in_dim(grad_hidden_full, mdl_index * col_count, col_count, 1)
    grad_conv_bias = jnp.sum(own_grad.astype(jnp.float32), 0)
    grad_taps = lax.dot_general(
        gathered, grad_hidden_full, (((0,), (0,)), ((), ())), preferred_element_type=jnp.float32
    )
    grad_taps = grad_taps.reshape(TAPS, col_count, C).transpose(0, 2, 1)
    grad_extended = jnp.concatenate([border(grad_hidden_full), jnp.zeros((1, C), jnp.bfloat16)], 0)

    def conv_turn(tap_index, running):
        where_from = lax.dynamic_index_in_dim(local_ids, tap_index, 1, keepdims=False)
        weight_tap = lax.dynamic_index_in_dim(tap_maps, TAPS - 1 - tap_index, 0, keepdims=False)
        return running + jnp.dot(
            grad_extended[where_from], weight_tap, preferred_element_type=jnp.float32
        )

    conv_grad = lax.fori_loop(0, TAPS, conv_turn, jnp.zeros((row_count, col_count), jnp.float32))
    point_grad = grad_one + conv_grad
    block_grads = jnp.concatenate(
        [
            grad_taps,
            grad_linear[None],
            grad_query_map[None],
            grad_key_map[None],
            grad_value_map[None],
            grad_projection[None],
            grad_first_mlp,
            grad_second_mlp,
        ],
        0,
    )
    slot_grads = jnp.zeros_like(block_grads).at[owner_slot].set(block_grads)
    reduced = reduce_rows(merge_columns(slot_grads))
    vector_local = jnp.concatenate(
        [
            jnp.stack(
                [
                    grad_conv_bias,
                    grad_linear_bias,
                    grad_gain_zero,
                    grad_shift_zero,
                    grad_gain_one,
                    grad_shift_one,
                    grad_query_bias,
                    grad_value_bias,
                    grad_proj_bias,
                    grad_gain_two,
                    grad_shift_two,
                ]
            ),
            grad_first_bias.reshape(ff_blocks, col_count),
            grad_out_bias[None],
        ],
        0,
    )
    vector_grad = lax.psum(vector_local, "pts")
    right_full = lax.all_gather(right_basis.astype(jnp.bfloat16), "pts", axis=1, tiled=True).astype(
        right_basis.dtype
    )
    right_product = jnp.einsum("brc,bcd->brd", reduced, right_full, precision=EXACT_PRECISION)
    left_product = row_eigen_basis
    rotated_gradient = (
        lax.psum_scatter(
            jnp.einsum(
                "ual,uaq->luq", left_product, right_product, precision=EXACT_PRECISION
            ).astype(jnp.bfloat16),
            "pts",
            scatter_dimension=0,
            tiled=True,
        )
        .astype(jnp.float32)
        .transpose(1, 0, 2)
    )
    new_first = BETA_ONE * first_moment + (1.0 - BETA_ONE) * rotated_gradient
    new_second = BETA_TWO * second_moment + (1.0 - BETA_TWO) * rotated_gradient * rotated_gradient
    direction = (
        new_first
        / (1.0 - BETA_ONE**STEP)
        / (jnp.sqrt(new_second / (1.0 - BETA_TWO**STEP)) + ADAM_EPS)
    )
    turned_matrix = jnp.einsum("bic,bdc->bid", direction, right_full, precision=EXACT_PRECISION)
    left_product = row_eigen_basis
    update_direction = jnp.zeros_like(turned_matrix) + jnp.einsum(
        "zua,zaf->zuf",
        left_product,
        lax.all_gather(turned_matrix.astype(jnp.bfloat16), "pts", axis=1, tiled=True).astype(
            jnp.float32
        ),
        precision=EXACT_PRECISION,
    )
    new_weights = weights - matrix_rate * (update_direction + MATRIX_DECAY * weights)
    new_vector_first = BETA_ONE * vector_first + (1.0 - BETA_ONE) * vector_grad
    new_vector_second = BETA_TWO * vector_second + (1.0 - BETA_TWO) * vector_grad * vector_grad
    vector_step = (
        new_vector_first
        / (1.0 - BETA_ONE**STEP)
        / (jnp.sqrt(new_vector_second / (1.0 - BETA_TWO**STEP)) + ADAM_EPS)
    )
    new_vectors = vectors - VECTOR_RATE * vector_step
    return (
        result,
        point_grad,
        reduced,
        new_first,
        new_second,
        new_weights,
        new_weights.astype(jnp.bfloat16),
        vector_grad,
        new_vector_first,
        new_vector_second,
        new_vectors,
    )


def solution(mesh):
    placed = (
        P("pts", "mdl"),
        P("pts", "mdl"),
        P("pts", None),
        P(),
        P("pts"),
        P("pts"),
        P(),
        P("mdl", "pts", None),
        P("mdl", "pts", None),
        P("mdl", "pts", None),
        P("mdl", "pts", None),
        P("mdl", "pts", None),
        P(None, "mdl"),
        P(None, "mdl"),
        P(None, "mdl"),
    )
    return jax.shard_map(
        local,
        mesh=mesh,
        in_specs=placed,
        out_specs=(
            P("pts", "mdl"),
            P("pts", "mdl"),
            P("mdl", "pts", None),
            P("mdl", "pts", None),
            P("mdl", "pts", None),
            P("mdl", "pts", None),
            P("mdl", "pts", None),
            P(None, "mdl"),
            P(None, "mdl"),
            P(None, "mdl"),
            P(None, "mdl"),
        ),
        check_vma=False,
    )
```

profile of v0, /device:TPU:29, one launch (start us, length us, event | category | flops | bytes accessed | tf_op | source)
XLA Modules:
  0.0 1789.7 jit_solution(657612484327053408)
XLA Ops:
  9.6 85.8 %all-gather.10.cloned.1.call-done = bf16[10,512,512]{2,1,0:T(8,128)(2,1)} async-done(((bf16[10,64,512]{2,1,0:T(8,128)(2,1)}), bf16[10,512,512]{2,1,0:T(8,128)(2,1)}) %all-gather.10.cloned.1.call-update) | async-done | bytes 5242896 | tf_op jit(solution)/shard_map/all_gather | solution.py:43
  95.4 14.1 copy.165
  127.1 97.1 %gather_fusion.1 = bf16[27648,128]{1,0:T(8,128)(2,1)} fusion(bf16[1537,128]{1,0:T(8,128)(2,1)S(1)} %maximum_maximum_fusion.1, s32[27648]{0:T(1024)S(1)} %broadcast_clamp_fusion.1), kind=kCustom, calls=%fused_computation.1 | custom fusion | bytes 14266368 | tf_op jit(solution)/shard_map/gather | solution.py:210
  224.2 11.9 reshape.362
  236.1 13.4 copy.167
  280.5 32.9 %all-reduce.11.cloned.1.call-done = bf16[1024,512]{1,0:T(8,128)(2,1)} async-done(((bf16[1024,512]{1,0:T(8,128)(2,1)}), bf16[1024,512]{1,0:T(8,128)(2,1)}) %all-reduce.11.cloned.1.call-update) | async-done | bytes 1048592 | tf_op jit(solution)/shard_map/psum | solution.py:69
  338.2 11.8 gather_fusion.3
  370.2 24.5 %all-gather.20.cloned.1.call-done = bf16[2048,512]{1,0:T(8,128)(2,1)} async-done(((bf16[2048,128]{1,0:T(8,128)(2,1)}), bf16[2048,512]{1,0:T(8,128)(2,1)}) %all-gather.20.cloned.1.call-update) | async-done | bytes 2097168 | tf_op jit(solution)/shard_map/all_gather | solution.py:59
  417.1 87.3 %while.42 = (s32[]{:T(128)}, bf16[2,1024,8,16]{1,3,2,0:T(8,128)(2,1)}, f32[2,8,1024]{2,1,0:T(8,128)S(1)}, bf16[2,1024,8,16]{1,3,2,0:T(8,128)(2,1)S(1)}, pred[2,1...) while((s32[]{:T(128)}, ...), condition=%wide.region_22.23_spmd, body=%wide.region_19.22_spmd.sunk | while | flops 640803840 | bytes 106188896 | solution.py:268
  418.3 13.5 fusion.214
  431.8 14.2 fusion.215
  446.0 14.7 fusion.216
  461.9 13.5 fusion.214
  475.5 14.2 fusion.215
  489.7 14.7 fusion.216
  513.4 31.1 %reduce-scatter.19.cloned.1.call-done = bf16[128,2048]{1,0:T(8,128)(2,1)} async-done(((bf16[512,2048]{1,0:T(8,128)(2,1)}), bf16[128,2048]{1,0:T(8,128)(2,1)}) %reduce-scatter.19.cloned.1.call-update) | async-done | bytes 524304
  552.8 17.7 all_to_all.84
  591.3 11.4 all-gather.12.cloned.1.call-done
  610.3 10.6 all-gather.14.cloned.1.call-done
  630.7 21.2 %reduce-scatter.13.cloned.1.call-done = bf16[1024,128]{0,1:T(8,128)(2,1)} async-done(((bf16[1024,512]{0,1:T(8,128)(2,1)}), bf16[1024,128]{0,1:T(8,128)(2,1)}) %reduce-scatter.13.cloned.1.call-update) | async-done | bytes 262160 | tf_op jit(solution)/shard_map/reduce_scatter | solution.py:63
  659.4 20.7 %reduce-scatter.11.cloned.1.call-done = bf16[1024,128]{0,1:T(8,128)(2,1)} async-done(((bf16[1024,512]{0,1:T(8,128)(2,1)}), bf16[1024,128]{0,1:T(8,128)(2,1)}) %reduce-scatter.11.cloned.1.call-update) | async-done | bytes 262160 | tf_op jit(solution)/shard_map/reduce_scatter | solution.py:63
  688.2 17.6 all_to_all.85
  714.0 23.7 %all-gather.22.cloned.1.call-done = bf16[2048,512]{1,0:T(8,128)(2,1)} async-done(((bf16[2048,128]{1,0:T(8,128)(2,1)}), bf16[2048,512]{1,0:T(8,128)(2,1)}) %all-gather.22.cloned.1.call-update) | async-done | bytes 2097168 | tf_op jit(solution)/shard_map/all_gather | solution.py:59
  741.5 201.8 %while.43 = (s32[]{:T(128)}, bf16[2,1024,8,16]{1,3,2,0:T(8,128)(2,1)}, bf16[2,1024,8,16]{1,3,2,0:T(8,128)(2,1)}, bf16[2,1024,8,16]{1,3,2,0:T(8,128)(2,1)}, bf16[...) while((s32[]{:T(128)}, ...), condition=%wide.region_38.39_spmd, body=%wide.region_36.38_spmd.sunk | while | flops 1471407104 | bytes 263707840 | solution.py:324
  742.9 13.1 fusion.225
  756.0 23.2 %multiply_reduce_fusion.8 = (f32[8,1024]{1,0:T(8,128)S(1)}, f32[8,1024,1024]{1,2,0:T(8,128)}) fusion(f32[8,1024,1024]{1,2,0:T(8,128)} %fusion.225, f32[8,1024]{1,0:T(8,128)S(1)} %dynamic-slice_bitcast_fusion.2, pred[1024,1024]{0,1:T(8,128)(4,1)S(1)} %or_and_fusion.5, bf16[2,1024,8,16]{1,3,2,0:T(8,128)(2,1)S(1)} %copy-done.16, ...), kind=kOutput, calls=%fused_computation.45.clone.1 | convolution fusion | flops 310370304 | bytes 68748288 | tf_op jit(solution)/shard_map/while/body/eval_jaxpr/qhd,khd->hqk/dot_general | solution.py:137
  779.2 28.2 %multiply_convert_fusion.4 = bf16[8,1024,1024]{1,2,0:T(8,128)(2,1)} fusion(f32[8,1024,1024]{1,2,0:T(8,128)} %get-tuple-element.702, f32[8,1024,1024]{1,2,0:T(8,128)} %fusion.225, f32[8,1024]{1,0:T(8,128)S(1)} %get-tuple-element.703, f32[8,1024]{1,0:T(8,128)S(1)} %dynamic-slice_bitcast_fusion.2, pred[1024,1024]{0,1:T(8,128)(4,1)S(1)} %or_and_fusion.5), kind=kLoop, calls=%fused_computation.44.clone.1 | loop fusion | flops 50331648 | bytes 85000192 | tf_op jit(solution)/shard_map/while/body/eval_jaxpr/convert_element_type | solution.py:145
  807.4 10.9 fusion.227
  827.1 15.2 fusion.228
  843.5 13.1 fusion.225
  856.6 23.2 %multiply_reduce_fusion.8 = (f32[8,1024]{1,0:T(8,128)S(1)}, f32[8,1024,1024]{1,2,0:T(8,128)}) fusion(f32[8,1024,1024]{1,2,0:T(8,128)} %fusion.225, f32[8,1024]{1,0:T(8,128)S(1)} %dynamic-slice_bitcast_fusion.2, pred[1024,1024]{0,1:T(8,128)(4,1)S(1)} %or_and_fusion.5, bf16[2,1024,8,16]{1,3,2,0:T(8,128)(2,1)S(1)} %copy-done.16, ...), kind=kOutput, calls=%fused_computation.45.clone.1 | convolution fusion | flops 310370304 | bytes 68748288 | tf_op jit(solution)/shard_map/while/body/eval_jaxpr/qhd,khd->hqk/dot_general | solution.py:137
  879.8 28.2 %multiply_convert_fusion.4 = bf16[8,1024,1024]{1,2,0:T(8,128)(2,1)} fusion(f32[8,1024,1024]{1,2,0:T(8,128)} %get-tuple-element.702, f32[8,1024,1024]{1,2,0:T(8,128)} %fusion.225, f32[8,1024]{1,0:T(8,128)S(1)} %get-tuple-element.703, f32[8,1024]{1,0:T(8,128)S(1)} %dynamic-slice_bitcast_fusion.2, pred[1024,1024]{0,1:T(8,128)(4,1)S(1)} %or_and_fusion.5), kind=kLoop, calls=%fused_computation.44.clone.1 | loop fusion | flops 50331648 | bytes 85000192 | tf_op jit(solution)/shard_map/while/body/eval_jaxpr/convert_element_type | solution.py:145
  908.0 10.9 fusion.227
  927.7 15.1 fusion.228
  956.0 31.1 %reduce-scatter.21.cloned.1.call-done = bf16[128,2048]{1,0:T(8,128)(2,1)} async-done(((bf16[512,2048]{1,0:T(8,128)(2,1)}), bf16[128,2048]{1,0:T(8,128)(2,1)}) %reduce-scatter.21.cloned.1.call-update) | async-done | bytes 524304
  994.5 17.7 all_to_all.86
  1037.3 13.9 reshape.349
  1051.2 10.3 copy.197
  1089.8 11.4 copy.203
  1106.3 19.4 %scatter_fusion = f32[40,512,128]{2,1,0:T(8,128)} fusion(f32[40,512,128]{2,1,0:T(8,128)} %broadcast_in_dim.161, s32[40]{0:T(128)S(1)} %copy-done.82, f32[40,512,128]{2,1,0:T(8,128)} %copy.203), kind=kCustom, calls=%fused_computation.13 | custom fusion | bytes 31457440 | tf_op jit(solution)/shard_map/scatter | solution.py:404
  1130.5 62.9 %all_to_all.87 = bf16[40,512,128]{2,1,0:T(8,128)(2,1)} all-to-all(bf16[40,512,128]{2,1,0:T(8,128)(2,1)S(1)} %convert_element_type.233), channel_id=1, replica_groups=mesh['pts'=8,'mdl'=4] {'mdl'}, dimensions={0} | all-to-all | bytes 10485760 | tf_op jit(solution)/shard_map/all_to_all | solution.py:47
  1201.3 14.1 copy.205
  1215.5 147.8 %reduce-scatter.15.cloned.1.call-done = bf16[10,64,512]{2,0,1:T(8,128)(2,1)} async-done(((bf16[10,512,512]{2,0,1:T(8,128)(2,1)}), bf16[10,64,512]{2,0,1:T(8,128)(2,1)}) %reduce-scatter.15.cloned.1.call-update) | async-done | bytes 655376 | tf_op jit(solution)/shard_map/reduce_scatter | solution.py:53
  1367.3 10.6 convert_bitcast_fusion
  1377.9 14.1 copy.208
  1402.7 25.9 %psum.119 = f32[16,128]{1,0:T(8,128)S(1)} all-reduce(f32[16,128]{1,0:T(8,128)S(1)} %concatenate.23), channel_id=1, replica_groups=mesh['pts'=8,'mdl'=4] {'pts'}, use_global_device_ids=true, to_apply=%region_68.69 | all-reduce | flops 2048 | bytes 16384 | tf_op jit(solution)/shard_map/psum | solution.py:428
  1431.0 114.3 %reduce-scatter.17.cloned.1.call-done = bf16[64,10,512]{2,1,0:T(8,128)(2,1)} async-done(((bf16[512,10,512]{2,1,0:T(8,128)(2,1)}), bf16[64,10,512]{2,1,0:T(8,128)(2,1)}) %reduce-scatter.17.cloned.1.call-update) | async-done | bytes 655376 | tf_op jit(solution)/shard_map/reduce_scatter | solution.py:435
  1559.8 205.7 %while.44 = (s32[]{:T(128)}, f32[1024,128]{1,0:T(8,128)S(1)}, s32[1024,27]{0,1:T(8,128)}, bf16[1537,512]{1,0:T(8,128)(2,1)S(1)}, bf16[27,512,128]{1,2,0:T(8,128)...) while((s32[]{:T(128)}, f32[1024,128]{1,0:T(8,128)S(1)}, s32[1024,27]{0,1:T(8,128)}, ...), condition=%wide.region_51.52_spmd.clone, body=%wide.region_50.51_spmd.clone.sunk | while | flops 134483968 | bytes 4346013 | solution.py:389
  (527 shorter events, 567.0 us)
Async XLA Ops:
  7.2 1360.1 %copy-start = (f32[10,64,512]{2,1,0:T(8,128)S(1)}, f32[10,64,512]{2,1,0:T(8,128)}, u32[]{:S(2)}) copy-start(f32[10,64,512]{2,1,0:T(8,128)} %param.29) | copy-start | bytes 3932164
  7.2 88.2 %all-gather.10.cloned.1.call-start = ((), (), s32[]{:S(2)}) async-start(), calls=%async_computation.12 | async-start | bytes 5898240 | tf_op jit(solution)/shard_map/all_gather | solution.py:43
  109.5 126.7 %all-to-all-start = ((bf16[10,512,512]{1,0,2:T(8,128)(2,1)}), bf16[10,512,512]{1,0,2:T(8,128)(2,1)}, u32[]{:S(2)}, u32[]{:S(2)}) async-start(bf16[10,512,512]{1,0,2:T(8,128)(2,1)} %copy.165), calls=%async_computation | async-start | bytes 16777216 | tf_op jit(solution)/shard_map/all_to_all | solution.py:39
  115.8 197.6 %all-reduce.11.cloned.1.call-start = ((), (), s32[]{:S(2)}) async-start(), calls=%async_computation.13 | async-start | bytes 2097152 | tf_op jit(solution)/shard_map/psum | solution.py:69
  115.8 11.0 collective-permute-start
  117.1 9.7 collective-permute-start.1
  125.5 98.7 %copy-start.81 = (s32[40]{0:T(128)}, s32[40]{0:T(128)S(1)}, u32[]{:S(2)}) copy-start(s32[40]{0:T(128)S(1)} %compare_select_fusion.7) | copy-start | bytes 484
  126.2 202.1 %copy-start.75 = (s32[1024]{0:T(1024)}, s32[1024]{0:T(1024)S(1)}, u32[]{:S(2)}) copy-start(s32[1024]{0:T(1024)S(1)} %get-tuple-element.535) | copy-start | bytes 12292
  126.8 194.6 %copy-start.71 = (f32[128]{0:T(128)}, f32[128]{0:T(128)S(1)}, u32[]{:S(2)}) copy-start(f32[128]{0:T(128)S(1)} %get-tuple-element.531) | copy-start | bytes 1540
  126.8 200.9 %copy-start.73 = (f32[128]{0:T(128)}, f32[128]{0:T(128)S(1)}, u32[]{:S(2)}) copy-start(f32[128]{0:T(128)S(1)} %get-tuple-element.529) | copy-start | bytes 1540
  126.8 97.4 %copy-start.54 = (bf16[1537]{0:T(1024)(128)(2,1)}, bf16[1537]{0:T(1024)(128)(2,1)S(1)}, u32[]{:S(2)}) copy-start(bf16[1537]{0:T(1024)(128)(2,1)S(1)} %pad.9.clone) | copy-start | bytes 9226
  321.6 28.4 %copy-start.7 = (f32[1024,128]{0,1:T(8,128)}, f32[1024,128]{0,1:T(8,128)S(1)}, u32[]{:S(2)}) copy-start(f32[1024,128]{0,1:T(8,128)S(1)} %get-tuple-element.505) | copy-start | bytes 1572868
  332.4 29.6 %all-to-all-start.1 = ((bf16[8,256,128]{2,1,0:T(8,128)(2,1)}), bf16[8,256,128]{2,1,0:T(8,128)(2,1)S(1)}, u32[]{:S(2)}, u32[]{:S(2)}) async-start(bf16[8,256,128]{2,1,0:T(8,128)(2,1)} %bitcast.38), calls=%async_computation.1 | async-start | bytes 1048576 | tf_op jit(solution)/shard_map/all_to_all | solution.py:81
  337.8 56.9 %all-gather.20.cloned.1.call-start = ((), (), s32[]{:S(2)}) async-start(), calls=%async_computation.23 | async-start | bytes 2621440 | tf_op jit(solution)/shard_map/all_gather | solution.py:59
  370.1 174.4 %reduce-scatter.19.cloned.1.call-start = ((), (), s32[]{:S(2)}) async-start(), calls=%async_computation.25 | async-start | bytes 2621440
  513.3 33.2 %copy-start.76 = (f32[128]{0:T(128)S(1)}, f32[128]{0:T(128)}, u32[]{:S(2)}) copy-start(f32[128]{0:T(128)} %get-tuple-element.525) | copy-start | bytes 1540
  513.4 89.3 %all-gather.12.cloned.1.call-start = ((), (), s32[]{:S(2)}) async-start(), calls=%async_computation.14 | async-start | bytes 1310720 | tf_op jit(solution)/shard_map/all_gather | solution.py:59
  544.5 26.0 %copy-start.58 = (s32[1024]{0:T(1024)S(1)}, s32[1024]{0:T(1024)}, u32[]{:S(2)}) copy-start(s32[1024]{0:T(1024)} %get-tuple-element.534) | copy-start | bytes 12292
  552.8 23.8 %copy-start.8 = (f32[1024,128]{0,1:T(8,128)S(1)}, f32[1024,128]{0,1:T(8,128)}, u32[]{:S(2)}) copy-start(f32[1024,128]{0,1:T(8,128)} %copy-done.7) | copy-start | bytes 1572868
  577.7 102.4 %copy-start.5 = (f32[1024,128]{0,1:T(8,128)}, f32[1024,128]{0,1:T(8,128)S(1)}, u32[]{:S(2)}) copy-start(f32[1024,128]{0,1:T(8,128)S(1)} %get-tuple-element.500) | copy-start | bytes 1572868
  583.9 96.2 %copy-start.40 = (f32[1024]{0:T(1024)}, f32[1024]{0:T(1024)S(1)}, u32[]{:S(2)}) copy-start(f32[1024]{0:T(1024)S(1)} %get-tuple-element.538) | copy-start | bytes 12292
  583.9 96.2 %copy-start.42 = (f32[1024]{0:T(1024)}, f32[1024]{0:T(1024)S(1)}, u32[]{:S(2)}) copy-start(f32[1024]{0:T(1024)S(1)} %get-tuple-element.539) | copy-start | bytes 12292
  584.8 36.1 %all-gather.14.cloned.1.call-start = ((), (), s32[]{:S(2)}) async-start(), calls=%async_computation.16 | async-start | bytes 1310720 | tf_op jit(solution)/shard_map/all_gather | solution.py:59
  585.4 66.5 %reduce-scatter.13.cloned.1.call-start = ((), (), s32[]{:S(2)}) async-start(), calls=%async_computation.17 | async-start | bytes 1310720 | tf_op jit(solution)/shard_map/reduce_scatter | solution.py:63
  627.3 52.8 %reduce-scatter.11.cloned.1.call-start = ((), (), s32[]{:S(2)}) async-start(), calls=%async_computation.15 | async-start | bytes 1310720 | tf_op jit(solution)/shard_map/reduce_scatter | solution.py:63
  627.3 52.8 %copy-start.77 = (f32[128]{0:T(128)S(1)}, f32[128]{0:T(128)}, u32[]{:S(2)}) copy-start(f32[128]{0:T(128)} %get-tuple-element.522) | copy-start | bytes 1540
  630.5 107.2 %all-gather.22.cloned.1.call-start = ((), (), s32[]{:S(2)}) async-start(), calls=%async_computation.24 | async-start | bytes 2621440 | tf_op jit(solution)/shard_map/all_gather | solution.py:59
  630.7 57.5 %copy-start.31 = (bf16[1024,128]{0,1:T(8,128)(2,1)}, bf16[1024,128]{0,1:T(8,128)(2,1)S(1)}, u32[]{:S(2)}) copy-start(bf16[1024,128]{0,1:T(8,128)(2,1)S(1)} %copy.182) | copy-start | bytes 786436
  659.4 46.4 %copy-start.64 = (f32[1024]{0:T(1024)}, f32[1024]{0:T(1024)S(1)}, u32[]{:S(2)}) copy-start(f32[1024]{0:T(1024)S(1)} %get-tuple-element.481) | copy-start | bytes 12292
  659.4 46.3 %copy-start.56 = (f32[1024]{0:T(1024)}, f32[1024]{0:T(1024)S(1)}, u32[]{:S(2)}) copy-start(f32[1024]{0:T(1024)S(1)} %broadcast_multiply_fusion.2) | copy-start | bytes 12292
  713.9 273.2 %reduce-scatter.21.cloned.1.call-start = ((), (), s32[]{:S(2)}) async-start(), calls=%async_computation.26 | async-start | bytes 2621440
  956.0 56.3 %copy-start.59 = (s32[1024]{0:T(1024)S(1)}, s32[1024]{0:T(1024)}, u32[]{:S(2)}) copy-start(s32[1024]{0:T(1024)} %get-tuple-element.534) | copy-start | bytes 12292
  956.0 115.3 %all-reduce.13.cloned.1.call-start = ((), (), s32[]{:S(2)}) async-start(), calls=%async_computation.18 | async-start | bytes 2097152 | tf_op jit(solution)/shard_map/psum | solution.py:69
  994.5 23.2 %copy-start.9 = (f32[1024,128]{0,1:T(8,128)S(1)}, f32[1024,128]{0,1:T(8,128)}, u32[]{:S(2)}) copy-start(f32[1024,128]{0,1:T(8,128)} %copy-done.7) | copy-start | bytes 1572868
  994.5 23.2 %copy-start.51 = (f32[1024]{0:T(1024)S(1)}, f32[1024]{0:T(1024)}, u32[]{:S(2)}) copy-start(f32[1024]{0:T(1024)} %copy-done.50) | copy-start | bytes 12292
  994.5 23.2 %copy-start.53 = (f32[1024]{0:T(1024)S(1)}, f32[1024]{0:T(1024)}, u32[]{:S(2)}) copy-start(f32[1024]{0:T(1024)} %copy-done.52) | copy-start | bytes 12292
  994.5 23.2 %copy-start.74 = (f32[128]{0:T(128)S(1)}, f32[128]{0:T(128)}, u32[]{:S(2)}) copy-start(f32[128]{0:T(128)} %copy-done.73) | copy-start | bytes 1540
  1034.9 180.6 %all-gather.16.cloned.1.call-start = ((), (), s32[]{:S(2)}) async-start(), calls=%async_computation.20 | async-start | bytes 5898240 | tf_op jit(solution)/shard_map/all_gather | solution.py:429
  1037.3 326.1 %reduce-scatter.15.cloned.1.call-start = ((), (), s32[]{:S(2)}) async-start(), calls=%async_computation.19 | async-start | bytes 9437184 | tf_op jit(solution)/shard_map/reduce_scatter | solution.py:53
  1215.4 329.8 %reduce-scatter.17.cloned.1.call-start = ((), (), s32[]{:S(2)}) async-start(), calls=%async_computation.21 | async-start | bytes 9437184 | tf_op jit(solution)/shard_map/reduce_scatter | solution.py:435
  1392.1 36.4 %copy-start.61 = (f32[16,128]{1,0:T(8,128)S(1)}, f32[16,128]{1,0:T(8,128)}, u32[]{:S(2)}) copy-start(f32[16,128]{1,0:T(8,128)} %param.33) | copy-start | bytes 24580
  1392.1 36.4 %copy-start.69 = (f32[16,128]{1,0:T(8,128)S(1)}, f32[16,128]{1,0:T(8,128)}, u32[]{:S(2)}) copy-start(f32[16,128]{1,0:T(8,128)} %param.35) | copy-start | bytes 24580
  1392.1 36.4 %copy-start.70 = (f32[16,128]{1,0:T(8,128)S(1)}, f32[16,128]{1,0:T(8,128)}, u32[]{:S(2)}) copy-start(f32[16,128]{1,0:T(8,128)} %param.34) | copy-start | bytes 24580
  1392.1 37.1 %copy-start.55 = (bf16[1537]{0:T(1024)(128)(2,1)S(1)}, bf16[1537]{0:T(1024)(128)(2,1)}, u32[]{:S(2)}) copy-start(bf16[1537]{0:T(1024)(128)(2,1)} %copy-done.54) | copy-start | bytes 9226
  1392.2 383.9 %all-gather.18.cloned.1.call-start = ((), (), s32[]{:S(2)}) async-start(), calls=%async_computation.22 | async-start | bytes 5898240 | tf_op jit(solution)/shard_map/all_gather | solution.py:458
  1396.1 33.1 %collective-permute-start.2 = (bf16[256,512]{1,0:T(8,128)(2,1)}, bf16[256,512]{1,0:T(8,128)(2,1)}, u32[]{:S(2)}, u32[]{:S(2)}) collective-permute-start(bf16[256,512]{1,0:T(8,128)(2,1)} %get-tuple-element.516), channel_id=1, source_target_pairs={{0,4},{4,8},{8,12},{12,16},{16,20},{20,24},{24,28},{1,5},{5,9},{9,... | collective-permute-start | bytes 786440 | tf_op jit(solution)/shard_map/ppermute | solution.py:30
  1397.4 31.8 %collective-permute-start.3 = (bf16[256,512]{1,0:T(8,128)(2,1)}, bf16[256,512]{1,0:T(8,128)(2,1)}, u32[]{:S(2)}, u32[]{:S(2)}) collective-permute-start(bf16[256,512]{1,0:T(8,128)(2,1)} %get-tuple-element.517), channel_id=1, source_target_pairs={{4,0},{8,4},{12,8},{16,12},{20,16},{24,20},{28,24},{5,1},{9,5},{13... | collective-permute-start | bytes 786440 | tf_op jit(solution)/shard_map/ppermute | solution.py:33
  1428.6 123.1 %copy-start.62 = (f32[16,128]{1,0:T(8,128)}, f32[16,128]{1,0:T(8,128)S(1)}, u32[]{:S(2)}) copy-start(f32[16,128]{1,0:T(8,128)S(1)} %psum.119) | copy-start | bytes 24580
  (66 other events, 529.0 us)
Sparse Core Ops, SparseCore 0:
  10.8 84.5 all-gather.9
  275.3 37.9 all-reduce.10
  370.2 24.4 all-gather.19
  513.5 30.9 reduce-scatter.18
  584.9 17.6 all-gather.11
  604.1 16.8 all-gather.13
  627.4 24.4 reduce-scatter.12
  655.1 24.9 reduce-scatter.10
  714.0 23.6 all-gather.21
  956.1 30.9 reduce-scatter.20
  1035.1 36.1 all-reduce.12
  1073.9 84.4 all-gather.15
  1215.6 147.7 reduce-scatter.14
  1392.2 153.0 reduce-scatter.16
  1559.9 84.2 all-gather.17
where the time goes:
time: 1810 us; the launch traced here: 1790 us
  waiting for transfers between devices  561 us (31%)
  local copies, waits for them, and re-layouts  506 us (28%)
  matrix products  340 us (19%)
  blocking collectives  178 us (10%)
  other arithmetic  162 us (9%)
  starting transfers between devices  23.9 us (1%)
    reduce_scatter x1, waiting for transfers between devices, reduce_rows(): lax.psum_scatter(grad_blocks.astype(jnp.bfloat16), 'pts', scatter_dimensi...  148 us
    gather x27, local copies, waits for them, and re-layouts, conv_turn(): grad_extended[where_from]  137 us
    reduce_scatter x1, waiting for transfers between devices, local(): lax.psum_scatter(jnp.einsum('ual,uaq->luq', left_product, right_product,...  114 us
    gather x2, local copies, waits for them, and re-layouts, local(): gathered = extended[local_ids].reshape(row_count, TAPS * col_count)  109 us
    all_gather x1, waiting for transfers between devices, collect_rows(): return lax.all_gather(owned_rows, 'pts', axis=1, tiled=True)  85.8 us
    all_gather x4, waiting for transfers between devices, widen(): return lax.all_gather(shard_rows, 'mdl', axis=1, tiled=True)  70.3 us
    all_to_all x1, blocking collectives, merge_columns(): lax.all_to_all(grad_blocks.astype(jnp.bfloat16), 'mdl', split_axis=0, con...  62.9 us
    unnamed x17, waiting for transfers between devices  62.9 us
  transfers between devices with their start and end apart: 21, of which 13 were waited for; matrix products, arithmetic and copies ran while one was open for 28% of the time, Pallas kernels for 0%

commit v1 on v0

v1 whole, which is shorter than its diff:
```python
import functools

import jax
import jax.numpy as jnp
from jax import lax
from jax.experimental import pallas as pl
from jax.experimental.pallas import tpu as pltpu
from jax.sharding import PartitionSpec as P

C = 512
HD = 16
FF = 2048
TAPS = 27
HALO = 256
PATCH = 1024
STEP = 5

NORM_EPS = 1e-05
BETA_ONE = 0.9
BETA_TWO = 0.999
ADAM_EPS = 1e-08
VECTOR_RATE = 0.5
MATRIX_DECAY = 0.05
TILE = 256
WINDOW = TILE + 2 * HALO
BF = jnp.bfloat16
F32 = jnp.float32
VMEM_LIMIT = 48 * 1024 * 1024

NN = (((1,), (0,)), ((), ()))
NT = (((1,), (1,)), ((), ()))
TN = (((0,), (0,)), ((), ()))


def dot(a, b, dims=NN):
    return lax.dot_general(a, b, dims, preferred_element_type=F32)


def params(**kw):
    return pltpu.CompilerParams(vmem_limit_bytes=VMEM_LIMIT, **kw)


def one_hot_window(ids_ref, tap, tile):
    row = ids_ref[pl.ds(tap, 1), pl.ds(tile * TILE, TILE)]
    places = lax.broadcasted_iota(jnp.int32, (WINDOW, TILE), 0) + tile * TILE
    return jnp.where(places == row, 1.0, 0.0).astype(BF)


def gather_kernel(ids_ref, ext_ref, out_ref):
    tap = pl.program_id(0)
    for tile in range(out_ref.shape[2] // TILE):
        hot = one_hot_window(ids_ref, tap, tile)
        taken = dot(ext_ref[:, tile * TILE : tile * TILE + WINDOW], hot)
        out_ref[0, :, tile * TILE : (tile + 1) * TILE] = taken.astype(BF)


def gather_taps(ids, ext):
    taps, rows = ids.shape
    cols = ext.shape[0]
    return pl.pallas_call(
        gather_kernel,
        grid=(taps,),
        in_specs=[
            pl.BlockSpec(ids.shape, lambda t: (0, 0)),
            pl.BlockSpec(ext.shape, lambda t: (0, 0)),
        ],
        out_specs=pl.BlockSpec((1, cols, rows), lambda t: (t, 0, 0)),
        out_shape=jax.ShapeDtypeStruct((taps, cols, rows), BF),
        compiler_params=params(),
        cost_estimate=pl.CostEstimate(
            flops=2 * taps * rows * WINDOW * cols * 2,
            bytes_accessed=taps * rows * cols * 2,
            transcendentals=0,
        ),
        name="gather_taps",
    )(ids, ext)


GROUP = 3


def conv_kernel(slot_ref, *refs):
    w_refs, x_ref, out_ref, acc_ref = refs[:GROUP], refs[GROUP], refs[GROUP + 1], refs[GROUP + 2]
    step = pl.program_id(0)

    @pl.when(step == 0)
    def _():
        acc_ref[...] = jnp.zeros_like(acc_ref)

    total = acc_ref[...]
    for j in range(GROUP):
        w = w_refs[j][...].reshape(C, x_ref.shape[1])
        total = total + dot(w, x_ref[j])
    acc_ref[...] = total

    @pl.when(step == pl.num_programs(0) - 1)
    def _():
        out_ref[...] = acc_ref[...].T.astype(BF)


def weight_spec(shape, pick):
    return pl.BlockSpec(
        (shape[0], 1, shape[2], shape[3]), lambda t, slots: (0, slots[pick(t)], 0, 0)
    )


def conv_forward(owner_slot, blocks, taken):
    taps, cols, rows = taken.shape
    specs = [weight_spec(blocks.shape, lambda t, j=j: t * GROUP + j) for j in range(GROUP)]
    return pl.pallas_call(
        conv_kernel,
        grid_spec=pltpu.PrefetchScalarGridSpec(
            num_scalar_prefetch=1,
            grid=(taps // GROUP,),
            in_specs=specs + [pl.BlockSpec((GROUP, cols, rows), lambda t, s: (t, 0, 0))],
            out_specs=pl.BlockSpec((rows, C), lambda t, s: (0, 0)),
            scratch_shapes=[pltpu.VMEM((C, rows), F32)],
        ),
        out_shape=jax.ShapeDtypeStruct((rows, C), BF),
        compiler_params=params(),
        cost_estimate=pl.CostEstimate(
            flops=2 * taps * rows * C * cols,
            bytes_accessed=taps * (rows + C) * cols * 2,
            transcendentals=0,
        ),
        name="conv_forward",
    )(owner_slot, *([blocks] * GROUP), taken)


def tap_grad_kernel(back_ref, x_ref, out_ref):
    grad = dot(back_ref[...], x_ref[0], NT)
    out_ref[...] = grad.astype(BF).reshape(out_ref.shape)


def tap_grads(back, taken, parts):
    taps, cols, rows = taken.shape
    share = C // parts
    return pl.pallas_call(
        tap_grad_kernel,
        grid=(taps,),
        in_specs=[
            pl.BlockSpec((C, rows), lambda t: (0, 0)),
            pl.BlockSpec((1, cols, rows), lambda t: (t, 0, 0)),
        ],
        out_specs=pl.BlockSpec((parts, 1, share, cols), lambda t: (0, t, 0, 0)),
        out_shape=jax.ShapeDtypeStruct((parts, taps, share, cols), BF),
        compiler_params=params(),
        cost_estimate=pl.CostEstimate(
            flops=2 * taps * rows * C * cols,
            bytes_accessed=taps * (rows + C) * cols * 2,
            transcendentals=0,
        ),
        name="tap_grads",
    )(back, taken)


def conv_back_kernel(slot_ref, w_ref, ids_ref, back_ref, out_ref, acc_ref):
    tap = pl.program_id(0)
    cols, rows = acc_ref.shape

    @pl.when(tap == 0)
    def _():
        acc_ref[...] = jnp.zeros_like(acc_ref)

    turned = dot(w_ref[...].reshape(C, cols), back_ref[...], TN).astype(BF)
    for tile in range(rows // TILE):
        hot = one_hot_window(ids_ref, tap, tile)
        acc_ref[:, tile * TILE : (tile + 1) * TILE] += dot(
            turned[:, tile * TILE : tile * TILE + WINDOW], hot
        )

    @pl.when(tap == pl.num_programs(0) - 1)
    def _():
        out_ref[...] = acc_ref[...].T


def conv_back(owner_slot, blocks, ids, back_ext):
    taps, rows = ids.shape
    cols = blocks.shape[3]
    return pl.pallas_call(
        conv_back_kernel,
        grid_spec=pltpu.PrefetchScalarGridSpec(
            num_scalar_prefetch=1,
            grid=(taps,),
            in_specs=[
                weight_spec(blocks.shape, lambda t: taps - 1 - t),
                pl.BlockSpec(ids.shape, lambda t, s: (0, 0)),
                pl.BlockSpec(back_ext.shape, lambda t, s: (0, 0)),
            ],
            out_specs=pl.BlockSpec((rows, cols), lambda t, s: (0, 0)),
            scratch_shapes=[pltpu.VMEM((cols, rows), F32)],
        ),
        out_shape=jax.ShapeDtypeStruct((rows, cols), F32),
        compiler_params=params(),
        cost_estimate=pl.CostEstimate(
            flops=taps * rows * (WINDOW * 4 + 3 * C) * cols,
            bytes_accessed=taps * C * cols * 2,
            transcendentals=0,
        ),
        name="conv_back",
    )(owner_slot, blocks, ids, back_ext)


def head_lanes(ext, cols, head):
    lane = lax.broadcasted_iota(jnp.int32, ext.shape, 1)
    return jnp.where((lane >= cols) | (lane // HD == head), ext, jnp.zeros_like(ext))


def attend_kernel(q_ref, k_ref, v_ref, out_ref, lse_ref):
    head = pl.program_id(0)
    rows, width = q_ref.shape
    keys = k_ref[...]
    values = v_ref[0]
    for tile in range(rows // TILE):
        span = slice(tile * TILE, (tile + 1) * TILE)
        queries = head_lanes(q_ref[span, :], width // 2, head)
        scores = dot(keys, queries, NT)
        top = jnp.max(scores, 0, keepdims=True)
        soft = jnp.exp(scores - top).astype(BF)
        summed = dot(values, soft)
        total = summed[HD : HD + 1]
        out_ref[:, span] = (summed[:HD] / total).astype(BF)
        lse_ref[0, :, span] = top + jnp.log(total)


def attend(q_ext, k_ext, v_aug):
    rows, width = q_ext.shape
    heads = v_aug.shape[0]
    return pl.pallas_call(
        attend_kernel,
        grid=(heads,),
        in_specs=[
            pl.BlockSpec((rows, width), lambda h: (0, 0)),
            pl.BlockSpec((rows, width), lambda h: (0, 0)),
            pl.BlockSpec((1, 2 * HD, rows), lambda h: (h, 0, 0)),
        ],
        out_specs=[
            pl.BlockSpec((HD, rows), lambda h: (h, 0)),
            pl.BlockSpec((1, 1, rows), lambda h: (h, 0, 0)),
        ],
        out_shape=[
            jax.ShapeDtypeStruct((heads * HD, rows), BF),
            jax.ShapeDtypeStruct((heads, 1, rows), F32),
        ],
        compiler_params=params(),
        cost_estimate=pl.CostEstimate(
            flops=2 * heads * rows * rows * width, bytes_accessed=rows * width * 6, transcendentals=heads * rows * rows
        ),
        name="attend",
    )(q_ext, k_ext, v_aug)


def attend_back_kernel(
    q_ref, k_ref, kt_ref, v_ref, do_ref, lse_ref, inner_ref, dq_ref, dk_ref, dv_ref, dk_acc, dv_acc
):
    head = pl.program_id(0)
    rows, width = q_ref.shape
    cols = width // 2

    @pl.when(head == 0)
    def _():
        dk_acc[...] = jnp.zeros_like(dk_acc)
        dv_acc[...] = jnp.zeros_like(dv_acc)

    queries = head_lanes(q_ref[...], cols, head)
    pure = queries[:, :cols]
    grad = head_lanes(do_ref[...], cols, head)
    lse = lse_ref[0]
    inner = inner_ref[0]
    dq = jnp.zeros((HD, rows), F32)
    for tile in range(rows // TILE):
        span = slice(tile * TILE, (tile + 1) * TILE)
        scores = dot(k_ref[span, :], queries, NT)
        soft = jnp.exp(scores - lse)
        grad_soft = dot(v_ref[span, :], grad, NT)
        grad_scores = (soft * (grad_soft - inner)).astype(BF)
        dv_acc[span, :] += dot(soft.astype(BF), grad)
        dk_acc[span, :] += dot(grad_scores, pure)
        dq = dq + dot(kt_ref[:, span], grad_scores)
    dq_ref[...] = (dq * HD ** (-0.5)).astype(BF)

    @pl.when(head == pl.num_programs(0) - 1)
    def _():
        dk_ref[...] = dk_acc[...].astype(BF)
        dv_ref[...] = dv_acc[...].astype(BF)


def attend_back(q_ext, k_ext, keys_t, values, grad, lse, inner):
    rows, width = q_ext.shape
    cols = width // 2
    heads = cols // HD
    whole = lambda h: (0, 0)
    return pl.pallas_call(
        attend_back_kernel,
        grid=(heads,),
        in_specs=[
            pl.BlockSpec((rows, width), whole),
            pl.BlockSpec((rows, width), whole),
            pl.BlockSpec((HD, rows), lambda h: (h, 0)),
            pl.BlockSpec((rows, cols), whole),
            pl.BlockSpec((rows, cols), whole),
            pl.BlockSpec((1, 1, rows), lambda h: (h, 0, 0)),
            pl.BlockSpec((1, 1, rows), lambda h: (h, 0, 0)),
        ],
        out_specs=[
            pl.BlockSpec((HD, rows), lambda h: (h, 0)),
            pl.BlockSpec((rows, cols), whole),
            pl.BlockSpec((rows, cols), whole),
        ],
        out_shape=[
            jax.ShapeDtypeStruct((cols, rows), BF),
            jax.ShapeDtypeStruct((rows, cols), BF),
            jax.ShapeDtypeStruct((rows, cols), BF),
        ],
        scratch_shapes=[pltpu.VMEM((rows, cols), F32), pltpu.VMEM((rows, cols), F32)],
        compiler_params=params(),
        cost_estimate=pl.CostEstimate(
            flops=5 * heads * rows * rows * width, bytes_accessed=rows * width * 20, transcendentals=heads * rows * rows
        ),
        name="attend_back",
    )(q_ext, k_ext, keys_t, values, grad, lse, inner)


def widen(shard_rows):
    return lax.all_gather(shard_rows, "mdl", axis=1, tiled=True)


def add_parts(partial_value):
    return lax.psum_scatter(
        partial_value.astype(BF), "mdl", scatter_dimension=1, tiled=True
    ).astype(F32)


def trade(buffer):
    return lax.all_to_all(buffer, "pts", split_axis=0, concat_axis=0, tiled=True)


def scan_index(row_ids, scan_lengths):
    bounds = jnp.cumsum(scan_lengths)
    return jnp.sum((row_ids[..., None] >= bounds[:-1]).astype(jnp.int32), -1)


def count(mask):
    return jnp.sum(mask.astype(jnp.int32), 1)


def unit_rows(values):
    mean = jnp.mean(values, -1, keepdims=True)
    centred = values - mean
    inv_std = lax.rsqrt(jnp.mean(centred * centred, -1, keepdims=True) + NORM_EPS)
    return centred * inv_std, inv_std


def unit_back(grad_unit, unit, inv_std):
    mean = jnp.mean(grad_unit, -1, keepdims=True)
    cross = jnp.mean(grad_unit * unit, -1, keepdims=True)
    return inv_std * (grad_unit - mean - unit * cross)


def gelu_slope(pre_act):
    return (
        0.5 * (1.0 + lax.erf(pre_act * 0.7071067811865476))
        + pre_act * jnp.exp(-0.5 * pre_act * pre_act) * 0.3989422804014327
    )


def adam(first, second, grad):
    new_first = BETA_ONE * first + (1.0 - BETA_ONE) * grad
    new_second = BETA_TWO * second + (1.0 - BETA_TWO) * grad * grad
    direction = (
        new_first
        / (1.0 - BETA_ONE**STEP)
        / (jnp.sqrt(new_second / (1.0 - BETA_TWO**STEP)) + ADAM_EPS)
    )
    return new_first, new_second, direction


def local(
    points,
    cotangent,
    neighbours,
    scan_lengths,
    to_patch,
    from_patch,
    owner_slot,
    weights,
    row_eigen_basis,
    right_basis,
    first_moment,
    second_moment,
    vectors,
    vector_first,
    vector_second,
):
    rows, cols = points.shape
    slot_count = from_patch.shape[0]
    pts = lax.axis_size("pts")
    mdl = lax.axis_size("mdl")
    pts_index = lax.axis_index("pts")
    mdl_index = lax.axis_index("mdl")
    heads = cols // HD
    ff_blocks = FF // C
    patch_count = slot_count // PATCH
    capacity = 2 * rows // pts
    matrix_rate = 1.6 * C ** (-0.5)

    def own(full):
        return lax.dynamic_slice_in_dim(full, mdl_index * cols, cols, full.ndim - 1)

    spread = lax.all_to_all(
        weights.astype(BF), "mdl", split_axis=2, concat_axis=0, tiled=True
    )
    blocks = lax.all_gather(spread, "pts", axis=0)
    vec = lax.all_gather(vectors, "mdl", axis=1, tiled=True)
    points_full = widen(points)
    cot_full = widen(cotangent)

    def block(b):
        return blocks[:, owner_slot[b]].reshape(C, cols)

    up = [(i, i + 1) for i in range(pts - 1)]
    down = [(i + 1, i) for i in range(pts - 1)]
    low_halo = lax.ppermute(points[rows - HALO :], "pts", up)
    high_halo = lax.ppermute(points[:HALO], "pts", down)
    ext = jnp.concatenate([low_halo, points, high_halo], 0).T
    row_ids = pts_index * rows + jnp.arange(rows, dtype=jnp.int32)
    own_scan = scan_index(row_ids, scan_lengths)
    near = neighbours.T
    usable = (near >= 0) & (scan_index(jnp.maximum(near, 0), scan_lengths) == own_scan[None, :])
    ids = jnp.where(usable, near - (pts_index * rows - HALO), -1)
    taken = gather_taps(ids, ext)
    conv_part = conv_forward(owner_slot, blocks, taken)

    target = to_patch // slot_count
    place = jnp.arange(rows, dtype=jnp.int32)
    rank = count((target[None, :] == target[:, None]) & (place[None, :] < place[:, None]))
    send_pos = target * capacity + rank
    buffer_ids = jnp.arange(pts * capacity, dtype=jnp.int32)
    pack = (buffer_ids[:, None] == send_pos[None, :]).astype(BF)
    held = jnp.zeros((rows + PATCH,), jnp.int32)
    held_patch = jnp.zeros((rows + PATCH,), jnp.int32)
    offset = jnp.int32(0)
    for patch in range(patch_count):
        part = from_patch[patch * PATCH : (patch + 1) * PATCH]
        held = lax.dynamic_update_slice(held, part, (offset,))
        held_patch = lax.dynamic_update_slice(
            held_patch, jnp.full((PATCH,), patch, jnp.int32), (offset,)
        )
        offset = offset + jnp.sum((part >= 0).astype(jnp.int32))
    held = held[:rows]
    held_patch = held_patch[:rows]
    source = held // rows
    arrival = source * capacity + count(
        (source[None, :] == source[:, None]) & (held[None, :] < held[:, None])
    )
    order_key = held_patch * (pts * rows) + held
    order = count(order_key[None, :] < order_key[:, None])
    scan_count = scan_lengths.shape[0]
    held_group = held_patch * scan_count + scan_index(held, scan_lengths)
    sorting = order[None, :] == place[:, None]
    arrival = jnp.sum(jnp.where(sorting, arrival[None, :], 0), 1)
    group = jnp.sum(jnp.where(sorting, held_group[None, :], 0), 1)
    unpack = (buffer_ids[None, :] == arrival[:, None]).astype(BF)
    group_ids = jnp.arange(cols, dtype=jnp.int32)
    same = group[:, None] == group_ids[None, :]
    group_q = same.astype(BF)
    group_k = jnp.where(same | (group_ids[None, :] >= patch_count * scan_count), 0.0, -1e30).astype(BF)

    def to_slots(values):
        return dot(unpack, trade(dot(pack, values).astype(BF))).astype(BF)

    def from_slots(values):
        return dot(pack, trade(dot(unpack, values, TN).astype(BF)), TN).astype(BF)

    pair = jnp.stack([block(TAPS), block(TAPS + 4)])
    pair = lax.all_gather(pair, "mdl", axis=2, tiled=True)
    linear_full, projection_full = pair[0], pair[1]
    hidden = (lax.psum(conv_part, "mdl").astype(F32) + vec[0]).astype(BF)
    mixed = dot(hidden, linear_full) + vec[1]
    mixed_unit, mixed_std = unit_rows(mixed)
    stream_one = points_full.astype(F32) + mixed_unit * vec[2] + vec[3]
    one_unit, one_std = unit_rows(stream_one)
    normed = (one_unit * vec[4] + vec[5]).astype(BF)

    slot_in = widen(to_slots(own(normed)))
    query_map, key_map, value_map = block(TAPS + 1), block(TAPS + 2), block(TAPS + 3)
    projection = block(TAPS + 4)
    queries = (dot(slot_in, query_map) + vectors[6]).astype(BF)
    keys_all = dot(slot_in, key_map).astype(BF)
    values_all = (dot(slot_in, value_map) + vectors[7]).astype(BF)
    q_ext = jnp.concatenate([queries * BF(HD ** (-0.5)), group_q], 1)
    k_ext = jnp.concatenate([keys_all, group_k], 1)
    v_aug = jnp.concatenate(
        [values_all.T.reshape(heads, HD, rows), jnp.ones((heads, HD, rows), BF)], 1
    )
    attended_t, lse = attend(q_ext, k_ext, v_aug)
    attended = attended_t.T
    attended_rows = widen(from_slots(attended))
    branch = (dot(attended_rows, projection_full, NT) + vec[8]).astype(BF)

    stream_two = stream_one + branch.astype(F32)
    two_unit, two_std = unit_rows(stream_two)
    normed_two = (two_unit * vec[9] + vec[10]).astype(BF)
    first_mlp = jnp.concatenate([block(TAPS + 5 + k) for k in range(ff_blocks)], 1)
    second_mlp = jnp.concatenate([block(TAPS + 5 + ff_blocks + k) for k in range(ff_blocks)], 1)
    first_bias = vectors[11 : 11 + ff_blocks].reshape(ff_blocks * cols)
    pre_act = dot(normed_two, first_mlp) + first_bias
    activ = jax.nn.gelu(pre_act, approximate=False).astype(BF)
    out_part = dot(activ, second_mlp, NT)
    result = (own(stream_two) + add_parts(out_part) + vectors[11 + ff_blocks]).astype(BF)
    cot = cotangent.astype(F32)
    grad_pre = (dot(cot_full, second_mlp) * gelu_slope(pre_act)).astype(BF)
    grad_two_part = dot(grad_pre, first_mlp, NT)
    scaled_part = grad_two_part * vec[9]
    row_sums = lax.psum(
        jnp.stack([jnp.sum(scaled_part, 1), jnp.sum(scaled_part * two_unit, 1)]), "mdl"
    )
    grad_normed_two = add_parts(grad_two_part)
    own_two_unit = own(two_unit)
    grad_two = cot + two_std * (
        grad_normed_two * vectors[9]
        - row_sums[0][:, None] / C
        - own_two_unit * row_sums[1][:, None] / C
    )

    grad_branch = grad_two.astype(BF)
    grad_slot = widen(to_slots(grad_branch))
    grad_branch_full = widen(grad_branch)
    grad_attended = dot(grad_slot, projection).astype(BF)
    inner = jnp.sum(
        (grad_attended.astype(F32) * attended.astype(F32)).reshape(rows, heads, HD), -1
    ).T.reshape(heads, 1, rows)
    grad_queries_t, grad_keys, grad_values = attend_back(
        q_ext, k_ext, keys_all.T, values_all, grad_attended, lse, inner
    )
    grad_queries = grad_queries_t.T
    slot_back = (
        dot(grad_queries, query_map, NT)
        + dot(grad_keys, key_map, NT)
        + dot(grad_values, value_map, NT)
    )
    grad_normed = widen(from_slots(add_parts(slot_back).astype(BF))).astype(F32)
    grad_one = grad_branch_full.astype(F32) + unit_back(grad_normed * vec[4], one_unit, one_std)
    own_grad_one = grad_two + own(grad_one - grad_branch_full.astype(F32))
    grad_mixed = unit_back(grad_one * vec[2], mixed_unit, mixed_std).astype(BF)

    back = dot(linear_full, grad_mixed, NT).astype(BF)
    early = [
        dot(hidden, own(grad_mixed), TN),
        dot(slot_in, grad_queries, TN),
        dot(slot_in, grad_keys, TN),
        dot(slot_in, grad_values, TN),
        dot(grad_slot, attended, TN),
    ]
    early += [
        dot(normed_two, grad_pre[:, k * cols : (k + 1) * cols], TN) for k in range(ff_blocks)
    ]
    early += [dot(cot_full, activ[:, k * cols : (k + 1) * cols], TN) for k in range(ff_blocks)]
    early = jnp.stack([e.astype(BF).reshape(pts, C // pts, cols) for e in early], 1)
    early = lax.psum_scatter(early, "pts", scatter_dimension=0)
    late = lax.psum_scatter(tap_grads(back, taken, pts), "pts", scatter_dimension=0)
    summed = jnp.concatenate([late, early], 0)
    block_of_slot = jnp.zeros_like(owner_slot).at[owner_slot].set(
        jnp.arange(owner_slot.shape[0], dtype=jnp.int32)
    )
    reduced = lax.all_to_all(
        summed[block_of_slot], "mdl", split_axis=0, concat_axis=2, tiled=True
    )

    low_back = lax.ppermute(back[:, rows - HALO :], "pts", up)
    high_back = lax.ppermute(back[:, :HALO], "pts", down)
    back_ext = jnp.concatenate([low_back, back, high_back], 1)
    point_grad = own_grad_one + conv_back(owner_slot, blocks, ids, back_ext)

    def total(values):
        return jnp.sum(values.astype(F32), 0)

    vector_local = jnp.stack(
        [
            lax.dynamic_slice_in_dim(jnp.sum(back.astype(F32), 1), mdl_index * cols, cols, 0),
            total(own(grad_mixed)),
            total(own_grad_one * own(mixed_unit)),
            total(own_grad_one),
            total(own(grad_normed) * own(one_unit)),
            total(own(grad_normed)),
            total(grad_queries),
            total(grad_values),
            total(grad_branch),
            total(grad_normed_two * own_two_unit),
            total(grad_normed_two),
        ]
    )
    vector_local = jnp.concatenate(
        [vector_local, total(grad_pre).reshape(ff_blocks, cols), total(cot)[None]], 0
    )
    vector_grad = lax.psum(vector_local, "pts")

    right = lax.all_gather(right_basis.astype(BF), "pts", axis=0)
    right = right.transpose(1, 0, 2, 3).reshape(right_basis.shape[0], C, C)
    left = row_eigen_basis.astype(BF)
    turned = jnp.einsum("brc,bcd->brd", reduced.astype(BF), right, preferred_element_type=F32)
    spread_grad = jnp.einsum(
        "bru,brd->bud", left, turned.astype(BF), preferred_element_type=F32
    ).astype(BF)
    spread_grad = spread_grad.reshape(left.shape[0], pts, C // pts, C).transpose(1, 0, 2, 3)
    rotated = lax.psum_scatter(spread_grad, "pts", scatter_dimension=0).astype(F32)
    new_first, new_second, direction = adam(first_moment, second_moment, rotated)
    turned_back = jnp.einsum(
        "bic,bdc->bid", direction.astype(BF), right, preferred_element_type=F32
    ).astype(BF)
    turned_all = lax.all_gather(turned_back, "pts", axis=0)
    turned_all = turned_all.transpose(1, 0, 2, 3).reshape(left.shape[0], C, C)
    update = jnp.einsum("bua,baf->buf", left, turned_all, preferred_element_type=F32)
    new_weights = weights - matrix_rate * (update + MATRIX_DECAY * weights)
    new_vector_first, new_vector_second, vector_step = adam(
        vector_first, vector_second, vector_grad
    )
    new_vectors = vectors - VECTOR_RATE * vector_step
    return (
        result,
        point_grad,
        reduced.astype(F32),
        new_first,
        new_second,
        new_weights,
        new_weights.astype(BF),
        vector_grad,
        new_vector_first,
        new_vector_second,
        new_vectors,
    )


def solution(mesh):
    by_rows = P("pts", "mdl")
    owned = P("mdl", "pts", None)
    vector = P(None, "mdl")
    return jax.shard_map(
        local,
        mesh=mesh,
        in_specs=(
            by_rows,
            by_rows,
            P("pts", None),
            P(),
            P("pts"),
            P("pts"),
            P(),
            owned,
            owned,
            owned,
            owned,
            owned,
            vector,
            vector,
            vector,
        ),
        out_specs=(
            by_rows,
            by_rows,
            owned,
            owned,
            owned,
            owned,
            owned,
            vector,
            vector,
            vector,
            vector,
        ),
        check_vma=False,
    )
```

time: 1810 us -> 1030 us (0.57)
  local copies, waits for them, and re-layouts: 506 us -> 52.1 us
  matrix products: 340 us -> 82.4 us
  other arithmetic: 162 us -> 40.2 us
  Pallas kernels: 0 us -> 116 us
  blocking collectives: 178 us -> 78.8 us
  between operations: 15.9 us -> 43.1 us
    gather x37 -> x1, local copies, waits for them, and re-layouts: 293 us -> 1.51 us  [local(): summed[block_of_slot]]
    dot_general x68 -> x38, matrix products: 340 us -> 82.4 us  [the longest x35 67.5 us: dot(): return lax.dot_general(a, b, dims, preferred_element_type=F32)]
    pallas_call x0 -> x6, Pallas kernels: none -> 116 us  [the longest x1 22.9 us: attend_back(): pl.pallas_call(attend_back_kernel, grid=(heads,), in_specs=[pl.BlockSpec(...]
    all_gather x3 -> x4, waiting for transfers between devices: 85.8 us -> 190 us  [the longest x1 80.3 us: local(): right = lax.all_gather(right_basis.astype(BF), 'pts', axis=0)]
    reduce_scatter x4 -> x3, waiting for transfers between devices: 304 us -> 217 us  [the longest x1 98.2 us: local(): lax.psum_scatter(spread_grad, 'pts', scatter_dimension=0).astype(F32)]
    convert_element_type x10, other arithmetic: 68 us -> 8.47 us  [the longest x1 1.89 us: local(): (own(stream_two) + add_parts(out_part) + vectors[11 + ff_blocks]).astype(BF)]
    all_to_all x1, blocking collectives: 62.9 us -> 12.4 us  [local(): lax.all_to_all(weights.astype(BF), 'mdl', split_axis=2, concat_axis=0, ti...]
    scatter x5 -> x1, local copies, waits for them, and re-layouts: 40.9 us -> 0.7 us  [local(): jnp.zeros_like(owner_slot).at[owner_slot]]
  transfers between devices with their start and end apart: 21 -> 25, of which waited for: 13 -> 19; matrix products, arithmetic and copies ran while one was open for 28% -> 9% of each run, Pallas kernels for 0% -> 6%
where the time goes in v1:
time: 1030 us; the launch traced here: 1010 us
  waiting for transfers between devices  572 us (56%)
  Pallas kernels  116 us (11%)
  matrix products  82.4 us (8%)
  blocking collectives  78.8 us (8%)
  local copies, waits for them, and re-layouts  52.1 us (5%)
  between operations  43.1 us (4%)
  other arithmetic  40.2 us (4%)
  starting transfers between devices  27.7 us (3%)
    reduce_scatter x1, waiting for transfers between devices, local(): lax.psum_scatter(spread_grad, 'pts', scatter_dimension=0).astype(F32)  98.2 us
    reduce_scatter x1, waiting for transfers between devices, local(): lax.psum_scatter(tap_grads(back, taken, pts), 'pts', scatter_dimension=0)  83.4 us
    all_gather x7, waiting for transfers between devices, widen(): return lax.all_gather(shard_rows, 'mdl', axis=1, tiled=True)  82.9 us
    all_gather x1, waiting for transfers between devices, local(): right = lax.all_gather(right_basis.astype(BF), 'pts', axis=0)  80.3 us
    dot_general x35, matrix products, dot(): return lax.dot_general(a, b, dims, preferred_element_type=F32)  67.5 us
    all_gather x1, waiting for transfers between devices, local(): blocks = lax.all_gather(spread, 'pts', axis=0)  62 us
    unnamed x21, waiting for transfers between devices  59.4 us
    all_to_all x2, blocking collectives, trade(): lax.all_to_all(buffer, 'pts', split_axis=0, concat_axis=0, tiled=True)  35.5 us
  transfers between devices with their start and end apart: 25, of which 19 were waited for; matrix products, arithmetic and copies ran while one was open for 9% of the time, Pallas kernels for 6%

profile of v1, /device:TPU:29, one launch (start us, length us, event | category | flops | bytes accessed | tf_op | source)
XLA Modules:
  0.0 1012.0 jit_solution(4125016068659579585)
XLA Ops:
  11.9 12.4 %all_to_all.81 = bf16[4,2,40960]{2,1,0:T(2,128)(2,1)S(1)} all-to-all(bf16[4,2,40960]{2,1,0:T(2,128)(2,1)S(1)} %reshape.204), channel_id=1, replica_groups=mesh['pts'=8,'mdl'=4] {'mdl'}, dimensions={0} | all-to-all | bytes 1310720 | tf_op jit(solution)/shard_map/all_to_all | solution.py:410
  29.0 4.0 collective-permute-start.1
  34.3 15.2 %gather_taps.1.refs_3_.x_ref = bf16[27,128,1024]{2,1,0:T(8,128)(2,1)} custom-call(s32[27,1024]{1,0:T(8,128)S(1)} %select_bitcast_fusion.ids_ref, bf16[128,1536]{1,0:T(8,128)(2,1)S(1)} %maximum_bitcast_fusion.ext_ref), custom_call_target="tpu_custom_call" | custom-call | flops 10871635968 | bytes 7077888 | tf_op jit(solution)/shard_map/gather_taps/pallas_call | solution.py:60
  49.6 62.0 %all-gather.16.cloned.1.call-done.refs_0_.refs_1_.refs_2_.w_ref = bf16[8,40,64,128]{3,2,1,0:T(8,128)(2,1)} async-done(((bf16[1,40,64,128]{3,2,1,0:T(8,128)(2,1)}), bf16[8,40,64,128]{3,2,1,0:T(8,128)(2,1)}) %all-gather.16.cloned.1.call-update) | async-done | bytes 5242896 | tf_op jit(solution)/shard_map/all_gather | solution.py:413
  111.6 13.5 %conv_forward.1 = bf16[1024,512]{1,0:T(8,128)(2,1)} custom-call(s32[40]{0:T(128)S(1)} %copy-done, bf16[8,40,64,128]{3,2,1,0:T(8,128)(2,1)} %all-gather.16.cloned.1.call-done.refs_0_.refs_1_.refs_2_.w_ref, bf16[8,40,64,128]{3,2,1,0:T(8,128)(2,1)} %all-gather.16.cloned.1.call-done.refs_0_.refs_1_.refs_2_.w_ref, ...), custom_call_target="tpu_custom_call" | custom-call | flops 3623878656 | bytes 10616832 | tf_op jit(solution)/shard_map/conv_forward/pallas_call | solution.py:110
  154.8 5.5 all_gather.48
  163.8 18.2 %all-gather.18.cloned.1.call-done = bf16[2,512,512]{2,1,0:T(8,128)(2,1)} async-done(((bf16[2,512,128]{2,1,0:T(8,128)(2,1)}), bf16[2,512,512]{2,1,0:T(8,128)(2,1)}) %all-gather.18.cloned.1.call-update) | async-done | bytes 1048592 | tf_op jit(solution)/shard_map/all_gather | solution.py:476
  184.8 15.6 %all-gather.14.cloned.1.call-done = bf16[1024,512]{1,0:T(8,128)(2,1)} async-done(((bf16[1024,128]{1,0:T(8,128)(2,1)}), bf16[1024,512]{1,0:T(8,128)(2,1)}) %all-gather.14.cloned.1.call-update) | async-done | bytes 1048592 | tf_op jit(solution)/shard_map/all_gather | solution.py:325
  206.4 5.4 all-to-all-start.1
  215.0 9.7 all-to-all-done.1
  227.7 16.5 %all-gather.20.cloned.1.call-done = bf16[1024,512]{1,0:T(8,128)(2,1)} async-done(((bf16[1024,128]{1,0:T(8,128)(2,1)}), bf16[1024,512]{1,0:T(8,128)(2,1)}) %all-gather.20.cloned.1.call-update) | async-done | bytes 1048592 | tf_op jit(solution)/shard_map/all_gather | solution.py:325
  249.0 20.7 %attend.1 = (bf16[128,1024]{1,0:T(8,128)(2,1)S(1)}, f32[8,1,1024]{2,1,0:T(1,128)S(1)}) custom-call(bf16[1024,256]{1,0:T(8,128)(2,1)S(1)} %copy.135.q_ref, bf16[1024,256]{1,0:T(8,128)(2,1)S(1)} %copy.136.k_ref, bf16[8,32,1024]{2,1,0:T(8,128)(2,1)S(1)} %concatenate.30.v_ref), custom_call_target="tpu_custom_call" | custom-call | flops 4294967296 | bytes 1572864 | tf_op jit(solution)/shard_map/attend/pallas_call | solution.py:229
  271.2 17.9 %all_to_all.82 = bf16[8,256,128]{2,1,0:T(8,128)(2,1)S(1)} all-to-all(bf16[8,256,128]{2,1,0:T(8,128)(2,1)S(1)} %bitcast.257), channel_id=1, replica_groups=mesh['pts'=8,'mdl'=4] {'pts'}, dimensions={0} | all-to-all | bytes 1048576 | tf_op jit(solution)/shard_map/all_to_all | solution.py:335
  289.1 3.1 fusion.48
  293.4 16.2 %all-gather.22.cloned.1.call-done = bf16[1024,512]{1,0:T(8,128)(2,1)} async-done(((bf16[1024,128]{1,0:T(8,128)(2,1)}), bf16[1024,512]{1,0:T(8,128)(2,1)}) %all-gather.22.cloned.1.call-update) | async-done | bytes 1048592 | tf_op jit(solution)/shard_map/all_gather | solution.py:325
  309.7 3.3 fusion.116
  316.3 6.3 fusion.27
  322.6 5.5 all-gather.24.cloned.1.call-done
  328.2 3.7 convert_reduce_fusion.3
  336.1 2.9 copy.139
  341.7 5.3 psum.22
  347.1 13.6 %reduce-scatter.21.cloned.1.call-done = bf16[128,1024]{1,0:T(8,128)(2,1)} async-done(((bf16[512,1024]{1,0:T(8,128)(2,1)}), bf16[128,1024]{1,0:T(8,128)(2,1)}) %reduce-scatter.21.cloned.1.call-update) | async-done | bytes 262160
  365.6 17.6 %all_to_all.83 = bf16[8,256,128]{2,1,0:T(8,128)(2,1)S(1)} all-to-all(bf16[8,256,128]{2,1,0:T(8,128)(2,1)S(1)} %bitcast.258), channel_id=1, replica_groups=mesh['pts'=8,'mdl'=4] {'pts'}, dimensions={0} | all-to-all | bytes 1048576 | tf_op jit(solution)/shard_map/all_to_all | solution.py:335
  385.8 17.4 %all-gather.28.cloned.1.call-done = bf16[1024,512]{1,0:T(8,128)(2,1)} async-done(((bf16[1024,128]{1,0:T(8,128)(2,1)}), bf16[1024,512]{1,0:T(8,128)(2,1)}) %all-gather.28.cloned.1.call-update) | async-done | bytes 1048592 | tf_op jit(solution)/shard_map/all_gather | solution.py:325
  407.0 22.9 %attend_back.1 = (bf16[128,1024]{1,0:T(8,128)(2,1)S(1)}, bf16[1024,128]{1,0:T(8,128)(2,1)S(1)}, bf16[1024,128]{1,0:T(8,128)(2,1)S(1)}) custom-call(bf16[1024,256]{1,0:T(8,128)(2,1)S(1)} %copy.135.q_ref, bf16[1024,256]{1,0:T(8,128)(2,1)S(1)} %copy.136.k_ref, bf16[128,1024]{1,0:T(8,128)(2,1)S(1)} %bitcast.221, bf16[1024,128]{1,0:T(8,128)(2,1)S(1)} %fusion.47.v_ref, ...), custom_call_target="tpu_custom_call" | custom-call | flops 10737418240 | bytes 5242880 | tf_op jit(solution)/shard_map/attend_back/pallas_call | solution.py:293
  432.6 24.6 %reduce-scatter.23.cloned.1.call-done = bf16[128,1024]{1,0:T(8,128)(2,1)} async-done(((bf16[512,1024]{1,0:T(8,128)(2,1)}), bf16[128,1024]{1,0:T(8,128)(2,1)}) %reduce-scatter.23.cloned.1.call-update) | async-done | bytes 262160
  457.2 4.2 fusion.24
  461.5 5.4 all-to-all-start.4
  468.2 11.6 %all-to-all-done.4 = bf16[8,256,128]{2,1,0:T(8,128)(2,1)S(1)} async-done(((bf16[8,256,128]{2,1,0:T(8,128)(2,1)}), bf16[8,256,128]{2,1,0:T(8,128)(2,1)S(1)}, u32[]{:S(2)}, u32[]{:S(2)}) %all-to-all-start.4) | async-done | bytes 524320 | tf_op jit(solution)/shard_map/all_to_all | solution.py:335
  479.8 3.1 fusion.49
  507.4 11.7 %all-gather.26.cloned.1.call-done = bf16[1024,512]{1,0:T(8,128)(2,1)} async-done(((bf16[1024,128]{1,0:T(8,128)(2,1)}), bf16[1024,512]{1,0:T(8,128)(2,1)}) %all-gather.26.cloned.1.call-update) | async-done | bytes 1048592 | tf_op jit(solution)/shard_map/all_gather | solution.py:325
  519.1 3.1 multiply_reduce_fusion.7
  529.5 21.1 %tap_grads.1 = bf16[8,27,64,128]{3,2,1,0:T(8,128)(2,1)} custom-call(bf16[512,1024]{1,0:T(8,128)(2,1)S(1)} %get-tuple-element.113.back_ref, bf16[27,128,1024]{2,1,0:T(8,128)(2,1)} %gather_taps.1.refs_3_.x_ref), custom_call_target="tpu_custom_call" | custom-call | flops 3623878656 | bytes 10616832 | tf_op jit(solution)/shard_map/tap_grads/pallas_call | solution.py:138
  553.6 35.3 %reduce-scatter.15.cloned.1.call-done = bf16[1,13,64,128]{3,2,1,0:T(8,128)(2,1)} async-done(((bf16[8,13,64,128]{3,2,1,0:T(8,128)(2,1)}), bf16[1,13,64,128]{3,2,1,0:T(8,128)(2,1)}) %reduce-scatter.15.cloned.1.call-update) | async-done | bytes 213008 | tf_op jit(solution)/shard_map/reduce_scatter | solution.py:560
  588.9 83.4 %reduce-scatter.13.cloned.1.call-done = bf16[1,27,64,128]{3,2,1,0:T(8,128)(2,1)} async-done(((bf16[8,27,64,128]{3,2,1,0:T(8,128)(2,1)}), bf16[1,27,64,128]{3,2,1,0:T(8,128)(2,1)}) %reduce-scatter.13.cloned.1.call-update) | async-done | bytes 442384 | tf_op jit(solution)/shard_map/reduce_scatter | solution.py:561
  675.0 4.4 all-to-all-start.5
  679.4 80.3 %all-gather.32.cloned.1.call-done = bf16[80,64,512]{2,1,0:T(8,128)(2,1)} async-done(((bf16[10,64,512]{2,1,0:T(8,128)(2,1)}), bf16[80,64,512]{2,1,0:T(8,128)(2,1)}) %all-gather.32.cloned.1.call-update) | async-done | bytes 5242896 | tf_op jit(solution)/shard_map/all_gather | solution.py:598
  759.7 5.5 copy.150
  765.2 7.6 convolution_convert_fusion
  772.8 5.4 copy.171
  782.6 98.2 %reduce-scatter.17.cloned.1.call-done = bf16[1,10,64,512]{3,2,1,0:T(8,128)(2,1)} async-done(((bf16[8,10,64,512]{3,2,1,0:T(8,128)(2,1)}), bf16[1,10,64,512]{3,2,1,0:T(8,128)(2,1)}) %reduce-scatter.17.cloned.1.call-update) | async-done | bytes 655376 | tf_op jit(solution)/shard_map/reduce_scatter | solution.py:606
  884.6 5.1 convolution_convert_fusion.3
  889.8 19.7 %reduce-scatter.19.cloned.1.call-done = bf16[128,1024]{1,0:T(8,128)(2,1)} async-done(((bf16[512,1024]{1,0:T(8,128)(2,1)}), bf16[128,1024]{1,0:T(8,128)(2,1)}) %reduce-scatter.19.cloned.1.call-update) | async-done | bytes 262160
  915.2 4.0 collective-permute-start.3
  924.1 20.0 %psum.23 = f32[16,128]{1,0:T(8,128)S(1)} all-reduce(f32[16,128]{1,0:T(8,128)S(1)} %concatenate.35), channel_id=1, replica_groups=mesh['pts'=8,'mdl'=4] {'pts'}, use_global_device_ids=true, to_apply=%region_42.43 | all-reduce | flops 2048 | bytes 16384 | tf_op jit(solution)/shard_map/psum | solution.py:596
  944.8 22.5 %conv_back.1 = f32[1024,128]{1,0:T(8,128)S(1)} custom-call(s32[40]{0:T(128)S(1)} %copy-done, bf16[8,40,64,128]{3,2,1,0:T(8,128)(2,1)} %all-gather.16.cloned.1.call-done.refs_0_.refs_1_.refs_2_.w_ref, s32[27,1024]{1,0:T(8,128)S(1)} %select_bitcast_fusion.ids_ref, bf16[512,1536]{1,0:T(8,128)(2,1)S(1)} %pad_maximum_fusion.back_ref), custom_call_target="tpu_custom_call" | custom-call | flops 16307453952 | bytes 3538944 | tf_op jit(solution)/shard_map/conv_back/pallas_call | solution.py:180
  969.4 29.8 %all-gather.34.cloned.1.call-done = bf16[80,64,512]{2,1,0:T(8,128)(2,1)} async-done(((bf16[10,64,512]{2,1,0:T(8,128)(2,1)}), bf16[80,64,512]{2,1,0:T(8,128)(2,1)}) %all-gather.34.cloned.1.call-update) | async-done | bytes 5242896 | tf_op jit(solution)/shard_map/all_gather | solution.py:611
  999.2 3.0 copy.152
  (346 shorter events, 125.4 us)
Async XLA Ops:
  7.2 104.4 %all-gather.16.cloned.1.call-start = ((), (), s32[]{:S(2)}) async-start(), calls=%async_computation.13 | async-start | bytes 5898240 | tf_op jit(solution)/shard_map/all_gather | solution.py:413
  27.4 136.4 %all-reduce.4.cloned.1.call-start = ((), (), s32[]{:S(2)}) async-start(), calls=%async_computation.14 | async-start | bytes 2097152 | tf_op jit(solution)/shard_map/psum | solution.py:478
  27.7 5.6 collective-permute-start
  29.0 5.3 collective-permute-start.1
  34.3 77.3 %copy-start = (s32[40]{0:T(128)S(1)}, s32[40]{0:T(128)}, u32[]{:S(2)}) copy-start(s32[40]{0:T(128)} %slot_ref.3) | copy-start | bytes 484
  125.1 57.0 %all-gather.18.cloned.1.call-start = ((), (), s32[]{:S(2)}) async-start(), calls=%async_computation.15 | async-start | bytes 1310720 | tf_op jit(solution)/shard_map/all_gather | solution.py:476
  150.8 12.4 %copy-start.66 = (s32[1024]{0:T(1024)S(1)}, s32[1024]{0:T(1024)}, u32[]{:S(2)}) copy-start(s32[1024]{0:T(1024)} %param.19) | copy-start | bytes 12292
  154.2 46.2 %all-gather.14.cloned.1.call-start = ((), (), s32[]{:S(2)}) async-start(), calls=%async_computation.12 | async-start | bytes 1310720 | tf_op jit(solution)/shard_map/all_gather | solution.py:325
  160.3 23.9 %copy-start.64 = (f32[1,512]{1,0:T(1,128)}, f32[1,512]{1,0:T(1,128)S(1)}, u32[]{:S(2)}) copy-start(f32[1,512]{1,0:T(1,128)S(1)} %get-tuple-element.73) | copy-start | bytes 6148
  160.3 23.9 %copy-start.73 = (f32[1,512]{1,0:T(1,128)}, f32[1,512]{1,0:T(1,128)S(1)}, u32[]{:S(2)}) copy-start(f32[1,512]{1,0:T(1,128)S(1)} %get-tuple-element.77) | copy-start | bytes 6148
  184.8 17.8 %copy-start.60 = (f32[1024]{0:T(1024)}, f32[1024]{0:T(1024)S(1)}, u32[]{:S(2)}) copy-start(f32[1024]{0:T(1024)S(1)} %add_rsqrt_fusion.2) | copy-start | bytes 12292
  206.4 18.3 %all-to-all-start.1 = ((bf16[8,256,128]{2,1,0:T(8,128)(2,1)}), bf16[8,256,128]{2,1,0:T(8,128)(2,1)S(1)}, u32[]{:S(2)}, u32[]{:S(2)}) async-start(bf16[8,256,128]{2,1,0:T(8,128)(2,1)} %bitcast.18), calls=%async_computation.1 | async-start | bytes 1048576 | tf_op jit(solution)/shard_map/all_to_all | solution.py:335
  211.8 32.3 %all-gather.20.cloned.1.call-start = ((), (), s32[]{:S(2)}) async-start(), calls=%async_computation.16 | async-start | bytes 1310720 | tf_op jit(solution)/shard_map/all_gather | solution.py:325
  226.9 19.9 %copy-start.26 = (bf16[8,1,64,128]{3,2,1,0:T(8,128)(2,1)S(1)}, bf16[8,1,64,128]{3,2,1,0:T(8,128)(2,1)}, u32[]{:S(2)}) copy-start(bf16[8,1,64,128]{3,2,1,0:T(8,128)(2,1)} %get-tuple-element.55) | copy-start | bytes 393220
  226.9 82.7 %all-gather.22.cloned.1.call-start = ((), (), s32[]{:S(2)}) async-start(), calls=%async_computation.17 | async-start | bytes 1310720 | tf_op jit(solution)/shard_map/all_gather | solution.py:325
  227.5 134.3 %copy-start.69 = (f32[128]{0:T(128)}, f32[128]{0:T(128)S(1)}, u32[]{:S(2)}) copy-start(f32[128]{0:T(128)S(1)} %get-tuple-element.80) | copy-start | bytes 1540
  292.2 36.0 %all-gather.24.cloned.1.call-start = ((), (), s32[]{:S(2)}) async-start(), calls=%async_computation.18 | async-start | bytes 1310720 | tf_op jit(solution)/shard_map/all_gather | solution.py:325
  293.0 67.7 %reduce-scatter.21.cloned.1.call-start = ((), (), s32[]{:S(2)}) async-start(), calls=%async_computation.28 | async-start | bytes 1310720
  316.2 11.9 %copy-start.44 = (bf16[8,1,64,128]{3,2,1,0:T(8,128)(2,1)S(1)}, bf16[8,1,64,128]{3,2,1,0:T(8,128)(2,1)}, u32[]{:S(2)}) copy-start(bf16[8,1,64,128]{3,2,1,0:T(8,128)(2,1)} %get-tuple-element.46) | copy-start | bytes 393220
  316.2 11.9 %copy-start.46 = (bf16[8,1,64,128]{3,2,1,0:T(8,128)(2,1)S(1)}, bf16[8,1,64,128]{3,2,1,0:T(8,128)(2,1)}, u32[]{:S(2)}) copy-start(bf16[8,1,64,128]{3,2,1,0:T(8,128)(2,1)} %get-tuple-element.47) | copy-start | bytes 393220
  316.3 11.9 %copy-start.47 = (bf16[8,1,64,128]{3,2,1,0:T(8,128)(2,1)S(1)}, bf16[8,1,64,128]{3,2,1,0:T(8,128)(2,1)}, u32[]{:S(2)}) copy-start(bf16[8,1,64,128]{3,2,1,0:T(8,128)(2,1)} %get-tuple-element.48) | copy-start | bytes 393220
  336.0 67.1 %all-gather.28.cloned.1.call-start = ((), (), s32[]{:S(2)}) async-start(), calls=%async_computation.20 | async-start | bytes 1310720 | tf_op jit(solution)/shard_map/all_gather | solution.py:325
  339.0 22.8 %copy-start.17 = (bf16[1024,128]{1,0:T(8,128)(2,1)S(1)}, bf16[1024,128]{1,0:T(8,128)(2,1)}, u32[]{:S(2)}) copy-start(bf16[1024,128]{1,0:T(8,128)(2,1)} %param.16) | copy-start | bytes 786436
  347.0 18.5 %copy-start.56 = (f32[1,1024]{1,0:T(1,128)}, f32[1,1024]{1,0:T(1,128)S(1)}, u32[]{:S(2)}) copy-start(f32[1,1024]{1,0:T(1,128)S(1)} %get-tuple-element.84) | copy-start | bytes 12292
  347.1 18.5 %copy-start.58 = (f32[1,1024]{1,0:T(1,128)}, f32[1,1024]{1,0:T(1,128)S(1)}, u32[]{:S(2)}) copy-start(f32[1,1024]{1,0:T(1,128)S(1)} %get-tuple-element.85) | copy-start | bytes 12292
  385.4 71.9 %reduce-scatter.23.cloned.1.call-start = ((), (), s32[]{:S(2)}) async-start(), calls=%async_computation.29 | async-start | bytes 1310720
  407.0 23.0 %copy-start.27 = (bf16[8,1,64,128]{3,2,1,0:T(8,128)(2,1)S(1)}, bf16[8,1,64,128]{3,2,1,0:T(8,128)(2,1)}, u32[]{:S(2)}) copy-start(bf16[8,1,64,128]{3,2,1,0:T(8,128)(2,1)} %get-tuple-element.55) | copy-start | bytes 393220
  432.6 34.3 %copy-start.8 = (bf16[1024,512]{1,0:T(8,128)(2,1)S(1)}, bf16[1024,512]{1,0:T(8,128)(2,1)}, u32[]{:S(2)}) copy-start(bf16[1024,512]{1,0:T(8,128)(2,1)} %all-gather.24.cloned.1.call-done) | copy-start | bytes 3145732
  461.5 18.3 %all-to-all-start.4 = ((bf16[8,256,128]{2,1,0:T(8,128)(2,1)}), bf16[8,256,128]{2,1,0:T(8,128)(2,1)S(1)}, u32[]{:S(2)}, u32[]{:S(2)}) async-start(bf16[8,256,128]{2,1,0:T(8,128)(2,1)} %bitcast.67), calls=%async_computation.4 | async-start | bytes 1048576 | tf_op jit(solution)/shard_map/all_to_all | solution.py:335
  466.9 38.1 %all-gather.30.cloned.1.call-start = ((), (), s32[]{:S(2)}) async-start(), calls=%async_computation.21 | async-start | bytes 1310720 | tf_op jit(solution)/shard_map/all_gather | solution.py:325
  482.9 36.2 %all-gather.26.cloned.1.call-start = ((), (), s32[]{:S(2)}) async-start(), calls=%async_computation.19 | async-start | bytes 1310720 | tf_op jit(solution)/shard_map/all_gather | solution.py:325
  499.0 89.9 %reduce-scatter.15.cloned.1.call-start = ((), (), s32[]{:S(2)}) async-start(), calls=%async_computation.23 | async-start | bytes 1916928 | tf_op jit(solution)/shard_map/reduce_scatter | solution.py:560
  503.8 15.2 %copy-start.2 = (f32[1024,512]{1,0:T(8,128)S(1)}, f32[1024,512]{1,0:T(8,128)}, u32[]{:S(2)}) copy-start(f32[1024,512]{1,0:T(8,128)} %copy-done.1) | copy-start | bytes 6291460
  507.4 14.8 %copy-start.61 = (f32[1024]{0:T(1024)S(1)}, f32[1024]{0:T(1024)}, u32[]{:S(2)}) copy-start(f32[1024]{0:T(1024)} %copy-done.60) | copy-start | bytes 12292
  527.2 145.1 %reduce-scatter.13.cloned.1.call-start = ((), (), s32[]{:S(2)}) async-start(), calls=%async_computation.22 | async-start | bytes 3981312 | tf_op jit(solution)/shard_map/reduce_scatter | solution.py:561
  550.6 209.1 %all-gather.32.cloned.1.call-start = ((), (), s32[]{:S(2)}) async-start(), calls=%async_computation.25 | async-start | bytes 5898240 | tf_op jit(solution)/shard_map/all_gather | solution.py:598
  675.0 90.2 %all-to-all-start.5 = ((bf16[40,64,128]{2,1,0:T(8,128)(2,1)}), bf16[40,64,128]{2,1,0:T(8,128)(2,1)S(1)}, u32[]{:S(2)}, u32[]{:S(2)}) async-start(bf16[40,64,128]{2,1,0:T(8,128)(2,1)} %gather_fusion), calls=%async_computation.7 | async-start | bytes 1310720 | tf_op jit(solution)/shard_map/all_to_all | solution.py:566
  679.4 201.4 %reduce-scatter.17.cloned.1.call-start = ((), (), s32[]{:S(2)}) async-start(), calls=%async_computation.24 | async-start | bytes 5898240 | tf_op jit(solution)/shard_map/reduce_scatter | solution.py:606
  778.2 131.2 %reduce-scatter.19.cloned.1.call-start = ((), (), s32[]{:S(2)}) async-start(), calls=%async_computation.27 | async-start | bytes 1310720
  782.5 216.7 %all-gather.34.cloned.1.call-start = ((), (), s32[]{:S(2)}) async-start(), calls=%async_computation.26 | async-start | bytes 5898240 | tf_op jit(solution)/shard_map/all_gather | solution.py:611
  884.6 26.6 %copy-start.71 = (f32[128]{0:T(128)S(1)}, f32[128]{0:T(128)}, u32[]{:S(2)}) copy-start(f32[128]{0:T(128)} %get-tuple-element.81) | copy-start | bytes 1540
  889.7 23.4 %copy-start.15 = (bf16[1024,512]{1,0:T(8,128)(2,1)S(1)}, bf16[1024,512]{1,0:T(8,128)(2,1)}, u32[]{:S(2)}) copy-start(bf16[1024,512]{1,0:T(8,128)(2,1)} %all-gather.26.cloned.1.call-done) | copy-start | bytes 3145732
  913.7 31.0 %collective-permute-start.2 = (bf16[512,256]{1,0:T(8,128)(2,1)S(1)}, bf16[512,256]{1,0:T(8,128)(2,1)S(1)}, u32[]{:S(2)}, u32[]{:S(2)}) collective-permute-start(bf16[512,256]{1,0:T(8,128)(2,1)S(1)} %get-tuple-element.62), channel_id=1, source_target_pairs={{0,4},{4,8},{8,12},{12,16},{16,20},{20,24},{24,28},{1,5},{5,9},{9,... | collective-permute-start | bytes 786440 | tf_op jit(solution)/shard_map/ppermute | solution.py:570
  915.2 29.5 %collective-permute-start.3 = (bf16[512,256]{1,0:T(8,128)(2,1)S(1)}, bf16[512,256]{1,0:T(8,128)(2,1)S(1)}, u32[]{:S(2)}, u32[]{:S(2)}) collective-permute-start(bf16[512,256]{1,0:T(8,128)(2,1)S(1)} %get-tuple-element.63), channel_id=1, source_target_pairs={{4,0},{8,4},{12,8},{16,12},{20,16},{24,20},{28,24},{5,1},{9,5},{13... | collective-permute-start | bytes 786440 | tf_op jit(solution)/shard_map/ppermute | solution.py:571
  921.3 22.7 %copy-start.55 = (f32[16,128]{1,0:T(8,128)S(1)}, f32[16,128]{1,0:T(8,128)}, u32[]{:S(2)}) copy-start(f32[16,128]{1,0:T(8,128)} %param.27) | copy-start | bytes 24580
  921.3 22.7 %copy-start.67 = (f32[16,128]{1,0:T(8,128)S(1)}, f32[16,128]{1,0:T(8,128)}, u32[]{:S(2)}) copy-start(f32[16,128]{1,0:T(8,128)} %param.29) | copy-start | bytes 24580
  921.4 22.7 %copy-start.68 = (f32[16,128]{1,0:T(8,128)S(1)}, f32[16,128]{1,0:T(8,128)}, u32[]{:S(2)}) copy-start(f32[16,128]{1,0:T(8,128)} %param.28) | copy-start | bytes 24580
  944.1 23.3 %copy-start.62 = (f32[16,128]{1,0:T(8,128)}, f32[16,128]{1,0:T(8,128)S(1)}, u32[]{:S(2)}) copy-start(f32[16,128]{1,0:T(8,128)S(1)} %psum.23) | copy-start | bytes 24580
  (56 other events, 187.2 us)
Sparse Core Ops, SparseCore 0:
  27.6 83.9 all-gather.15
  125.2 36.7 all-reduce.3
  164.2 17.8 all-gather.17
  183.5 16.8 all-gather.13
  227.0 17.0 all-gather.19
  292.3 17.2 all-gather.21
  311.3 16.8 all-gather.23
  336.1 24.4 reduce-scatter.20
  385.5 17.5 all-gather.27
  432.7 24.4 reduce-scatter.22
  483.0 17.0 all-gather.29
  502.2 16.8 all-gather.25
  527.3 61.5 reduce-scatter.14
  592.4 79.8 reduce-scatter.12
  674.9 84.7 all-gather.31
  778.4 102.4 reduce-scatter.16
  883.8 25.6 reduce-scatter.18
  912.3 86.8 all-gather.33

commit v2 on v1

--- a/solution.py
+++ b/solution.py
@@ -40,6 +40,77 @@
     return pltpu.CompilerParams(vmem_limit_bytes=VMEM_LIMIT, **kw)
 
 
+MESH = pl.DeviceIdType.MESH
+
+
+def push(src, dst, send_sem, recv_sem, **target):
+    return pltpu.make_async_remote_copy(
+        src_ref=src,
+        dst_ref=dst,
+        send_sem=send_sem,
+        recv_sem=recv_sem,
+        device_id=target,
+        device_id_type=MESH,
+    )
+
+
+def greet(peers):
+    barrier = pltpu.get_barrier_semaphore()
+    for peer in peers:
+        pl.semaphore_signal(barrier, inc=1, device_id=peer, device_id_type=MESH)
+    pl.semaphore_wait(barrier, len(peers))
+
+
+def others(index, size):
+    return [lax.rem(index + step, size) for step in range(1, size)]
+
+
+class Layout:
+    def __init__(self, pts, mdl, blocks):
+        self.pts, self.mdl = pts, mdl
+        self.slots = blocks // mdl
+        self.each = min(k for k in range(1, self.slots + 1) if self.slots % k == 0 and self.slots // k <= pts)
+        self.active = self.slots // self.each
+        self.first = (pts - self.active) // 2
+        self.width = mdl // 2 if pts % (mdl // 2) == 0 else 1
+        self.depth = pts // self.width
+
+
+def fetch_copies(plan, src, dst, sems, act):
+    send, recv, here = sems
+    me = lax.axis_index("pts")
+    for i in range(plan.active):
+        target = plan.first + i
+        piece = src.at[pl.ds(i * plan.each, plan.each)]
+
+        @pl.when(me != target)
+        def _():
+            copy = push(piece, dst.at[:, me], send.at[i], recv.at[me], pts=target)
+            if act == "start":
+                copy.start()
+            else:
+                copy.wait_send()
+
+        @pl.when(me == target)
+        def _():
+            copy = pltpu.make_async_copy(piece, dst.at[:, me], here)
+            if act == "start":
+                copy.start()
+            else:
+                copy.wait()
+                for source in others(me, plan.pts):
+                    push(piece, dst.at[:, source], send.at[i], recv.at[source], pts=source).wait_recv()
+
+
+def fetch_sems(plan):
+    dma = pltpu.SemaphoreType.DMA
+    return [dma((plan.active,)), dma((plan.pts,)), dma(())]
+
+
+def fetch_shape(plan, src):
+    return jax.ShapeDtypeStruct((plan.each, plan.pts) + src.shape[1:], src.dtype)
+
+
 def one_hot_window(ids_ref, tap, tile):
     row = ids_ref[pl.ds(tap, 1), pl.ds(tile * TILE, TILE)]
     places = lax.broadcasted_iota(jnp.int32, (WINDOW, TILE), 0) + tile * TILE
@@ -79,8 +150,7 @@
 GROUP = 3
 
 
-def conv_kernel(slot_ref, *refs):
-    w_refs, x_ref, out_ref, acc_ref = refs[:GROUP], refs[GROUP], refs[GROUP + 1], refs[GROUP + 2]
+def conv_kernel(w_ref, x_ref, out_ref, acc_ref):
     step = pl.program_id(0)
 
     @pl.when(step == 0)
@@ -89,8 +159,7 @@
 
     total = acc_ref[...]
     for j in range(GROUP):
-        w = w_refs[j][...].reshape(C, x_ref.shape[1])
-        total = total + dot(w, x_ref[j])
+        total = total + dot(w_ref[:, j].reshape(C, x_ref.shape[1]), x_ref[j])
     acc_ref[...] = total
 
     @pl.when(step == pl.num_programs(0) - 1)
@@ -98,24 +167,18 @@
         out_ref[...] = acc_ref[...].T.astype(BF)
 
 
-def weight_spec(shape, pick):
-    return pl.BlockSpec(
-        (shape[0], 1, shape[2], shape[3]), lambda t, slots: (0, slots[pick(t)], 0, 0)
-    )
-
-
-def conv_forward(owner_slot, blocks, taken):
+def conv_forward(blocks, taken):
     taps, cols, rows = taken.shape
-    specs = [weight_spec(blocks.shape, lambda t, j=j: t * GROUP + j) for j in range(GROUP)]
+    parts, _, share, _ = blocks.shape
     return pl.pallas_call(
         conv_kernel,
-        grid_spec=pltpu.PrefetchScalarGridSpec(
-            num_scalar_prefetch=1,
-            grid=(taps // GROUP,),
-            in_specs=specs + [pl.BlockSpec((GROUP, cols, rows), lambda t, s: (t, 0, 0))],
-            out_specs=pl.BlockSpec((rows, C), lambda t, s: (0, 0)),
-            scratch_shapes=[pltpu.VMEM((C, rows), F32)],
-        ),
+        grid=(taps // GROUP,),
+        in_specs=[
+            pl.BlockSpec((parts, GROUP, share, cols), lambda t: (0, t, 0, 0)),
+            pl.BlockSpec((GROUP, cols, rows), lambda t: (t, 0, 0)),
+        ],
+        out_specs=pl.BlockSpec((rows, C), lambda t: (0, 0)),
+        scratch_shapes=[pltpu.VMEM((C, rows), F32)],
         out_shape=jax.ShapeDtypeStruct((rows, C), BF),
         compiler_params=params(),
         cost_estimate=pl.CostEstimate(
@@ -124,81 +187,160 @@
             transcendentals=0,
         ),
         name="conv_forward",
-    )(owner_slot, *([blocks] * GROUP), taken)
-
-
-def tap_grad_kernel(back_ref, x_ref, out_ref):
-    grad = dot(back_ref[...], x_ref[0], NT)
-    out_ref[...] = grad.astype(BF).reshape(out_ref.shape)
-
-
-def tap_grads(back, taken, parts):
+    )(blocks, taken)
+
+
+PACK = 5
+
+
+def back_kernel(
+    plan, back_ref, x_ref, w_ref, ids_ref, early_ref, out_ref, turn_ref,
+    own, side, acc, far, turn_acc, side_send, side_recv, far_send, far_recv,
+):
+    width, depth = plan.width, plan.depth
+    cols, rows = turn_acc.shape
+    share = C // plan.pts
+    taps = x_ref.shape[0]
+    extra = early_ref.shape[0]
+    groups = own.shape[1]
+    me = lax.axis_index("pts")
+    y, z = lax.rem(me, width), me // width
+    side_peers = [z * width + v for v in others(y, width)]
+    far_peers = [v * width + y for v in others(z, depth)]
+    greet([{"pts": v} for v in side_peers + far_peers])
+
+    def store(block, group, place):
+        grid = block.astype(BF).reshape(depth, width, share, cols)
+        for v in range(width):
+            own[v, group, :, pl.ds(place, 1)] = grid[:, v][:, None]
+
+    def grads(group):
+        low = max(group * PACK, extra)
+        for b in range(group * PACK, min(extra, (group + 1) * PACK)):
+            store(early_ref[b], group, b - group * PACK)
+
+        def one(place, carry):
+            tap = group * PACK + place - extra
+            store(
+                dot(back_ref[:, HALO : HALO + rows], x_ref[pl.ds(tap, 1)][0], NT), group, place
+            )
+            return carry
+
+        if low < (group + 1) * PACK:
+            lax.fori_loop(low - group * PACK, PACK, one, 0)
+
+    def side_copy(group, v):
+        return push(
+            own.at[v, group], side.at[group, y], side_send.at[group, v], side_recv.at[group, y],
+            pts=z * width + v,
+        )
+
+    def side_wait(group, v):
+        return push(
+            own.at[v, group], side.at[group, v], side_send.at[group, v], side_recv.at[group, v],
+            pts=z * width + v,
+        )
+
+    def far_copy(group, v):
+        return push(
+            acc.at[group, v], far.at[group, z], far_send.at[group, v], far_recv.at[group, z],
+            pts=v * width + y,
+        )
+
+    def far_wait(group, v):
+        return push(
+            acc.at[group, v], far.at[group, v], far_send.at[group, v], far_recv.at[group, v],
+            pts=v * width + y,
+        )
+
+    def start_side(group):
+        grads(group)
+        for v in others(y, width):
+            side_copy(group, v).start()
+
+    def start_far(group):
+        total = own[pl.ds(y, 1), group][0].astype(F32)
+        for v in others(y, width):
+            side_wait(group, v).wait_recv()
+            total = total + side[group, pl.ds(v, 1)][0].astype(F32)
+        acc[group] = total.astype(BF)
+        for v in others(z, depth):
+            far_copy(group, v).start()
+
+    def finish(group):
+        total = acc[group, pl.ds(z, 1)][0].astype(F32)
+        for v in others(z, depth):
+            far_wait(group, v).wait_recv()
+            total = total + far[group, pl.ds(v, 1)][0].astype(F32)
+        out_ref[group * PACK : (group + 1) * PACK] = total.astype(BF)
+
+    def turn(tap, carry):
+        weight = w_ref[:, pl.ds(taps - 1 - tap, 1)].reshape(C, cols)
+        turned = dot(weight, back_ref[...], TN).astype(BF)
+        for tile in range(rows // TILE):
+            hot = one_hot_window(ids_ref, tap, tile)
+            turn_acc[:, tile * TILE : (tile + 1) * TILE] += dot(
+                turned[:, tile * TILE : tile * TILE + WINDOW], hot
+            )
+        return carry
+
+    turn_acc[...] = jnp.zeros_like(turn_acc)
+    lag = 2
+    for group in range(groups):
+        start_side(group)
+        if group >= lag:
+            start_far(group - lag)
+    left = list(range(groups - lag, groups))
+    cuts = [taps * i // (len(left) + 1) for i in range(len(left) + 2)]
+    for i, group in enumerate(left):
+        lax.fori_loop(cuts[i], cuts[i + 1], turn, 0)
+        start_far(group)
+    lax.fori_loop(cuts[-2], cuts[-1], turn, 0)
+    turn_ref[...] = turn_acc[...].T
+    for group in range(groups):
+        finish(group)
+    for group in range(groups):
+        for v in others(y, width):
+            side_copy(group, v).wait_send()
+        for v in others(z, depth):
+            far_copy(group, v).wait_send()
+
+
+def back_pass(plan, back_ext, taken, blocks, ids, early):
     taps, cols, rows = taken.shape
-    share = C // parts
+    total = taps + early.shape[0]
+    groups = total // PACK
+    share = C // plan.pts
+    width, depth = plan.width, plan.depth
+    dma = pltpu.SemaphoreType.DMA
+    vmem = pl.BlockSpec(memory_space=pltpu.VMEM)
     return pl.pallas_call(
-        tap_grad_kernel,
-        grid=(taps,),
-        in_specs=[
-            pl.BlockSpec((C, rows), lambda t: (0, 0)),
-            pl.BlockSpec((1, cols, rows), lambda t: (t, 0, 0)),
-        ],
-        out_specs=pl.BlockSpec((parts, 1, share, cols), lambda t: (0, t, 0, 0)),
-        out_shape=jax.ShapeDtypeStruct((parts, taps, share, cols), BF),
-        compiler_params=params(),
+        functools.partial(back_kernel, plan),
+        in_specs=[vmem] * 5,
+        out_specs=[vmem] * 2,
+        out_shape=[
+            jax.ShapeDtypeStruct((total, share, cols), BF),
+            jax.ShapeDtypeStruct((rows, cols), F32),
+        ],
+        scratch_shapes=[
+            pltpu.VMEM((width, groups, depth, PACK, share, cols), BF),
+            pltpu.VMEM((groups, width, depth, PACK, share, cols), BF),
+            pltpu.VMEM((groups, depth, PACK, share, cols), BF),
+            pltpu.VMEM((groups, depth, PACK, share, cols), BF),
+            pltpu.VMEM((cols, rows), F32),
+            dma((groups, width)),
+            dma((groups, width)),
+            dma((groups, depth)),
+            dma((groups, depth)),
+        ],
+        compiler_params=params(collective_id=1, has_side_effects=True),
         cost_estimate=pl.CostEstimate(
-            flops=2 * taps * rows * C * cols,
-            bytes_accessed=taps * (rows + C) * cols * 2,
+            flops=taps * rows * (WINDOW * 4 + 5 * C) * cols,
+            bytes_accessed=30000000,
             transcendentals=0,
         ),
-        name="tap_grads",
-    )(back, taken)
-
-
-def conv_back_kernel(slot_ref, w_ref, ids_ref, back_ref, out_ref, acc_ref):
-    tap = pl.program_id(0)
-    cols, rows = acc_ref.shape
-
-    @pl.when(tap == 0)
-    def _():
-        acc_ref[...] = jnp.zeros_like(acc_ref)
-
-    turned = dot(w_ref[...].reshape(C, cols), back_ref[...], TN).astype(BF)
-    for tile in range(rows // TILE):
-        hot = one_hot_window(ids_ref, tap, tile)
-        acc_ref[:, tile * TILE : (tile + 1) * TILE] += dot(
-            turned[:, tile * TILE : tile * TILE + WINDOW], hot
-        )
-
-    @pl.when(tap == pl.num_programs(0) - 1)
-    def _():
-        out_ref[...] = acc_ref[...].T
-
-
-def conv_back(owner_slot, blocks, ids, back_ext):
-    taps, rows = ids.shape
-    cols = blocks.shape[3]
-    return pl.pallas_call(
-        conv_back_kernel,
-        grid_spec=pltpu.PrefetchScalarGridSpec(
-            num_scalar_prefetch=1,
-            grid=(taps,),
-            in_specs=[
-                weight_spec(blocks.shape, lambda t: taps - 1 - t),
-                pl.BlockSpec(ids.shape, lambda t, s: (0, 0)),
-                pl.BlockSpec(back_ext.shape, lambda t, s: (0, 0)),
-            ],
-            out_specs=pl.BlockSpec((rows, cols), lambda t, s: (0, 0)),
-            scratch_shapes=[pltpu.VMEM((cols, rows), F32)],
-        ),
-        out_shape=jax.ShapeDtypeStruct((rows, cols), F32),
-        compiler_params=params(),
-        cost_estimate=pl.CostEstimate(
-            flops=taps * rows * (WINDOW * 4 + 3 * C) * cols,
-            bytes_accessed=taps * C * cols * 2,
-            transcendentals=0,
-        ),
-        name="conv_back",
-    )(owner_slot, blocks, ids, back_ext)
+        name="back_pass",
+    )(back_ext, taken, blocks, ids, early)
 
 
 def head_lanes(ext, cols, head):
@@ -206,8 +348,29 @@
     return jnp.where((lane >= cols) | (lane // HD == head), ext, jnp.zeros_like(ext))
 
 
-def attend_kernel(q_ref, k_ref, v_ref, out_ref, lse_ref):
+def fetch_step(plan, srcs, dsts, sems):
+    me = lax.axis_index("pts")
+
+    @pl.when(pl.program_id(0) == 0)
+    def _():
+        greet([{"pts": v} for v in others(me, plan.pts)])
+        for src, dst, group in zip(srcs, dsts, sems):
+            fetch_copies(plan, src, dst, group, "start")
+
+
+def fetch_end(plan, srcs, dsts, sems):
+    @pl.when(pl.program_id(0) == pl.num_programs(0) - 1)
+    def _():
+        for src, dst, group in zip(srcs, dsts, sems):
+            fetch_copies(plan, src, dst, group, "wait")
+
+
+def attend_kernel(
+    plan, q_ref, k_ref, v_ref, one, two, out_ref, lse_ref, one_to, two_to, *sems
+):
     head = pl.program_id(0)
+    moves = (plan, (one, two), (one_to, two_to), (sems[:3], sems[3:]))
+    fetch_step(*moves)
     rows, width = q_ref.shape
     keys = k_ref[...]
     values = v_ref[0]
@@ -221,39 +384,50 @@
         total = summed[HD : HD + 1]
         out_ref[:, span] = (summed[:HD] / total).astype(BF)
         lse_ref[0, :, span] = top + jnp.log(total)
-
-
-def attend(q_ext, k_ext, v_aug):
+    fetch_end(*moves)
+
+
+def attend(plan, q_ext, k_ext, v_aug, one, two):
     rows, width = q_ext.shape
     heads = v_aug.shape[0]
     return pl.pallas_call(
-        attend_kernel,
+        functools.partial(attend_kernel, plan),
         grid=(heads,),
         in_specs=[
             pl.BlockSpec((rows, width), lambda h: (0, 0)),
             pl.BlockSpec((rows, width), lambda h: (0, 0)),
             pl.BlockSpec((1, 2 * HD, rows), lambda h: (h, 0, 0)),
+            pl.BlockSpec(memory_space=pl.ANY),
+            pl.BlockSpec(memory_space=pl.ANY),
         ],
         out_specs=[
             pl.BlockSpec((HD, rows), lambda h: (h, 0)),
             pl.BlockSpec((1, 1, rows), lambda h: (h, 0, 0)),
+            pl.BlockSpec(memory_space=pl.ANY),
+            pl.BlockSpec(memory_space=pl.ANY),
         ],
         out_shape=[
             jax.ShapeDtypeStruct((heads * HD, rows), BF),
             jax.ShapeDtypeStruct((heads, 1, rows), F32),
-        ],
-        compiler_params=params(),
+            fetch_shape(plan, one),
+            fetch_shape(plan, two),
+        ],
+        scratch_shapes=fetch_sems(plan) + fetch_sems(plan),
+        compiler_params=params(collective_id=2, has_side_effects=True),
         cost_estimate=pl.CostEstimate(
             flops=2 * heads * rows * rows * width, bytes_accessed=rows * width * 6, transcendentals=heads * rows * rows
         ),
         name="attend",
-    )(q_ext, k_ext, v_aug)
+    )(q_ext, k_ext, v_aug, one, two)
 
 
 def attend_back_kernel(
-    q_ref, k_ref, kt_ref, v_ref, do_ref, lse_ref, inner_ref, dq_ref, dk_ref, dv_ref, dk_acc, dv_acc
+    plan, q_ref, k_ref, kt_ref, v_ref, do_ref, lse_ref, inner_ref, one, two,
+    dq_ref, dk_ref, dv_ref, one_to, two_to, dk_acc, dv_acc, *sems,
 ):
     head = pl.program_id(0)
+    moves = (plan, (one, two), (one_to, two_to), (sems[:3], sems[3:]))
+    fetch_step(*moves)
     rows, width = q_ref.shape
     cols = width // 2
 
@@ -284,14 +458,16 @@
         dk_ref[...] = dk_acc[...].astype(BF)
         dv_ref[...] = dv_acc[...].astype(BF)
 
-
-def attend_back(q_ext, k_ext, keys_t, values, grad, lse, inner):
+    fetch_end(*moves)
+
+
+def attend_back(plan, q_ext, k_ext, keys_t, values, grad, lse, inner, one, two):
     rows, width = q_ext.shape
     cols = width // 2
     heads = cols // HD
     whole = lambda h: (0, 0)
     return pl.pallas_call(
-        attend_back_kernel,
+        functools.partial(attend_back_kernel, plan),
         grid=(heads,),
         in_specs=[
             pl.BlockSpec((rows, width), whole),
@@ -301,67 +477,32 @@
             pl.BlockSpec((rows, cols), whole),
             pl.BlockSpec((1, 1, rows), lambda h: (h, 0, 0)),
             pl.BlockSpec((1, 1, rows), lambda h: (h, 0, 0)),
+            pl.BlockSpec(memory_space=pl.ANY),
+            pl.BlockSpec(memory_space=pl.ANY),
         ],
         out_specs=[
             pl.BlockSpec((HD, rows), lambda h: (h, 0)),
             pl.BlockSpec((rows, cols), whole),
             pl.BlockSpec((rows, cols), whole),
+            pl.BlockSpec(memory_space=pl.ANY),
+            pl.BlockSpec(memory_space=pl.ANY),
         ],
         out_shape=[
             jax.ShapeDtypeStruct((cols, rows), BF),
             jax.ShapeDtypeStruct((rows, cols), BF),
             jax.ShapeDtypeStruct((rows, cols), BF),
-        ],
-        scratch_shapes=[pltpu.VMEM((rows, cols), F32), pltpu.VMEM((rows, cols), F32)],
-        compiler_params=params(),
+            fetch_shape(plan, one),
+            fetch_shape(plan, two),
+        ],
+        scratch_shapes=[pltpu.VMEM((rows, cols), F32), pltpu.VMEM((rows, cols), F32)]
+        + fetch_sems(plan)
+        + fetch_sems(plan),
+        compiler_params=params(collective_id=3, has_side_effects=True),
         cost_estimate=pl.CostEstimate(
             flops=5 * heads * rows * rows * width, bytes_accessed=rows * width * 20, transcendentals=heads * rows * rows
         ),
         name="attend_back",
-    )(q_ext, k_ext, keys_t, values, grad, lse, inner)
-
-
-def widen(shard_rows):
-    return lax.all_gather(shard_rows, "mdl", axis=1, tiled=True)
-
-
-def add_parts(partial_value):
-    return lax.psum_scatter(
-        partial_value.astype(BF), "mdl", scatter_dimension=1, tiled=True
-    ).astype(F32)
-
-
-def trade(buffer):
-    return lax.all_to_all(buffer, "pts", split_axis=0, concat_axis=0, tiled=True)
-
-
-def scan_index(row_ids, scan_lengths):
-    bounds = jnp.cumsum(scan_lengths)
-    return jnp.sum((row_ids[..., None] >= bounds[:-1]).astype(jnp.int32), -1)
-
-
-def count(mask):
-    return jnp.sum(mask.astype(jnp.int32), 1)
-
-
-def unit_rows(values):
-    mean = jnp.mean(values, -1, keepdims=True)
-    centred = values - mean
-    inv_std = lax.rsqrt(jnp.mean(centred * centred, -1, keepdims=True) + NORM_EPS)
-    return centred * inv_std, inv_std
-
-
-def unit_back(grad_unit, unit, inv_std):
-    mean = jnp.mean(grad_unit, -1, keepdims=True)
-    cross = jnp.mean(grad_unit * unit, -1, keepdims=True)
-    return inv_std * (grad_unit - mean - unit * cross)
-
-
-def gelu_slope(pre_act):
-    return (
-        0.5 * (1.0 + lax.erf(pre_act * 0.7071067811865476))
-        + pre_act * jnp.exp(-0.5 * pre_act * pre_act) * 0.3989422804014327
-    )
+    )(q_ext, k_ext, keys_t, values, grad, lse, inner, one, two)
 
 
 def adam(first, second, grad):
@@ -373,6 +514,228 @@
         / (jnp.sqrt(new_second / (1.0 - BETA_TWO**STEP)) + ADAM_EPS)
     )
     return new_first, new_second, direction
+
+
+def owner_kernel(
+    plan, grad_ref, left_ref, right_ref, first_ref, second_ref, rows_ref, result_ref,
+    whole, results, whole_send, whole_recv, whole_here,
+    rows_send, rows_recv, rows_here, back_send, back_recv, back_here,
+):
+    pts, mdl, each = plan.pts, plan.mdl, plan.each
+    slots = plan.slots
+    share, cols = grad_ref.shape[1:]
+    me, plane = lax.axis_index("pts"), lax.axis_index("mdl")
+    is_active = (me >= plan.first) & (me < plan.first + plan.active)
+    greet(
+        [
+            {"pts": p, "mdl": m}
+            for i, p in enumerate([me] + others(me, pts))
+            for j, m in enumerate([plane] + others(plane, mdl))
+            if i + j > 0
+        ]
+    )
+
+    def to_whole(act):
+        for step in range(mdl):
+            m = lax.rem(plane + step, mdl)
+            for i in range(plan.active):
+                target = plan.first + i
+                piece = grad_ref.at[pl.ds(m * slots + i * each, each)]
+                if step == 0:
+
+                    @pl.when(me == target)
+                    def _():
+                        copy = pltpu.make_async_copy(piece, whole.at[me, plane], whole_here)
+                        copy.start() if act == "start" else copy.wait()
+
+                    remote = me != target
+                else:
+                    remote = me >= 0
+
+                @pl.when(remote)
+                def _():
+                    copy = push(
+                        piece, whole.at[me, plane], whole_send.at[step, i],
+                        whole_recv.at[me, plane], pts=target, mdl=m,
+                    )
+                    copy.start() if act == "start" else copy.wait_send()
+
+    def to_rows(act):
+        for m in others(plane, mdl):
+            copy = push(
+                grad_ref.at[pl.ds(m * slots, slots)], rows_ref.at[plane], rows_send.at[m],
+                rows_recv.at[plane], mdl=m,
+            )
+            if act == "start":
+                copy.start()
+            else:
+                copy.wait_send()
+                push(
+                    grad_ref.at[pl.ds(m * slots, slots)], rows_ref.at[m], rows_send.at[m],
+                    rows_recv.at[m], mdl=m,
+                ).wait_recv()
+        copy = pltpu.make_async_copy(
+            grad_ref.at[pl.ds(plane * slots, slots)], rows_ref.at[plane], rows_here
+        )
+        copy.start() if act == "start" else copy.wait()
+
+    to_whole("start")
+    to_rows("start")
+
+    base = (me - plan.first) * each
+
+    def result_copy(k, p):
+        return push(
+            results.at[k, :, p], result_ref.at[base + k], back_send.at[k, p],
+            back_recv.at[base + k], pts=p,
+        )
+
+    def result_here(k):
+        return pltpu.make_async_copy(
+            results.at[k, :, me], result_ref.at[base + k], back_here.at[k]
+        )
+
+    @pl.when(is_active)
+    def _():
+        pltpu.make_async_copy(
+            grad_ref.at[pl.ds(plane * slots + base, each)], whole.at[me, plane], whole_here
+        ).wait()
+        for p_step in range(pts):
+            for m_step in range(mdl):
+                if p_step + m_step > 0:
+                    p, m = lax.rem(me + p_step, pts), lax.rem(plane + m_step, mdl)
+                    push(
+                        grad_ref.at[pl.ds(0, each)], whole.at[p, m], whole_send.at[0, 0],
+                        whole_recv.at[p, m], pts=p, mdl=m,
+                    ).wait_recv()
+        for k in range(each):
+            left = left_ref[k].reshape(C, C)
+            right = right_ref[k].reshape(C, C)
+            turned = jnp.zeros((C, C), F32)
+            for m in range(mdl):
+                columns = whole[:, m, k].reshape(C, cols)
+                half = dot(left, columns, TN).astype(BF)
+                turned = turned + dot(half, right[m * cols : (m + 1) * cols])
+            rotated = turned.astype(BF)
+            _, _, direction = adam(
+                first_ref[k].reshape(C, C).astype(F32),
+                second_ref[k].reshape(C, C).astype(F32),
+                rotated.astype(F32),
+            )
+            update = dot(left, dot(direction.astype(BF), right, NT).astype(BF))
+            results[k, 0] = rotated.reshape(pts, share, C)
+            results[k, 1] = update.astype(BF).reshape(pts, share, C)
+            for p in others(me, pts):
+                result_copy(k, p).start()
+            result_here(k).start()
+
+    to_rows("wait")
+    for i in range(plan.active):
+        source = plan.first + i
+        for k in range(each):
+
+            @pl.when(me != source)
+            def _():
+                push(
+                    results.at[k, :, me], result_ref.at[i * each + k], back_send.at[k, source],
+                    back_recv.at[i * each + k], pts=source,
+                ).wait_recv()
+
+    @pl.when(is_active)
+    def _():
+        for k in range(each):
+            result_here(k).wait()
+            for p in others(me, pts):
+                result_copy(k, p).wait_send()
+
+    for step in range(mdl):
+        m = lax.rem(plane + step, mdl)
+        for i in range(plan.active):
+            target = plan.first + i
+
+            @pl.when((me != target) if step == 0 else (me >= 0))
+            def _():
+                push(
+                    grad_ref.at[pl.ds(m * slots + i * each, each)], whole.at[me, plane],
+                    whole_send.at[step, i], whole_recv.at[me, plane], pts=target, mdl=m,
+                ).wait_send()
+
+
+def owner_update(plan, grads, left, right, first, second):
+    share, cols = grads.shape[1:]
+    pts, mdl, each = plan.pts, plan.mdl, plan.each
+    dma = pltpu.SemaphoreType.DMA
+    vmem = pl.BlockSpec(memory_space=pltpu.VMEM)
+    return pl.pallas_call(
+        functools.partial(owner_kernel, plan),
+        in_specs=[vmem] * 5,
+        out_specs=[vmem] * 2,
+        out_shape=[
+            jax.ShapeDtypeStruct((mdl, plan.slots, share, cols), BF),
+            jax.ShapeDtypeStruct((plan.slots, 2, share, C), BF),
+        ],
+        scratch_shapes=[
+            pltpu.VMEM((pts, mdl, each, share, cols), BF),
+            pltpu.VMEM((each, 2, pts, share, C), BF),
+            dma((mdl, plan.active)),
+            dma((pts, mdl)),
+            dma(()),
+            dma((mdl,)),
+            dma((mdl,)),
+            dma(()),
+            dma((each, pts)),
+            dma((plan.slots,)),
+            dma((each,)),
+        ],
+        compiler_params=params(collective_id=4, has_side_effects=True),
+        cost_estimate=pl.CostEstimate(
+            flops=8 * each * C * C * C, bytes_accessed=10000000, transcendentals=each * C * C
+        ),
+        name="owner_update",
+    )(grads, left, right, first, second)
+
+
+def widen(shard_rows):
+    return lax.all_gather(shard_rows, "mdl", axis=1, tiled=True)
+
+
+def add_parts(partial_value):
+    return lax.psum_scatter(
+        partial_value.astype(BF), "mdl", scatter_dimension=1, tiled=True
+    ).astype(F32)
+
+
+def trade(buffer):
+    return lax.all_to_all(buffer, "pts", split_axis=0, concat_axis=0, tiled=True)
+
+
+def scan_index(row_ids, scan_lengths):
+    bounds = jnp.cumsum(scan_lengths)
+    return jnp.sum((row_ids[..., None] >= bounds[:-1]).astype(jnp.int32), -1)
+
+
+def count(mask):
+    return jnp.sum(mask.astype(jnp.int32), 1)
+
+
+def unit_rows(values):
+    mean = jnp.mean(values, -1, keepdims=True)
+    centred = values - mean
+    inv_std = lax.rsqrt(jnp.mean(centred * centred, -1, keepdims=True) + NORM_EPS)
+    return centred * inv_std, inv_std
+
+
+def unit_back(grad_unit, unit, inv_std):
+    mean = jnp.mean(grad_unit, -1, keepdims=True)
+    cross = jnp.mean(grad_unit * unit, -1, keepdims=True)
+    return inv_std * (grad_unit - mean - unit * cross)
+
+
+def gelu_slope(pre_act):
+    return (
+        0.5 * (1.0 + lax.erf(pre_act * 0.7071067811865476))
+        + pre_act * jnp.exp(-0.5 * pre_act * pre_act) * 0.3989422804014327
+    )
 
 
 def local(
@@ -403,6 +766,7 @@
     patch_count = slot_count // PATCH
     capacity = 2 * rows // pts
     matrix_rate = 1.6 * C ** (-0.5)
+    plan = Layout(pts, mdl, owner_slot.shape[0])
 
     def own(full):
         return lax.dynamic_slice_in_dim(full, mdl_index * cols, cols, full.ndim - 1)
@@ -410,13 +774,13 @@
     spread = lax.all_to_all(
         weights.astype(BF), "mdl", split_axis=2, concat_axis=0, tiled=True
     )
-    blocks = lax.all_gather(spread, "pts", axis=0)
+    blocks = lax.all_gather(spread[owner_slot], "pts", axis=0)
     vec = lax.all_gather(vectors, "mdl", axis=1, tiled=True)
     points_full = widen(points)
     cot_full = widen(cotangent)
 
     def block(b):
-        return blocks[:, owner_slot[b]].reshape(C, cols)
+        return blocks[:, b].reshape(C, cols)
 
     up = [(i, i + 1) for i in range(pts - 1)]
     down = [(i + 1, i) for i in range(pts - 1)]
@@ -429,7 +793,7 @@
     usable = (near >= 0) & (scan_index(jnp.maximum(near, 0), scan_lengths) == own_scan[None, :])
     ids = jnp.where(usable, near - (pts_index * rows - HALO), -1)
     taken = gather_taps(ids, ext)
-    conv_part = conv_forward(owner_slot, blocks, taken)
+    conv_part = conv_forward(blocks, taken)
 
     target = to_patch // slot_count
     place = jnp.arange(rows, dtype=jnp.int32)
@@ -493,7 +857,9 @@
     v_aug = jnp.concatenate(
         [values_all.T.reshape(heads, HD, rows), jnp.ones((heads, HD, rows), BF)], 1
     )
-    attended_t, lse = attend(q_ext, k_ext, v_aug)
+    attended_t, lse, left_whole, right_whole = attend(
+        plan, q_ext, k_ext, v_aug, row_eigen_basis.astype(BF), right_basis.astype(BF)
+    )
     attended = attended_t.T
     attended_rows = widen(from_slots(attended))
     branch = (dot(attended_rows, projection_full, NT) + vec[8]).astype(BF)
@@ -530,8 +896,17 @@
     inner = jnp.sum(
         (grad_attended.astype(F32) * attended.astype(F32)).reshape(rows, heads, HD), -1
     ).T.reshape(heads, 1, rows)
-    grad_queries_t, grad_keys, grad_values = attend_back(
-        q_ext, k_ext, keys_all.T, values_all, grad_attended, lse, inner
+    grad_queries_t, grad_keys, grad_values, first_whole, second_whole = attend_back(
+        plan,
+        q_ext,
+        k_ext,
+        keys_all.T,
+        values_all,
+        grad_attended,
+        lse,
+        inner,
+        first_moment.astype(BF),
+        second_moment.astype(BF),
     )
     grad_queries = grad_queries_t.T
     slot_back = (
@@ -556,21 +931,20 @@
         dot(normed_two, grad_pre[:, k * cols : (k + 1) * cols], TN) for k in range(ff_blocks)
     ]
     early += [dot(cot_full, activ[:, k * cols : (k + 1) * cols], TN) for k in range(ff_blocks)]
-    early = jnp.stack([e.astype(BF).reshape(pts, C // pts, cols) for e in early], 1)
-    early = lax.psum_scatter(early, "pts", scatter_dimension=0)
-    late = lax.psum_scatter(tap_grads(back, taken, pts), "pts", scatter_dimension=0)
-    summed = jnp.concatenate([late, early], 0)
-    block_of_slot = jnp.zeros_like(owner_slot).at[owner_slot].set(
-        jnp.arange(owner_slot.shape[0], dtype=jnp.int32)
-    )
-    reduced = lax.all_to_all(
-        summed[block_of_slot], "mdl", split_axis=0, concat_axis=2, tiled=True
-    )
-
+    early = jnp.stack([e.astype(BF) for e in early])
     low_back = lax.ppermute(back[:, rows - HALO :], "pts", up)
     high_back = lax.ppermute(back[:, :HALO], "pts", down)
     back_ext = jnp.concatenate([low_back, back, high_back], 1)
-    point_grad = own_grad_one + conv_back(owner_slot, blocks, ids, back_ext)
+    summed, conv_grad = back_pass(plan, back_ext, taken, blocks[:, :TAPS], ids, early)
+    point_grad = own_grad_one + conv_grad
+    block_of_slot = jnp.zeros_like(owner_slot).at[owner_slot].set(
+        jnp.arange(owner_slot.shape[0], dtype=jnp.int32)
+    )
+    summed = summed[(block_of_slot + early.shape[0]) % owner_slot.shape[0]]
+    grad_rows, results = owner_update(
+        plan, summed, left_whole, right_whole, first_whole, second_whole
+    )
+    reduced = grad_rows.transpose(1, 2, 0, 3).reshape(plan.slots, C // pts, C)
 
     def total(values):
         return jnp.sum(values.astype(F32), 0)
@@ -595,22 +969,8 @@
     )
     vector_grad = lax.psum(vector_local, "pts")
 
-    right = lax.all_gather(right_basis.astype(BF), "pts", axis=0)
-    right = right.transpose(1, 0, 2, 3).reshape(right_basis.shape[0], C, C)
-    left = row_eigen_basis.astype(BF)
-    turned = jnp.einsum("brc,bcd->brd", reduced.astype(BF), right, preferred_element_type=F32)
-    spread_grad = jnp.einsum(
-        "bru,brd->bud", left, turned.astype(BF), preferred_element_type=F32
-    ).astype(BF)
-    spread_grad = spread_grad.reshape(left.shape[0], pts, C // pts, C).transpose(1, 0, 2, 3)
-    rotated = lax.psum_scatter(spread_grad, "pts", scatter_dimension=0).astype(F32)
-    new_first, new_second, direction = adam(first_moment, second_moment, rotated)
-    turned_back = jnp.einsum(
-        "bic,bdc->bid", direction.astype(BF), right, preferred_element_type=F32
-    ).astype(BF)
-    turned_all = lax.all_gather(turned_back, "pts", axis=0)
-    turned_all = turned_all.transpose(1, 0, 2, 3).reshape(left.shape[0], C, C)
-    update = jnp.einsum("bua,baf->buf", left, turned_all, preferred_element_type=F32)
+    rotated, update = results[:, 0].astype(F32), results[:, 1].astype(F32)
+    new_first, new_second, _ = adam(first_moment, second_moment, rotated)
     new_weights = weights - matrix_rate * (update + MATRIX_DECAY * weights)
     new_vector_first, new_vector_second, vector_step = adam(
         vector_first, vector_second, vector_grad

time: 1030 us -> 789 us (0.77)
  waiting for transfers between devices: 572 us -> 264 us
  Pallas kernels: 116 us -> 237 us
  between operations: 43.1 us -> 18 us
  matrix products: 82.4 us -> 58.3 us
    reduce_scatter x3 -> x0, waiting for transfers between devices: 217 us -> none  [the longest x1 98.2 us: local(): lax.psum_scatter(spread_grad, 'pts', scatter_dimension=0).astype(F32)]
    pallas_call x5, Pallas kernels: 101 us -> 222 us  [the longest x1 79.2 us: owner_update(): pl.pallas_call(functools.partial(owner_kernel, plan), in_specs=[vmem] * 5...]
    all_gather x3 -> x1, waiting for transfers between devices: 172 us -> 61.9 us  [local(): blocks = lax.all_gather(spread[owner_slot], 'pts', axis=0)]
    all_to_all x2 -> x3, blocking collectives: 35.5 us -> 60 us  [trade(): lax.all_to_all(buffer, 'pts', split_axis=0, concat_axis=0, tiled=True)]
    psum x1, waiting for transfers between devices: 0.02 us -> 22.3 us  [local(): hidden = (lax.psum(conv_part, 'mdl').astype(F32) + vec[0]).astype(BF)]
    unnamed x21 -> x16, waiting for transfers between devices: 59.4 us -> 43.1 us
    dot_general x3 -> x0, matrix products: 14.9 us -> none  [the longest x1 7.6 us: local(): jnp.einsum('bru,brd->bud', left, turned.astype(BF), preferred_element_typ...]
    all_gather x7, waiting for transfers between devices: 82.9 us -> 96.6 us  [widen(): return lax.all_gather(shard_rows, 'mdl', axis=1, tiled=True)]
  transfers between devices with their start and end apart: 25 -> 19, of which waited for: 19 -> 15; matrix products, arithmetic and copies ran while one was open for 9% -> 9% of each run, Pallas kernels for 6% -> 2%
where the time goes in v2:
time: 789 us; the launch traced here: 779 us
  waiting for transfers between devices  264 us (33%)
  Pallas kernels  237 us (30%)
  blocking collectives  85 us (11%)
  matrix products  58.3 us (7%)
  other arithmetic  50.4 us (6%)
  local copies, waits for them, and re-layouts  44.9 us (6%)
  starting transfers between devices  21.3 us (3%)
  between operations  18 us (2%)
    all_gather x7, waiting for transfers between devices, widen(): return lax.all_gather(shard_rows, 'mdl', axis=1, tiled=True)  96.6 us
    pallas_call x1, Pallas kernels, owner_update(): pl.pallas_call(functools.partial(owner_kernel, plan), in_specs=[vmem] * 5...  79.2 us
    pallas_call x1, Pallas kernels, back_pass(): pl.pallas_call(functools.partial(back_kernel, plan), in_specs=[vmem] * 5,...  69.6 us
    all_gather x1, waiting for transfers between devices, local(): blocks = lax.all_gather(spread[owner_slot], 'pts', axis=0)  61.9 us
    all_to_all x3, blocking collectives, trade(): lax.all_to_all(buffer, 'pts', split_axis=0, concat_axis=0, tiled=True)  60 us
    dot_general x35, matrix products, dot(): return lax.dot_general(a, b, dims, preferred_element_type=F32)  58.3 us
    unnamed x16, waiting for transfers between devices  43.1 us
    pallas_call x1, Pallas kernels, attend(): pl.pallas_call(functools.partial(attend_kernel, plan), grid=(heads,), in_...  30.2 us
  transfers between devices with their start and end apart: 19, of which 15 were waited for; matrix products, arithmetic and copies ran while one was open for 9% of the time, Pallas kernels for 2%

profile of v2, /device:TPU:29, one launch (start us, length us, event | category | flops | bytes accessed | tf_op | source)
XLA Modules:
  0.0 779.1 jit_solution(9661595759924990864)
XLA Ops:
  12.8 4.1 all-to-all-start
  17.0 9.3 %all-to-all-done = bf16[4,2,40960]{2,1,0:T(2,128)(2,1)S(1)} async-done(((bf16[4,2,40960]{2,1,0:T(2,128)(2,1)}), bf16[4,2,40960]{2,1,0:T(2,128)(2,1)S(1)}, u32[]{:S(2)}, u32[]{:S(2)}) %all-to-all-start) | async-done | bytes 655392 | tf_op jit(solution)/shard_map/all_to_all | solution.py:774
  32.8 4.0 collective-permute-start.1
  38.2 15.2 %gather_taps.1.x_ref = bf16[27,128,1024]{2,1,0:T(8,128)(2,1)} custom-call(s32[27,1024]{1,0:T(8,128)S(1)} %select_bitcast_fusion.ids_ref, bf16[128,1536]{1,0:T(8,128)(2,1)S(1)} %maximum_bitcast_fusion.ext_ref), custom_call_target="tpu_custom_call" | custom-call | flops 10871635968 | bytes 7077888 | tf_op jit(solution)/shard_map/gather_taps/pallas_call | solution.py:131
  53.4 61.9 %all-gather.27.cloned.1.call-done = bf16[320,64,128]{2,1,0:T(8,128)(2,1)} async-done(((bf16[40,64,128]{2,1,0:T(8,128)(2,1)}), bf16[320,64,128]{2,1,0:T(8,128)(2,1)}) %all-gather.27.cloned.1.call-update) | async-done | bytes 5242896 | tf_op jit(solution)/shard_map/all_gather | solution.py:777
  115.3 12.6 %conv_forward.1 = bf16[1024,512]{1,0:T(8,128)(2,1)} custom-call(bf16[8,40,64,128]{3,2,1,0:T(8,128)(2,1)} %bitcast.225, bf16[27,128,1024]{2,1,0:T(8,128)(2,1)} %gather_taps.1.x_ref), custom_call_target="tpu_custom_call" | custom-call | flops 3623878656 | bytes 10616832 | tf_op jit(solution)/shard_map/conv_forward/pallas_call | solution.py:173
  128.0 2.5 fusion.123
  134.5 5.7 all_gather.36
  142.3 22.3 %all-reduce.4.cloned.1.call-done = bf16[1024,512]{1,0:T(8,128)(2,1)} async-done(((bf16[1024,512]{1,0:T(8,128)(2,1)}), bf16[1024,512]{1,0:T(8,128)(2,1)}) %all-reduce.4.cloned.1.call-update) | async-done | bytes 1048592 | tf_op jit(solution)/shard_map/psum | solution.py:842
  164.6 20.3 %all-gather.13.cloned.1.call-done = bf16[2,512,512]{2,1,0:T(8,128)(2,1)} async-done(((bf16[2,512,128]{2,1,0:T(8,128)(2,1)}), bf16[2,512,512]{2,1,0:T(8,128)(2,1)}) %all-gather.13.cloned.1.call-update) | async-done | bytes 1048592 | tf_op jit(solution)/shard_map/all_gather | solution.py:840
  187.6 15.6 %all-gather.11.cloned.1.call-done = bf16[1024,512]{1,0:T(8,128)(2,1)} async-done(((bf16[1024,128]{1,0:T(8,128)(2,1)}), bf16[1024,512]{1,0:T(8,128)(2,1)}) %all-gather.11.cloned.1.call-update) | async-done | bytes 1048592 | tf_op jit(solution)/shard_map/all_gather | solution.py:699
  210.5 5.4 all-to-all-start.1
  219.1 9.7 %all-to-all-done.1 = bf16[8,256,128]{2,1,0:T(8,128)(2,1)S(1)} async-done(((bf16[8,256,128]{2,1,0:T(8,128)(2,1)}), bf16[8,256,128]{2,1,0:T(8,128)(2,1)S(1)}, u32[]{:S(2)}, u32[]{:S(2)}) %all-to-all-start.1) | async-done | bytes 524320 | tf_op jit(solution)/shard_map/all_to_all | solution.py:709
  234.0 14.2 %all-gather.15.cloned.1.call-done = bf16[1024,512]{1,0:T(8,128)(2,1)} async-done(((bf16[1024,128]{1,0:T(8,128)(2,1)}), bf16[1024,512]{1,0:T(8,128)(2,1)}) %all-gather.15.cloned.1.call-update) | async-done | bytes 1048592 | tf_op jit(solution)/shard_map/all_gather | solution.py:699
  255.2 30.2 %attend.1 = (bf16[128,1024]{1,0:T(8,128)(2,1)S(1)}, f32[8,1,1024]{2,1,0:T(1,128)S(1)}, bf16[2,8,64,512]{3,2,1,0:T(8,128)(2,1)S(1)}, bf16[2,8,64,512]{3,2,1,0:T(8,128)(2,1)S(1)}) custom-call(bf16[1024,256]{1,0:T(8,128)(2,1)S(1)} %copy.145.q_ref, bf16[1024,256]{1,0:T(8,128)(2,1)S(1)} %copy.146.k_ref, bf16[8,32,1024]{2,1,0:T(8,128)(2,1)S(1)} %concatenate.27.v_ref, ...), custom_call_target="tpu_custom_call" | custom-call | flops 4294967296 | bytes 1572864 | tf_op jit(solution)/shard_map/attend/pallas_call | solution.py:393
  287.0 24.5 %all_to_all.66 = bf16[8,256,128]{2,1,0:T(8,128)(2,1)S(1)} all-to-all(bf16[8,256,128]{2,1,0:T(8,128)(2,1)S(1)} %bitcast.246), channel_id=1, replica_groups=mesh['pts'=8,'mdl'=4] {'pts'}, dimensions={0} | all-to-all | bytes 1048576 | tf_op jit(solution)/shard_map/all_to_all | solution.py:709
  311.5 3.1 fusion.47
  316.0 16.4 %all-gather.17.cloned.1.call-done = bf16[1024,512]{1,0:T(8,128)(2,1)} async-done(((bf16[1024,128]{1,0:T(8,128)(2,1)}), bf16[1024,512]{1,0:T(8,128)(2,1)}) %all-gather.17.cloned.1.call-update) | async-done | bytes 1048592 | tf_op jit(solution)/shard_map/all_gather | solution.py:699
  332.4 3.1 fusion.127
  338.0 6.3 fusion.27
  344.3 6.6 all-gather.19.cloned.1.call-done
  350.9 3.7 convert_reduce_fusion.3
  356.7 2.7 convert_bitcast_fusion.1
  359.5 2.9 copy.149
  362.5 2.7 multiply_reduce_fusion.6
  365.2 5.3 psum.22
  370.5 13.5 %reduce-scatter.12.cloned.1.call-done = bf16[128,1024]{1,0:T(8,128)(2,1)} async-done(((bf16[512,1024]{1,0:T(8,128)(2,1)}), bf16[128,1024]{1,0:T(8,128)(2,1)}) %reduce-scatter.12.cloned.1.call-update) | async-done | bytes 262160
  389.0 17.7 %all_to_all.67 = bf16[8,256,128]{2,1,0:T(8,128)(2,1)S(1)} all-to-all(bf16[8,256,128]{2,1,0:T(8,128)(2,1)S(1)} %bitcast.247), channel_id=1, replica_groups=mesh['pts'=8,'mdl'=4] {'pts'}, dimensions={0} | all-to-all | bytes 1048576 | tf_op jit(solution)/shard_map/all_to_all | solution.py:709
  412.7 14.0 %all-gather.23.cloned.1.call-done = bf16[1024,512]{1,0:T(8,128)(2,1)} async-done(((bf16[1024,128]{1,0:T(8,128)(2,1)}), bf16[1024,512]{1,0:T(8,128)(2,1)}) %all-gather.23.cloned.1.call-update) | async-done | bytes 1048592 | tf_op jit(solution)/shard_map/all_gather | solution.py:699
  426.8 2.4 bitcast_multiply_fusion
  434.1 30.1 %attend_back.1 = (bf16[128,1024]{1,0:T(8,128)(2,1)S(1)}, bf16[1024,128]{1,0:T(8,128)(2,1)S(1)}, bf16[1024,128]{1,0:T(8,128)(2,1)S(1)}, bf16[2,8,64,512]{3,2,1,0:T(8,128)(2,1)S(1)}, bf16[2,8,64,512]{3,2,1,0:T(8,128)(2,1)S(1)}) custom-call(bf16[1024,256]{1,0:T(8,128)(2,1)S(1)} %copy.145.q_ref, bf16[1024,256]{1,0:T(8,128)(2,1)S(1)} %copy-done.1, ...), custom_call_target="tpu_custom_call" | custom-call | flops 10737418240 | bytes 5242880 | tf_op jit(solution)/shard_map/attend_back/pallas_call | solution.py:469
  467.2 2.4 copy.173
  473.3 27.6 %reduce-scatter.14.cloned.1.call-done = bf16[128,1024]{1,0:T(8,128)(2,1)} async-done(((bf16[512,1024]{1,0:T(8,128)(2,1)}), bf16[128,1024]{1,0:T(8,128)(2,1)}) %reduce-scatter.14.cloned.1.call-update) | async-done | bytes 262160
  501.0 3.4 fusion.24
  504.5 17.8 %all_to_all.68 = bf16[8,256,128]{2,1,0:T(8,128)(2,1)S(1)} all-to-all(bf16[8,256,128]{2,1,0:T(8,128)(2,1)S(1)} %bitcast.242), channel_id=1, replica_groups=mesh['pts'=8,'mdl'=4] {'pts'}, dimensions={0} | all-to-all | bytes 1048576 | tf_op jit(solution)/shard_map/all_to_all | solution.py:709
  522.2 3.1 fusion.48
  526.2 4.7 slice.248.w_ref
  533.8 14.0 %all-gather.21.cloned.1.call-done = bf16[1024,512]{1,0:T(8,128)(2,1)} async-done(((bf16[1024,128]{1,0:T(8,128)(2,1)}), bf16[1024,512]{1,0:T(8,128)(2,1)}) %all-gather.21.cloned.1.call-update) | async-done | bytes 1048592 | tf_op jit(solution)/shard_map/all_gather | solution.py:699
  547.9 2.9 convert_element_type.300
  551.1 15.8 %all-gather.25.cloned.1.call-done = bf16[1024,512]{1,0:T(8,128)(2,1)} async-done(((bf16[1024,128]{1,0:T(8,128)(2,1)}), bf16[1024,512]{1,0:T(8,128)(2,1)}) %all-gather.25.cloned.1.call-update) | async-done | bytes 1048592 | tf_op jit(solution)/shard_map/all_gather | solution.py:699
  566.9 2.4 multiply_reduce_fusion.8
  569.4 2.8 multiply_reduce_fusion.7
  581.5 4.7 collective-permute-start.3
  586.2 2.7 convert_reduce_fusion.5
  590.5 14.0 %psum.23 = f32[16,128]{1,0:T(8,128)S(1)} all-reduce(f32[16,128]{1,0:T(8,128)S(1)} %concatenate.31), channel_id=1, replica_groups=mesh['pts'=8,'mdl'=4] {'pts'}, use_global_device_ids=true, to_apply=%region_39.40 | all-reduce | flops 2048 | bytes 16384 | tf_op jit(solution)/shard_map/psum | solution.py:970
  612.5 69.6 %back_pass.1 = (bf16[40,64,128]{2,1,0:T(8,128)(2,1)S(1)}, f32[1024,128]{1,0:T(8,128)S(1)}) custom-call(bf16[512,1536]{1,0:T(8,128)(2,1)S(1)} %pad_maximum_fusion.back_ref, bf16[27,128,1024]{2,1,0:T(8,128)(2,1)} %gather_taps.1.x_ref, bf16[8,27,64,128]{3,2,1,0:T(8,128)(2,1)} %slice.248.w_ref, s32[27,1024]{1,0:T(8,128)S(1)} %select_bitcast_fusion.ids_ref, ...), custom_call_target="tpu_custom_call" | custom-call | flops 19931332608 | bytes 30000000 | tf_op jit(solution)/shard_map/back_pass/pallas_call | solution.py:317
  686.5 79.2 %owner_update.1 = (bf16[4,10,64,128]{3,2,1,0:T(8,128)(2,1)S(1)}, bf16[10,2,64,512]{3,2,1,0:T(8,128)(2,1)}) custom-call(bf16[40,64,128]{2,1,0:T(8,128)(2,1)S(1)} %gather_fusion.1, bf16[2,8,64,512]{3,2,1,0:T(8,128)(2,1)S(1)} %copy-done.6, bf16[2,8,64,512]{3,2,1,0:T(8,128)(2,1)S(1)} %copy-done.8, bf16[2,8,64,512]{3,2,1,0:T(8,128)(2,1)S(1)} %copy-done.10, ...), custom_call_target="tpu_custom_call" | custom-call | flops 2147483648 | bytes 10000000 | tf_op jit(solution)/shard_map/owner_update/pallas_call | solution.py:669
  767.5 3.8 fusion.121
  (369 shorter events, 101.9 us)
Async XLA Ops:
  12.8 13.5 %all-to-all-start = ((bf16[4,2,40960]{2,1,0:T(2,128)(2,1)}), bf16[4,2,40960]{2,1,0:T(2,128)(2,1)S(1)}, u32[]{:S(2)}, u32[]{:S(2)}) async-start(bf16[4,2,40960]{2,1,0:T(2,128)(2,1)} %reshape.206), calls=%async_computation | async-start | bytes 1310720 | tf_op jit(solution)/shard_map/all_to_all | solution.py:774
  17.0 98.3 %all-gather.27.cloned.1.call-start = ((), (), s32[]{:S(2)}) async-start(), calls=%async_computation.17 | async-start | bytes 5898240 | tf_op jit(solution)/shard_map/all_gather | solution.py:777
  31.3 133.3 %all-reduce.4.cloned.1.call-start = ((), (), s32[]{:S(2)}) async-start(), calls=%async_computation.9 | async-start | bytes 2097152 | tf_op jit(solution)/shard_map/psum | solution.py:842
  31.5 5.6 collective-permute-start
  32.8 5.3 collective-permute-start.1
  128.0 56.9 %all-gather.13.cloned.1.call-start = ((), (), s32[]{:S(2)}) async-start(), calls=%async_computation.10 | async-start | bytes 1310720 | tf_op jit(solution)/shard_map/all_gather | solution.py:840
  130.5 117.7 %copy-start.42 = (bf16[8,1,64,128]{3,2,1,0:T(8,128)(2,1)}, bf16[8,1,64,128]{3,2,1,0:T(8,128)(2,1)S(1)}, u32[]{:S(2)}) copy-start(bf16[8,1,64,128]{3,2,1,0:T(8,128)(2,1)S(1)} %get-tuple-element.74) | copy-start | bytes 393220
  130.5 122.6 %copy-start.40 = (bf16[8,1,64,128]{3,2,1,0:T(8,128)(2,1)}, bf16[8,1,64,128]{3,2,1,0:T(8,128)(2,1)S(1)}, u32[]{:S(2)}) copy-start(bf16[8,1,64,128]{3,2,1,0:T(8,128)(2,1)S(1)} %get-tuple-element.72) | copy-start | bytes 393220
  131.9 71.4 %all-gather.11.cloned.1.call-start = ((), (), s32[]{:S(2)}) async-start(), calls=%async_computation.8 | async-start | bytes 1310720 | tf_op jit(solution)/shard_map/all_gather | solution.py:699
  140.8 46.2 %copy-start.78 = (f32[1,512]{1,0:T(1,128)}, f32[1,512]{1,0:T(1,128)S(1)}, u32[]{:S(2)}) copy-start(f32[1,512]{1,0:T(1,128)S(1)} %get-tuple-element.91) | copy-start | bytes 6148
  140.8 46.3 %copy-start.97 = (f32[1,512]{1,0:T(1,128)}, f32[1,512]{1,0:T(1,128)S(1)}, u32[]{:S(2)}) copy-start(f32[1,512]{1,0:T(1,128)S(1)} %get-tuple-element.95) | copy-start | bytes 6148
  140.8 65.3 %copy-start.72 = (f32[1,512]{1,0:T(1,128)}, f32[1,512]{1,0:T(1,128)S(1)}, u32[]{:S(2)}) copy-start(f32[1,512]{1,0:T(1,128)S(1)} %get-tuple-element.92) | copy-start | bytes 6148
  142.3 64.3 %copy-start.86 = (s32[1024]{0:T(1024)}, s32[1024]{0:T(1024)S(1)}, u32[]{:S(2)}) copy-start(s32[1024]{0:T(1024)S(1)} %multiply_add_fusion.4) | copy-start | bytes 12292
  187.6 17.8 %copy-start.70 = (f32[1024]{0:T(1024)}, f32[1024]{0:T(1024)S(1)}, u32[]{:S(2)}) copy-start(f32[1024]{0:T(1024)S(1)} %add_rsqrt_fusion.2) | copy-start | bytes 12292
  210.5 18.3 %all-to-all-start.1 = ((bf16[8,256,128]{2,1,0:T(8,128)(2,1)}), bf16[8,256,128]{2,1,0:T(8,128)(2,1)S(1)}, u32[]{:S(2)}, u32[]{:S(2)}) async-start(bf16[8,256,128]{2,1,0:T(8,128)(2,1)} %bitcast.17), calls=%async_computation.1 | async-start | bytes 1048576 | tf_op jit(solution)/shard_map/all_to_all | solution.py:709
  215.9 32.3 %all-gather.15.cloned.1.call-start = ((), (), s32[]{:S(2)}) async-start(), calls=%async_computation.11 | async-start | bytes 1310720 | tf_op jit(solution)/shard_map/all_gather | solution.py:699
  231.0 101.4 %all-gather.17.cloned.1.call-start = ((), (), s32[]{:S(2)}) async-start(), calls=%async_computation.12 | async-start | bytes 1310720 | tf_op jit(solution)/shard_map/all_gather | solution.py:699
  253.1 32.3 %copy-start = (bf16[1024,256]{1,0:T(8,128)(2,1)}, bf16[1024,256]{1,0:T(8,128)(2,1)S(1)}, u32[]{:S(2)}) copy-start(bf16[1024,256]{1,0:T(8,128)(2,1)S(1)} %copy.146.k_ref) | copy-start | bytes 1572868
  255.2 30.3 %copy-start.91 = (s32[1024]{0:T(1024)S(1)}, s32[1024]{0:T(1024)}, u32[]{:S(2)}) copy-start(s32[1024]{0:T(1024)} %copy-done.90) | copy-start | bytes 12292
  285.4 26.1 %copy-start.87 = (s32[1024]{0:T(1024)S(1)}, s32[1024]{0:T(1024)}, u32[]{:S(2)}) copy-start(s32[1024]{0:T(1024)} %copy-done.86) | copy-start | bytes 12292
  311.5 20.9 %copy-start.23 = (bf16[1024,512]{1,0:T(8,128)(2,1)S(1)}, bf16[1024,512]{1,0:T(8,128)(2,1)}, u32[]{:S(2)}) copy-start(bf16[1024,512]{1,0:T(8,128)(2,1)} %all-gather.11.cloned.1.call-done) | copy-start | bytes 3145732
  311.5 20.9 %copy-start.73 = (f32[1,512]{1,0:T(1,128)S(1)}, f32[1,512]{1,0:T(1,128)}, u32[]{:S(2)}) copy-start(f32[1,512]{1,0:T(1,128)} %copy-done.72) | copy-start | bytes 6148
  311.5 20.9 %copy-start.99 = (f32[1,512]{1,0:T(1,128)S(1)}, f32[1,512]{1,0:T(1,128)}, u32[]{:S(2)}) copy-start(f32[1,512]{1,0:T(1,128)} %get-tuple-element.87) | copy-start | bytes 6148
  314.6 36.3 %all-gather.19.cloned.1.call-start = ((), (), s32[]{:S(2)}) async-start(), calls=%async_computation.13 | async-start | bytes 1310720 | tf_op jit(solution)/shard_map/all_gather | solution.py:699
  315.4 68.7 %reduce-scatter.12.cloned.1.call-start = ((), (), s32[]{:S(2)}) async-start(), calls=%async_computation.19 | async-start | bytes 1310720
  359.5 67.3 %all-gather.23.cloned.1.call-start = ((), (), s32[]{:S(2)}) async-start(), calls=%async_computation.15 | async-start | bytes 1310720 | tf_op jit(solution)/shard_map/all_gather | solution.py:699
  362.4 22.8 %copy-start.32 = (bf16[1024,128]{1,0:T(8,128)(2,1)S(1)}, bf16[1024,128]{1,0:T(8,128)(2,1)}, u32[]{:S(2)}) copy-start(bf16[1024,128]{1,0:T(8,128)(2,1)} %param.16) | copy-start | bytes 786436
  362.4 22.8 %copy-start.84 = (f32[128]{0:T(128)S(1)}, f32[128]{0:T(128)}, u32[]{:S(2)}) copy-start(f32[128]{0:T(128)} %get-tuple-element.98) | copy-start | bytes 1540
  362.5 25.0 %copy-start.88 = (s32[1024]{0:T(1024)S(1)}, s32[1024]{0:T(1024)}, u32[]{:S(2)}) copy-start(s32[1024]{0:T(1024)} %copy-done.86) | copy-start | bytes 12292
  370.5 18.5 %copy-start.66 = (f32[1,1024]{1,0:T(1,128)}, f32[1,1024]{1,0:T(1,128)S(1)}, u32[]{:S(2)}) copy-start(f32[1,1024]{1,0:T(1,128)S(1)} %get-tuple-element.102) | copy-start | bytes 12292
  370.5 18.5 %copy-start.68 = (f32[1,1024]{1,0:T(1,128)}, f32[1,1024]{1,0:T(1,128)S(1)}, u32[]{:S(2)}) copy-start(f32[1,1024]{1,0:T(1,128)S(1)} %get-tuple-element.103) | copy-start | bytes 12292
  387.5 19.3 %copy-start.92 = (s32[1024]{0:T(1024)S(1)}, s32[1024]{0:T(1024)}, u32[]{:S(2)}) copy-start(s32[1024]{0:T(1024)} %copy-done.90) | copy-start | bytes 12292
  409.0 17.8 %copy-start.39 = (bf16[8,1,64,128]{3,2,1,0:T(8,128)(2,1)S(1)}, bf16[8,1,64,128]{3,2,1,0:T(8,128)(2,1)}, u32[]{:S(2)}) copy-start(bf16[8,1,64,128]{3,2,1,0:T(8,128)(2,1)} %copy-done.38) | copy-start | bytes 393220
  409.0 92.0 %reduce-scatter.14.cloned.1.call-start = ((), (), s32[]{:S(2)}) async-start(), calls=%async_computation.20 | async-start | bytes 1310720
  434.1 30.1 %copy-start.45 = (bf16[8,1,64,128]{3,2,1,0:T(8,128)(2,1)S(1)}, bf16[8,1,64,128]{3,2,1,0:T(8,128)(2,1)}, u32[]{:S(2)}) copy-start(bf16[8,1,64,128]{3,2,1,0:T(8,128)(2,1)} %get-tuple-element.73) | copy-start | bytes 393220
  469.6 61.3 %reduce-scatter.10.cloned.1.call-start = ((), (), s32[]{:S(2)}) async-start(), calls=%async_computation.18 | async-start | bytes 1310720
  471.4 29.6 %copy-start.93 = (s32[1024]{0:T(1024)S(1)}, s32[1024]{0:T(1024)}, u32[]{:S(2)}) copy-start(s32[1024]{0:T(1024)} %copy-done.90) | copy-start | bytes 12292
  472.7 75.2 %all-gather.21.cloned.1.call-start = ((), (), s32[]{:S(2)}) async-start(), calls=%async_computation.14 | async-start | bytes 1310720 | tf_op jit(solution)/shard_map/all_gather | solution.py:699
  473.3 48.9 %copy-start.89 = (s32[1024]{0:T(1024)S(1)}, s32[1024]{0:T(1024)}, u32[]{:S(2)}) copy-start(s32[1024]{0:T(1024)} %copy-done.86) | copy-start | bytes 12292
  473.3 93.6 %all-gather.25.cloned.1.call-start = ((), (), s32[]{:S(2)}) async-start(), calls=%async_computation.16 | async-start | bytes 1310720 | tf_op jit(solution)/shard_map/all_gather | solution.py:699
  533.8 33.1 %copy-start.79 = (f32[1,512]{1,0:T(1,128)S(1)}, f32[1,512]{1,0:T(1,128)}, u32[]{:S(2)}) copy-start(f32[1,512]{1,0:T(1,128)} %copy-done.78) | copy-start | bytes 6148
  550.8 18.6 %copy-start.16 = (f32[1024,512]{1,0:T(8,128)S(1)}, f32[1024,512]{1,0:T(8,128)}, u32[]{:S(2)}) copy-start(f32[1024,512]{1,0:T(8,128)} %copy-done.15) | copy-start | bytes 6291460
  550.8 18.6 %copy-start.65 = (f32[1024]{0:T(1024)S(1)}, f32[1024]{0:T(1024)}, u32[]{:S(2)}) copy-start(f32[1024]{0:T(1024)} %copy-done.64) | copy-start | bytes 12292
  580.2 30.7 %collective-permute-start.2 = (bf16[512,256]{1,0:T(8,128)(2,1)}, bf16[512,256]{1,0:T(8,128)(2,1)}, u32[]{:S(2)}, u32[]{:S(2)}) collective-permute-start(bf16[512,256]{1,0:T(8,128)(2,1)} %get-tuple-element.82), channel_id=1, source_target_pairs={{0,4},{4,8},{8,12},{12,16},{16,20},{20,24},{24,28},{1,5},{5,9},{9,... | collective-permute-start | bytes 786440 | tf_op jit(solution)/shard_map/ppermute | solution.py:935
  581.5 29.4 %collective-permute-start.3 = (bf16[512,256]{1,0:T(8,128)(2,1)}, bf16[512,256]{1,0:T(8,128)(2,1)}, u32[]{:S(2)}, u32[]{:S(2)}) collective-permute-start(bf16[512,256]{1,0:T(8,128)(2,1)} %get-tuple-element.83), channel_id=1, source_target_pairs={{4,0},{8,4},{12,8},{16,12},{20,16},{24,20},{28,24},{5,1},{9,5},{13... | collective-permute-start | bytes 786440 | tf_op jit(solution)/shard_map/ppermute | solution.py:936
  612.5 70.3 %copy-start.6 = (bf16[2,8,64,512]{3,2,1,0:T(8,128)(2,1)S(1)}, bf16[2,8,64,512]{3,2,1,0:T(8,128)(2,1)}, u32[]{:S(2)}) copy-start(bf16[2,8,64,512]{3,2,1,0:T(8,128)(2,1)} %copy-done.5) | copy-start | bytes 3145732
  686.5 80.4 %copy-start.25 = (f32[10,64,512]{2,1,0:T(8,128)S(1)}, f32[10,64,512]{2,1,0:T(8,128)}, u32[]{:S(2)}) copy-start(f32[10,64,512]{2,1,0:T(8,128)} %param.25) | copy-start | bytes 3932164
  686.5 80.4 %copy-start.26 = (f32[10,64,512]{2,1,0:T(8,128)S(1)}, f32[10,64,512]{2,1,0:T(8,128)}, u32[]{:S(2)}) copy-start(f32[10,64,512]{2,1,0:T(8,128)} %param.26) | copy-start | bytes 3932164
  (79 other events, 321.6 us)
Sparse Core Ops, SparseCore 0:
  31.4 83.7 all-gather.26
  128.0 36.4 all-reduce.3
  166.8 18.0 all-gather.12
  186.4 16.8 all-gather.10
  231.1 17.0 all-gather.14
  314.7 17.6 all-gather.16
  334.0 16.8 all-gather.18
  359.6 24.4 reduce-scatter.11
  409.1 17.6 all-gather.22
  469.7 31.2 reduce-scatter.13
  504.3 24.8 reduce-scatter.9
  530.6 17.2 all-gather.20
  550.0 16.8 all-gather.24

commit v3 on v2

--- a/solution.py
+++ b/solution.py
@@ -1,4 +1,5 @@
 import functools
+import types
 
 import jax
 import jax.numpy as jnp
@@ -111,86 +112,504 @@
     return jax.ShapeDtypeStruct((plan.each, plan.pts) + src.shape[1:], src.dtype)
 
 
+def call(kernel, name, collective, inputs, outputs, scratch, flops, smem=()):
+    vmem = pltpu.VMEM
+    names = list(inputs) + list(outputs) + list(scratch)
+
+    def body(*refs):
+        kernel(types.SimpleNamespace(**dict(zip(names, refs))))
+
+    results = pl.pallas_call(
+        body,
+        in_specs=[
+            pl.BlockSpec(memory_space=pltpu.SMEM if key in smem else vmem) for key in inputs
+        ],
+        out_specs=[pl.BlockSpec(memory_space=vmem) for _ in outputs],
+        out_shape=[jax.ShapeDtypeStruct(*shape) for shape in outputs.values()],
+        scratch_shapes=list(scratch.values()),
+        compiler_params=params(collective_id=collective, has_side_effects=True),
+        cost_estimate=pl.CostEstimate(
+            flops=flops, bytes_accessed=20000000, transcendentals=1000000
+        ),
+        name=name,
+    )(*inputs.values())
+    return dict(zip(outputs, results))
+
+
+def dma(*shape):
+    return pltpu.SemaphoreType.DMA(shape)
+
+
+class Gather:
+    def __init__(self, plan, part, sems):
+        self.part, self.sems = part, sems
+        self.plane = lax.axis_index("mdl")
+        self.size = plan.mdl // 2
+        self.x, self.core = self.plane // 2, lax.rem(self.plane, 2)
+
+    @staticmethod
+    def semaphores(plan):
+        return dict(x_send=dma(plan.mdl // 2), recv=dma(plan.mdl), core_send=dma(plan.mdl // 2))
+
+    def along(self, m, target, send):
+        return push(self.part(m), self.part(m), send, self.sems["recv"].at[m], mdl=target)
+
+    def x_copy(self, x):
+        return self.along(self.plane, x * 2 + self.core, self.sems["x_send"].at[x])
+
+    def core_copy(self, x):
+        return self.along(
+            x * 2 + self.core, self.x * 2 + 1 - self.core, self.sems["core_send"].at[x]
+        )
+
+    def arrived(self, m):
+        self.along(m, m, self.sems["x_send"].at[0]).wait_recv()
+
+    def start(self):
+        for x in others(self.x, self.size):
+            self.x_copy(x).start()
+        self.core_copy(self.x).start()
+
+    def forward(self):
+        for x in others(self.x, self.size):
+            self.arrived(x * 2 + self.core)
+            self.core_copy(x).start()
+
+    def finish(self):
+        for x in [self.x] + others(self.x, self.size):
+            self.arrived(x * 2 + 1 - self.core)
+        for x in others(self.x, self.size):
+            self.x_copy(x).wait_send()
+            self.core_copy(x).wait_send()
+        self.core_copy(self.x).wait_send()
+
+    def run(self):
+        self.start()
+        self.forward()
+        self.finish()
+
+
+class Sum:
+    def __init__(self, plan, parts, bufs):
+        self.parts, self.bufs = parts, bufs
+        self.plane = lax.axis_index("mdl")
+        self.size = plan.mdl // 2
+        self.x, self.core = self.plane // 2, lax.rem(self.plane, 2)
+
+    @staticmethod
+    def buffers(plan, shape):
+        x = plan.mdl // 2
+        vmem = pltpu.VMEM((x,) + shape, BF)
+        return dict(
+            near=vmem, middle=vmem, far=vmem,
+            near_send=dma(x), near_recv=dma(x), far_send=dma(x), far_recv=dma(x),
+        )
+
+    def near_copy(self, x):
+        b = self.bufs
+        return push(
+            self.parts.at[x * 2 + 1 - self.core], b["near"].at[x], b["near_send"].at[x],
+            b["near_recv"].at[x], mdl=self.x * 2 + 1 - self.core,
+        )
+
+    def far_copy(self, x, slot):
+        b = self.bufs
+        return push(
+            b["middle"].at[x], b["far"].at[slot], b["far_send"].at[x], b["far_recv"].at[slot],
+            mdl=x * 2 + self.core,
+        )
+
+    def both(self, x):
+        self.near_copy(x).wait_recv()
+        own = self.parts[pl.ds(x * 2 + self.core, 1)][0].astype(F32)
+        return own + self.bufs["near"][pl.ds(x, 1)][0].astype(F32)
+
+    def start(self):
+        for x in others(self.x, self.size) + [self.x]:
+            self.near_copy(x).start()
+
+    def middle(self):
+        for x in others(self.x, self.size):
+            self.bufs["middle"][pl.ds(x, 1)] = self.both(x).astype(BF)[None]
+            self.far_copy(x, self.x).start()
+
+    def finish(self):
+        total = self.both(self.x)
+        for x in others(self.x, self.size):
+            self.far_copy(x, x).wait_recv()
+            total = total + self.bufs["far"][pl.ds(x, 1)][0].astype(F32)
+        for x in others(self.x, self.size):
+            self.near_copy(x).wait_send()
+            self.far_copy(x, self.x).wait_send()
+        self.near_copy(self.x).wait_send()
+        return total
+
+    def run(self):
+        self.start()
+        self.middle()
+        return self.finish()
+
+
+class Trade:
+    def __init__(self, plan, out_index, in_index, bufs):
+        self.out_index, self.in_index, self.bufs = out_index, in_index, bufs
+        self.size = plan.pts
+        self.me = lax.axis_index("pts")
+
+    @staticmethod
+    def buffers(plan, cols, rows):
+        capacity = 2 * rows // plan.pts
+        vmem = pltpu.VMEM((plan.pts, cols, capacity), BF)
+        return dict(leave=vmem, land=vmem, send=dma(plan.pts), recv=dma(plan.pts))
+
+    def hot(self, index, part):
+        capacity = self.bufs["leave"].shape[2]
+        row = index[...]
+        places = lax.broadcasted_iota(jnp.int32, (capacity, row.shape[1]), 0) + part * capacity
+        return jnp.where(places == row, 1.0, 0.0).astype(BF)
+
+    def copy(self, part, slot):
+        b = self.bufs
+        return push(
+            b["leave"].at[part], b["land"].at[slot], b["send"].at[part], b["recv"].at[slot],
+            pts=part,
+        )
+
+    def run(self, values):
+        b = self.bufs
+        for part in others(self.me, self.size):
+            b["leave"][pl.ds(part, 1)] = dot(values, self.hot(self.out_index, part), NT).astype(BF)[None]
+            self.copy(part, self.me).start()
+        own = dot(values, self.hot(self.out_index, self.me), NT).astype(BF)
+        total = dot(own, self.hot(self.in_index, self.me))
+        for step in range(1, self.size):
+            part = lax.rem(self.me + self.size - step, self.size)
+            hot = self.hot(self.in_index, part)
+            self.copy(part, part).wait_recv()
+            total = total + dot(b["land"][pl.ds(part, 1)][0], hot)
+        for part in others(self.me, self.size):
+            self.copy(part, self.me).wait_send()
+        return total.astype(BF)
+
+
+def named(prefix, buffers):
+    return {prefix + key: value for key, value in buffers.items()}
+
+
+def taken_from(refs, prefix, buffers):
+    return {key: getattr(refs, prefix + key) for key in buffers}
+
+
+def everyone(plan):
+    me, plane = lax.axis_index("pts"), lax.axis_index("mdl")
+    return [{"pts": p} for p in others(me, plan.pts)] + [{"mdl": m} for m in others(plane, plan.mdl)]
+
+
+def unit_columns(values):
+    mean = jnp.sum(values, 0, keepdims=True) / C
+    centred = values - mean
+    inv_std = lax.rsqrt(jnp.sum(centred * centred, 0, keepdims=True) / C + NORM_EPS)
+    return centred * inv_std, inv_std
+
+
 def one_hot_window(ids_ref, tap, tile):
     row = ids_ref[pl.ds(tap, 1), pl.ds(tile * TILE, TILE)]
     places = lax.broadcasted_iota(jnp.int32, (WINDOW, TILE), 0) + tile * TILE
     return jnp.where(places == row, 1.0, 0.0).astype(BF)
 
 
-def gather_kernel(ids_ref, ext_ref, out_ref):
-    tap = pl.program_id(0)
-    for tile in range(out_ref.shape[2] // TILE):
-        hot = one_hot_window(ids_ref, tap, tile)
-        taken = dot(ext_ref[:, tile * TILE : tile * TILE + WINDOW], hot)
-        out_ref[0, :, tile * TILE : (tile + 1) * TILE] = taken.astype(BF)
-
-
-def gather_taps(ids, ext):
-    taps, rows = ids.shape
-    cols = ext.shape[0]
-    return pl.pallas_call(
-        gather_kernel,
-        grid=(taps,),
-        in_specs=[
-            pl.BlockSpec(ids.shape, lambda t: (0, 0)),
-            pl.BlockSpec(ext.shape, lambda t: (0, 0)),
-        ],
-        out_specs=pl.BlockSpec((1, cols, rows), lambda t: (t, 0, 0)),
-        out_shape=jax.ShapeDtypeStruct((taps, cols, rows), BF),
-        compiler_params=params(),
-        cost_estimate=pl.CostEstimate(
-            flops=2 * taps * rows * WINDOW * cols * 2,
-            bytes_accessed=taps * rows * cols * 2,
-            transcendentals=0,
+PACK = 5
+ORDER = [TAPS, TAPS + 4] + list(range(TAPS)) + [TAPS + 1, TAPS + 2, TAPS + 3]
+ORDER = ORDER + list(range(TAPS + 5, TAPS + 5 + 2 * FF // C))
+PLACE = {block: place for place, block in enumerate(ORDER)}
+
+
+def front_kernel(plan, r):
+    pts, mdl, slots = plan.pts, plan.mdl, plan.slots
+    width, depth = plan.width, plan.depth
+    me, plane = lax.axis_index("pts"), lax.axis_index("mdl")
+    y, z = lax.rem(me, width), me // width
+    cols, rows = r.points.shape
+    total = r.blocks.shape[1]
+    groups = total // PACK
+    conv_groups = -(-(2 + TAPS) // PACK)
+    greet(everyone(plan))
+
+    def spread_copy(m, slot):
+        return push(
+            r.owned.at[m], r.spread.at[pl.ds(slot * slots, slots)], r.spread_send.at[m],
+            r.spread_recv.at[slot], mdl=m,
+        )
+
+    for m in others(plane, mdl):
+        spread_copy(m, plane).start()
+
+    def vec_copy(m, slot):
+        return push(
+            r.vectors, r.vec_all.at[slot], r.vec_send.at[m], r.vec_recv.at[slot], mdl=m
+        )
+
+    for m in others(plane, mdl):
+        vec_copy(m, plane).start()
+
+    def up_copy():
+        return push(
+            r.points.at[:, rows - HALO : rows], r.ext.at[:, 0:HALO], r.halo_send.at[0],
+            r.halo_recv.at[0], pts=me + 1,
+        )
+
+    def down_copy():
+        return push(
+            r.points.at[:, 0:HALO], r.ext.at[:, HALO + rows : 2 * HALO + rows], r.halo_send.at[1],
+            r.halo_recv.at[1], pts=me - 1,
+        )
+
+    @pl.when(me < pts - 1)
+    def _():
+        up_copy().start()
+
+    @pl.when(me == pts - 1)
+    def _():
+        r.ext[:, HALO + rows :] = jnp.zeros((cols, HALO), BF)
+
+    @pl.when(me > 0)
+    def _():
+        down_copy().start()
+
+    @pl.when(me == 0)
+    def _():
+        r.ext[:, :HALO] = jnp.zeros((cols, HALO), BF)
+
+    r.ext[:, HALO : HALO + rows] = r.points[...]
+    r.spread[pl.ds(plane * slots, slots)] = r.owned[pl.ds(plane, 1)][0]
+    r.vec_all[pl.ds(plane, 1)] = r.vectors[...][None]
+    r.points_full[pl.ds(plane * cols, cols), :] = r.points[...]
+    r.cot_full[pl.ds(plane * cols, cols), :] = r.cot[...]
+    for m in others(plane, mdl):
+        spread_copy(m, m).wait_recv()
+
+    def order(place, carry):
+        r.blocks[pl.ds(me, 1), pl.ds(place, 1)] = r.spread[pl.ds(r.slots[place], 1)][None]
+        return carry
+
+    lax.fori_loop(0, total, order, 0)
+
+    def group_of(source, group):
+        return r.blocks.at[source, group * PACK : (group + 1) * PACK]
+
+    def far_copy(group, v, source):
+        return push(
+            group_of(source, group), group_of(source, group), r.far_send.at[group, v],
+            r.far_recv.at[group, source // width], pts=v * width + y,
+        )
+
+    def side_copy(group, v, source):
+        return push(
+            group_of(source, group), group_of(source, group),
+            r.side_send.at[group, v, source // width], r.side_recv.at[group, source],
+            pts=z * width + v,
+        )
+
+    for group in range(groups):
+        for v in others(z, depth):
+            far_copy(group, v, me).start()
+        for v in others(y, width):
+            side_copy(group, v, me).start()
+
+    points_gather = Gather(
+        plan, lambda m: r.points_full.at[pl.ds(m * cols, cols)],
+        taken_from(r, "points_", Gather.semaphores(plan)),
+    )
+    cot_gather = Gather(
+        plan, lambda m: r.cot_full.at[pl.ds(m * cols, cols)],
+        taken_from(r, "cot_", Gather.semaphores(plan)),
+    )
+    points_gather.start()
+    cot_gather.start()
+
+    @pl.when(me > 0)
+    def _():
+        push(
+            r.points.at[:, 0:HALO], r.ext.at[:, 0:HALO], r.halo_send.at[0], r.halo_recv.at[0],
+            pts=me - 1,
+        ).wait_recv()
+
+    @pl.when(me < pts - 1)
+    def _():
+        push(
+            r.points.at[:, 0:HALO], r.ext.at[:, HALO + rows : 2 * HALO + rows], r.halo_send.at[1],
+            r.halo_recv.at[1], pts=me + 1,
+        ).wait_recv()
+
+    def take(tap, carry):
+        for tile in range(rows // TILE):
+            hot = one_hot_window(r.ids, tap, tile)
+            picked = dot(r.ext[:, tile * TILE : tile * TILE + WINDOW], hot).astype(BF)
+            r.taken[pl.ds(tap, 1), :, tile * TILE : (tile + 1) * TILE] = picked[None]
+        return carry
+
+    cuts = [TAPS * i // groups for i in range(groups + 1)]
+    for group in range(groups):
+        lax.fori_loop(cuts[group], cuts[group + 1], take, 0)
+        for v in others(z, depth):
+            source = v * width + y
+            far_copy(group, v, source).wait_recv()
+            for u in others(y, width):
+                side_copy(group, u, source).start()
+
+    def complete(group):
+        for u in others(y, width):
+            for v in range(depth):
+                side_copy(group, u, v * width + u).wait_recv()
+
+    pair_gather = Gather(
+        plan, lambda m: r.pair.at[m], taken_from(r, "pair_", Gather.semaphores(plan))
+    )
+    for group in range(conv_groups):
+        complete(group)
+        if group == 0:
+            for i in range(2):
+                r.pair[pl.ds(plane, 1), i] = r.blocks[:, i].reshape(1, C, cols)
+            pair_gather.start()
+        low = max(group * PACK - 2, 0)
+        high = min(group * PACK - 2 + PACK, TAPS)
+        if cols % 128 == 0:
+            weight = jnp.concatenate(
+                [r.blocks[:, t + 2].reshape(C, cols) for t in range(low, high)], 1
+            )
+            part = dot(weight, r.taken[low:high].reshape((high - low) * cols, rows))
+        else:
+            part = sum(dot(r.blocks[:, t + 2].reshape(C, cols), r.taken[t]) for t in range(low, high))
+        if group == 0:
+            r.acc[...] = part
+            pair_gather.forward()
+        else:
+            r.acc[...] += part
+
+    points_gather.forward()
+    cot_gather.forward()
+    r.parts[...] = r.acc[...].astype(BF).reshape(mdl, cols, rows)
+    hidden_sum = Sum(plan, r.parts, taken_from(r, "sum_", Sum.buffers(plan, (cols, rows))))
+    hidden_sum.start()
+    for m in others(plane, mdl):
+        vec_copy(m, m).wait_recv()
+    for m in range(mdl):
+        r.vec[m * cols : (m + 1) * cols, :] = r.vec_all[m].T
+    pair_gather.finish()
+    points_gather.finish()
+    hidden_sum.middle()
+    bias = r.vec[pl.ds(plane * cols, cols), 0:1]
+    r.hidden[pl.ds(plane * cols, cols), :] = (hidden_sum.finish() + bias).astype(BF)
+    Gather(
+        plan, lambda m: r.hidden.at[pl.ds(m * cols, cols)],
+        taken_from(r, "hidden_", Gather.semaphores(plan)),
+    ).run()
+    hidden = r.hidden[...]
+    for m in range(mdl):
+        r.acc[m * cols : (m + 1) * cols, :] = dot(r.pair[m, 0], hidden, TN)
+    span_size = 128
+
+    def norms(step, carry):
+        span = pl.ds(pl.multiple_of(step * span_size, span_size), span_size)
+        unit, inv_std = unit_columns(r.acc[:, span] + r.vec[:, 1:2])
+        r.mixed_unit[:, span] = unit
+        r.mixed_std[:, span] = inv_std
+        stream = r.points_full[:, span].astype(F32) + unit * r.vec[:, 2:3] + r.vec[:, 3:4]
+        r.stream[:, span] = stream
+        unit, inv_std = unit_columns(stream)
+        r.one_unit[:, span] = unit
+        r.one_std[:, span] = inv_std
+        r.normed[:, span] = (unit * r.vec[:, 4:5] + r.vec[:, 5:6]).astype(BF)
+        return carry
+
+    lax.fori_loop(0, rows // span_size, norms, 0)
+    trade = Trade(
+        plan, r.send_pos, r.arrival, taken_from(r, "trade_", Trade.buffers(plan, cols, rows))
+    )
+    r.slot_in[pl.ds(plane * cols, cols), :] = trade.run(r.normed[pl.ds(plane * cols, cols), :])
+    Gather(
+        plan, lambda m: r.slot_in.at[pl.ds(m * cols, cols)],
+        taken_from(r, "slot_", Gather.semaphores(plan)),
+    ).run()
+    for group in range(conv_groups, groups):
+        complete(group)
+    cot_gather.finish()
+
+    @pl.when(me < pts - 1)
+    def _():
+        up_copy().wait_send()
+
+    @pl.when(me > 0)
+    def _():
+        down_copy().wait_send()
+
+    for m in others(plane, mdl):
+        spread_copy(m, plane).wait_send()
+        vec_copy(m, plane).wait_send()
+    for group in range(groups):
+        for v in others(z, depth):
+            far_copy(group, v, me).wait_send()
+        for u in others(y, width):
+            for v in range(depth):
+                side_copy(group, u, v * width + y).wait_send()
+
+
+def front(plan, slots, owned, points, cot, vectors, ids, send_pos, arrival):
+    cols, rows = points.shape
+    pts, mdl = plan.pts, plan.mdl
+    share = C // pts
+    total = len(ORDER)
+    groups = total // PACK
+    vmem = pltpu.VMEM
+    scratch = dict(
+        spread=vmem((total, share, cols), BF),
+        vec_all=vmem((mdl,) + vectors.shape, F32),
+        ext=vmem((cols, rows + 2 * HALO), BF),
+        acc=vmem((C, rows), F32),
+        parts=vmem((mdl, cols, rows), BF),
+        normed=vmem((C, rows), BF),
+        points_full=vmem((C, rows), BF),
+        spread_send=dma(mdl),
+        spread_recv=dma(mdl),
+        vec_send=dma(mdl),
+        vec_recv=dma(mdl),
+        halo_send=dma(2),
+        halo_recv=dma(2),
+        far_send=dma(groups, plan.depth),
+        far_recv=dma(groups, plan.depth),
+        side_send=dma(groups, plan.width, plan.depth),
+        side_recv=dma(groups, pts),
+        **named("sum_", Sum.buffers(plan, (cols, rows))),
+        **named("trade_", Trade.buffers(plan, cols, rows)),
+    )
+    for prefix in ("points_", "cot_", "pair_", "hidden_", "slot_"):
+        scratch.update(named(prefix, Gather.semaphores(plan)))
+    return call(
+        functools.partial(front_kernel, plan),
+        "front",
+        5,
+        dict(
+            slots=slots, owned=owned, points=points, cot=cot, vectors=vectors, ids=ids,
+            send_pos=send_pos, arrival=arrival,
         ),
-        name="gather_taps",
-    )(ids, ext)
-
-
-GROUP = 3
-
-
-def conv_kernel(w_ref, x_ref, out_ref, acc_ref):
-    step = pl.program_id(0)
-
-    @pl.when(step == 0)
-    def _():
-        acc_ref[...] = jnp.zeros_like(acc_ref)
-
-    total = acc_ref[...]
-    for j in range(GROUP):
-        total = total + dot(w_ref[:, j].reshape(C, x_ref.shape[1]), x_ref[j])
-    acc_ref[...] = total
-
-    @pl.when(step == pl.num_programs(0) - 1)
-    def _():
-        out_ref[...] = acc_ref[...].T.astype(BF)
-
-
-def conv_forward(blocks, taken):
-    taps, cols, rows = taken.shape
-    parts, _, share, _ = blocks.shape
-    return pl.pallas_call(
-        conv_kernel,
-        grid=(taps // GROUP,),
-        in_specs=[
-            pl.BlockSpec((parts, GROUP, share, cols), lambda t: (0, t, 0, 0)),
-            pl.BlockSpec((GROUP, cols, rows), lambda t: (t, 0, 0)),
-        ],
-        out_specs=pl.BlockSpec((rows, C), lambda t: (0, 0)),
-        scratch_shapes=[pltpu.VMEM((C, rows), F32)],
-        out_shape=jax.ShapeDtypeStruct((rows, C), BF),
-        compiler_params=params(),
-        cost_estimate=pl.CostEstimate(
-            flops=2 * taps * rows * C * cols,
-            bytes_accessed=taps * (rows + C) * cols * 2,
-            transcendentals=0,
+        dict(
+            blocks=((pts, total, share, cols), BF),
+            taken=((TAPS, cols, rows), BF),
+            cot_full=((C, rows), BF),
+            pair=((mdl, 2, C, cols), BF),
+            vec=((C, vectors.shape[0]), F32),
+            hidden=((C, rows), BF),
+            mixed_unit=((C, rows), F32),
+            mixed_std=((1, rows), F32),
+            stream=((C, rows), F32),
+            one_unit=((C, rows), F32),
+            one_std=((1, rows), F32),
+            slot_in=((C, rows), BF),
         ),
-        name="conv_forward",
-    )(blocks, taken)
-
-
-PACK = 5
+        scratch,
+        4 * TAPS * rows * (WINDOW + C) * cols,
+        smem=("slots",),
+    )
 
 
 def back_kernel(
@@ -275,7 +694,7 @@
         out_ref[group * PACK : (group + 1) * PACK] = total.astype(BF)
 
     def turn(tap, carry):
-        weight = w_ref[:, pl.ds(taps - 1 - tap, 1)].reshape(C, cols)
+        weight = w_ref[:, pl.ds(taps + 1 - tap, 1)].reshape(C, cols)
         turned = dot(weight, back_ref[...], TN).astype(BF)
         for tile in range(rows // TILE):
             hot = one_hot_window(ids_ref, tap, tile)
@@ -771,29 +1190,11 @@
     def own(full):
         return lax.dynamic_slice_in_dim(full, mdl_index * cols, cols, full.ndim - 1)
 
-    spread = lax.all_to_all(
-        weights.astype(BF), "mdl", split_axis=2, concat_axis=0, tiled=True
-    )
-    blocks = lax.all_gather(spread[owner_slot], "pts", axis=0)
-    vec = lax.all_gather(vectors, "mdl", axis=1, tiled=True)
-    points_full = widen(points)
-    cot_full = widen(cotangent)
-
-    def block(b):
-        return blocks[:, b].reshape(C, cols)
-
-    up = [(i, i + 1) for i in range(pts - 1)]
-    down = [(i + 1, i) for i in range(pts - 1)]
-    low_halo = lax.ppermute(points[rows - HALO :], "pts", up)
-    high_halo = lax.ppermute(points[:HALO], "pts", down)
-    ext = jnp.concatenate([low_halo, points, high_halo], 0).T
     row_ids = pts_index * rows + jnp.arange(rows, dtype=jnp.int32)
     own_scan = scan_index(row_ids, scan_lengths)
     near = neighbours.T
     usable = (near >= 0) & (scan_index(jnp.maximum(near, 0), scan_lengths) == own_scan[None, :])
     ids = jnp.where(usable, near - (pts_index * rows - HALO), -1)
-    taken = gather_taps(ids, ext)
-    conv_part = conv_forward(blocks, taken)
 
     target = to_patch // slot_count
     place = jnp.arange(rows, dtype=jnp.int32)
@@ -836,17 +1237,30 @@
     def from_slots(values):
         return dot(pack, trade(dot(unpack, values, TN).astype(BF)), TN).astype(BF)
 
-    pair = jnp.stack([block(TAPS), block(TAPS + 4)])
-    pair = lax.all_gather(pair, "mdl", axis=2, tiled=True)
-    linear_full, projection_full = pair[0], pair[1]
-    hidden = (lax.psum(conv_part, "mdl").astype(F32) + vec[0]).astype(BF)
-    mixed = dot(hidden, linear_full) + vec[1]
-    mixed_unit, mixed_std = unit_rows(mixed)
-    stream_one = points_full.astype(F32) + mixed_unit * vec[2] + vec[3]
-    one_unit, one_std = unit_rows(stream_one)
-    normed = (one_unit * vec[4] + vec[5]).astype(BF)
-
-    slot_in = widen(to_slots(own(normed)))
+    owned = weights.astype(BF).reshape(plan.slots, C // pts, mdl, cols).transpose(2, 0, 1, 3)
+    first = front(
+        plan,
+        owner_slot[jnp.array(ORDER)],
+        owned,
+        points.T,
+        cotangent.T,
+        vectors,
+        ids,
+        send_pos[None],
+        arrival[None],
+    )
+    blocks, taken, vec = first["blocks"], first["taken"], first["vec"].T
+    cot_full = first["cot_full"].T
+    linear_full = first["pair"][:, 0].transpose(1, 0, 2).reshape(C, C)
+    projection_full = first["pair"][:, 1].transpose(1, 0, 2).reshape(C, C)
+    hidden = first["hidden"].T
+    mixed_unit, mixed_std = first["mixed_unit"].T, first["mixed_std"].T
+    stream_one, one_unit, one_std = first["stream"].T, first["one_unit"].T, first["one_std"].T
+    slot_in = first["slot_in"].T
+
+    def block(b):
+        return blocks[:, PLACE[b]].reshape(C, cols)
+
     query_map, key_map, value_map = block(TAPS + 1), block(TAPS + 2), block(TAPS + 3)
     projection = block(TAPS + 4)
     queries = (dot(slot_in, query_map) + vectors[6]).astype(BF)
@@ -932,10 +1346,12 @@
     ]
     early += [dot(cot_full, activ[:, k * cols : (k + 1) * cols], TN) for k in range(ff_blocks)]
     early = jnp.stack([e.astype(BF) for e in early])
+    up = [(i, i + 1) for i in range(pts - 1)]
+    down = [(i + 1, i) for i in range(pts - 1)]
     low_back = lax.ppermute(back[:, rows - HALO :], "pts", up)
     high_back = lax.ppermute(back[:, :HALO], "pts", down)
     back_ext = jnp.concatenate([low_back, back, high_back], 1)
-    summed, conv_grad = back_pass(plan, back_ext, taken, blocks[:, :TAPS], ids, early)
+    summed, conv_grad = back_pass(plan, back_ext, taken, blocks, ids, early)
     point_grad = own_grad_one + conv_grad
     block_of_slot = jnp.zeros_like(owner_slot).at[owner_slot].set(
         jnp.arange(owner_slot.shape[0], dtype=jnp.int32)

time: 789 us -> 713 us (0.904)
  waiting for transfers between devices: 264 us -> 93.4 us
  Pallas kernels: 237 us -> 348 us
  starting transfers between devices: 21.3 us -> 6.66 us
  local copies, waits for them, and re-layouts: 44.9 us -> 55.7 us
    pallas_call x2 -> x1, Pallas kernels: 27.8 us -> 137 us  [call(): pl.pallas_call(body, in_specs=[pl.BlockSpec(memory_space=pltpu.SMEM if ke...]
    all_gather x2 -> x0, waiting for transfers between devices: 82.2 us -> none  [the longest x1 61.9 us: local(): blocks = lax.all_gather(spread[owner_slot], 'pts', axis=0)]
    all_gather x7 -> x4, waiting for transfers between devices: 96.6 us -> 53.7 us  [widen(): return lax.all_gather(shard_rows, 'mdl', axis=1, tiled=True)]
    psum x1 -> x0, waiting for transfers between devices: 22.3 us -> none  [local(): hidden = (lax.psum(conv_part, 'mdl').astype(F32) + vec[0]).astype(BF)]
    all_to_all x2 -> x0, waiting for transfers between devices: 19 us -> none  [the longest x1 9.69 us: trade(): lax.all_to_all(buffer, 'pts', split_axis=0, concat_axis=0, tiled=True)]
    all_to_all x2 -> x0, starting transfers between devices: 9.56 us -> none  [the longest x1 5.44 us: trade(): lax.all_to_all(buffer, 'pts', split_axis=0, concat_axis=0, tiled=True)]
    pallas_call x0 -> x3, local copies, waits for them, and re-layouts: none -> 8.77 us  [call(): pl.pallas_call(body, in_specs=[pl.BlockSpec(memory_space=pltpu.SMEM if ke...]
    dot_general x35 -> x32, matrix products: 58.3 us -> 53.1 us  [dot(): return lax.dot_general(a, b, dims, preferred_element_type=F32)]
  transfers between devices with their start and end apart: 19 -> 9, of which waited for: 15 -> 6; matrix products, arithmetic and copies ran while one was open for 9% -> 7% of each run, Pallas kernels for 2% -> 0%
where the time goes in v3:
time: 713 us; the launch traced here: 707 us
  Pallas kernels  348 us (49%)
  waiting for transfers between devices  93.4 us (13%)
  blocking collectives  77.7 us (11%)
  local copies, waits for them, and re-layouts  55.7 us (8%)
  other arithmetic  53.9 us (8%)
  matrix products  53.1 us (7%)
  between operations  17.7 us (2%)
    pallas_call x1, Pallas kernels, call(): pl.pallas_call(body, in_specs=[pl.BlockSpec(memory_space=pltpu.SMEM if ke...  137 us
    pallas_call x1, Pallas kernels, owner_update(): pl.pallas_call(functools.partial(owner_kernel, plan), in_specs=[vmem] * 5...  79.1 us
    pallas_call x1, Pallas kernels, back_pass(): pl.pallas_call(functools.partial(back_kernel, plan), in_specs=[vmem] * 5,...  70.8 us
    all_to_all x3, blocking collectives, trade(): lax.all_to_all(buffer, 'pts', split_axis=0, concat_axis=0, tiled=True)  58.7 us
    all_gather x4, waiting for transfers between devices, widen(): return lax.all_gather(shard_rows, 'mdl', axis=1, tiled=True)  53.7 us
    dot_general x32, matrix products, dot(): return lax.dot_general(a, b, dims, preferred_element_type=F32)  53.1 us
    unnamed x10, waiting for transfers between devices  39.7 us
    pallas_call x1, Pallas kernels, attend(): pl.pallas_call(functools.partial(attend_kernel, plan), grid=(heads,), in_...  31.4 us
  transfers between devices with their start and end apart: 9, of which 6 were waited for; matrix products, arithmetic and copies ran while one was open for 7% of the time, Pallas kernels for 0%

profile of v3, /device:TPU:29, one launch (start us, length us, event | category | flops | bytes accessed | tf_op | source)
XLA Modules:
  0.0 706.5 jit_solution(1124688962610844844)
XLA Ops:
  26.3 2.2 convert_element_type.248.one
  28.6 2.3 convert_element_type.249.two
  31.1 137.1 %front.1 = (bf16[8,40,64,128]{3,2,1,0:T(8,128)(2,1)}, bf16[27,128,1024]{2,1,0:T(8,128)(2,1)}, bf16[512,1024]{1,0:T(8,128)(2,1)S(1)}, bf16[4,2,512,128]{3,2,1,0:T...) custom-call(s32[40]{0:T(128)S(1)} %gather_fusion, ...), custom_call_target="tpu_custom_call" | custom-call | flops 18119393280 | bytes 20000000 | tf_op jit(solution)/shard_map/front/pallas_call | solution.py:122
  168.3 3.2 fusion.123
  181.8 31.4 %attend.1 = (bf16[128,1024]{1,0:T(8,128)(2,1)S(1)}, f32[8,1,1024]{2,1,0:T(1,128)S(1)}, bf16[2,8,64,512]{3,2,1,0:T(8,128)(2,1)S(1)}, bf16[2,8,64,512]{3,2,1,0:T(8,128)(2,1)S(1)}) custom-call(bf16[1024,256]{1,0:T(8,128)(2,1)S(1)} %copy-done.4, bf16[1024,256]{1,0:T(8,128)(2,1)S(1)} %copy-done.6, bf16[8,32,1024]{2,1,0:T(8,128)(2,1)S(1)} %concatenate.23.v_ref, ...), custom_call_target="tpu_custom_call" | custom-call | flops 4294967296 | bytes 1572864 | tf_op jit(solution)/shard_map/attend/pallas_call | solution.py:812
  213.2 1.5 fusion.15
  214.7 23.4 %all_to_all.36 = bf16[8,256,128]{2,1,0:T(8,128)(2,1)S(1)} all-to-all(bf16[8,256,128]{2,1,0:T(8,128)(2,1)S(1)} %bitcast.269), channel_id=1, replica_groups=mesh['pts'=8,'mdl'=4] {'pts'}, dimensions={0} | all-to-all | bytes 1048576 | tf_op jit(solution)/shard_map/all_to_all | solution.py:1128
  238.1 3.1 fusion.50
  241.3 2.9 copy.91
  247.7 11.3 %all-gather.5.cloned.1.call-done = bf16[1024,512]{1,0:T(8,128)(2,1)} async-done(((bf16[1024,128]{1,0:T(8,128)(2,1)}), bf16[1024,512]{1,0:T(8,128)(2,1)}) %all-gather.5.cloned.1.call-update) | async-done | bytes 1048592 | tf_op jit(solution)/shard_map/all_gather | solution.py:1118
  259.0 2.7 fusion.125
  262.2 1.7 add_convert_fusion.1
  264.0 6.0 fusion.22
  270.0 2.4 convert_reduce_fusion.3
  273.4 2.1 fusion.100
  275.5 2.7 convert_bitcast_fusion.1
  278.3 2.9 copy.98
  281.2 2.7 multiply_reduce_fusion.2
  283.9 5.3 psum.14
  289.3 13.6 %reduce-scatter.12.cloned.1.call-done = bf16[128,1024]{1,0:T(8,128)(2,1)} async-done(((bf16[512,1024]{1,0:T(8,128)(2,1)}), bf16[128,1024]{1,0:T(8,128)(2,1)}) %reduce-scatter.12.cloned.1.call-update) | async-done | bytes 262160
  304.0 2.1 convert_reduce_fusion.7
  307.8 17.6 %all_to_all.37 = bf16[8,256,128]{2,1,0:T(8,128)(2,1)S(1)} all-to-all(bf16[8,256,128]{2,1,0:T(8,128)(2,1)S(1)} %bitcast.270), channel_id=1, replica_groups=mesh['pts'=8,'mdl'=4] {'pts'}, dimensions={0} | all-to-all | bytes 1048576 | tf_op jit(solution)/shard_map/all_to_all | solution.py:1128
  325.3 2.2 fusion.52
  331.1 14.2 %all-gather.9.cloned.1.call-done = bf16[1024,512]{1,0:T(8,128)(2,1)} async-done(((bf16[1024,128]{1,0:T(8,128)(2,1)}), bf16[1024,512]{1,0:T(8,128)(2,1)}) %all-gather.9.cloned.1.call-update) | async-done | bytes 1048592 | tf_op jit(solution)/shard_map/all_gather | solution.py:1118
  345.3 1.7 bitcast_multiply_fusion.6
  353.1 30.1 %attend_back.1 = (bf16[128,1024]{1,0:T(8,128)(2,1)S(1)}, bf16[1024,128]{1,0:T(8,128)(2,1)S(1)}, bf16[1024,128]{1,0:T(8,128)(2,1)S(1)}, bf16[2,8,64,512]{3,2,1,0:T(8,128)(2,1)S(1)}, bf16[2,8,64,512]{3,2,1,0:T(8,128)(2,1)S(1)}) custom-call(bf16[1024,256]{1,0:T(8,128)(2,1)S(1)} %copy-done.5, bf16[1024,256]{1,0:T(8,128)(2,1)S(1)} %copy-done.7, ...), custom_call_target="tpu_custom_call" | custom-call | flops 10737418240 | bytes 5242880 | tf_op jit(solution)/shard_map/attend_back/pallas_call | solution.py:888
  386.2 2.4 copy.116
  388.7 2.9 convolution_convert_fusion.1
  391.7 2.3 copy.112
  394.6 25.5 %reduce-scatter.14.cloned.1.call-done = bf16[128,1024]{1,0:T(8,128)(2,1)} async-done(((bf16[512,1024]{1,0:T(8,128)(2,1)}), bf16[128,1024]{1,0:T(8,128)(2,1)}) %reduce-scatter.14.cloned.1.call-update) | async-done | bytes 262160
  420.1 3.4 fusion.19
  423.5 17.8 %all_to_all.38 = bf16[8,256,128]{2,1,0:T(8,128)(2,1)S(1)} all-to-all(bf16[8,256,128]{2,1,0:T(8,128)(2,1)S(1)} %bitcast.265), channel_id=1, replica_groups=mesh['pts'=8,'mdl'=4] {'pts'}, dimensions={0} | all-to-all | bytes 1048576 | tf_op jit(solution)/shard_map/all_to_all | solution.py:1128
  441.3 3.1 fusion.51
  444.6 2.9 copy.104
  447.5 2.9 copy.106
  451.6 1.8 add_convert_fusion.3
  453.4 13.3 %all-gather.7.cloned.1.call-done = bf16[1024,512]{1,0:T(8,128)(2,1)} async-done(((bf16[1024,128]{1,0:T(8,128)(2,1)}), bf16[1024,512]{1,0:T(8,128)(2,1)}) %all-gather.7.cloned.1.call-update) | async-done | bytes 1048592 | tf_op jit(solution)/shard_map/all_gather | solution.py:1118
  466.7 2.8 convert_element_type.264
  470.8 14.9 %all-gather.11.cloned.1.call-done = bf16[1024,512]{1,0:T(8,128)(2,1)} async-done(((bf16[1024,128]{1,0:T(8,128)(2,1)}), bf16[1024,512]{1,0:T(8,128)(2,1)}) %all-gather.11.cloned.1.call-update) | async-done | bytes 1048592 | tf_op jit(solution)/shard_map/all_gather | solution.py:1118
  485.8 2.5 multiply_reduce_fusion.4
  488.6 3.0 multiply_reduce_fusion.3
  509.7 4.9 collective-permute-start.1
  514.7 3.0 convert_reduce_fusion.5
  520.3 13.6 %psum.15 = f32[16,128]{1,0:T(8,128)S(1)} all-reduce(f32[16,128]{1,0:T(8,128)S(1)} %concatenate.27), channel_id=1, replica_groups=mesh['pts'=8,'mdl'=4] {'pts'}, use_global_device_ids=true, to_apply=%region_34.35 | all-reduce | flops 2048 | bytes 16384 | tf_op jit(solution)/shard_map/psum | solution.py:1386
  535.3 2.0 fusion.79.early_ref
  538.4 70.8 %back_pass.1 = (bf16[40,64,128]{2,1,0:T(8,128)(2,1)S(1)}, f32[1024,128]{1,0:T(8,128)S(1)}) custom-call(bf16[512,1536]{1,0:T(8,128)(2,1)S(1)} %pad_maximum_fusion.back_ref, bf16[27,128,1024]{2,1,0:T(8,128)(2,1)} %get-tuple-element.51.x_ref, bf16[8,40,64,128]{3,2,1,0:T(8,128)(2,1)} %get-tuple-element.38.w_ref, ...), custom_call_target="tpu_custom_call" | custom-call | flops 19931332608 | bytes 30000000 | tf_op jit(solution)/shard_map/back_pass/pallas_call | solution.py:736
  613.7 79.1 %owner_update.1 = (bf16[4,10,64,128]{3,2,1,0:T(8,128)(2,1)S(1)}, bf16[10,2,64,512]{3,2,1,0:T(8,128)(2,1)}) custom-call(bf16[40,64,128]{2,1,0:T(8,128)(2,1)S(1)} %gather_fusion.1, bf16[2,8,64,512]{3,2,1,0:T(8,128)(2,1)S(1)} %copy-done.19, bf16[2,8,64,512]{3,2,1,0:T(8,128)(2,1)S(1)} %copy-done.21, bf16[2,8,64,512]{3,2,1,0:T(8,128)(2,1)S(1)} %copy-done.23, ...), custom_call_target="tpu_custom_call" | custom-call | flops 2147483648 | bytes 10000000 | tf_op jit(solution)/shard_map/owner_update/pallas_call | solution.py:1088
  694.6 3.8 fusion.120
  (279 shorter events, 81.7 us)
Async XLA Ops:
  7.2 251.8 %all-gather.5.cloned.1.call-start = ((), (), s32[]{:S(2)}) async-start(), calls=%async_computation.6 | async-start | bytes 1310720 | tf_op jit(solution)/shard_map/all_gather | solution.py:1118
  13.3 290.7 %copy-start.81 = (f32[128]{0:T(128)}, f32[128]{0:T(128)S(1)}, u32[]{:S(2)}) copy-start(f32[128]{0:T(128)S(1)} %get-tuple-element.115) | copy-start | bytes 1540
  23.1 302.2 %copy-start.9 = (s32[1024]{0:T(1024)}, s32[1024]{0:T(1024)S(1)}, u32[]{:S(2)}) copy-start(s32[1024]{0:T(1024)S(1)} %get-tuple-element.79) | copy-start | bytes 12292
  25.1 5.7 copy-start.32
  168.2 4.3 copy-start.11
  168.2 4.3 copy-start.13
  168.2 4.3 copy-start.15
  171.5 5.3 copy-start.49
  241.2 61.7 %reduce-scatter.12.cloned.1.call-start = ((), (), s32[]{:S(2)}) async-start(), calls=%async_computation.11 | async-start | bytes 1310720
  261.7 8.3 %copy-start.28 = (f32[1024,512]{1,0:T(8,128)}, f32[1024,512]{1,0:T(8,128)S(1)}, u32[]{:S(2)}) copy-start(f32[1024,512]{1,0:T(8,128)S(1)} %get-tuple-element.125) | copy-start | bytes 6291460
  262.1 41.9 %copy-start.71 = (f32[1024]{0:T(1024)}, f32[1024]{0:T(1024)S(1)}, u32[]{:S(2)}) copy-start(f32[1024]{0:T(1024)S(1)} %add_rsqrt_fusion) | copy-start | bytes 12292
  263.9 6.1 copy-start.54
  264.0 6.0 copy-start.16
  264.0 6.0 copy-start.62
  264.0 6.0 copy-start.64
  264.0 6.0 copy-start.66
  264.0 6.0 copy-start.68
  278.2 67.1 %all-gather.9.cloned.1.call-start = ((), (), s32[]{:S(2)}) async-start(), calls=%async_computation.8 | async-start | bytes 1310720 | tf_op jit(solution)/shard_map/all_gather | solution.py:1118
  281.2 22.8 %copy-start.43 = (bf16[1024,128]{1,0:T(8,128)(2,1)S(1)}, bf16[1024,128]{1,0:T(8,128)(2,1)}, u32[]{:S(2)}) copy-start(bf16[1024,128]{1,0:T(8,128)(2,1)} %param.17) | copy-start | bytes 786436
  289.3 18.4 %copy-start.73 = (f32[1,1024]{1,0:T(1,128)}, f32[1,1024]{1,0:T(1,128)S(1)}, u32[]{:S(2)}) copy-start(f32[1,1024]{1,0:T(1,128)S(1)} %get-tuple-element.119) | copy-start | bytes 12292
  289.3 18.4 %copy-start.75 = (f32[1,1024]{1,0:T(1,128)}, f32[1,1024]{1,0:T(1,128)S(1)}, u32[]{:S(2)}) copy-start(f32[1,1024]{1,0:T(1,128)S(1)} %get-tuple-element.120) | copy-start | bytes 12292
  327.5 92.5 %reduce-scatter.14.cloned.1.call-start = ((), (), s32[]{:S(2)}) async-start(), calls=%async_computation.12 | async-start | bytes 1310720
  330.2 15.1 %copy-start.52 = (bf16[128,1024]{0,1:T(8,128)(2,1)S(1)}, bf16[128,1024]{0,1:T(8,128)(2,1)}, u32[]{:S(2)}) copy-start(bf16[128,1024]{0,1:T(8,128)(2,1)} %copy.100) | copy-start | bytes 786436
  331.1 18.1 %copy-start.5 = (bf16[1024,256]{1,0:T(8,128)(2,1)S(1)}, bf16[1024,256]{1,0:T(8,128)(2,1)}, u32[]{:S(2)}) copy-start(bf16[1024,256]{1,0:T(8,128)(2,1)} %copy.94.q_ref) | copy-start | bytes 1572868
  353.1 30.1 %copy-start.51 = (bf16[8,1,64,128]{3,2,1,0:T(8,128)(2,1)S(1)}, bf16[8,1,64,128]{3,2,1,0:T(8,128)(2,1)}, u32[]{:S(2)}) copy-start(bf16[8,1,64,128]{3,2,1,0:T(8,128)(2,1)} %get-tuple-element.101) | copy-start | bytes 393220
  388.6 61.9 %reduce-scatter.10.cloned.1.call-start = ((), (), s32[]{:S(2)}) async-start(), calls=%async_computation.10 | async-start | bytes 1310720
  391.7 28.4 %copy-start.10 = (s32[1024]{0:T(1024)S(1)}, s32[1024]{0:T(1024)}, u32[]{:S(2)}) copy-start(s32[1024]{0:T(1024)} %copy-done.9) | copy-start | bytes 12292
  394.0 72.8 %all-gather.7.cloned.1.call-start = ((), (), s32[]{:S(2)}) async-start(), calls=%async_computation.7 | async-start | bytes 1310720 | tf_op jit(solution)/shard_map/all_gather | solution.py:1118
  394.5 91.3 %all-gather.11.cloned.1.call-start = ((), (), s32[]{:S(2)}) async-start(), calls=%async_computation.9 | async-start | bytes 1310720 | tf_op jit(solution)/shard_map/all_gather | solution.py:1118
  447.5 4.1 copy-start.83
  453.4 32.4 %copy-start.79 = (f32[512]{0:T(512)S(1)}, f32[512]{0:T(512)}, u32[]{:S(2)}) copy-start(f32[512]{0:T(512)} %get-tuple-element.74) | copy-start | bytes 6148
  469.5 18.8 %copy-start.78 = (f32[512]{0:T(512)S(1)}, f32[512]{0:T(512)}, u32[]{:S(2)}) copy-start(f32[512]{0:T(512)} %get-tuple-element.73) | copy-start | bytes 6148
  493.6 14.0 %copy-start.39 = (bf16[512,1024]{1,0:T(8,128)(2,1)}, bf16[512,1024]{1,0:T(8,128)(2,1)S(1)}, u32[]{:S(2)}) copy-start(bf16[512,1024]{1,0:T(8,128)(2,1)S(1)} %get-tuple-element.131) | copy-start | bytes 3145732
  495.8 4.0 copy-start.55
  505.4 9.3 %copy-start.44 = (bf16[1024,128]{1,0:T(8,128)(2,1)S(1)}, bf16[1024,128]{1,0:T(8,128)(2,1)}, u32[]{:S(2)}) copy-start(bf16[1024,128]{1,0:T(8,128)(2,1)} %param.17) | copy-start | bytes 786436
  505.4 9.3 %copy-start.46 = (bf16[1024,128]{1,0:T(8,128)(2,1)S(1)}, bf16[1024,128]{1,0:T(8,128)(2,1)}, u32[]{:S(2)}) copy-start(bf16[1024,128]{1,0:T(8,128)(2,1)} %copy-done.45) | copy-start | bytes 786436
  505.4 9.3 %copy-start.72 = (f32[1024]{0:T(1024)S(1)}, f32[1024]{0:T(1024)}, u32[]{:S(2)}) copy-start(f32[1024]{0:T(1024)} %copy-done.71) | copy-start | bytes 12292
  505.4 9.3 %copy-start.74 = (f32[1,1024]{1,0:T(1,128)S(1)}, f32[1,1024]{1,0:T(1,128)}, u32[]{:S(2)}) copy-start(f32[1,1024]{1,0:T(1,128)} %copy-done.73) | copy-start | bytes 12292
  505.4 9.3 %copy-start.76 = (f32[1,1024]{1,0:T(1,128)S(1)}, f32[1,1024]{1,0:T(1,128)}, u32[]{:S(2)}) copy-start(f32[1,1024]{1,0:T(1,128)} %copy-done.75) | copy-start | bytes 12292
  505.4 9.3 %copy-start.82 = (f32[128]{0:T(128)S(1)}, f32[128]{0:T(128)}, u32[]{:S(2)}) copy-start(f32[128]{0:T(128)} %copy-done.81) | copy-start | bytes 1540
  508.4 28.9 %collective-permute-start = (bf16[512,256]{1,0:T(8,128)(2,1)}, bf16[512,256]{1,0:T(8,128)(2,1)S(1)}, u32[]{:S(2)}, u32[]{:S(2)}) collective-permute-start(bf16[512,256]{1,0:T(8,128)(2,1)} %get-tuple-element.108), channel_id=1, source_target_pairs={{0,4},{4,8},{8,12},{12,16},{16,20},{20,24},{24,28},{1,5},{5,9},{9,... | collective-permute-start | bytes 786440 | tf_op jit(solution)/shard_map/ppermute | solution.py:1351
  509.7 27.6 %collective-permute-start.1 = (bf16[512,256]{1,0:T(8,128)(2,1)}, bf16[512,256]{1,0:T(8,128)(2,1)}, u32[]{:S(2)}, u32[]{:S(2)}) collective-permute-start(bf16[512,256]{1,0:T(8,128)(2,1)} %get-tuple-element.109), channel_id=1, source_target_pairs={{4,0},{8,4},{12,8},{16,12},{20,16},{24,20},{28,24},{5,1},{9,5},{13... | collective-permute-start | bytes 786440 | tf_op jit(solution)/shard_map/ppermute | solution.py:1352
  517.8 16.2 %copy-start.80 = (f32[16,128]{1,0:T(8,128)S(1)}, f32[16,128]{1,0:T(8,128)}, u32[]{:S(2)}) copy-start(f32[16,128]{1,0:T(8,128)} %param.30) | copy-start | bytes 24580
  518.8 18.5 %copy-start.40 = (bf16[512,1024]{1,0:T(8,128)(2,1)S(1)}, bf16[512,1024]{1,0:T(8,128)(2,1)}, u32[]{:S(2)}) copy-start(bf16[512,1024]{1,0:T(8,128)(2,1)} %copy-done.39) | copy-start | bytes 3145732
  534.0 4.4 copy-start.77
  538.4 71.6 %copy-start.19 = (bf16[2,8,64,512]{3,2,1,0:T(8,128)(2,1)S(1)}, bf16[2,8,64,512]{3,2,1,0:T(8,128)(2,1)}, u32[]{:S(2)}) copy-start(bf16[2,8,64,512]{3,2,1,0:T(8,128)(2,1)} %copy-done.18) | copy-start | bytes 3145732
  613.7 80.3 %copy-start.35 = (f32[10,64,512]{2,1,0:T(8,128)S(1)}, f32[10,64,512]{2,1,0:T(8,128)}, u32[]{:S(2)}) copy-start(f32[10,64,512]{2,1,0:T(8,128)} %param.26) | copy-start | bytes 3932164
  613.7 80.3 %copy-start.37 = (f32[10,64,512]{2,1,0:T(8,128)S(1)}, f32[10,64,512]{2,1,0:T(8,128)}, u32[]{:S(2)}) copy-start(f32[10,64,512]{2,1,0:T(8,128)} %param.27) | copy-start | bytes 3932164
  (46 other events, 92.3 us)
Sparse Core Ops, SparseCore 0:
  241.3 17.5 all-gather.4
  278.4 24.4 reduce-scatter.11
  327.7 17.5 all-gather.8
  388.7 31.2 reduce-scatter.13
  423.0 24.8 reduce-scatter.9
  449.4 17.2 all-gather.6
  468.9 16.8 all-gather.10

commit v4 on v3

--- a/solution.py
+++ b/solution.py
@@ -26,7 +26,7 @@
 WINDOW = TILE + 2 * HALO
 BF = jnp.bfloat16
 F32 = jnp.float32
-VMEM_LIMIT = 48 * 1024 * 1024
+VMEM_LIMIT = 56 * 1024 * 1024
 
 NN = (((1,), (0,)), ((), ()))
 NT = (((1,), (1,)), ((), ()))
@@ -112,19 +112,20 @@
     return jax.ShapeDtypeStruct((plan.each, plan.pts) + src.shape[1:], src.dtype)
 
 
-def call(kernel, name, collective, inputs, outputs, scratch, flops, smem=()):
+def call(kernel, name, collective, inputs, outputs, scratch, flops, smem=(), free=()):
     vmem = pltpu.VMEM
     names = list(inputs) + list(outputs) + list(scratch)
 
+    def space(key):
+        return pltpu.SMEM if key in smem else pl.ANY if key in free else vmem
+
     def body(*refs):
         kernel(types.SimpleNamespace(**dict(zip(names, refs))))
 
     results = pl.pallas_call(
         body,
-        in_specs=[
-            pl.BlockSpec(memory_space=pltpu.SMEM if key in smem else vmem) for key in inputs
-        ],
-        out_specs=[pl.BlockSpec(memory_space=vmem) for _ in outputs],
+        in_specs=[pl.BlockSpec(memory_space=space(key)) for key in inputs],
+        out_specs=[pl.BlockSpec(memory_space=space(key)) for key in outputs],
         out_shape=[jax.ShapeDtypeStruct(*shape) for shape in outputs.values()],
         scratch_shapes=list(scratch.values()),
         compiler_params=params(collective_id=collective, has_side_effects=True),
@@ -275,13 +276,16 @@
             pts=part,
         )
 
-    def run(self, values):
+    def start(self, values):
         b = self.bufs
         for part in others(self.me, self.size):
             b["leave"][pl.ds(part, 1)] = dot(values, self.hot(self.out_index, part), NT).astype(BF)[None]
             self.copy(part, self.me).start()
-        own = dot(values, self.hot(self.out_index, self.me), NT).astype(BF)
-        total = dot(own, self.hot(self.in_index, self.me))
+        b["land"][pl.ds(self.me, 1)] = dot(values, self.hot(self.out_index, self.me), NT).astype(BF)[None]
+
+    def finish(self):
+        b = self.bufs
+        total = dot(b["land"][pl.ds(self.me, 1)][0], self.hot(self.in_index, self.me))
         for step in range(1, self.size):
             part = lax.rem(self.me + self.size - step, self.size)
             hot = self.hot(self.in_index, part)
@@ -290,6 +294,10 @@
         for part in others(self.me, self.size):
             self.copy(part, self.me).wait_send()
         return total.astype(BF)
+
+    def run(self, values):
+        self.start(values)
+        return self.finish()
 
 
 def named(prefix, buffers):
@@ -533,6 +541,8 @@
     ).run()
     for group in range(conv_groups, groups):
         complete(group)
+    for i in range(r.rest.shape[0]):
+        r.rest[i] = r.blocks[:, TAPS + 2 + i].reshape(C, cols)
     cot_gather.finish()
 
     @pl.when(me < pts - 1)
@@ -605,6 +615,7 @@
             one_unit=((C, rows), F32),
             one_std=((1, rows), F32),
             slot_in=((C, rows), BF),
+            rest=((total - TAPS - 2, C, cols), BF),
         ),
         scratch,
         4 * TAPS * rows * (WINDOW + C) * cols,
@@ -612,316 +623,648 @@
     )
 
 
-def back_kernel(
-    plan, back_ref, x_ref, w_ref, ids_ref, early_ref, out_ref, turn_ref,
-    own, side, acc, far, turn_acc, side_send, side_recv, far_send, far_recv,
-):
-    width, depth = plan.width, plan.depth
-    cols, rows = turn_acc.shape
-    share = C // plan.pts
-    taps = x_ref.shape[0]
-    extra = early_ref.shape[0]
-    groups = own.shape[1]
-    me = lax.axis_index("pts")
+def fetches(plan, srcs, dsts, refs, act):
+    for place, (src, dst) in enumerate(zip(srcs, dsts)):
+        sems = [getattr(refs, f"fetch{place}_{key}") for key in ("send", "recv", "here")]
+        fetch_copies(plan, src, dst, sems, act)
+
+
+def fetch_scratch(plan):
+    return {
+        f"fetch{place}_{key}": sem
+        for place in range(2)
+        for key, sem in zip(("send", "recv", "here"), fetch_sems(plan))
+    }
+
+
+def head_lanes(ext, cols, head):
+    lane = lax.broadcasted_iota(jnp.int32, ext.shape, 1)
+    return jnp.where((lane >= cols) | (lane // HD == head), ext, jnp.zeros_like(ext))
+
+
+def head_rows(head):
+    return pl.ds(pl.multiple_of(head * HD, HD), HD)
+
+
+def attend_kernel(plan, r):
+    plane = lax.axis_index("mdl")
+    rows, cols = r.values.shape
+    heads = cols // HD
+    greet(everyone(plan))
+    moves = (plan, (r.left, r.right), (r.left_whole, r.right_whole), r)
+    fetches(*moves, "start")
+    slot_in = r.slot_in[...]
+    queries = (dot(slot_in, r.rest[0], TN) + r.vectors[6:7, :]).astype(BF)
+    r.q_ext[:, :cols] = queries * BF(HD ** (-0.5))
+    r.q_ext[:, cols:] = r.group_q[...]
+    r.k_ext[:, :cols] = dot(slot_in, r.rest[1], TN).astype(BF)
+    r.k_ext[:, cols:] = r.group_k[...]
+    values = dot(slot_in, r.rest[2], TN) + r.vectors[7:8, :]
+    r.values[...] = values.astype(BF)
+    r.v_aug[:, :HD] = values.T.astype(BF).reshape(heads, HD, rows)
+    r.v_aug[:, HD:] = jnp.ones((heads, HD, rows), BF)
+
+    def one(head, carry):
+        keys = r.k_ext[...]
+        values_t = r.v_aug[pl.ds(head, 1)][0]
+        for tile in range(rows // TILE):
+            span = slice(tile * TILE, (tile + 1) * TILE)
+            scores = dot(keys, head_lanes(r.q_ext[span, :], cols, head), NT)
+            top = jnp.max(scores, 0, keepdims=True)
+            soft = jnp.exp(scores - top).astype(BF)
+            summed = dot(values_t, soft)
+            total = summed[HD : HD + 1]
+            r.attended[head_rows(head), span] = (summed[:HD] / total).astype(BF)
+            r.lse[pl.ds(head, 1), :, span] = (top + jnp.log(total))[None]
+        return carry
+
+    lax.fori_loop(0, heads, one, 0)
+    trade = Trade(
+        plan, r.arrival, r.send_pos, taken_from(r, "trade_", Trade.buffers(plan, cols, rows))
+    )
+    r.attended_rows[pl.ds(plane * cols, cols), :] = trade.run(r.attended[...])
+    Gather(
+        plan, lambda m: r.attended_rows.at[pl.ds(m * cols, cols)],
+        taken_from(r, "rows_", Gather.semaphores(plan)),
+    ).run()
+    fetches(*moves, "wait")
+
+
+def attend(plan, slot_in, rest, vectors, group_q, group_k, send_pos, arrival, left, right):
+    rows, cols = group_q.shape
+    heads = cols // HD
+    fetched = fetch_shape(plan, left)
+    return call(
+        functools.partial(attend_kernel, plan),
+        "attend",
+        2,
+        dict(
+            slot_in=slot_in, rest=rest, vectors=vectors, group_q=group_q, group_k=group_k,
+            send_pos=send_pos, arrival=arrival, left=left, right=right,
+        ),
+        dict(
+            q_ext=((rows, 2 * cols), BF),
+            k_ext=((rows, 2 * cols), BF),
+            values=((rows, cols), BF),
+            attended=((cols, rows), BF),
+            lse=((heads, 1, rows), F32),
+            attended_rows=((C, rows), BF),
+            left_whole=(fetched.shape, fetched.dtype),
+            right_whole=(fetched.shape, fetched.dtype),
+        ),
+        dict(
+            v_aug=pltpu.VMEM((heads, 2 * HD, rows), BF),
+            **fetch_scratch(plan),
+            **named("trade_", Trade.buffers(plan, cols, rows)),
+            **named("rows_", Gather.semaphores(plan)),
+        ),
+        4 * heads * rows * rows * cols,
+        free=("left", "right", "left_whole", "right_whole"),
+    )
+
+
+def attend_back_kernel(plan, r):
+    plane = lax.axis_index("mdl")
+    rows, cols = r.values.shape
+    heads = cols // HD
+    greet(everyone(plan))
+    moves = (plan, (r.first, r.second), (r.first_whole, r.second_whole), r)
+    fetches(*moves, "start")
+    grad_slot = r.grad_slot[...]
+    grad_t = dot(r.pair[pl.ds(plane, 1), 1][0], grad_slot, TN).astype(BF).astype(F32)
+    r.grad[...] = grad_t.T.astype(BF)
+    weighed = grad_t * r.attended[...].astype(F32)
+    r.inner[...] = jnp.sum(weighed.reshape(heads, HD, rows), 1, keepdims=True)
+    r.keys_t[...] = r.k_ext[:, :cols].astype(F32).T.astype(BF)
+    r.dk_acc[...] = jnp.zeros_like(r.dk_acc)
+    r.dv_acc[...] = jnp.zeros_like(r.dv_acc)
+
+    def one(head, carry):
+        queries = head_lanes(r.q_ext[...], cols, head)
+        pure = queries[:, :cols]
+        grad = head_lanes(r.grad[...], cols, head)
+        lse = r.lse[pl.ds(head, 1)][0]
+        inner = r.inner[pl.ds(head, 1)][0]
+        keys_t = r.keys_t[head_rows(head), :]
+        dq = jnp.zeros((HD, rows), F32)
+        for tile in range(rows // TILE):
+            span = slice(tile * TILE, (tile + 1) * TILE)
+            scores = dot(r.k_ext[span, :], queries, NT)
+            soft = jnp.exp(scores - lse)
+            grad_soft = dot(r.values[span, :], grad, NT)
+            grad_scores = (soft * (grad_soft - inner)).astype(BF)
+            r.dv_acc[span, :] += dot(soft.astype(BF), grad)
+            r.dk_acc[span, :] += dot(grad_scores, pure)
+            dq = dq + dot(keys_t[:, span], grad_scores)
+        r.dq[head_rows(head), :] = (dq * HD ** (-0.5)).astype(BF)
+        return carry
+
+    lax.fori_loop(0, heads, one, 0)
+    dk = r.dk_acc[...].astype(BF)
+    dv = r.dv_acc[...].astype(BF)
+    back = dot(r.rest[0], r.dq[...]) + dot(r.rest[1], dk, NT) + dot(r.rest[2], dv, NT)
+    r.parts[...] = back.astype(BF).reshape(plan.mdl, cols, rows)
+    back_sum = Sum(plan, r.parts, taken_from(r, "sum_", Sum.buffers(plan, (cols, rows))))
+    back_sum.start()
+    r.weight_grads[0] = dot(r.slot_in[...], r.dq[...], NT).astype(BF)
+    r.weight_grads[1] = dot(r.slot_in[...], dk).astype(BF)
+    back_sum.middle()
+    r.weight_grads[2] = dot(r.slot_in[...], dv).astype(BF)
+    r.weight_grads[3] = dot(r.grad_slot[...], r.attended[...], NT).astype(BF)
+    trade = Trade(
+        plan, r.arrival, r.send_pos, taken_from(r, "trade_", Trade.buffers(plan, cols, rows))
+    )
+    trade.start(back_sum.finish().astype(BF))
+    r.sums[...] = jnp.zeros_like(r.sums)
+    r.sums[:, 0:1] = jnp.sum(r.dq[...].astype(F32), 1, keepdims=True)
+    r.sums[:, 1:2] = jnp.sum(dv.astype(F32), 0, keepdims=True).T
+    r.grad_normed[pl.ds(plane * cols, cols), :] = trade.finish()
+    Gather(
+        plan, lambda m: r.grad_normed.at[pl.ds(m * cols, cols)],
+        taken_from(r, "rows_", Gather.semaphores(plan)),
+    ).run()
+    fetches(*moves, "wait")
+
+
+def attend_back(plan, kept, grad_slot, slot_in, rest, pair, send_pos, arrival, first, second):
+    rows, cols = kept["values"].shape
+    heads = cols // HD
+    vmem = pltpu.VMEM
+    fetched = fetch_shape(plan, first)
+    names = ("q_ext", "k_ext", "values", "attended", "lse")
+    return call(
+        functools.partial(attend_back_kernel, plan),
+        "attend_back",
+        3,
+        dict(
+            **{key: kept[key] for key in names}, grad_slot=grad_slot, slot_in=slot_in, rest=rest,
+            pair=pair, send_pos=send_pos, arrival=arrival, first=first, second=second,
+        ),
+        dict(
+            grad_normed=((C, rows), BF),
+            weight_grads=((4, C, cols), BF),
+            sums=((cols, 8), F32),
+            first_whole=(fetched.shape, fetched.dtype),
+            second_whole=(fetched.shape, fetched.dtype),
+        ),
+        dict(
+            grad=vmem((rows, cols), BF),
+            inner=vmem((heads, 1, rows), F32),
+            keys_t=vmem((cols, rows), BF),
+            dk_acc=vmem((rows, cols), F32),
+            dv_acc=vmem((rows, cols), F32),
+            dq=vmem((cols, rows), BF),
+            parts=vmem((plan.mdl, cols, rows), BF),
+            **fetch_scratch(plan),
+            **named("sum_", Sum.buffers(plan, (cols, rows))),
+            **named("trade_", Trade.buffers(plan, cols, rows)),
+            **named("rows_", Gather.semaphores(plan)),
+        ),
+        10 * heads * rows * rows * cols,
+        free=("first", "second", "first_whole", "second_whole"),
+    )
+
+
+SPAN = 128
+
+
+def over_spans(rows, body, size=SPAN):
+    def step(index, carry):
+        body(pl.ds(pl.multiple_of(index * size, size), size))
+        return carry
+
+    lax.fori_loop(0, rows // size, step, 0)
+
+
+def beside(blocks):
+    def times(right, cols):
+        if cols % 128 == 0:
+            return dot(jnp.concatenate(blocks, 1), right[...])
+        return sum(
+            dot(block, right[i * cols : (i + 1) * cols, :]) for i, block in enumerate(blocks)
+        )
+
+    return times
+
+
+def mlp_kernel(plan, r):
+    mdl = plan.mdl
+    plane = lax.axis_index("mdl")
+    cols, rows = r.cot.shape
+    ff_blocks = FF // C
+    own = pl.ds(plane * cols, cols)
+    greet(everyone(plan))
+    r.acc[...] = beside([r.pair[m, 1] for m in range(mdl)])(r.attended_rows, cols)
+
+    def norms(span):
+        branch = (r.acc[:, span] + r.vec[:, 8:9]).astype(BF).astype(F32)
+        two = r.stream[:, span] + branch
+        r.two[:, span] = two
+        unit, inv_std = unit_columns(two)
+        r.two_unit[:, span] = unit
+        r.two_std[:, span] = inv_std
+        r.normed[:, span] = (unit * r.vec[:, 9:10] + r.vec[:, 10:11]).astype(BF)
+
+    over_spans(rows, norms)
+    for k in range(ff_blocks):
+        part = slice(k * cols, (k + 1) * cols)
+        r.pre[...] = dot(r.rest[3 + k], r.normed[...], TN) + r.vec[own, 11 + k : 12 + k]
+        r.grad_act[...] = dot(r.rest[3 + ff_blocks + k], r.cot_full[...], TN)
+
+        def bend(span):
+            pre = r.pre[:, span]
+            half = 0.5 * (1.0 + lax.erf(pre * 0.7071067811865476))
+            r.act[part, span] = (pre * half).astype(BF)
+            slope = half + pre * jnp.exp(-0.5 * pre * pre) * 0.3989422804014327
+            r.grad_pre[part, span] = (r.grad_act[:, span] * slope).astype(BF)
+
+        over_spans(rows, bend, 256)
+    r.acc[...] = beside([r.rest[3 + k] for k in range(ff_blocks)])(r.grad_pre, cols)
+
+    def stats(span):
+        scaled = r.acc[:, span] * r.vec[:, 9:10]
+        r.stats[pl.ds(plane, 1), 0:1, span] = jnp.sum(scaled, 0, keepdims=True)[None]
+        r.stats[pl.ds(plane, 1), 1:2, span] = jnp.sum(scaled * r.two_unit[:, span], 0, keepdims=True)[None]
+
+    over_spans(rows, stats)
+
+    def stats_copy(m, slot):
+        return push(
+            r.stats.at[slot], r.stats.at[slot], r.stats_send.at[m], r.stats_recv.at[slot], mdl=m
+        )
+
+    for m in others(plane, mdl):
+        stats_copy(m, plane).start()
+    r.parts[...] = r.acc[...].astype(BF).reshape(mdl, cols, rows)
+    shape = Sum.buffers(plan, (cols, rows))
+    grad_sum = Sum(plan, r.parts, taken_from(r, "grad_", shape))
+    grad_sum.start()
+    out = beside([r.rest[3 + ff_blocks + k] for k in range(ff_blocks)])(r.act, cols)
+    r.out_parts[...] = out.astype(BF).reshape(mdl, cols, rows)
+    grad_sum.middle()
+    out_sum = Sum(plan, r.out_parts, taken_from(r, "out_", shape))
+    out_sum.start()
+    for m in others(plane, mdl):
+        stats_copy(m, m).wait_recv()
+    mean = sum(r.stats[m, 0:1] for m in range(mdl)) / C
+    cross = sum(r.stats[m, 1:2] for m in range(mdl)) / C
+    cot = r.cot[...].astype(F32)
+    grad_normed = grad_sum.finish()
+    unit = r.two_unit[own, :]
+    grad_two = cot + r.two_std[...] * (grad_normed * r.vec[own, 9:10] - mean - unit * cross)
+    r.grad_two[...] = grad_two
+    branch = grad_two.astype(BF)
+    r.branch_full[own, :] = branch
+    trade = Trade(
+        plan, r.send_pos, r.arrival, taken_from(r, "trade_", Trade.buffers(plan, cols, rows))
+    )
+    trade.start(branch)
+    branch_gather = Gather(
+        plan, lambda m: r.branch_full.at[pl.ds(m * cols, cols)],
+        taken_from(r, "branch_", Gather.semaphores(plan)),
+    )
+    branch_gather.start()
+    out_sum.middle()
+
+    def along(values):
+        return jnp.sum(values.astype(F32), 1, keepdims=True)
+
+    r.sums[:, 0:1] = along(branch)
+    r.sums[:, 1:2] = along(grad_normed * unit)
+    r.sums[:, 2:3] = along(grad_normed)
+    for k in range(ff_blocks):
+        part = slice(k * cols, (k + 1) * cols)
+        r.sums[:, 3 + k : 4 + k] = along(r.grad_pre[part, :])
+        r.weight_grads[k] = dot(r.normed[...], r.grad_pre[part, :], NT).astype(BF)
+        r.weight_grads[ff_blocks + k] = dot(r.cot_full[...], r.act[part, :], NT).astype(BF)
+    r.sums[:, 3 + ff_blocks : 4 + ff_blocks] = along(cot)
+    r.grad_slot[own, :] = trade.finish()
+    slot_gather = Gather(
+        plan, lambda m: r.grad_slot.at[pl.ds(m * cols, cols)],
+        taken_from(r, "slot_", Gather.semaphores(plan)),
+    )
+    slot_gather.start()
+    branch_gather.forward()
+    bias = r.vec[own, 11 + ff_blocks : 12 + ff_blocks]
+    r.out[...] = (r.two[own, :] + out_sum.finish() + bias).T.astype(BF)
+    slot_gather.forward()
+    branch_gather.finish()
+    slot_gather.finish()
+    for m in others(plane, mdl):
+        stats_copy(m, plane).wait_send()
+
+
+def mlp(plan, attended_rows, first, rest, cot, send_pos, arrival):
+    cols, rows = cot.shape
+    ff_blocks = FF // C
+    vmem = pltpu.VMEM
+    names = ("pair", "stream", "vec", "cot_full")
+    scratch = dict(
+        acc=vmem((C, rows), F32),
+        two=vmem((C, rows), F32),
+        two_unit=vmem((C, rows), F32),
+        two_std=vmem((1, rows), F32),
+        normed=vmem((C, rows), BF),
+        pre=vmem((cols, rows), F32),
+        grad_act=vmem((cols, rows), F32),
+        act=vmem((ff_blocks * cols, rows), BF),
+        grad_pre=vmem((ff_blocks * cols, rows), BF),
+        stats=vmem((plan.mdl, 8, rows), F32),
+        stats_send=dma(plan.mdl),
+        stats_recv=dma(plan.mdl),
+        parts=vmem((plan.mdl, cols, rows), BF),
+        out_parts=vmem((plan.mdl, cols, rows), BF),
+        **named("grad_", Sum.buffers(plan, (cols, rows))),
+        **named("out_", Sum.buffers(plan, (cols, rows))),
+        **named("trade_", Trade.buffers(plan, cols, rows)),
+        **named("branch_", Gather.semaphores(plan)),
+        **named("slot_", Gather.semaphores(plan)),
+    )
+    return call(
+        functools.partial(mlp_kernel, plan),
+        "mlp",
+        6,
+        dict(
+            attended_rows=attended_rows, **{key: first[key] for key in names}, rest=rest, cot=cot,
+            send_pos=send_pos, arrival=arrival,
+        ),
+        dict(
+            grad_slot=((C, rows), BF),
+            branch_full=((C, rows), BF),
+            grad_two=((cols, rows), F32),
+            out=((rows, cols), BF),
+            weight_grads=((2 * ff_blocks, C, cols), BF),
+            sums=((cols, 4 + ff_blocks), F32),
+        ),
+        scratch,
+        16 * rows * C * cols * ff_blocks,
+    )
+
+
+BACK_ORDER = list(range(TAPS + 5, TAPS + 5 + 2 * FF // C)) + [TAPS + 1, TAPS + 2, TAPS + 3, TAPS + 4]
+BACK_ORDER = BACK_ORDER + [TAPS] + list(range(TAPS))
+
+
+def back_kernel(plan, r):
+    pts, width, depth = plan.pts, plan.width, plan.depth
+    cols, rows = r.turn_acc.shape
+    share = C // pts
+    taps = r.taken.shape[0]
+    mlp_count, attend_count = r.mlp_grads.shape[0], r.attend_grads.shape[0]
+    extra = mlp_count + attend_count + 1
+    groups = r.own.shape[1]
+    me, plane = lax.axis_index("pts"), lax.axis_index("mdl")
     y, z = lax.rem(me, width), me // width
-    side_peers = [z * width + v for v in others(y, width)]
-    far_peers = [v * width + y for v in others(z, depth)]
-    greet([{"pts": v} for v in side_peers + far_peers])
+    own_cols = pl.ds(plane * cols, cols)
+    middle = slice(HALO, HALO + rows)
+    greet([{"pts": v} for v in others(me, pts)])
 
     def store(block, group, place):
         grid = block.astype(BF).reshape(depth, width, share, cols)
         for v in range(width):
-            own[v, group, :, pl.ds(place, 1)] = grid[:, v][:, None]
+            r.own[v, group, :, pl.ds(place, 1)] = grid[:, v][:, None]
 
     def grads(group):
-        low = max(group * PACK, extra)
         for b in range(group * PACK, min(extra, (group + 1) * PACK)):
-            store(early_ref[b], group, b - group * PACK)
+            if b < mlp_count:
+                block = r.mlp_grads[b]
+            elif b < extra - 1:
+                block = r.attend_grads[b - mlp_count]
+            else:
+                block = dot(r.hidden[...], r.mixed[own_cols, :], NT)
+            store(block, group, b - group * PACK)
 
         def one(place, carry):
             tap = group * PACK + place - extra
-            store(
-                dot(back_ref[:, HALO : HALO + rows], x_ref[pl.ds(tap, 1)][0], NT), group, place
-            )
+            store(dot(r.back[:, middle], r.taken[pl.ds(tap, 1)][0], NT), group, place)
             return carry
 
+        low = max(group * PACK, extra)
         if low < (group + 1) * PACK:
             lax.fori_loop(low - group * PACK, PACK, one, 0)
 
-    def side_copy(group, v):
+    def side_copy(group, v, slot):
         return push(
-            own.at[v, group], side.at[group, y], side_send.at[group, v], side_recv.at[group, y],
-            pts=z * width + v,
-        )
-
-    def side_wait(group, v):
+            r.own.at[v, group], r.side.at[group, slot], r.side_send.at[group, v],
+            r.side_recv.at[group, slot], pts=z * width + v,
+        )
+
+    def far_copy(group, v, slot):
         return push(
-            own.at[v, group], side.at[group, v], side_send.at[group, v], side_recv.at[group, v],
-            pts=z * width + v,
-        )
-
-    def far_copy(group, v):
-        return push(
-            acc.at[group, v], far.at[group, z], far_send.at[group, v], far_recv.at[group, z],
-            pts=v * width + y,
-        )
-
-    def far_wait(group, v):
-        return push(
-            acc.at[group, v], far.at[group, v], far_send.at[group, v], far_recv.at[group, v],
-            pts=v * width + y,
+            r.acc.at[group, v], r.far.at[group, slot], r.far_send.at[group, v],
+            r.far_recv.at[group, slot], pts=v * width + y,
         )
 
     def start_side(group):
         grads(group)
         for v in others(y, width):
-            side_copy(group, v).start()
+            side_copy(group, v, y).start()
 
     def start_far(group):
-        total = own[pl.ds(y, 1), group][0].astype(F32)
+        total = r.own[pl.ds(y, 1), group][0].astype(F32)
         for v in others(y, width):
-            side_wait(group, v).wait_recv()
-            total = total + side[group, pl.ds(v, 1)][0].astype(F32)
-        acc[group] = total.astype(BF)
+            side_copy(group, v, v).wait_recv()
+            total = total + r.side[group, pl.ds(v, 1)][0].astype(F32)
+        r.acc[group] = total.astype(BF)
         for v in others(z, depth):
-            far_copy(group, v).start()
+            far_copy(group, v, z).start()
 
     def finish(group):
-        total = acc[group, pl.ds(z, 1)][0].astype(F32)
+        total = r.acc[group, pl.ds(z, 1)][0].astype(F32)
         for v in others(z, depth):
-            far_wait(group, v).wait_recv()
-            total = total + far[group, pl.ds(v, 1)][0].astype(F32)
-        out_ref[group * PACK : (group + 1) * PACK] = total.astype(BF)
+            far_copy(group, v, v).wait_recv()
+            total = total + r.far[group, pl.ds(v, 1)][0].astype(F32)
+        r.summed[group * PACK : (group + 1) * PACK] = total.astype(BF)
+
+    ready = (mlp_count + attend_count) // PACK
+    for group in range(ready):
+        start_side(group)
+
+    def norms(span):
+        grad = r.grad_normed[:, span].astype(F32) * r.vec[:, 4:5]
+        unit = r.one_unit[:, span]
+        delta = r.one_std[:, span] * (
+            grad
+            - jnp.sum(grad, 0, keepdims=True) / C
+            - unit * (jnp.sum(grad * unit, 0, keepdims=True) / C)
+        )
+        r.delta[:, span] = delta
+        grad = (r.branch_full[:, span].astype(F32) + delta) * r.vec[:, 2:3]
+        unit = r.mixed_unit[:, span]
+        r.mixed[:, span] = (
+            r.mixed_std[:, span]
+            * (
+                grad
+                - jnp.sum(grad, 0, keepdims=True) / C
+                - unit * (jnp.sum(grad * unit, 0, keepdims=True) / C)
+            )
+        ).astype(BF)
+
+    over_spans(rows, norms)
+    back = beside([r.pair[m, 0] for m in range(plan.mdl)])(r.mixed, cols)
+    r.back[:, middle] = back.astype(BF)
+
+    def up_copy(target):
+        return push(
+            r.back.at[:, rows : rows + HALO], r.back.at[:, 0:HALO], r.halo_send.at[0],
+            r.halo_recv.at[0], pts=target,
+        )
+
+    def down_copy(target):
+        return push(
+            r.back.at[:, HALO : 2 * HALO], r.back.at[:, HALO + rows : 2 * HALO + rows],
+            r.halo_send.at[1], r.halo_recv.at[1], pts=target,
+        )
+
+    @pl.when(me < pts - 1)
+    def _():
+        up_copy(me + 1).start()
+
+    @pl.when(me == pts - 1)
+    def _():
+        r.back[:, HALO + rows :] = jnp.zeros((C, HALO), BF)
+
+    @pl.when(me > 0)
+    def _():
+        down_copy(me - 1).start()
+
+    @pl.when(me == 0)
+    def _():
+        r.back[:, :HALO] = jnp.zeros((C, HALO), BF)
+
+    lag = 2
+    for group in range(ready, groups):
+        start_side(group)
+        if group >= lag:
+            start_far(group - lag)
+
+    grad_one = r.grad_two[...] + r.delta[own_cols, :]
+    r.grad_one[...] = grad_one
+
+    def along(values):
+        return jnp.sum(values.astype(F32), 1, keepdims=True)
+
+    grad_normed = r.grad_normed[own_cols, :].astype(F32)
+    columns = [
+        along(r.back[own_cols, middle]),
+        along(r.mixed[own_cols, :]),
+        along(grad_one * r.mixed_unit[own_cols, :]),
+        along(grad_one),
+        along(grad_normed * r.one_unit[own_cols, :]),
+        along(grad_normed),
+        r.attend_sums[:, 0:2],
+        r.mlp_sums[...],
+    ]
+    at = 0
+    for column in columns:
+        r.vectors[pl.ds(me, 1), :, at : at + column.shape[1]] = column[None]
+        at += column.shape[1]
+
+    def vector_copy(p, slot):
+        return push(
+            r.vectors.at[slot], r.vectors.at[slot], r.vector_send.at[p], r.vector_recv.at[slot],
+            pts=p,
+        )
+
+    for p in others(me, pts):
+        vector_copy(p, me).start()
+
+    @pl.when(me > 0)
+    def _():
+        up_copy(me - 1).wait_recv()
+
+    @pl.when(me < pts - 1)
+    def _():
+        down_copy(me + 1).wait_recv()
 
     def turn(tap, carry):
-        weight = w_ref[:, pl.ds(taps + 1 - tap, 1)].reshape(C, cols)
-        turned = dot(weight, back_ref[...], TN).astype(BF)
+        weight = r.blocks[:, pl.ds(taps + 1 - tap, 1)].reshape(C, cols)
+        turned = dot(weight, r.back[...], TN).astype(BF)
         for tile in range(rows // TILE):
-            hot = one_hot_window(ids_ref, tap, tile)
-            turn_acc[:, tile * TILE : (tile + 1) * TILE] += dot(
+            hot = one_hot_window(r.ids, tap, tile)
+            r.turn_acc[:, tile * TILE : (tile + 1) * TILE] += dot(
                 turned[:, tile * TILE : tile * TILE + WINDOW], hot
             )
         return carry
 
-    turn_acc[...] = jnp.zeros_like(turn_acc)
-    lag = 2
-    for group in range(groups):
-        start_side(group)
-        if group >= lag:
-            start_far(group - lag)
+    r.turn_acc[...] = jnp.zeros_like(r.turn_acc)
     left = list(range(groups - lag, groups))
     cuts = [taps * i // (len(left) + 1) for i in range(len(left) + 2)]
     for i, group in enumerate(left):
         lax.fori_loop(cuts[i], cuts[i + 1], turn, 0)
         start_far(group)
     lax.fori_loop(cuts[-2], cuts[-1], turn, 0)
-    turn_ref[...] = turn_acc[...].T
+    r.point_grad[...] = (r.turn_acc[...] + r.grad_one[...]).T
     for group in range(groups):
         finish(group)
+    total = r.vectors[pl.ds(me, 1)][0]
+    for p in others(me, pts):
+        vector_copy(p, p).wait_recv()
+        total = total + r.vectors[pl.ds(p, 1)][0]
+    r.vector_grad[...] = total.T
     for group in range(groups):
         for v in others(y, width):
-            side_copy(group, v).wait_send()
+            side_copy(group, v, y).wait_send()
         for v in others(z, depth):
-            far_copy(group, v).wait_send()
-
-
-def back_pass(plan, back_ext, taken, blocks, ids, early):
-    taps, cols, rows = taken.shape
-    total = taps + early.shape[0]
+            far_copy(group, v, z).wait_send()
+    for p in others(me, pts):
+        vector_copy(p, me).wait_send()
+
+    @pl.when(me < pts - 1)
+    def _():
+        up_copy(me + 1).wait_send()
+
+    @pl.when(me > 0)
+    def _():
+        down_copy(me - 1).wait_send()
+
+
+def back_pass(plan, first, ids, grad_normed, branch_full, grad_two, mlp_grads, attend_grads, mlp_sums, attend_sums):
+    taps, cols, rows = first["taken"].shape
+    total = len(BACK_ORDER)
     groups = total // PACK
     share = C // plan.pts
     width, depth = plan.width, plan.depth
-    dma = pltpu.SemaphoreType.DMA
-    vmem = pl.BlockSpec(memory_space=pltpu.VMEM)
-    return pl.pallas_call(
+    vmem = pltpu.VMEM
+    names = (
+        "taken", "blocks", "pair", "vec", "hidden", "mixed_unit", "mixed_std", "one_unit", "one_std"
+    )
+    return call(
         functools.partial(back_kernel, plan),
-        in_specs=[vmem] * 5,
-        out_specs=[vmem] * 2,
-        out_shape=[
-            jax.ShapeDtypeStruct((total, share, cols), BF),
-            jax.ShapeDtypeStruct((rows, cols), F32),
-        ],
-        scratch_shapes=[
-            pltpu.VMEM((width, groups, depth, PACK, share, cols), BF),
-            pltpu.VMEM((groups, width, depth, PACK, share, cols), BF),
-            pltpu.VMEM((groups, depth, PACK, share, cols), BF),
-            pltpu.VMEM((groups, depth, PACK, share, cols), BF),
-            pltpu.VMEM((cols, rows), F32),
-            dma((groups, width)),
-            dma((groups, width)),
-            dma((groups, depth)),
-            dma((groups, depth)),
-        ],
-        compiler_params=params(collective_id=1, has_side_effects=True),
-        cost_estimate=pl.CostEstimate(
-            flops=taps * rows * (WINDOW * 4 + 5 * C) * cols,
-            bytes_accessed=30000000,
-            transcendentals=0,
+        "back_pass",
+        1,
+        dict(
+            **{key: first[key] for key in names}, ids=ids, grad_normed=grad_normed,
+            branch_full=branch_full, grad_two=grad_two, mlp_grads=mlp_grads,
+            attend_grads=attend_grads, mlp_sums=mlp_sums, attend_sums=attend_sums,
         ),
-        name="back_pass",
-    )(back_ext, taken, blocks, ids, early)
-
-
-def head_lanes(ext, cols, head):
-    lane = lax.broadcasted_iota(jnp.int32, ext.shape, 1)
-    return jnp.where((lane >= cols) | (lane // HD == head), ext, jnp.zeros_like(ext))
-
-
-def fetch_step(plan, srcs, dsts, sems):
-    me = lax.axis_index("pts")
-
-    @pl.when(pl.program_id(0) == 0)
-    def _():
-        greet([{"pts": v} for v in others(me, plan.pts)])
-        for src, dst, group in zip(srcs, dsts, sems):
-            fetch_copies(plan, src, dst, group, "start")
-
-
-def fetch_end(plan, srcs, dsts, sems):
-    @pl.when(pl.program_id(0) == pl.num_programs(0) - 1)
-    def _():
-        for src, dst, group in zip(srcs, dsts, sems):
-            fetch_copies(plan, src, dst, group, "wait")
-
-
-def attend_kernel(
-    plan, q_ref, k_ref, v_ref, one, two, out_ref, lse_ref, one_to, two_to, *sems
-):
-    head = pl.program_id(0)
-    moves = (plan, (one, two), (one_to, two_to), (sems[:3], sems[3:]))
-    fetch_step(*moves)
-    rows, width = q_ref.shape
-    keys = k_ref[...]
-    values = v_ref[0]
-    for tile in range(rows // TILE):
-        span = slice(tile * TILE, (tile + 1) * TILE)
-        queries = head_lanes(q_ref[span, :], width // 2, head)
-        scores = dot(keys, queries, NT)
-        top = jnp.max(scores, 0, keepdims=True)
-        soft = jnp.exp(scores - top).astype(BF)
-        summed = dot(values, soft)
-        total = summed[HD : HD + 1]
-        out_ref[:, span] = (summed[:HD] / total).astype(BF)
-        lse_ref[0, :, span] = top + jnp.log(total)
-    fetch_end(*moves)
-
-
-def attend(plan, q_ext, k_ext, v_aug, one, two):
-    rows, width = q_ext.shape
-    heads = v_aug.shape[0]
-    return pl.pallas_call(
-        functools.partial(attend_kernel, plan),
-        grid=(heads,),
-        in_specs=[
-            pl.BlockSpec((rows, width), lambda h: (0, 0)),
-            pl.BlockSpec((rows, width), lambda h: (0, 0)),
-            pl.BlockSpec((1, 2 * HD, rows), lambda h: (h, 0, 0)),
-            pl.BlockSpec(memory_space=pl.ANY),
-            pl.BlockSpec(memory_space=pl.ANY),
-        ],
-        out_specs=[
-            pl.BlockSpec((HD, rows), lambda h: (h, 0)),
-            pl.BlockSpec((1, 1, rows), lambda h: (h, 0, 0)),
-            pl.BlockSpec(memory_space=pl.ANY),
-            pl.BlockSpec(memory_space=pl.ANY),
-        ],
-        out_shape=[
-            jax.ShapeDtypeStruct((heads * HD, rows), BF),
-            jax.ShapeDtypeStruct((heads, 1, rows), F32),
-            fetch_shape(plan, one),
-            fetch_shape(plan, two),
-        ],
-        scratch_shapes=fetch_sems(plan) + fetch_sems(plan),
-        compiler_params=params(collective_id=2, has_side_effects=True),
-        cost_estimate=pl.CostEstimate(
-            flops=2 * heads * rows * rows * width, bytes_accessed=rows * width * 6, transcendentals=heads * rows * rows
+        dict(
+            summed=((total, share, cols), BF),
+            point_grad=((rows, cols), F32),
+            vector_grad=((12 + FF // C, cols), F32),
         ),
-        name="attend",
-    )(q_ext, k_ext, v_aug, one, two)
-
-
-def attend_back_kernel(
-    plan, q_ref, k_ref, kt_ref, v_ref, do_ref, lse_ref, inner_ref, one, two,
-    dq_ref, dk_ref, dv_ref, one_to, two_to, dk_acc, dv_acc, *sems,
-):
-    head = pl.program_id(0)
-    moves = (plan, (one, two), (one_to, two_to), (sems[:3], sems[3:]))
-    fetch_step(*moves)
-    rows, width = q_ref.shape
-    cols = width // 2
-
-    @pl.when(head == 0)
-    def _():
-        dk_acc[...] = jnp.zeros_like(dk_acc)
-        dv_acc[...] = jnp.zeros_like(dv_acc)
-
-    queries = head_lanes(q_ref[...], cols, head)
-    pure = queries[:, :cols]
-    grad = head_lanes(do_ref[...], cols, head)
-    lse = lse_ref[0]
-    inner = inner_ref[0]
-    dq = jnp.zeros((HD, rows), F32)
-    for tile in range(rows // TILE):
-        span = slice(tile * TILE, (tile + 1) * TILE)
-        scores = dot(k_ref[span, :], queries, NT)
-        soft = jnp.exp(scores - lse)
-        grad_soft = dot(v_ref[span, :], grad, NT)
-        grad_scores = (soft * (grad_soft - inner)).astype(BF)
-        dv_acc[span, :] += dot(soft.astype(BF), grad)
-        dk_acc[span, :] += dot(grad_scores, pure)
-        dq = dq + dot(kt_ref[:, span], grad_scores)
-    dq_ref[...] = (dq * HD ** (-0.5)).astype(BF)
-
-    @pl.when(head == pl.num_programs(0) - 1)
-    def _():
-        dk_ref[...] = dk_acc[...].astype(BF)
-        dv_ref[...] = dv_acc[...].astype(BF)
-
-    fetch_end(*moves)
-
-
-def attend_back(plan, q_ext, k_ext, keys_t, values, grad, lse, inner, one, two):
-    rows, width = q_ext.shape
-    cols = width // 2
-    heads = cols // HD
-    whole = lambda h: (0, 0)
-    return pl.pallas_call(
-        functools.partial(attend_back_kernel, plan),
-        grid=(heads,),
-        in_specs=[
-            pl.BlockSpec((rows, width), whole),
-            pl.BlockSpec((rows, width), whole),
-            pl.BlockSpec((HD, rows), lambda h: (h, 0)),
-            pl.BlockSpec((rows, cols), whole),
-            pl.BlockSpec((rows, cols), whole),
-            pl.BlockSpec((1, 1, rows), lambda h: (h, 0, 0)),
-            pl.BlockSpec((1, 1, rows), lambda h: (h, 0, 0)),
-            pl.BlockSpec(memory_space=pl.ANY),
-            pl.BlockSpec(memory_space=pl.ANY),
-        ],
-        out_specs=[
-            pl.BlockSpec((HD, rows), lambda h: (h, 0)),
-            pl.BlockSpec((rows, cols), whole),
-            pl.BlockSpec((rows, cols), whole),
-            pl.BlockSpec(memory_space=pl.ANY),
-            pl.BlockSpec(memory_space=pl.ANY),
-        ],
-        out_shape=[
-            jax.ShapeDtypeStruct((cols, rows), BF),
-            jax.ShapeDtypeStruct((rows, cols), BF),
-            jax.ShapeDtypeStruct((rows, cols), BF),
-            fetch_shape(plan, one),
-            fetch_shape(plan, two),
-        ],
-        scratch_shapes=[pltpu.VMEM((rows, cols), F32), pltpu.VMEM((rows, cols), F32)]
-        + fetch_sems(plan)
-        + fetch_sems(plan),
-        compiler_params=params(collective_id=3, has_side_effects=True),
-        cost_estimate=pl.CostEstimate(
-            flops=5 * heads * rows * rows * width, bytes_accessed=rows * width * 20, transcendentals=heads * rows * rows
+        dict(
+            own=vmem((width, groups, depth, PACK, share, cols), BF),
+            side=vmem((groups, width, depth, PACK, share, cols), BF),
+            acc=vmem((groups, depth, PACK, share, cols), BF),
+            far=vmem((groups, depth, PACK, share, cols), BF),
+            turn_acc=vmem((cols, rows), F32),
+            grad_one=vmem((cols, rows), F32),
+            delta=vmem((C, rows), F32),
+            mixed=vmem((C, rows), BF),
+            back=vmem((C, rows + 2 * HALO), BF),
+            vectors=vmem((plan.pts, cols, 12 + FF // C), F32),
+            side_send=dma(groups, width),
+            side_recv=dma(groups, width),
+            far_send=dma(groups, depth),
+            far_recv=dma(groups, depth),
+            halo_send=dma(2),
+            halo_recv=dma(2),
+            vector_send=dma(plan.pts),
+            vector_recv=dma(plan.pts),
         ),
-        name="attend_back",
-    )(q_ext, k_ext, keys_t, values, grad, lse, inner, one, two)
+        taps * rows * (WINDOW * 4 + 5 * C) * cols,
+    )
 
 
 def adam(first, second, grad):
@@ -1114,20 +1457,6 @@
     )(grads, left, right, first, second)
 
 
-def widen(shard_rows):
-    return lax.all_gather(shard_rows, "mdl", axis=1, tiled=True)
-
-
-def add_parts(partial_value):
-    return lax.psum_scatter(
-        partial_value.astype(BF), "mdl", scatter_dimension=1, tiled=True
-    ).astype(F32)
-
-
-def trade(buffer):
-    return lax.all_to_all(buffer, "pts", split_axis=0, concat_axis=0, tiled=True)
-
-
 def scan_index(row_ids, scan_lengths):
     bounds = jnp.cumsum(scan_lengths)
     return jnp.sum((row_ids[..., None] >= bounds[:-1]).astype(jnp.int32), -1)
@@ -1135,26 +1464,6 @@
 
 def count(mask):
     return jnp.sum(mask.astype(jnp.int32), 1)
-
-
-def unit_rows(values):
-    mean = jnp.mean(values, -1, keepdims=True)
-    centred = values - mean
-    inv_std = lax.rsqrt(jnp.mean(centred * centred, -1, keepdims=True) + NORM_EPS)
-    return centred * inv_std, inv_std
-
-
-def unit_back(grad_unit, unit, inv_std):
-    mean = jnp.mean(grad_unit, -1, keepdims=True)
-    cross = jnp.mean(grad_unit * unit, -1, keepdims=True)
-    return inv_std * (grad_unit - mean - unit * cross)
-
-
-def gelu_slope(pre_act):
-    return (
-        0.5 * (1.0 + lax.erf(pre_act * 0.7071067811865476))
-        + pre_act * jnp.exp(-0.5 * pre_act * pre_act) * 0.3989422804014327
-    )
 
 
 def local(
@@ -1180,15 +1489,10 @@
     mdl = lax.axis_size("mdl")
     pts_index = lax.axis_index("pts")
     mdl_index = lax.axis_index("mdl")
-    heads = cols // HD
-    ff_blocks = FF // C
     patch_count = slot_count // PATCH
     capacity = 2 * rows // pts
     matrix_rate = 1.6 * C ** (-0.5)
     plan = Layout(pts, mdl, owner_slot.shape[0])
-
-    def own(full):
-        return lax.dynamic_slice_in_dim(full, mdl_index * cols, cols, full.ndim - 1)
 
     row_ids = pts_index * rows + jnp.arange(rows, dtype=jnp.int32)
     own_scan = scan_index(row_ids, scan_lengths)
@@ -1200,8 +1504,6 @@
     place = jnp.arange(rows, dtype=jnp.int32)
     rank = count((target[None, :] == target[:, None]) & (place[None, :] < place[:, None]))
     send_pos = target * capacity + rank
-    buffer_ids = jnp.arange(pts * capacity, dtype=jnp.int32)
-    pack = (buffer_ids[:, None] == send_pos[None, :]).astype(BF)
     held = jnp.zeros((rows + PATCH,), jnp.int32)
     held_patch = jnp.zeros((rows + PATCH,), jnp.int32)
     offset = jnp.int32(0)
@@ -1225,166 +1527,67 @@
     sorting = order[None, :] == place[:, None]
     arrival = jnp.sum(jnp.where(sorting, arrival[None, :], 0), 1)
     group = jnp.sum(jnp.where(sorting, held_group[None, :], 0), 1)
-    unpack = (buffer_ids[None, :] == arrival[:, None]).astype(BF)
     group_ids = jnp.arange(cols, dtype=jnp.int32)
     same = group[:, None] == group_ids[None, :]
     group_q = same.astype(BF)
     group_k = jnp.where(same | (group_ids[None, :] >= patch_count * scan_count), 0.0, -1e30).astype(BF)
 
-    def to_slots(values):
-        return dot(unpack, trade(dot(pack, values).astype(BF))).astype(BF)
-
-    def from_slots(values):
-        return dot(pack, trade(dot(unpack, values, TN).astype(BF)), TN).astype(BF)
-
     owned = weights.astype(BF).reshape(plan.slots, C // pts, mdl, cols).transpose(2, 0, 1, 3)
+    cot = cotangent.T
+    send_pos, arrival = send_pos[None], arrival[None]
     first = front(
+        plan, owner_slot[jnp.array(ORDER)], owned, points.T, cot, vectors, ids, send_pos, arrival
+    )
+    rest = first["rest"]
+    kept = attend(
         plan,
-        owner_slot[jnp.array(ORDER)],
-        owned,
-        points.T,
-        cotangent.T,
+        first["slot_in"],
+        rest,
         vectors,
-        ids,
-        send_pos[None],
-        arrival[None],
-    )
-    blocks, taken, vec = first["blocks"], first["taken"], first["vec"].T
-    cot_full = first["cot_full"].T
-    linear_full = first["pair"][:, 0].transpose(1, 0, 2).reshape(C, C)
-    projection_full = first["pair"][:, 1].transpose(1, 0, 2).reshape(C, C)
-    hidden = first["hidden"].T
-    mixed_unit, mixed_std = first["mixed_unit"].T, first["mixed_std"].T
-    stream_one, one_unit, one_std = first["stream"].T, first["one_unit"].T, first["one_std"].T
-    slot_in = first["slot_in"].T
-
-    def block(b):
-        return blocks[:, PLACE[b]].reshape(C, cols)
-
-    query_map, key_map, value_map = block(TAPS + 1), block(TAPS + 2), block(TAPS + 3)
-    projection = block(TAPS + 4)
-    queries = (dot(slot_in, query_map) + vectors[6]).astype(BF)
-    keys_all = dot(slot_in, key_map).astype(BF)
-    values_all = (dot(slot_in, value_map) + vectors[7]).astype(BF)
-    q_ext = jnp.concatenate([queries * BF(HD ** (-0.5)), group_q], 1)
-    k_ext = jnp.concatenate([keys_all, group_k], 1)
-    v_aug = jnp.concatenate(
-        [values_all.T.reshape(heads, HD, rows), jnp.ones((heads, HD, rows), BF)], 1
-    )
-    attended_t, lse, left_whole, right_whole = attend(
-        plan, q_ext, k_ext, v_aug, row_eigen_basis.astype(BF), right_basis.astype(BF)
-    )
-    attended = attended_t.T
-    attended_rows = widen(from_slots(attended))
-    branch = (dot(attended_rows, projection_full, NT) + vec[8]).astype(BF)
-
-    stream_two = stream_one + branch.astype(F32)
-    two_unit, two_std = unit_rows(stream_two)
-    normed_two = (two_unit * vec[9] + vec[10]).astype(BF)
-    first_mlp = jnp.concatenate([block(TAPS + 5 + k) for k in range(ff_blocks)], 1)
-    second_mlp = jnp.concatenate([block(TAPS + 5 + ff_blocks + k) for k in range(ff_blocks)], 1)
-    first_bias = vectors[11 : 11 + ff_blocks].reshape(ff_blocks * cols)
-    pre_act = dot(normed_two, first_mlp) + first_bias
-    activ = jax.nn.gelu(pre_act, approximate=False).astype(BF)
-    out_part = dot(activ, second_mlp, NT)
-    result = (own(stream_two) + add_parts(out_part) + vectors[11 + ff_blocks]).astype(BF)
-    cot = cotangent.astype(F32)
-    grad_pre = (dot(cot_full, second_mlp) * gelu_slope(pre_act)).astype(BF)
-    grad_two_part = dot(grad_pre, first_mlp, NT)
-    scaled_part = grad_two_part * vec[9]
-    row_sums = lax.psum(
-        jnp.stack([jnp.sum(scaled_part, 1), jnp.sum(scaled_part * two_unit, 1)]), "mdl"
-    )
-    grad_normed_two = add_parts(grad_two_part)
-    own_two_unit = own(two_unit)
-    grad_two = cot + two_std * (
-        grad_normed_two * vectors[9]
-        - row_sums[0][:, None] / C
-        - own_two_unit * row_sums[1][:, None] / C
-    )
-
-    grad_branch = grad_two.astype(BF)
-    grad_slot = widen(to_slots(grad_branch))
-    grad_branch_full = widen(grad_branch)
-    grad_attended = dot(grad_slot, projection).astype(BF)
-    inner = jnp.sum(
-        (grad_attended.astype(F32) * attended.astype(F32)).reshape(rows, heads, HD), -1
-    ).T.reshape(heads, 1, rows)
-    grad_queries_t, grad_keys, grad_values, first_whole, second_whole = attend_back(
+        group_q,
+        group_k,
+        send_pos,
+        arrival,
+        row_eigen_basis.astype(BF),
+        right_basis.astype(BF),
+    )
+    middle = mlp(plan, kept["attended_rows"], first, rest, cot, send_pos, arrival)
+    back = attend_back(
         plan,
-        q_ext,
-        k_ext,
-        keys_all.T,
-        values_all,
-        grad_attended,
-        lse,
-        inner,
+        kept,
+        middle["grad_slot"],
+        first["slot_in"],
+        rest,
+        first["pair"],
+        send_pos,
+        arrival,
         first_moment.astype(BF),
         second_moment.astype(BF),
     )
-    grad_queries = grad_queries_t.T
-    slot_back = (
-        dot(grad_queries, query_map, NT)
-        + dot(grad_keys, key_map, NT)
-        + dot(grad_values, value_map, NT)
-    )
-    grad_normed = widen(from_slots(add_parts(slot_back).astype(BF))).astype(F32)
-    grad_one = grad_branch_full.astype(F32) + unit_back(grad_normed * vec[4], one_unit, one_std)
-    own_grad_one = grad_two + own(grad_one - grad_branch_full.astype(F32))
-    grad_mixed = unit_back(grad_one * vec[2], mixed_unit, mixed_std).astype(BF)
-
-    back = dot(linear_full, grad_mixed, NT).astype(BF)
-    early = [
-        dot(hidden, own(grad_mixed), TN),
-        dot(slot_in, grad_queries, TN),
-        dot(slot_in, grad_keys, TN),
-        dot(slot_in, grad_values, TN),
-        dot(grad_slot, attended, TN),
-    ]
-    early += [
-        dot(normed_two, grad_pre[:, k * cols : (k + 1) * cols], TN) for k in range(ff_blocks)
-    ]
-    early += [dot(cot_full, activ[:, k * cols : (k + 1) * cols], TN) for k in range(ff_blocks)]
-    early = jnp.stack([e.astype(BF) for e in early])
-    up = [(i, i + 1) for i in range(pts - 1)]
-    down = [(i + 1, i) for i in range(pts - 1)]
-    low_back = lax.ppermute(back[:, rows - HALO :], "pts", up)
-    high_back = lax.ppermute(back[:, :HALO], "pts", down)
-    back_ext = jnp.concatenate([low_back, back, high_back], 1)
-    summed, conv_grad = back_pass(plan, back_ext, taken, blocks, ids, early)
-    point_grad = own_grad_one + conv_grad
-    block_of_slot = jnp.zeros_like(owner_slot).at[owner_slot].set(
-        jnp.arange(owner_slot.shape[0], dtype=jnp.int32)
-    )
-    summed = summed[(block_of_slot + early.shape[0]) % owner_slot.shape[0]]
+    last = back_pass(
+        plan,
+        first,
+        ids,
+        back["grad_normed"],
+        middle["branch_full"],
+        middle["grad_two"],
+        middle["weight_grads"],
+        back["weight_grads"],
+        middle["sums"],
+        back["sums"],
+    )
+    vector_grad = last["vector_grad"]
+    places = jnp.array([BACK_ORDER.index(b) for b in range(len(BACK_ORDER))], jnp.int32)
+    place_of_slot = jnp.zeros_like(owner_slot).at[owner_slot].set(places)
     grad_rows, results = owner_update(
-        plan, summed, left_whole, right_whole, first_whole, second_whole
+        plan,
+        last["summed"][place_of_slot],
+        kept["left_whole"],
+        kept["right_whole"],
+        back["first_whole"],
+        back["second_whole"],
     )
     reduced = grad_rows.transpose(1, 2, 0, 3).reshape(plan.slots, C // pts, C)
-
-    def total(values):
-        return jnp.sum(values.astype(F32), 0)
-
-    vector_local = jnp.stack(
-        [
-            lax.dynamic_slice_in_dim(jnp.sum(back.astype(F32), 1), mdl_index * cols, cols, 0),
-            total(own(grad_mixed)),
-            total(own_grad_one * own(mixed_unit)),
-            total(own_grad_one),
-            total(own(grad_normed) * own(one_unit)),
-            total(own(grad_normed)),
-            total(grad_queries),
-            total(grad_values),
-            total(grad_branch),
-            total(grad_normed_two * own_two_unit),
-            total(grad_normed_two),
-        ]
-    )
-    vector_local = jnp.concatenate(
-        [vector_local, total(grad_pre).reshape(ff_blocks, cols), total(cot)[None]], 0
-    )
-    vector_grad = lax.psum(vector_local, "pts")
-
     rotated, update = results[:, 0].astype(F32), results[:, 1].astype(F32)
     new_first, new_second, _ = adam(first_moment, second_moment, rotated)
     new_weights = weights - matrix_rate * (update + MATRIX_DECAY * weights)
@@ -1393,8 +1596,8 @@
     )
     new_vectors = vectors - VECTOR_RATE * vector_step
     return (
-        result,
-        point_grad,
+        middle["out"],
+        last["point_grad"],
         reduced.astype(F32),
         new_first,
         new_second,

time: 713 us -> 529 us (0.74)
  Pallas kernels: 348 us -> 490 us
  waiting for transfers between devices: 93.4 us -> 0 us
  blocking collectives: 77.7 us -> 0 us
  matrix products: 53.1 us -> 0 us
  local copies, waits for them, and re-layouts: 55.7 us -> 10 us
  other arithmetic: 53.9 us -> 21.7 us
  between operations: 17.7 us -> 3.1 us
    pallas_call x4 -> x5, Pallas kernels: 269 us -> 413 us  [call(): pl.pallas_call(body, in_specs=[pl.BlockSpec(memory_space=space(key)) for...]
    all_to_all x3 -> x0, blocking collectives: 58.7 us -> none  [trade(): lax.all_to_all(buffer, 'pts', split_axis=0, concat_axis=0, tiled=True)]
    all_gather x4 -> x0, waiting for transfers between devices: 53.7 us -> none  [widen(): return lax.all_gather(shard_rows, 'mdl', axis=1, tiled=True)]
    dot_general x32 -> x0, matrix products: 53.1 us -> none  [dot(): return lax.dot_general(a, b, dims, preferred_element_type=F32)]
    unnamed x10 -> x0, waiting for transfers between devices: 39.7 us -> none
    unnamed x176 -> x43, local copies, waits for them, and re-layouts: 25 us -> 4.49 us
    psum x2 -> x0, blocking collectives: 19 us -> none  [the longest x1 13.6 us: local(): vector_grad = lax.psum(vector_local, 'pts')]
    reduce_sum x11 -> x0, other arithmetic: 17.6 us -> none  [the longest x6 7.91 us: total(): return jnp.sum(values.astype(F32), 0)]
  transfers between devices with their start and end apart: 9 -> 0, of which waited for: 6 -> 0; matrix products, arithmetic and copies ran while one was open for 7% -> 0% of each run, Pallas kernels for 0% -> 0%
where the time goes in v4:
time: 529 us; the launch traced here: 525 us
  Pallas kernels  490 us (93%)
  other arithmetic  21.7 us (4%)
  local copies, waits for them, and re-layouts  10 us (2%)
    pallas_call x5, Pallas kernels, call(): pl.pallas_call(body, in_specs=[pl.BlockSpec(memory_space=space(key)) for...  413 us
    pallas_call x1, Pallas kernels, owner_update(): pl.pallas_call(functools.partial(owner_kernel, plan), in_specs=[vmem] * 5...  77.8 us

profile of v4, /device:TPU:29, one launch (start us, length us, event | category | flops | bytes accessed | tf_op | source)
XLA Modules:
  0.0 525.2 jit_solution(7083963297725635837)
XLA Ops:
  0.6 0.0 copy-start.7
  0.7 0.7 pad_clamp_fusion.1
  1.4 1.9 gather_fusion
  3.3 0.0 copy-start.12
  3.3 0.0 copy-start.17
  3.3 2.4 bitcast_bitcast_fusion.refs_1_
  5.7 0.0 copy-done.7
  5.7 0.8 copy.35
  6.6 0.8 copy.36
  7.4 0.2 reduce-window.4
  7.6 0.0 copy-done.10
  7.6 0.7 select_bitcast_fusion.refs_5_.refs_9_
  8.4 0.5 convert_reduce_fusion.2
  8.9 0.6 multiply_add_fusion.3
  9.5 0.6 convert_reduce_fusion.3
  12.1 0.2 slice_dynamic-update-slice_fusion
  12.3 1.0 convert_reduce_fusion
  13.4 0.6 convert_reduce_fusion.1
  13.9 1.8 select_reduce_fusion
  15.8 139.9 %front.1 = (bf16[8,40,64,128]{3,2,1,0:T(8,128)(2,1)}, bf16[27,128,1024]{2,1,0:T(8,128)(2,1)}, bf16[512,1024]{1,0:T(8,128)(2,1)}, bf16[4,2,512,128]{3,2,1,0:T(8,1...) custom-call(s32[40]{0:T(128)} %gather_fusion, ...), custom_call_target="tpu_custom_call" | custom-call | flops 18119393280 | bytes 20000000 | tf_op jit(solution)/shard_map/front/pallas_call | solution.py:125
  155.7 0.0 copy-start.5
  155.8 0.9 fusion.6.refs_3_
  156.7 0.9 select_convert_fusion.refs_4_
  157.6 0.9 convert_element_type.85.refs_7_
  158.5 0.9 convert_element_type.86.refs_8_
  159.4 52.7 %attend.1 = (bf16[1024,256]{1,0:T(8,128)(2,1)}, bf16[1024,256]{1,0:T(8,128)(2,1)}, bf16[1024,128]{1,0:T(8,128)(2,1)}, bf16[128,1024]{1,0:T(8,128)(2,1)}, f32[8,1...) custom-call(bf16[512,1024]{1,0:T(8,128)(2,1)} %get-tuple-element.48., ...), custom_call_target="tpu_custom_call" | custom-call | flops 4294967296 | bytes 20000000 | tf_op jit(solution)/shard_map/attend/pallas_call | solution.py:125
  212.2 0.0 copy-start.2
  212.2 56.9 %mlp.1 = (bf16[512,1024]{1,0:T(8,128)(2,1)}, bf16[512,1024]{1,0:T(8,128)(2,1)}, f32[128,1024]{1,0:T(8,128)}, bf16[1024,128]{1,0:T(8,128)(2,1)}, bf16[8,512,128]{2,1,0:T(8,128)(2,1)}, /*index=5*/f32[128,8]{1,0:T(8,128)}) custom-call(bf16[512,1024]{1,0:T(8,128)(2,1)} %get-tuple-element.50.refs_0_, ...), custom_call_target="tpu_custom_call" | custom-call | flops 4294967296 | bytes 20000000 | tf_op jit(solution)/shard_map/mlp/pallas_call | solution.py:125
  269.1 0.0 copy-start.3
  269.1 0.0 copy-done.2
  269.1 0.9 convert_element_type.87.refs_11_
  270.0 0.6 copy-done.3
  270.6 0.9 convert_element_type.88.refs_12_
  271.5 63.3 %attend_back.1 = (bf16[512,1024]{1,0:T(8,128)(2,1)}, bf16[4,512,128]{2,1,0:T(8,128)(2,1)}, f32[128,8]{1,0:T(8,128)}, bf16[2,8,64,512]{3,2,1,0:T(8,128)(2,1)}, bf16[2,8,64,512]{3,2,1,0:T(8,128)(2,1)}) custom-call(bf16[1024,256]{1,0:T(8,128)(2,1)} %get-tuple-element.63.refs_0_, bf16[1024,256]{1,0:T(8,128)(2,1)} %get-tuple-element.64.refs_1_, ...), custom_call_target="tpu_custom_call" | custom-call | flops 10737418240 | bytes 20000000 | tf_op jit(solution)/shard_map/attend_back/pallas_call | solution.py:125
  334.8 0.0 copy-start
  334.8 99.8 %back_pass.1 = (bf16[40,64,128]{2,1,0:T(8,128)(2,1)}, f32[1024,128]{1,0:T(8,128)}, f32[16,128]{1,0:T(8,128)}) custom-call(bf16[27,128,1024]{2,1,0:T(8,128)(2,1)} %get-tuple-element.56.refs_0_, bf16[8,40,64,128]{3,2,1,0:T(8,128)(2,1)} %get-tuple-element.57.refs_1_, bf16[4,2,512,128]{3,2,1,0:T(8,128)(2,1)} %get-tuple-element.51.refs_1_.refs_8_.refs_2_, ...), custom_call_target="tpu_custom_call" | custom-call | flops 19931332608 | bytes 20000000 | tf_op jit(solution)/shard_map/back_pass/pallas_call | solution.py:125
  434.6 0.8 scatter_custom_fusion
  435.5 2.6 gather_fusion.1
  438.1 77.8 %owner_update.1 = (bf16[4,10,64,128]{3,2,1,0:T(8,128)(2,1)}, bf16[10,2,64,512]{3,2,1,0:T(8,128)(2,1)}) custom-call(bf16[40,64,128]{2,1,0:T(8,128)(2,1)} %gather_fusion.1, bf16[2,8,64,512]{3,2,1,0:T(8,128)(2,1)} %get-tuple-element.78.left_ref, bf16[2,8,64,512]{3,2,1,0:T(8,128)(2,1)} %get-tuple-element.79.right_ref, ...), custom_call_target="tpu_custom_call" | custom-call | flops 2147483648 | bytes 10000000 | tf_op jit(solution)/shard_map/owner_update/pallas_call | solution.py:1431
  515.9 0.0 copy-start.1
  515.9 2.4 copy_bitcast_fusion
  518.4 0.0 copy-start.16
  518.4 3.8 fusion.17
  522.3 0.6 multiply_subtract_fusion
  522.9 0.7 copy.47
  523.6 0.0 copy-done.6
  523.6 0.8 copy.48
  524.4 0.6 copy.49
  (35 shorter events, 0.2 us)
Async XLA Ops:
  0.6 5.1 copy-start.7
  3.3 3.3 copy-start.8
  3.3 4.1 copy-start.18
  3.3 4.3 copy-start.10
  3.3 5.1 copy-start.13
  3.3 6.2 %copy-start.12 = (s32[2048]{0:T(1024)S(1)}, s32[2048]{0:T(1024)}, u32[]{:S(2)}) copy-start(s32[2048]{0:T(1024)} %param.22) | copy-start | bytes 24580
  3.3 6.2 %copy-start.17 = (pred[2048]{0:T(1024)(128)(4,1)S(1)}, pred[2048]{0:T(1024)(128)(4,1)}, u32[]{:S(2)}) copy-start(pred[2048]{0:T(1024)(128)(4,1)} %constant.79.clone.1) | copy-start | bytes 6148
  15.8 141.8 %copy-start.4 = (f32[10,64,512]{2,1,0:T(8,128)S(1)}, f32[10,64,512]{2,1,0:T(8,128)}, u32[]{:S(2)}) copy-start(f32[10,64,512]{2,1,0:T(8,128)} %param.25) | copy-start | bytes 3932164
  155.7 2.8 copy-start.5
  212.2 56.9 %copy-start.2 = (f32[10,64,512]{2,1,0:T(8,128)S(1)}, f32[10,64,512]{2,1,0:T(8,128)}, u32[]{:S(2)}) copy-start(f32[10,64,512]{2,1,0:T(8,128)} %param.27) | copy-start | bytes 3932164
  269.1 1.6 copy-start.3
  334.8 99.8 %copy-start = (s32[40]{0:T(128)S(1)}, s32[40]{0:T(128)}, u32[]{:S(2)}) copy-start(s32[40]{0:T(128)} %param.23) | copy-start | bytes 484
  515.9 2.4 copy-start.1
  518.4 3.9 copy-start.11
  518.4 3.9 copy-start.14
  518.4 3.9 copy-start.15
  518.4 3.9 copy-start.16
  518.4 4.5 copy-start.9
  518.4 5.2 copy-start.6

commit v5 on v4

v5 whole, which is shorter than its diff:
```python
import functools
import types

import jax
import jax.numpy as jnp
from jax import lax
from jax.experimental import pallas as pl
from jax.experimental.pallas import tpu as pltpu
from jax.sharding import PartitionSpec as P

C = 512
HD = 16
FF = 2048
TAPS = 27
HALO = 256
PATCH = 1024
STEP = 5

NORM_EPS = 1e-05
BETA_ONE = 0.9
BETA_TWO = 0.999
ADAM_EPS = 1e-08
VECTOR_RATE = 0.5
MATRIX_DECAY = 0.05
TILE = 256
WINDOW = TILE + 2 * HALO
BF = jnp.bfloat16
F32 = jnp.float32
VMEM_LIMIT = 56 * 1024 * 1024

NN = (((1,), (0,)), ((), ()))
NT = (((1,), (1,)), ((), ()))
TN = (((0,), (0,)), ((), ()))


def dot(a, b, dims=NN):
    return lax.dot_general(a, b, dims, preferred_element_type=F32)


def params(**kw):
    return pltpu.CompilerParams(vmem_limit_bytes=VMEM_LIMIT, **kw)


MESH = pl.DeviceIdType.MESH
PTS, MDL = "pts", "mdl"
START, WAIT = range(2)


def push(src, dst, send_sem, recv_sem, **target):
    return pltpu.make_async_remote_copy(
        src_ref=src,
        dst_ref=dst,
        send_sem=send_sem,
        recv_sem=recv_sem,
        device_id=target,
        device_id_type=MESH,
    )


def greet(peers):
    barrier = pltpu.get_barrier_semaphore()
    for peer in peers:
        pl.semaphore_signal(barrier, inc=1, device_id=peer, device_id_type=MESH)
    pl.semaphore_wait(barrier, len(peers))


def others(index, size):
    return [lax.rem(index + step, size) for step in range(1, size)]


class Layout:
    def __init__(self, pts, mdl, blocks, groups):
        self.pts, self.mdl, self.groups = pts, mdl, groups
        self.slots = blocks // mdl
        self.each = -(-self.slots // pts)
        self.shift = max(pts - self.slots, 0) // 2 if self.slots < pts else (pts - self.slots % pts) // 2
        self.width = mdl // 2 if pts % (mdl // 2) == 0 else 1
        self.depth = pts // self.width

    def worker(self, j):
        return (j + self.shift) % self.pts

    def work(self, me, k):
        return lax.rem(me + self.pts - self.shift, self.pts) + k * self.pts


def fetch_copies(plan, src, dst, sems, act):
    send, recv, here = sems
    me = lax.axis_index(PTS)
    for j in range(plan.slots):
        target, k = plan.worker(j), j // plan.pts

        @pl.when(me != target)
        def _():
            copy = push(src.at[j], dst.at[k, me], send.at[j], recv.at[k, me], pts=target)
            copy.start() if act == START else copy.wait_send()

        @pl.when(me == target)
        def _():
            copy = pltpu.make_async_copy(src.at[j], dst.at[k, me], here.at[k])
            if act == START:
                copy.start()
            else:
                copy.wait()
                for source in others(me, plan.pts):
                    push(
                        src.at[j], dst.at[k, source], send.at[j], recv.at[k, source], pts=source
                    ).wait_recv()


def fetch_sems(plan):
    return [dma(plan.slots), dma(plan.each, plan.pts), dma(plan.each)]


def fetch_shape(plan, src):
    return jax.ShapeDtypeStruct((plan.each, plan.pts) + src.shape[1:], BF)


class Late:
    def __init__(self, *what):
        self.what = what


def call(kernel, name, collective, inputs, outputs, scratch, flops, smem=(), free=()):
    vmem = pltpu.VMEM
    leaves, tree = jax.tree.flatten(scratch, is_leaf=lambda x: not isinstance(x, (dict, list)))
    late_in = [key for key, value in inputs.items() if isinstance(value, Late)]
    late_out = [key for key, value in outputs.items() if isinstance(value, Late)]
    values = {key: v.what[0] if key in late_in else v for key, v in inputs.items()}
    shapes = {key: v.what if key in late_out else v for key, v in outputs.items()}
    near = [vmem(values[key].shape, values[key].dtype) for key in late_in]
    near += [vmem(*shapes[key]) for key in late_out]
    late = late_in + late_out

    def space(key, value):
        return pltpu.SMEM if key in smem else pl.ANY if key in free or key in late else vmem

    def grouped(x):
        if isinstance(x, dict):
            return types.SimpleNamespace(**{key: grouped(value) for key, value in x.items()})
        return [grouped(value) for value in x] if isinstance(x, list) else x

    def body(*refs):
        count = len(inputs) + len(outputs)
        given = dict(zip(inputs, refs))
        given.update(zip(outputs, refs[len(inputs) : count]))
        own, sems = refs[count : count + len(late)], refs[count + len(late) : count + 2 * len(late)]
        r = grouped(jax.tree.unflatten(tree, refs[count + 2 * len(late) :]))
        for key, ref in given.items():
            setattr(r, key, ref)
        for key, ref, sem in zip(late, own, sems):
            pair = (given[key], ref) if key in late_in else (ref, given[key])
            setattr(r, key, ref)
            setattr(r, key + "_move", functools.partial(pltpu.make_async_copy, *pair, sem))
        kernel(r)

    results = pl.pallas_call(
        body,
        in_specs=[pl.BlockSpec(memory_space=space(*item)) for item in inputs.items()],
        out_specs=[pl.BlockSpec(memory_space=space(*item)) for item in outputs.items()],
        out_shape=[jax.ShapeDtypeStruct(*shape) for shape in shapes.values()],
        scratch_shapes=near + [dma() for _ in late] + leaves,
        compiler_params=params(collective_id=collective, has_side_effects=True),
        cost_estimate=pl.CostEstimate(
            flops=flops, bytes_accessed=20000000, transcendentals=1000000
        ),
        name=name,
    )(*values.values())
    return types.SimpleNamespace(**dict(zip(outputs, results)))


def moves(act, *copies):
    for make in copies:
        copy = make()
        copy.start() if act == START else copy.wait()


def dma(*shape):
    return pltpu.SemaphoreType.DMA(shape)


class Gather:
    def __init__(self, plan, part, sems):
        self.part, self.sems = part, sems
        self.plane = lax.axis_index(MDL)
        self.size = plan.mdl // 2
        self.x, self.core = self.plane // 2, lax.rem(self.plane, 2)

    @staticmethod
    def semaphores(plan):
        return dict(x_send=dma(plan.mdl // 2), recv=dma(plan.mdl), core_send=dma(plan.mdl // 2))

    def along(self, m, target, send):
        return push(self.part(m), self.part(m), send, self.sems.recv.at[m], mdl=target)

    def x_copy(self, x):
        return self.along(self.plane, x * 2 + self.core, self.sems.x_send.at[x])

    def core_copy(self, x):
        return self.along(
            x * 2 + self.core, self.x * 2 + 1 - self.core, self.sems.core_send.at[x]
        )

    def arrived(self, m):
        self.along(m, m, self.sems.x_send.at[0]).wait_recv()

    def start(self):
        for x in others(self.x, self.size):
            self.x_copy(x).start()
        self.core_copy(self.x).start()

    def forward(self):
        for x in others(self.x, self.size):
            self.arrived(x * 2 + self.core)
            self.core_copy(x).start()

    def finish(self):
        for x in [self.x] + others(self.x, self.size):
            self.arrived(x * 2 + 1 - self.core)
        for x in others(self.x, self.size):
            self.x_copy(x).wait_send()
            self.core_copy(x).wait_send()
        self.core_copy(self.x).wait_send()

    def run(self):
        self.start()
        self.forward()
        self.finish()


class Sum:
    def __init__(self, plan, parts, bufs):
        self.parts, self.bufs = parts, bufs
        self.plane = lax.axis_index(MDL)
        self.size = plan.mdl // 2
        self.x, self.core = self.plane // 2, lax.rem(self.plane, 2)

    @staticmethod
    def buffers(plan, shape):
        x = plan.mdl // 2
        vmem = pltpu.VMEM((x,) + shape, BF)
        return dict(
            near=vmem, middle=vmem, far=vmem,
            near_send=dma(x), near_recv=dma(x), far_send=dma(x), far_recv=dma(x),
        )

    def near_copy(self, x):
        b = self.bufs
        return push(
            self.parts.at[x * 2 + 1 - self.core], b.near.at[x], b.near_send.at[x],
            b.near_recv.at[x], mdl=self.x * 2 + 1 - self.core,
        )

    def far_copy(self, x, slot):
        b = self.bufs
        return push(
            b.middle.at[x], b.far.at[slot], b.far_send.at[x], b.far_recv.at[slot],
            mdl=x * 2 + self.core,
        )

    def both(self, x):
        self.near_copy(x).wait_recv()
        own = self.parts[pl.ds(x * 2 + self.core, 1)][0].astype(F32)
        return own + self.bufs.near[pl.ds(x, 1)][0].astype(F32)

    def start(self):
        for x in others(self.x, self.size) + [self.x]:
            self.near_copy(x).start()

    def middle(self):
        for x in others(self.x, self.size):
            self.bufs.middle[pl.ds(x, 1)] = self.both(x).astype(BF)[None]
            self.far_copy(x, self.x).start()

    def finish(self):
        total = self.both(self.x)
        for x in others(self.x, self.size):
            self.far_copy(x, x).wait_recv()
            total = total + self.bufs.far[pl.ds(x, 1)][0].astype(F32)
        for x in others(self.x, self.size):
            self.near_copy(x).wait_send()
            self.far_copy(x, self.x).wait_send()
        self.near_copy(self.x).wait_send()
        return total

    def run(self):
        self.start()
        self.middle()
        return self.finish()


class Trade:
    def __init__(self, plan, out_index, in_index, bufs):
        self.out_index, self.in_index, self.bufs = out_index, in_index, bufs
        self.size = plan.pts
        self.me = lax.axis_index(PTS)

    @staticmethod
    def buffers(plan, cols, rows):
        capacity = 2 * rows // plan.pts
        vmem = pltpu.VMEM((plan.pts, cols, capacity), BF)
        return dict(leave=vmem, land=vmem, send=dma(plan.pts), recv=dma(plan.pts))

    def hot(self, index, part):
        capacity = self.bufs.leave.shape[2]
        row = index[...]
        places = lax.broadcasted_iota(jnp.int32, (capacity, row.shape[1]), 0) + part * capacity
        return jnp.where(places == row, 1.0, 0.0).astype(BF)

    def copy(self, part, slot):
        b = self.bufs
        return push(
            b.leave.at[part], b.land.at[slot], b.send.at[part], b.recv.at[slot],
            pts=part,
        )

    def start(self, values):
        b = self.bufs
        for part in others(self.me, self.size):
            b.leave[pl.ds(part, 1)] = dot(values, self.hot(self.out_index, part), NT).astype(BF)[None]
            self.copy(part, self.me).start()
        b.land[pl.ds(self.me, 1)] = dot(values, self.hot(self.out_index, self.me), NT).astype(BF)[None]

    def finish(self):
        b = self.bufs
        total = dot(b.land[pl.ds(self.me, 1)][0], self.hot(self.in_index, self.me))
        for step in range(1, self.size):
            part = lax.rem(self.me + self.size - step, self.size)
            hot = self.hot(self.in_index, part)
            self.copy(part, part).wait_recv()
            total = total + dot(b.land[pl.ds(part, 1)][0], hot)
        for part in others(self.me, self.size):
            self.copy(part, self.me).wait_send()
        return total.astype(BF)

    def run(self, values):
        self.start(values)
        return self.finish()


class Reduce:
    def __init__(self, plan, bufs):
        self.bufs = bufs
        self.width, self.depth = plan.width, plan.depth
        self.me = lax.axis_index(PTS)
        self.y, self.z = lax.rem(self.me, self.width), self.me // self.width
        self.groups, _, self.pack, self.share, self.cols = bufs.acc.shape
        self.steps = self.groups + self.depth - 1

    @staticmethod
    def buffers(plan, blocks, pack, cols):
        groups, share, vmem = blocks // pack, C // plan.pts, pltpu.VMEM
        line = (plan.depth, pack, share, cols)
        way = dict(
            land=vmem((groups,) + line, BF),
            send=dma(groups, plan.depth),
            recv=dma(groups, plan.depth),
        )
        return dict(
            own=vmem((plan.width, groups) + line, BF),
            side=vmem((plan.width, groups) + line, BF),
            acc=vmem((groups,) + line, BF),
            up=way,
            down=way,
            side_send=dma(plan.width, groups),
            side_recv=dma(plan.width, groups),
        )

    def store(self, block, group, place):
        grid = block.astype(BF).reshape(self.depth, self.width, self.share, self.cols)
        for v in range(self.width):
            self.bufs.own[v, group, :, pl.ds(place, 1)] = grid[:, v][:, None]

    def side_copy(self, group, v, slot):
        b = self.bufs
        return push(
            b.own.at[v, group], b.side.at[slot, group], b.side_send.at[v, group],
            b.side_recv.at[slot, group], pts=self.z * self.width + v,
        )

    def line_copy(self, way, group, to, step):
        b = self.bufs
        near = jnp.clip(self.z + step, 0, self.depth - 1)
        return push(
            b.acc.at[group, to], way.land.at[group, to], way.send.at[group, to],
            way.recv.at[group, to], pts=near * self.width + self.y,
        )

    def start(self, group):
        for v in others(self.y, self.width):
            self.side_copy(group, v, self.y).start()

    def sum_side(self, group):
        b = self.bufs
        total = b.own[pl.ds(self.y, 1), pl.ds(group, 1)][0].astype(F32)
        for v in others(self.y, self.width):
            self.side_copy(group, v, v).wait_recv()
            total = total + b.side[pl.ds(v, 1), pl.ds(group, 1)][0].astype(F32)
        b.acc[pl.ds(group, 1)] = total.astype(BF)

    def relay(self, way, group, step, first):
        b = self.bufs

        @pl.when((group >= 0) & (group < self.groups))
        def _():
            for to in range(self.depth):

                @pl.when((to - self.z) * step > 0)
                def _():
                    @pl.when(jnp.logical_not(first))
                    def _():
                        self.line_copy(way, group, to, -step).wait_recv()
                        spot = (pl.ds(group, 1), to)
                        b.acc[spot] = (
                            b.acc[spot].astype(F32) + way.land[spot].astype(F32)
                        ).astype(BF)

                    self.line_copy(way, group, to, step).start()

    def step(self, s):
        if isinstance(s, int):
            if s < self.groups:
                self.sum_side(s)
        else:

            @pl.when((s >= 0) & (s < self.groups))
            def _():
                self.sum_side(s)

        self.relay(self.bufs.up, s - self.z, 1, self.z == 0)
        self.relay(self.bufs.down, s - (self.depth - 1 - self.z), -1, self.z == self.depth - 1)

    def finish(self, out):
        b, z = self.bufs, self.z

        def total(way, group):
            b.acc[group, pl.ds(z, 1)] = (
                b.acc[group, pl.ds(z, 1)].astype(F32) + way.land[group, pl.ds(z, 1)].astype(F32)
            ).astype(BF)

        for group in range(self.groups):

            @pl.when(z > 0)
            def _():
                self.line_copy(self.bufs.up, group, z, -1).wait_recv()
                total(b.up, group)

            @pl.when(z < self.depth - 1)
            def _():
                self.line_copy(self.bufs.down, group, z, 1).wait_recv()
                total(b.down, group)

            out[group * self.pack : (group + 1) * self.pack] = b.acc[group, pl.ds(z, 1)][0]

    def end(self):
        for group in range(self.groups):
            for v in others(self.y, self.width):
                self.side_copy(group, v, self.y).wait_send()
            for to in range(self.depth):

                @pl.when(to > self.z)
                def _():
                    self.line_copy(self.bufs.up, group, to, 1).wait_send()

                @pl.when(to < self.z)
                def _():
                    self.line_copy(self.bufs.down, group, to, -1).wait_send()


def everyone(plan):
    me, plane = lax.axis_index(PTS), lax.axis_index(MDL)
    return [{PTS: p} for p in others(me, plan.pts)] + [{MDL: m} for m in others(plane, plan.mdl)]


def unit_columns(values):
    mean = jnp.sum(values, 0, keepdims=True) / C
    centred = values - mean
    inv_std = lax.rsqrt(jnp.sum(centred * centred, 0, keepdims=True) / C + NORM_EPS)
    return centred * inv_std, inv_std


def one_hot_window(ids_ref, tap, tile):
    row = ids_ref[pl.ds(tap, 1), pl.ds(tile * TILE, TILE)]
    places = lax.broadcasted_iota(jnp.int32, (WINDOW, TILE), 0) + tile * TILE
    return jnp.where(places == row, 1.0, 0.0).astype(BF)


PACK = 5
ORDER = [TAPS, TAPS + 4] + list(range(TAPS)) + [TAPS + 1, TAPS + 2, TAPS + 3]
ORDER = ORDER + list(range(TAPS + 5, TAPS + 5 + 2 * FF // C))
PLACE = {block: place for place, block in enumerate(ORDER)}


def column(row):
    wide = jnp.broadcast_to(row.astype(F32), (8, row.shape[1]))
    return wide.T[:, 0:1].astype(jnp.int32)


def steps_passed(values, bounds):
    return sum((values >= bound).astype(jnp.int32) for bound in bounds)


def routes(plan, r, rows):
    capacity = 2 * rows // plan.pts
    slot_count = r.from_patch.shape[1]
    patches = slot_count // PATCH
    scans = r.scan_lengths.shape[0]
    target = steps_passed(r.to_patch[...], [p * slot_count for p in range(1, plan.pts)])
    size = 256
    rank = jnp.zeros((1, rows), jnp.int32)
    target_column = column(target)
    ahead = lax.broadcasted_iota(jnp.int32, (size, rows), 1)
    for low in range(0, rows, size):
        earlier = lax.broadcasted_iota(jnp.int32, (size, rows), 0) + low < ahead
        same = target_column[low : low + size] == target
        rank = rank + jnp.sum((earlier & same).astype(jnp.int32), 0, keepdims=True)
    r.send_pos[...] = target * capacity + rank
    held = r.from_patch[...]
    used = held >= 0
    lanes = lax.broadcasted_iota(jnp.int32, (1, slot_count), 1)
    patch = steps_passed(lanes, [p * PATCH for p in range(1, patches)])
    source = steps_passed(held, [p * rows for p in range(1, plan.pts)])
    bounds, bound = [], 0
    for i in range(scans - 1):
        bound = bound + r.scan_lengths[i]
        bounds.append(bound)
    group = patch * scans + (steps_passed(held, bounds) if bounds else 0)
    top = patches * plan.pts * rows
    order_key = jnp.where(used, patch * (plan.pts * rows) + held, top)
    held_key = jnp.where(used, held, top)
    order_column, held_column = column(order_key), column(held_key)
    first_key = source * rows
    order = jnp.zeros((1, slot_count), jnp.int32)
    rank = jnp.zeros((1, slot_count), jnp.int32)
    for low in range(0, slot_count, size):
        part = slice(low, low + size)
        order = order + jnp.sum(
            (order_column[part] < order_key).astype(jnp.int32), 0, keepdims=True
        )
        among = (held_column[part] < held_key) & (held_column[part] >= first_key)
        rank = rank + jnp.sum(among.astype(jnp.int32), 0, keepdims=True)
    base = plan.pts * capacity
    both = column(group * base + source * capacity + rank)
    order = column(jnp.where(used, order, slot_count))
    places = lax.broadcasted_iota(jnp.int32, (size, rows), 1)
    found = jnp.zeros((1, rows), jnp.int32)
    for low in range(0, slot_count, size):
        part = slice(low, low + size)
        found = found + jnp.sum(
            jnp.where(order[part] == places, both[part], 0), 0, keepdims=True
        )
    group = steps_passed(found, [base * g for g in range(1, patches * scans)])
    r.group[...] = group
    r.arrival[...] = found - group * base


def front_kernel(plan, r):
    pts, mdl, slots = plan.pts, plan.mdl, plan.slots
    width, depth = plan.width, plan.depth
    me, plane = lax.axis_index(PTS), lax.axis_index(MDL)
    y, z = lax.rem(me, width), me // width
    rows, cols = r.points_rows.shape
    share = C // pts
    total = r.blocks.shape[1]
    groups = total // PACK
    conv_groups = -(-(2 + TAPS) // PACK)
    for m in range(mdl):
        r.owned[m] = r.weights[:, :, m * cols : (m + 1) * cols].astype(BF)
    greet(everyone(plan))

    def spread_copy(m, slot):
        return push(
            r.owned.at[m], r.spread.at[pl.ds(slot * slots, slots)], r.spread_send.at[m],
            r.spread_recv.at[slot], mdl=m,
        )

    for m in others(plane, mdl):
        spread_copy(m, plane).start()

    def vec_copy(m, slot):
        return push(
            r.vectors, r.vec_all.at[slot], r.vec_send.at[m], r.vec_recv.at[slot], mdl=m
        )

    for m in others(plane, mdl):
        vec_copy(m, plane).start()

    r.points[...] = r.points_rows[...].astype(F32).T.astype(BF)

    def up_copy():
        return push(
            r.points.at[:, rows - HALO : rows], r.ext.at[:, 0:HALO], r.halo_send.at[0],
            r.halo_recv.at[0], pts=me + 1,
        )

    def down_copy():
        return push(
            r.points.at[:, 0:HALO], r.ext.at[:, HALO + rows : 2 * HALO + rows], r.halo_send.at[1],
            r.halo_recv.at[1], pts=me - 1,
        )

    @pl.when(me < pts - 1)
    def _():
        up_copy().start()

    @pl.when(me == pts - 1)
    def _():
        r.ext[:, HALO + rows :] = jnp.zeros((cols, HALO), BF)

    @pl.when(me > 0)
    def _():
        down_copy().start()

    @pl.when(me == 0)
    def _():
        r.ext[:, :HALO] = jnp.zeros((cols, HALO), BF)

    r.ext[:, HALO : HALO + rows] = r.points[...]
    r.spread[pl.ds(plane * slots, slots)] = r.owned[pl.ds(plane, 1)][0]
    r.vec_all[pl.ds(plane, 1)] = r.vectors[...][None]
    r.points_full[pl.ds(plane * cols, cols), :] = r.points[...]
    for m in others(plane, mdl):
        spread_copy(m, m).wait_recv()
    for place, block in enumerate(ORDER):
        r.blocks[pl.ds(me, 1), place] = r.spread[pl.ds(r.slots[block], 1)]

    def group_of(source, group):
        return r.blocks.at[source, group * PACK : (group + 1) * PACK]

    def far_copy(group, source, step):
        return push(
            group_of(source, group), group_of(source, group),
            r.far_send.at[(step + 1) // 2, group, source // width],
            r.far_recv.at[group, source // width], pts=jnp.clip(z + step, 0, depth - 1) * width + y,
        )

    def side_copy(group, v, source):
        return push(
            group_of(source, group), group_of(source, group),
            r.side_send.at[group, v, source // width], r.side_recv.at[group, source],
            pts=z * width + v,
        )

    def pass_on(group, source, act):
        from_z = source // width

        @pl.when((z < depth - 1) & (from_z <= z))
        def _():
            copy = far_copy(group, source, 1)
            copy.start() if act == START else copy.wait_send()

        @pl.when((z > 0) & (from_z >= z))
        def _():
            copy = far_copy(group, source, -1)
            copy.start() if act == START else copy.wait_send()

        for v in others(y, width):
            copy = side_copy(group, v, source)
            copy.start() if act == START else copy.wait_send()

    def relay(group, away, act):
        for from_z in (z - away, z + away):

            @pl.when((from_z >= 0) & (from_z < depth))
            def _():
                source = from_z * width + y
                if act == START:
                    far_copy(group, source, 1).wait_recv()
                pass_on(group, source, act)

    ahead = 2
    for group in range(ahead):
        pass_on(group, me, START)

    points_gather = Gather(
        plan, lambda m: r.points_full.at[pl.ds(m * cols, cols)],
        r.points_net,
    )
    cot_gather = Gather(
        plan, lambda m: r.cot_full.at[pl.ds(m * cols, cols)],
        r.cot_net,
    )
    points_gather.start()
    r.cot_full[pl.ds(plane * cols, cols), :] = r.cot_rows[...].astype(F32).T.astype(BF)
    cot_gather.start()
    routes(plan, r, rows)

    @pl.when(me > 0)
    def _():
        push(
            r.points.at[:, 0:HALO], r.ext.at[:, 0:HALO], r.halo_send.at[0], r.halo_recv.at[0],
            pts=me - 1,
        ).wait_recv()

    @pl.when(me < pts - 1)
    def _():
        push(
            r.points.at[:, 0:HALO], r.ext.at[:, HALO + rows : 2 * HALO + rows], r.halo_send.at[1],
            r.halo_recv.at[1], pts=me + 1,
        ).wait_recv()

    def take(tap, carry):
        for tile in range(rows // TILE):
            hot = one_hot_window(r.ids, tap, tile)
            picked = dot(r.ext[:, tile * TILE : tile * TILE + WINDOW], hot).astype(BF)
            r.taken[pl.ds(tap, 1), :, tile * TILE : (tile + 1) * TILE] = picked[None]
        return carry

    steps = groups + depth - 2
    cuts = [min(TAPS, -(-TAPS * i // groups)) for i in range(steps + 1)]
    for step in range(steps):
        if step + ahead < groups:
            pass_on(step + ahead, me, START)
        if cuts[step] < cuts[step + 1]:
            lax.fori_loop(cuts[step], cuts[step + 1], take, 0)
        for away in range(1, depth):
            if 0 <= step + 1 - away < groups:
                relay(step + 1 - away, away, START)
    moves(START, r.taken_move)

    def complete(group):
        for u in others(y, width):
            for v in range(depth):
                side_copy(group, u, v * width + u).wait_recv()

    pair_gather = Gather(
        plan, lambda m: r.pair.at[m], r.pair_net
    )
    for group in range(conv_groups):
        complete(group)
        if group == 0:
            for i in range(2):
                r.pair[pl.ds(plane, 1), i] = r.blocks[:, i].reshape(1, C, cols)
            pair_gather.start()
        low = max(group * PACK - 2, 0)
        high = min(group * PACK - 2 + PACK, TAPS)
        if cols % 128 == 0:
            weight = jnp.concatenate(
                [r.blocks[:, t + 2].reshape(C, cols) for t in range(low, high)], 1
            )
            part = dot(weight, r.taken[low:high].reshape((high - low) * cols, rows))
        else:
            part = sum(dot(r.blocks[:, t + 2].reshape(C, cols), r.taken[t]) for t in range(low, high))
        if group == 0:
            r.acc[...] = part
            pair_gather.forward()
        else:
            r.acc[...] += part

    taps_copy = pltpu.make_async_copy(r.blocks.at[:, 2 : 2 + TAPS], r.taps_far, r.taps_sem)
    taps_copy.start()
    points_gather.forward()
    cot_gather.forward()
    r.parts[...] = r.acc[...].astype(BF).reshape(mdl, cols, rows)
    hidden_sum = Sum(plan, r.parts, r.sum_net)
    hidden_sum.start()
    for m in others(plane, mdl):
        vec_copy(m, m).wait_recv()
    for m in range(mdl):
        r.vec[m * cols : (m + 1) * cols, :] = r.vec_all[m].T
    pair_gather.finish()
    points_gather.finish()
    hidden_sum.middle()
    bias = r.vec[pl.ds(plane * cols, cols), 0:1]
    r.hidden[pl.ds(plane * cols, cols), :] = (hidden_sum.finish() + bias).astype(BF)
    Gather(
        plan, lambda m: r.hidden.at[pl.ds(m * cols, cols)],
        r.hidden_net,
    ).run()
    hidden = r.hidden[...]
    for m in range(mdl):
        r.acc[m * cols : (m + 1) * cols, :] = dot(r.pair[m, 0], hidden, TN)
    span_size = 128

    def norms(step, carry):
        span = pl.ds(pl.multiple_of(step * span_size, span_size), span_size)
        unit, inv_std = unit_columns(r.acc[:, span] + r.vec[:, 1:2])
        r.mixed_unit[:, span] = unit.astype(BF)
        r.mixed_std[:, span] = inv_std
        stream = r.points_full[:, span].astype(F32) + unit * r.vec[:, 2:3] + r.vec[:, 3:4]
        r.stream[:, span] = stream
        unit, inv_std = unit_columns(stream)
        r.one_unit[:, span] = unit.astype(BF)
        r.one_std[:, span] = inv_std
        r.normed[:, span] = (unit * r.vec[:, 4:5] + r.vec[:, 5:6]).astype(BF)
        return carry

    lax.fori_loop(0, rows // span_size, norms, 0)
    trade = Trade(
        plan, r.send_pos, r.arrival, r.trade_net
    )
    trade.start(r.normed[pl.ds(plane * cols, cols), :])
    moves(START, r.hidden_move, r.mixed_unit_move, r.one_unit_move, r.stream_move, r.pair_move)
    for group in range(conv_groups, groups):
        complete(group)
    for i in range(r.rest.shape[0]):
        r.rest[i] = r.blocks[:, TAPS + 2 + i].reshape(C, cols)
    cot_gather.finish()
    moves(START, r.rest_move, r.cot_full_move)
    r.slot_in[pl.ds(plane * cols, cols), :] = trade.finish()
    Gather(
        plan, lambda m: r.slot_in.at[pl.ds(m * cols, cols)],
        r.slot_net,
    ).run()
    moves(START, r.slot_in_move)

    @pl.when(me < pts - 1)
    def _():
        up_copy().wait_send()

    @pl.when(me > 0)
    def _():
        down_copy().wait_send()

    for m in others(plane, mdl):
        spread_copy(m, plane).wait_send()
        vec_copy(m, plane).wait_send()
    for group in range(groups):
        pass_on(group, me, WAIT)
        for away in range(1, depth):
            relay(group, away, WAIT)
    moves(WAIT, r.taken_move, r.cot_full_move, r.pair_move, r.hidden_move, r.mixed_unit_move, r.one_unit_move, r.stream_move, r.slot_in_move, r.rest_move)
    taps_copy.wait()


def front(plan, slots, weights, points, cot, vectors, ids, to_patch, from_patch, scan_lengths):
    rows, cols = points.shape
    pts, mdl = plan.pts, plan.mdl
    share = C // pts
    total = len(ORDER)
    groups = total // PACK
    vmem = pltpu.VMEM
    ring = Gather.semaphores(plan)
    scratch = dict(
        points_net=ring,
        cot_net=ring,
        pair_net=ring,
        hidden_net=ring,
        slot_net=ring,
        owned=vmem((mdl, plan.slots, share, cols), BF),
        points=vmem((cols, rows), BF),
        spread=vmem((total, share, cols), BF),
        vec_all=vmem((mdl,) + vectors.shape, F32),
        ext=vmem((cols, rows + 2 * HALO), BF),
        acc=vmem((C, rows), F32),
        parts=vmem((mdl, cols, rows), BF),
        normed=vmem((C, rows), BF),
        points_full=vmem((C, rows), BF),
        spread_send=dma(mdl),
        spread_recv=dma(mdl),
        vec_send=dma(mdl),
        vec_recv=dma(mdl),
        halo_send=dma(2),
        halo_recv=dma(2),
        blocks=vmem((pts, total, share, cols), BF),
        taps_sem=dma(),
        far_send=dma(2, groups, plan.depth),
        far_recv=dma(groups, plan.depth),
        side_send=dma(groups, plan.width, plan.depth),
        side_recv=dma(groups, pts),
        sum_net=(Sum.buffers(plan, (cols, rows))),
        trade_net=(Trade.buffers(plan, cols, rows)),
    )
    return call(
        functools.partial(front_kernel, plan),
        "front",
        5,
        dict(
            slots=slots, weights=weights, points_rows=points, cot_rows=cot, vectors=vectors,
            ids=ids, to_patch=to_patch, from_patch=from_patch, scan_lengths=scan_lengths,
        ),
        dict(
            taps_far=((pts, TAPS, share, cols), BF),
            taken=Late((TAPS, cols, rows), BF),
            cot_full=Late((C, rows), BF),
            pair=Late((mdl, 2, C, cols), BF),
            vec=((C, vectors.shape[0]), F32),
            hidden=Late((C, rows), BF),
            mixed_unit=Late((C, rows), BF),
            mixed_std=((1, rows), F32),
            stream=Late((C, rows), F32),
            one_unit=Late((C, rows), BF),
            one_std=((1, rows), F32),
            send_pos=((1, rows), jnp.int32),
            arrival=((1, rows), jnp.int32),
            group=((1, rows), jnp.int32),
            slot_in=Late((C, rows), BF),
            rest=Late((total - TAPS - 2, C, cols), BF),
        ),
        scratch,
        4 * TAPS * rows * (WINDOW + C) * cols,
        smem=("slots", "scan_lengths"),
        free=("taps_far",),
    )


def fetches(plan, srcs, dsts, refs, act):
    for src, dst, sems in zip(srcs, dsts, refs.fetch_net):
        fetch_copies(plan, src, dst, sems, act)


def head_lanes(ext, cols, head):
    lane = lax.broadcasted_iota(jnp.int32, ext.shape, 1)
    return jnp.where((lane >= cols) | (lane // HD == head), ext, jnp.zeros_like(ext))


def head_rows(head):
    return pl.ds(pl.multiple_of(head * HD, HD), HD)


def attend_kernel(plan, r):
    plane = lax.axis_index(MDL)
    rows, cols = r.values.shape
    heads = cols // HD
    moves(START, r.left32_move, r.right32_move)
    greet(everyone(plan))
    moves(WAIT, r.left32_move, r.right32_move)
    r.left[...] = r.left32[...].astype(BF)
    r.right[...] = r.right32[...].astype(BF)
    fetched = (plan, (r.left, r.right), (r.left_whole, r.right_whole), r)
    fetches(*fetched, START)
    group = column(r.group[...])
    lane = lax.broadcasted_iota(jnp.int32, (rows, cols), 1)
    same = lane == group
    slot_in = r.slot_in[...]
    queries = (dot(slot_in, r.rest[0], TN) + r.vectors[6:7, :]).astype(BF)
    r.q_ext[:, :cols] = queries * BF(HD ** (-0.5))
    r.q_ext[:, cols:] = jnp.where(same, 1.0, 0.0).astype(BF)
    r.k_ext[:, :cols] = dot(slot_in, r.rest[1], TN).astype(BF)
    r.k_ext[:, cols:] = jnp.where(same | (lane >= plan.groups), 0.0, -1e30).astype(BF)
    values = dot(slot_in, r.rest[2], TN) + r.vectors[7:8, :]
    r.values[...] = values.astype(BF)
    r.v_aug[:, :HD] = values.T.astype(BF).reshape(heads, HD, rows)
    r.v_aug[:, HD:] = jnp.ones((heads, HD, rows), BF)
    moves(START, r.q_ext_move, r.k_ext_move, r.values_move)

    def one(head, carry):
        keys = r.k_ext[...]
        values_t = r.v_aug[pl.ds(head, 1)][0]
        for tile in range(rows // TILE):
            span = slice(tile * TILE, (tile + 1) * TILE)
            scores = dot(keys, head_lanes(r.q_ext[span, :], cols, head), NT)
            top = jnp.max(scores, 0, keepdims=True)
            soft = jnp.exp(scores - top).astype(BF)
            summed = dot(values_t, soft)
            total = summed[HD : HD + 1]
            r.attended[head_rows(head), span] = (summed[:HD] / total).astype(BF)
            r.lse[pl.ds(head, 1), :, span] = (top + jnp.log(total))[None]
        return carry

    lax.fori_loop(0, heads, one, 0)
    moves(START, r.attended_move, r.lse_move)
    trade = Trade(
        plan, r.arrival, r.send_pos, r.trade_net
    )
    r.attended_rows[pl.ds(plane * cols, cols), :] = trade.run(r.attended[...])
    Gather(
        plan, lambda m: r.attended_rows.at[pl.ds(m * cols, cols)],
        r.rows_net,
    ).run()
    fetches(*fetched, WAIT)
    moves(WAIT, r.q_ext_move, r.k_ext_move, r.values_move, r.attended_move, r.lse_move)


def attend(plan, slot_in, rest, vectors, group, send_pos, arrival, left, right):
    rows, cols = group.shape[1], vectors.shape[1]
    heads = cols // HD
    fetched = fetch_shape(plan, left)
    vmem = pltpu.VMEM
    return call(
        functools.partial(attend_kernel, plan),
        "attend",
        2,
        dict(
            slot_in=slot_in, rest=rest, vectors=vectors, group=group,
            send_pos=send_pos, arrival=arrival, left32=Late(left), right32=Late(right),
        ),
        dict(
            q_ext=Late((rows, 2 * cols), BF),
            k_ext=Late((rows, 2 * cols), BF),
            values=Late((rows, cols), BF),
            attended=Late((cols, rows), BF),
            lse=Late((heads, 1, rows), F32),
            attended_rows=((C, rows), BF),
            left_whole=(fetched.shape, fetched.dtype),
            right_whole=(fetched.shape, fetched.dtype),
        ),
        dict(
            left=vmem(left.shape, BF),
            right=vmem(right.shape, BF),
            v_aug=vmem((heads, 2 * HD, rows), BF),
            fetch_net=[fetch_sems(plan), fetch_sems(plan)],
            trade_net=(Trade.buffers(plan, cols, rows)),
            rows_net=(Gather.semaphores(plan)),
        ),
        4 * heads * rows * rows * cols,
        free=("left_whole", "right_whole"),
    )


def attend_back_kernel(plan, r):
    plane = lax.axis_index(MDL)
    rows, cols = r.values.shape
    heads = cols // HD
    greet(everyone(plan))
    moves(START, r.second32_move, r.slot_in_move, r.rest_move)
    fetched = (plan, (r.second,), (r.second_whole,), r)
    mlp_count = r.mlp_grads.shape[0]
    reduce = Reduce(
        plan, r.reduce_net
    )
    for group in range(reduce.groups):
        for place in range(MLP_PACK):
            reduce.store(r.mlp_grads[group * MLP_PACK + place], group, place)
        reduce.start(group)
    moves(WAIT, r.second32_move)
    r.second[...] = r.second32[...].astype(BF)
    fetches(*fetched, START)
    grad_slot = r.grad_slot[...]
    grad_t = dot(r.pair[pl.ds(plane, 1), 1][0], grad_slot, TN).astype(BF).astype(F32)
    r.grad[...] = grad_t.T.astype(BF)
    weighed = grad_t * r.attended[...].astype(F32)
    r.inner[...] = jnp.sum(weighed.reshape(heads, HD, rows), 1, keepdims=True)
    r.keys_t[...] = r.k_ext[:, :cols].astype(F32).T.astype(BF)
    r.dk_acc[...] = jnp.zeros_like(r.dk_acc)
    r.dv_acc[...] = jnp.zeros_like(r.dv_acc)

    def one(head, carry):
        queries = head_lanes(r.q_ext[...], cols, head)
        pure = queries[:, :cols]
        grad = head_lanes(r.grad[...], cols, head)
        lse = r.lse[pl.ds(head, 1)][0]
        inner = r.inner[pl.ds(head, 1)][0]
        keys_t = r.keys_t[head_rows(head), :]
        dq = jnp.zeros((HD, rows), F32)
        for tile in range(rows // TILE):
            span = slice(tile * TILE, (tile + 1) * TILE)
            scores = dot(r.k_ext[span, :], queries, NT)
            soft = jnp.exp(scores - lse)
            grad_soft = dot(r.values[span, :], grad, NT)
            grad_scores = (soft * (grad_soft - inner)).astype(BF)
            r.dv_acc[span, :] += dot(soft.astype(BF), grad)
            r.dk_acc[span, :] += dot(grad_scores, pure)
            dq = dq + dot(keys_t[:, span], grad_scores)
        r.dq[head_rows(head), :] = (dq * HD ** (-0.5)).astype(BF)
        reduce.step(head - delay)
        return carry

    delay = max(heads - reduce.steps, 0)
    lax.fori_loop(0, heads, one, 0)
    for s in range(heads - delay, reduce.steps):
        reduce.step(s)
    moves(WAIT, r.slot_in_move, r.rest_move)
    dk = r.dk_acc[...].astype(BF)
    dv = r.dv_acc[...].astype(BF)
    back = dot(r.rest[0], r.dq[...]) + dot(r.rest[1], dk, NT) + dot(r.rest[2], dv, NT)
    r.parts[...] = back.astype(BF).reshape(plan.mdl, cols, rows)
    back_sum = Sum(plan, r.parts, r.sum_net)
    back_sum.start()
    r.weight_grads[0] = dot(r.slot_in[...], r.dq[...], NT).astype(BF)
    r.weight_grads[1] = dot(r.slot_in[...], dk).astype(BF)
    back_sum.middle()
    r.weight_grads[2] = dot(r.slot_in[...], dv).astype(BF)
    r.weight_grads[3] = dot(r.grad_slot[...], r.attended[...], NT).astype(BF)
    trade = Trade(
        plan, r.arrival, r.send_pos, r.trade_net
    )
    trade.start(back_sum.finish().astype(BF))
    moves(START, r.weight_grads_move)
    r.sums[...] = jnp.zeros_like(r.sums)
    r.sums[:, 0:1] = jnp.sum(r.dq[...].astype(F32), 1, keepdims=True)
    r.sums[:, 1:2] = jnp.sum(dv.astype(F32), 0, keepdims=True).T
    r.grad_normed[pl.ds(plane * cols, cols), :] = trade.finish()
    Gather(
        plan, lambda m: r.grad_normed.at[pl.ds(m * cols, cols)],
        r.rows_net,
    ).run()
    reduce.finish(r.mlp_summed)
    reduce.end()
    fetches(*fetched, WAIT)
    moves(WAIT, r.weight_grads_move)


MLP_PACK = 4


def attend_back(
    plan, kept, grad_slot, slot_in, rest, pair, send_pos, arrival, mlp_grads, second
):
    rows, cols = kept.values.shape
    heads = cols // HD
    vmem = pltpu.VMEM
    fetched = fetch_shape(plan, second)
    return call(
        functools.partial(attend_back_kernel, plan),
        "attend_back",
        3,
        dict(
            q_ext=kept.q_ext, k_ext=kept.k_ext, values=kept.values, attended=kept.attended, lse=kept.lse, grad_slot=grad_slot, slot_in=Late(slot_in), rest=Late(rest),
            pair=pair, send_pos=send_pos, arrival=arrival, mlp_grads=mlp_grads, second32=Late(second),
        ),
        dict(
            grad_normed=((C, rows), BF),
            weight_grads=Late((4, C, cols), BF),
            sums=((cols, 8), F32),
            mlp_summed=((mlp_grads.shape[0], C // plan.pts, cols), BF),
            second_whole=(fetched.shape, fetched.dtype),
        ),
        dict(
            second=vmem(second.shape, BF),
            grad=vmem((rows, cols), BF),
            inner=vmem((heads, 1, rows), F32),
            keys_t=vmem((cols, rows), BF),
            dk_acc=vmem((rows, cols), F32),
            dv_acc=vmem((rows, cols), F32),
            dq=vmem((cols, rows), BF),
            parts=vmem((plan.mdl, cols, rows), BF),
            reduce_net=(Reduce.buffers(plan, mlp_grads.shape[0], MLP_PACK, cols)),
            fetch_net=[fetch_sems(plan)],
            sum_net=(Sum.buffers(plan, (cols, rows))),
            trade_net=(Trade.buffers(plan, cols, rows)),
            rows_net=(Gather.semaphores(plan)),
        ),
        10 * heads * rows * rows * cols,
        free=("second_whole",),
    )


SPAN = 128


def over_spans(rows, body, size=SPAN):
    def step(index, carry):
        body(pl.ds(pl.multiple_of(index * size, size), size))
        return carry

    lax.fori_loop(0, rows // size, step, 0)


def beside(blocks):
    def times(right, cols):
        if cols % 128 == 0:
            return dot(jnp.concatenate(blocks, 1), right[...])
        return sum(
            dot(block, right[i * cols : (i + 1) * cols, :]) for i, block in enumerate(blocks)
        )

    return times


def mlp_kernel(plan, r):
    mdl = plan.mdl
    plane = lax.axis_index(MDL)
    cols, rows = r.cot.shape
    ff_blocks = FF // C
    own = pl.ds(plane * cols, cols)
    moves(START, r.first32_move, r.stream_move, r.rest_move, r.cot_full_move)
    r.cot[...] = r.cot_rows[...].astype(F32).T.astype(BF)
    greet(everyone(plan))
    moves(WAIT, r.first32_move)
    r.first[...] = r.first32[...].astype(BF)
    fetched = (plan, (r.first,), (r.first_whole,), r)
    fetches(*fetched, START)
    r.acc[...] = beside([r.pair[m, 1] for m in range(mdl)])(r.attended_rows, cols)
    moves(WAIT, r.stream_move, r.rest_move, r.cot_full_move)

    def norms(span):
        branch = (r.acc[:, span] + r.vec[:, 8:9]).astype(BF).astype(F32)
        two = r.stream[:, span] + branch
        r.two[:, span] = two
        unit, inv_std = unit_columns(two)
        r.two_unit[:, span] = unit
        r.two_std[:, span] = inv_std
        r.normed[:, span] = (unit * r.vec[:, 9:10] + r.vec[:, 10:11]).astype(BF)

    over_spans(rows, norms)
    for k in range(ff_blocks):
        part = slice(k * cols, (k + 1) * cols)
        r.pre[...] = dot(r.rest[3 + k], r.normed[...], TN) + r.vec[own, 11 + k : 12 + k]
        r.grad_act[...] = dot(r.rest[3 + ff_blocks + k], r.cot_full[...], TN)

        def bend(span):
            pre = r.pre[:, span]
            half = 0.5 * (1.0 + lax.erf(pre * 0.7071067811865476))
            r.act[part, span] = (pre * half).astype(BF)
            slope = half + pre * jnp.exp(-0.5 * pre * pre) * 0.3989422804014327
            r.grad_pre[part, span] = (r.grad_act[:, span] * slope).astype(BF)

        over_spans(rows, bend, 256)
    r.acc[...] = beside([r.rest[3 + k] for k in range(ff_blocks)])(r.grad_pre, cols)

    def stats(span):
        scaled = r.acc[:, span] * r.vec[:, 9:10]
        r.stats[pl.ds(plane, 1), 0:1, span] = jnp.sum(scaled, 0, keepdims=True)[None]
        r.stats[pl.ds(plane, 1), 1:2, span] = jnp.sum(scaled * r.two_unit[:, span], 0, keepdims=True)[None]

    over_spans(rows, stats)

    def stats_copy(m, slot):
        return push(
            r.stats.at[slot], r.stats.at[slot], r.stats_send.at[m], r.stats_recv.at[slot], mdl=m
        )

    for m in others(plane, mdl):
        stats_copy(m, plane).start()
    r.parts[...] = r.acc[...].astype(BF).reshape(mdl, cols, rows)
    shape = Sum.buffers(plan, (cols, rows))
    grad_sum = Sum(plan, r.parts, r.grad_net)
    grad_sum.start()
    out = beside([r.rest[3 + ff_blocks + k] for k in range(ff_blocks)])(r.act, cols)
    r.out_parts[...] = out.astype(BF).reshape(mdl, cols, rows)
    grad_sum.middle()
    out_sum = Sum(plan, r.out_parts, r.out_net)
    out_sum.start()
    for m in others(plane, mdl):
        stats_copy(m, m).wait_recv()
    mean = sum(r.stats[m, 0:1] for m in range(mdl)) / C
    cross = sum(r.stats[m, 1:2] for m in range(mdl)) / C
    cot = r.cot[...].astype(F32)
    grad_normed = grad_sum.finish()
    unit = r.two_unit[own, :]
    grad_two = cot + r.two_std[...] * (grad_normed * r.vec[own, 9:10] - mean - unit * cross)
    r.grad_two[...] = grad_two
    branch = grad_two.astype(BF)
    r.branch_full[own, :] = branch
    trade = Trade(
        plan, r.send_pos, r.arrival, r.trade_net
    )
    trade.start(branch)
    branch_gather = Gather(
        plan, lambda m: r.branch_full.at[pl.ds(m * cols, cols)],
        r.branch_net,
    )
    branch_gather.start()
    out_sum.middle()

    def along(values):
        return jnp.sum(values.astype(F32), 1, keepdims=True)

    r.sums[:, 0:1] = along(branch)
    r.sums[:, 1:2] = along(grad_normed * unit)
    r.sums[:, 2:3] = along(grad_normed)
    for k in range(ff_blocks):
        part = slice(k * cols, (k + 1) * cols)
        r.sums[:, 3 + k : 4 + k] = along(r.grad_pre[part, :])
        r.weight_grads[k] = dot(r.normed[...], r.grad_pre[part, :], NT).astype(BF)
        r.weight_grads[ff_blocks + k] = dot(r.cot_full[...], r.act[part, :], NT).astype(BF)
    r.sums[:, 3 + ff_blocks : 4 + ff_blocks] = along(cot)
    r.grad_slot[own, :] = trade.finish()
    slot_gather = Gather(
        plan, lambda m: r.grad_slot.at[pl.ds(m * cols, cols)],
        r.slot_net,
    )
    slot_gather.start()
    moves(START, r.weight_grads_move, r.grad_two_move)
    branch_gather.forward()
    bias = r.vec[own, 11 + ff_blocks : 12 + ff_blocks]
    r.out[...] = (r.two[own, :] + out_sum.finish() + bias).T.astype(BF)
    slot_gather.forward()
    branch_gather.finish()
    moves(START, r.branch_full_move)
    slot_gather.finish()
    fetches(*fetched, WAIT)
    moves(WAIT, r.weight_grads_move, r.grad_two_move, r.branch_full_move)
    for m in others(plane, mdl):
        stats_copy(m, plane).wait_send()


def mlp(plan, attended_rows, first, rest, cot, send_pos, arrival, moment):
    rows, cols = cot.shape
    ff_blocks = FF // C
    vmem = pltpu.VMEM
    scratch = dict(
        cot=vmem((cols, rows), BF),
        first=vmem(moment.shape, BF),
        acc=vmem((C, rows), F32),
        two=vmem((C, rows), F32),
        two_unit=vmem((C, rows), F32),
        two_std=vmem((1, rows), F32),
        normed=vmem((C, rows), BF),
        pre=vmem((cols, rows), F32),
        grad_act=vmem((cols, rows), F32),
        act=vmem((ff_blocks * cols, rows), BF),
        grad_pre=vmem((ff_blocks * cols, rows), BF),
        stats=vmem((plan.mdl, 8, rows), F32),
        stats_send=dma(plan.mdl),
        stats_recv=dma(plan.mdl),
        parts=vmem((plan.mdl, cols, rows), BF),
        out_parts=vmem((plan.mdl, cols, rows), BF),
        grad_net=(Sum.buffers(plan, (cols, rows))),
        out_net=(Sum.buffers(plan, (cols, rows))),
        trade_net=(Trade.buffers(plan, cols, rows)),
        branch_net=(Gather.semaphores(plan)),
        slot_net=(Gather.semaphores(plan)),
        fetch_net=[fetch_sems(plan)],
    )
    return call(
        functools.partial(mlp_kernel, plan),
        "mlp",
        6,
        dict(
            attended_rows=attended_rows, pair=first.pair, stream=Late(first.stream), vec=first.vec, cot_full=Late(first.cot_full), rest=Late(rest), cot_rows=cot,
            send_pos=send_pos, arrival=arrival, first32=Late(moment),
        ),
        dict(
            first_whole=(fetch_shape(plan, moment).shape, BF),
            grad_slot=((C, rows), BF),
            branch_full=Late((C, rows), BF),
            grad_two=Late((cols, rows), F32),
            out=((rows, cols), BF),
            weight_grads=Late((2 * ff_blocks, C, cols), BF),
            sums=((cols, 4 + ff_blocks), F32),
        ),
        scratch,
        16 * rows * C * cols * ff_blocks,
        free=("first_whole",),
    )


BACK_ORDER = [TAPS + 1, TAPS + 2, TAPS + 3, TAPS + 4, TAPS] + list(range(TAPS))
MLP_ORDER = list(range(TAPS + 5, TAPS + 5 + 2 * FF // C))
BACK_PACK = 4


def back_kernel(plan, r):
    pts = plan.pts
    cols, rows = r.turn_acc.shape
    taps = r.taken.shape[0]
    ready = r.attend_grads.shape[0]
    extra = ready + 1
    me, plane = lax.axis_index(PTS), lax.axis_index(MDL)
    own_cols = pl.ds(plane * cols, cols)
    middle = slice(HALO, HALO + rows)
    moves(START, r.grad_normed_move, r.branch_full_move, r.one_unit_move, r.mixed_unit_move, r.pair_move, r.hidden_move, r.taken_move, r.taps_move, r.grad_two_move)
    greet([{PTS: v} for v in others(me, pts)] + [{MDL: plane + 1 - 2 * lax.rem(plane, 2)}])
    reduce = Reduce(
        plan, r.reduce_net
    )
    groups = reduce.groups
    for b in range(ready):
        reduce.store(r.attend_grads[b], b // BACK_PACK, b % BACK_PACK)
    reduce.start(0)
    moves(WAIT, r.grad_normed_move, r.branch_full_move, r.one_unit_move, r.mixed_unit_move, r.pair_move, r.hidden_move, r.taken_move, r.taps_move, r.grad_two_move)

    def grads(group):
        if group == ready // BACK_PACK:
            reduce.store(dot(r.hidden[...], r.mixed[own_cols, :], NT), group, ready % BACK_PACK)

        def one(place, carry):
            tap = group * BACK_PACK + place - extra
            reduce.store(
                dot(r.back[:, middle], r.taken[pl.ds(tap, 1)][0], NT), group, place
            )
            return carry

        low = max(group * BACK_PACK, extra)
        lax.fori_loop(low - group * BACK_PACK, BACK_PACK, one, 0)

    def norms(span):
        grad = r.grad_normed[:, span].astype(F32) * r.vec[:, 4:5]
        unit = r.one_unit[:, span].astype(F32)
        delta = r.one_std[:, span] * (
            grad
            - jnp.sum(grad, 0, keepdims=True) / C
            - unit * (jnp.sum(grad * unit, 0, keepdims=True) / C)
        )
        r.delta[:, span] = delta
        grad = (r.branch_full[:, span].astype(F32) + delta) * r.vec[:, 2:3]
        unit = r.mixed_unit[:, span].astype(F32)
        r.mixed[:, span] = (
            r.mixed_std[:, span]
            * (
                grad
                - jnp.sum(grad, 0, keepdims=True) / C
                - unit * (jnp.sum(grad * unit, 0, keepdims=True) / C)
            )
        ).astype(BF)

    over_spans(rows, norms)
    back = beside([r.pair[m, 0] for m in range(plan.mdl)])(r.mixed, cols)
    r.back[:, middle] = back.astype(BF)

    core = lax.rem(plane, 2)
    mine = pl.ds(core * (C // 2), C // 2)
    low_end, high_end = slice(0, HALO), slice(HALO + rows, 2 * HALO + rows)

    def up_copy(target):
        return push(
            r.back.at[mine, rows : rows + HALO], r.back.at[mine, low_end], r.halo_send.at[0],
            r.halo_recv.at[0], pts=target,
        )

    def down_copy(target):
        return push(
            r.back.at[mine, HALO : 2 * HALO], r.back.at[mine, high_end],
            r.halo_send.at[1], r.halo_recv.at[1], pts=target,
        )

    def core_copy(end, which, part):
        half = pl.ds(part * (C // 2), C // 2)
        return push(
            r.back.at[half, end], r.back.at[half, end], r.core_send.at[which],
            r.core_recv.at[which], mdl=plane + 1 - 2 * core,
        )

    @pl.when(me < pts - 1)
    def _():
        up_copy(me + 1).start()

    @pl.when(me == pts - 1)
    def _():
        r.back[:, HALO + rows :] = jnp.zeros((C, HALO), BF)

    @pl.when(me > 0)
    def _():
        down_copy(me - 1).start()

    @pl.when(me == 0)
    def _():
        r.back[:, :HALO] = jnp.zeros((C, HALO), BF)

    for group in range(1, groups):
        grads(group)
        reduce.start(group)
        if group >= LAG:
            reduce.step(group - LAG)

    grad_one = r.grad_two[...] + r.delta[own_cols, :]
    r.grad_one[...] = grad_one

    def along(values):
        return jnp.sum(values.astype(F32), 1, keepdims=True)

    grad_normed = r.grad_normed[own_cols, :].astype(F32)
    columns = [
        along(r.back[own_cols, middle]),
        along(r.mixed[own_cols, :]),
        along(grad_one * r.mixed_unit[own_cols, :]),
        along(grad_one),
        along(grad_normed * r.one_unit[own_cols, :]),
        along(grad_normed),
        r.attend_sums[:, 0:2],
        r.mlp_sums[...],
    ]
    at = 0
    for column in columns:
        r.vectors[pl.ds(me, 1), :, at : at + column.shape[1]] = column[None]
        at += column.shape[1]

    def vector_copy(p, slot):
        return push(
            r.vectors.at[slot], r.vectors.at[slot], r.vector_send.at[p], r.vector_recv.at[slot],
            pts=p,
        )

    for p in others(me, pts):
        vector_copy(p, me).start()

    @pl.when(me > 0)
    def _():
        up_copy(me - 1).wait_recv()
        core_copy(low_end, 0, core).start()

    @pl.when(me < pts - 1)
    def _():
        down_copy(me + 1).wait_recv()
        core_copy(high_end, 1, core).start()

    @pl.when(me > 0)
    def _():
        core_copy(low_end, 0, 1 - core).wait_recv()

    @pl.when(me < pts - 1)
    def _():
        core_copy(high_end, 1, 1 - core).wait_recv()

    def turn(tap, carry):
        weight = r.taps[:, pl.ds(taps - 1 - tap, 1)].reshape(C, cols)
        turned = dot(weight, r.back[...], TN).astype(BF)
        for tile in range(rows // TILE):
            hot = one_hot_window(r.ids, tap, tile)
            r.turn_acc[:, tile * TILE : (tile + 1) * TILE] += dot(
                turned[:, tile * TILE : tile * TILE + WINDOW], hot
            )
        return carry

    r.turn_acc[...] = jnp.zeros_like(r.turn_acc)
    left = list(range(groups - LAG, reduce.steps))
    cuts = [taps * i // len(left) for i in range(len(left) + 1)]
    for i, s in enumerate(left):
        lax.fori_loop(cuts[i], cuts[i + 1], turn, 0)
        reduce.step(s)
    r.point_grad[...] = (r.turn_acc[...] + r.grad_one[...]).T
    reduce.finish(r.summed)
    total = r.vectors[pl.ds(me, 1)][0]
    for p in others(me, pts):
        vector_copy(p, p).wait_recv()
        total = total + r.vectors[pl.ds(p, 1)][0]
    r.vector_grad[...] = total.T
    reduce.end()
    for p in others(me, pts):
        vector_copy(p, me).wait_send()

    @pl.when(me < pts - 1)
    def _():
        up_copy(me + 1).wait_send()
        core_copy(high_end, 1, core).wait_send()

    @pl.when(me > 0)
    def _():
        down_copy(me - 1).wait_send()
        core_copy(low_end, 0, core).wait_send()


LAG = 2


def back_pass(
    plan, first, ids, grad_normed, branch_full, grad_two, attend_grads, mlp_sums, attend_sums
):
    taps, cols, rows = first.taken.shape
    total = len(BACK_ORDER)
    share = C // plan.pts
    vmem = pltpu.VMEM
    return call(
        functools.partial(back_kernel, plan),
        "back_pass",
        1,
        dict(
            taken=Late(first.taken), pair=Late(first.pair), vec=first.vec, hidden=Late(first.hidden), mixed_unit=Late(first.mixed_unit), mixed_std=first.mixed_std, one_unit=Late(first.one_unit), one_std=first.one_std, taps=Late(first.taps_far), ids=ids,
            grad_normed=Late(grad_normed),
            branch_full=Late(branch_full), grad_two=Late(grad_two), attend_grads=attend_grads, mlp_sums=mlp_sums, attend_sums=attend_sums,
        ),
        dict(
            summed=((total, share, cols), BF),
            point_grad=((rows, cols), F32),
            vector_grad=((12 + FF // C, cols), F32),
        ),
        dict(
            reduce_net=(Reduce.buffers(plan, total, BACK_PACK, cols)),
            turn_acc=vmem((cols, rows), F32),
            grad_one=vmem((cols, rows), F32),
            delta=vmem((C, rows), F32),
            mixed=vmem((C, rows), BF),
            back=vmem((C, rows + 2 * HALO), BF),
            vectors=vmem((plan.pts, cols, 12 + FF // C), F32),
            halo_send=dma(2),
            halo_recv=dma(2),
            core_send=dma(2),
            core_recv=dma(2),
            vector_send=dma(plan.pts),
            vector_recv=dma(plan.pts),
        ),
        taps * rows * (WINDOW * 4 + 5 * C) * cols,
    )


def adam(first, second, grad):
    new_first = BETA_ONE * first + (1.0 - BETA_ONE) * grad
    new_second = BETA_TWO * second + (1.0 - BETA_TWO) * grad * grad
    direction = (
        new_first
        / (1.0 - BETA_ONE**STEP)
        / (jnp.sqrt(new_second / (1.0 - BETA_TWO**STEP)) + ADAM_EPS)
    )
    return new_first, new_second, direction


def owner_kernel(plan, r):
    pts, mdl, slots = plan.pts, plan.mdl, plan.slots
    share, cols = r.summed.shape[1:]
    me, plane = lax.axis_index(PTS), lax.axis_index(MDL)
    moves(START, r.left_move, r.right_move, r.first_move, r.second_move)
    greet(
        [
            {PTS: p, MDL: m}
            for i, p in enumerate([me] + others(me, pts))
            for j, m in enumerate([plane] + others(plane, mdl))
            if i + j > 0
        ]
    )

    count = r.summed.shape[0]
    r.listed[:count] = r.summed[...]
    r.listed[count:] = r.mlp_summed[...]

    def order(slot, carry):
        r.grads[pl.ds(slot, 1)] = r.listed[pl.ds(r.places[slot], 1)]
        return carry

    def whole_copy(j, step):
        m = lax.rem(plane + step, mdl)
        target, k = plan.worker(j), j // pts
        piece, spot = r.grads.at[m * slots + j], r.whole.at[k, me, plane]

        def near():
            return pltpu.make_async_copy(piece, spot, r.whole_here.at[k])

        def far():
            return push(
                piece, spot, r.whole_send.at[step, j], r.whole_recv.at[k, me, plane], pts=target,
                mdl=m,
            )

        return (me == target) & (step == 0), near, far

    def rows_copy(m, slot):
        return push(
            r.grads.at[pl.ds(m * slots, slots)], r.rows.at[slot], r.rows_send.at[m],
            r.rows_recv.at[slot], mdl=m,
        )

    def rows_here():
        return pltpu.make_async_copy(
            r.grads.at[pl.ds(plane * slots, slots)], r.rows.at[plane], r.rows_home
        )

    for step in range(mdl):
        m = lax.rem(plane + step, mdl)
        lax.fori_loop(m * slots, (m + 1) * slots, order, 0)
        for j in range(slots):
            home, near, far = whole_copy(j, step)

            @pl.when(home)
            def _():
                near().start()

            @pl.when(jnp.logical_not(home))
            def _():
                far().start()

    for m in others(plane, mdl):
        rows_copy(m, plane).start()
    rows_here().start()
    moves(WAIT, r.left_move, r.right_move, r.first_move, r.second_move)

    def result_copy(k, kind, p):
        return push(
            r.turned.at[k, kind, p], r.results.at[plan.work(me, k), kind], r.back_send.at[k, kind, p],
            r.back_recv.at[plan.work(me, k), kind], pts=p,
        )

    def result_here(k, kind):
        return pltpu.make_async_copy(
            r.turned.at[k, kind, me], r.results.at[plan.work(me, k), kind], r.back_home.at[k, kind]
        )

    def send_result(k, kind, value):
        r.turned[k, kind] = value.astype(BF).reshape(pts, share, C)
        for p in others(me, pts):
            result_copy(k, kind, p).start()
        result_here(k, kind).start()

    for k in range(plan.each):

        @pl.when(plan.work(me, k) < slots)
        def _():
            pltpu.make_async_copy(
                r.grads.at[0], r.whole.at[k, me, plane], r.whole_here.at[k]
            ).wait()
            for p_step in range(pts):
                for m_step in range(mdl):
                    if p_step + m_step > 0:
                        p, m = lax.rem(me + p_step, pts), lax.rem(plane + m_step, mdl)
                        push(
                            r.grads.at[0], r.whole.at[k, p, m], r.whole_send.at[0, 0],
                            r.whole_recv.at[k, p, m], pts=p, mdl=m,
                        ).wait_recv()
            left = r.left[k].reshape(C, C)
            right = r.right[k].reshape(C, C)
            halves = [
                dot(left, r.whole[k, :, m].reshape(C, cols), TN).astype(BF) for m in range(mdl)
            ]
            if cols % 128 == 0:
                rotated = dot(jnp.concatenate(halves, 1), right)
            else:
                rotated = sum(
                    dot(half, right[m * cols : (m + 1) * cols]) for m, half in enumerate(halves)
                )
            send_result(k, 0, rotated)
            _, _, direction = adam(
                r.first[k].reshape(C, C).astype(F32),
                r.second[k].reshape(C, C).astype(F32),
                rotated.astype(BF).astype(F32),
            )
            send_result(k, 1, dot(left, dot(direction.astype(BF), right, NT).astype(BF)))

    for m in others(plane, mdl):
        rows_copy(m, plane).wait_send()
        rows_copy(m, m).wait_recv()
    rows_here().wait()
    for j in range(slots):
        source, k = plan.worker(j), j // pts
        for kind in range(2):

            @pl.when(me != source)
            def _():
                push(
                    r.turned.at[k, kind, me], r.results.at[j, kind], r.back_send.at[k, kind, source],
                    r.back_recv.at[j, kind], pts=source,
                ).wait_recv()

    for k in range(plan.each):

        @pl.when(plan.work(me, k) < slots)
        def _():
            for kind in range(2):
                result_here(k, kind).wait()
                for p in others(me, pts):
                    result_copy(k, kind, p).wait_send()

    for step in range(mdl):
        for j in range(slots):
            home, near, far = whole_copy(j, step)

            @pl.when(jnp.logical_not(home))
            def _():
                far().wait_send()


def owner_update(plan, places, summed, mlp_summed, left, right, first, second):
    _, share, cols = summed.shape
    blocks = len(BACK_ORDER) + len(MLP_ORDER)
    pts, mdl, each, slots = plan.pts, plan.mdl, plan.each, plan.slots
    vmem = pltpu.VMEM
    return call(
        functools.partial(owner_kernel, plan),
        "owner_update",
        4,
        dict(places=places, summed=summed, mlp_summed=mlp_summed, left=Late(left), right=Late(right), first=Late(first), second=Late(second)),
        dict(
            rows=((mdl, slots, share, cols), BF),
            results=((slots, 2, share, C), BF),
        ),
        dict(
            grads=vmem((blocks, share, cols), BF),
            listed=vmem((blocks, share, cols), BF),
            whole=vmem((each, pts, mdl, share, cols), BF),
            turned=vmem((each, 2, pts, share, C), BF),
            whole_send=dma(mdl, slots),
            whole_recv=dma(each, pts, mdl),
            whole_here=dma(each),
            rows_send=dma(mdl),
            rows_recv=dma(mdl),
            rows_home=dma(),
            back_send=dma(each, 2, pts),
            back_recv=dma(slots, 2),
            back_home=dma(each, 2),
        ),
        8 * each * C * C * C,
        smem=("places",),
    )


def scan_index(row_ids, scan_lengths):
    bounds = jnp.cumsum(scan_lengths)
    return jnp.sum((row_ids[..., None] >= bounds[:-1]).astype(jnp.int32), -1)


def local(
    points,
    cotangent,
    neighbours,
    scan_lengths,
    to_patch,
    from_patch,
    owner_slot,
    weights,
    row_eigen_basis,
    right_basis,
    first_moment,
    second_moment,
    vectors,
    vector_first,
    vector_second,
):
    rows, cols = points.shape
    slot_count = from_patch.shape[0]
    pts = lax.axis_size(PTS)
    mdl = lax.axis_size(MDL)
    pts_index = lax.axis_index(PTS)
    patch_count = slot_count // PATCH
    matrix_rate = 1.6 * C ** (-0.5)
    plan = Layout(pts, mdl, owner_slot.shape[0], patch_count * scan_lengths.shape[0])

    row_ids = pts_index * rows + jnp.arange(rows, dtype=jnp.int32)
    own_scan = scan_index(row_ids, scan_lengths)
    near = neighbours.T
    usable = (near >= 0) & (scan_index(jnp.maximum(near, 0), scan_lengths) == own_scan[None, :])
    ids = jnp.where(usable, near - (pts_index * rows - HALO), -1)

    first = front(
        plan,
        owner_slot,
        weights,
        points,
        cotangent,
        vectors,
        ids,
        to_patch[None],
        from_patch[None],
        scan_lengths,
    )
    rest, send_pos, arrival = first.rest, first.send_pos, first.arrival
    kept = attend(
        plan,
        first.slot_in,
        rest,
        vectors,
        first.group,
        send_pos,
        arrival,
        row_eigen_basis,
        right_basis,
    )
    middle = mlp(
        plan, kept.attended_rows, first, rest, cotangent, send_pos, arrival, first_moment
    )
    back = attend_back(
        plan,
        kept,
        middle.grad_slot,
        first.slot_in,
        rest,
        first.pair,
        send_pos,
        arrival,
        middle.weight_grads,
        second_moment,
    )
    last = back_pass(
        plan,
        first,
        ids,
        back.grad_normed,
        middle.branch_full,
        middle.grad_two,
        back.weight_grads,
        middle.sums,
        back.sums,
    )
    vector_grad = last.vector_grad
    listed = BACK_ORDER + MLP_ORDER
    places = jnp.array([listed.index(b) for b in range(len(listed))], jnp.int32)
    slot_ids = jnp.arange(len(listed), dtype=jnp.int32)
    place_of_slot = jnp.sum(
        jnp.where(owner_slot[None, :] == slot_ids[:, None], places[None, :], 0), 1
    )
    ended = owner_update(
        plan,
        place_of_slot,
        last.summed,
        back.mlp_summed,
        kept.left_whole,
        kept.right_whole,
        middle.first_whole,
        back.second_whole,
    )
    reduced = ended.rows.transpose(1, 2, 0, 3).reshape(plan.slots, C // pts, C)
    results = ended.results
    rotated, update = results[:, 0].astype(F32), results[:, 1].astype(F32)
    new_first, new_second, _ = adam(first_moment, second_moment, rotated)
    new_weights = weights - matrix_rate * (update + MATRIX_DECAY * weights)
    new_vector_first, new_vector_second, vector_step = adam(
        vector_first, vector_second, vector_grad
    )
    new_vectors = vectors - VECTOR_RATE * vector_step
    return (
        middle.out,
        last.point_grad,
        reduced.astype(F32),
        new_first,
        new_second,
        new_weights,
        new_weights.astype(BF),
        vector_grad,
        new_vector_first,
        new_vector_second,
        new_vectors,
    )


def solution(mesh):
    by_rows = P(PTS, MDL)
    owned = P(MDL, PTS, None)
    vector = P(None, MDL)
    return jax.shard_map(
        local,
        mesh=mesh,
        in_specs=(
            by_rows,
            by_rows,
            P(PTS, None),
            P(),
            P(PTS),
            P(PTS),
            P(),
            owned,
            owned,
            owned,
            owned,
            owned,
            vector,
            vector,
            vector,
        ),
        out_specs=(
            by_rows,
            by_rows,
            owned,
            owned,
            owned,
            owned,
            owned,
            vector,
            vector,
            vector,
            vector,
        ),
        check_vma=False,
    )
```

time: 529 us -> 454 us (0.86)
  Pallas kernels: 490 us -> 434 us
  other arithmetic: 21.7 us -> 8.77 us
  local copies, waits for them, and re-layouts: 10 us -> 2.15 us
    pallas_call x6, Pallas kernels: 490 us -> 434 us  [call(): pl.pallas_call(body, in_specs=[pl.BlockSpec(memory_space=space(*item)) fo...]
    convert_element_type x6 -> x0, other arithmetic: 5.52 us -> none  [the longest x1 0.93 us: local(): row_eigen_basis.astype(BF)]
where the time goes in v5:
time: 454 us; the launch traced here: 447 us
  Pallas kernels  434 us (96%)
  other arithmetic  8.77 us (2%)
    pallas_call x6, Pallas kernels, call(): pl.pallas_call(body, in_specs=[pl.BlockSpec(memory_space=space(*item)) fo...  434 us

profile of v5, /device:TPU:29, one launch (start us, length us, event | category | flops | bytes accessed | tf_op | source)
XLA Modules:
  0.0 446.6 jit_solution(2757522283092453228)
XLA Ops:
  0.6 0.8 reduce-window.4
  1.5 1.6 select_bitcast_fusion.refs_5_.refs_9_
  3.2 121.3 %front.1 = (bf16[8,27,64,128]{3,2,1,0:T(8,128)(2,1)}, bf16[27,128,1024]{2,1,0:T(8,128)(2,1)}, bf16[512,1024]{1,0:T(8,128)(2,1)}, bf16[4,2,512,128]{3,2,1,0:T(8,1...) custom-call(s32[40]{0:T(128)} %refs_0_.1, ...), custom_call_target="tpu_custom_call" | custom-call | flops 18119393280 | bytes 20000000 | tf_op jit(solution)/shard_map/front/pallas_call | solution.py:157
  124.5 56.0 %attend.1 = (bf16[1024,256]{1,0:T(8,128)(2,1)}, bf16[1024,256]{1,0:T(8,128)(2,1)}, bf16[1024,128]{1,0:T(8,128)(2,1)}, bf16[128,1024]{1,0:T(8,128)(2,1)}, f32[8,1...) custom-call(bf16[512,1024]{1,0:T(8,128)(2,1)} %get-tuple-element.52., ...), custom_call_target="tpu_custom_call" | custom-call | flops 4294967296 | bytes 20000000 | tf_op jit(solution)/shard_map/attend/pallas_call | solution.py:157
  180.4 47.4 %mlp.1 = (bf16[2,8,64,512]{3,2,1,0:T(8,128)(2,1)}, bf16[512,1024]{1,0:T(8,128)(2,1)}, bf16[512,1024]{1,0:T(8,128)(2,1)}, f32[128,1024]{1,0:T(8,128)}, bf16[1024,...) custom-call(bf16[512,1024]{1,0:T(8,128)(2,1)} %get-tuple-element.57.refs_0_, ...), custom_call_target="tpu_custom_call" | custom-call | flops 4294967296 | bytes 20000000 | tf_op jit(solution)/shard_map/mlp/pallas_call | solution.py:157
  227.9 71.6 %attend_back.1 = (bf16[512,1024]{1,0:T(8,128)(2,1)}, bf16[4,512,128]{2,1,0:T(8,128)(2,1)}, f32[128,8]{1,0:T(8,128)}, bf16[8,64,128]{2,1,0:T(8,128)(2,1)}, bf16[2,8,64,512]{3,2,1,0:T(8,128)(2,1)}) custom-call(bf16[1024,256]{1,0:T(8,128)(2,1)} %get-tuple-element.70.refs_0_, bf16[1024,256]{1,0:T(8,128)(2,1)} %get-tuple-element.71.refs_1_, ...), custom_call_target="tpu_custom_call" | custom-call | flops 10737418240 | bytes 20000000 | tf_op jit(solution)/shard_map/attend_back/pallas_call | solution.py:157
  299.5 0.0 copy-start.10
  299.5 0.0 copy-start.11
  299.5 74.7 %back_pass.1 = (bf16[32,64,128]{2,1,0:T(8,128)(2,1)}, f32[1024,128]{1,0:T(8,128)}, f32[16,128]{1,0:T(8,128)}) custom-call(bf16[27,128,1024]{2,1,0:T(8,128)(2,1)} %get-tuple-element.63.refs_0_, bf16[4,2,512,128]{3,2,1,0:T(8,128)(2,1)} %get-tuple-element.58.refs_1_.refs_8_, f32[512,16]{1,0:T(8,128)} %get-tuple-element.60.refs_3_.refs_2_, ...), custom_call_target="tpu_custom_call" | custom-call | flops 19931332608 | bytes 20000000 | tf_op jit(solution)/shard_map/back_pass/pallas_call | solution.py:157
  374.2 0.0 copy-done.10
  374.2 0.0 copy-done.11
  374.3 0.6 select_reduce_fusion.refs_0_
  374.9 0.0 copy-start
  374.9 0.0 copy-start.1
  374.9 0.0 copy-start.2
  374.9 63.4 %owner_update.1 = (bf16[4,10,64,128]{3,2,1,0:T(8,128)(2,1)}, bf16[10,2,64,512]{3,2,1,0:T(8,128)(2,1)}) custom-call(s32[40]{0:T(128)} %select_reduce_fusion.refs_0_, bf16[32,64,128]{2,1,0:T(8,128)(2,1)} %get-tuple-element.84.refs_1_, bf16[8,64,128]{2,1,0:T(8,128)(2,1)} %get-tuple-element.85.refs_2_, bf16[2,8,64,512]{3,2,1,0:T(8,128)(2,1)} %get-tuple-element.86.refs_3_, ...), custom_call_target="tpu_custom_call" | custom-call | flops 2147483648 | bytes 20000000 | tf_op jit(solution)/shard_map/owner_update/pallas_call | solution.py:157
  438.3 0.0 copy-done
  438.3 0.0 copy-done.1
  438.3 0.0 copy-done.2
  438.3 0.0 copy-start.3
  438.3 3.8 fusion.8
  442.1 0.0 copy-start.6
  442.1 0.0 copy-start.7
  442.1 0.0 copy-start.8
  442.1 0.0 copy-start.9
  442.1 0.0 copy-start.5
  442.1 0.0 copy-start.4
  442.1 0.0 copy-done.3
  442.1 1.2 copy_bitcast_fusion
  443.4 0.0 copy-done.6
  443.4 0.0 copy-done.7
  443.4 0.0 copy-done.8
  443.4 0.0 copy-done.9
  443.4 0.6 multiply_subtract_fusion
  444.0 0.0 copy-done.5
  444.0 0.7 copy.34
  444.7 0.0 copy-done.4
  444.7 0.8 copy.35
  445.5 0.6 copy.36
  (1 shorter events, 0.0 us)
Async XLA Ops:
  299.5 74.8 %copy-start.10 = (s32[40]{0:T(128)S(1)}, s32[40]{0:T(128)}, u32[]{:S(2)}) copy-start(s32[40]{0:T(128)} %refs_0_.1) | copy-start | bytes 484
  299.5 74.8 %copy-start.11 = (s32[40]{0:T(128)S(1)}, s32[40]{0:T(128)}, u32[]{:S(2)}) copy-start(s32[40]{0:T(128)} %constant.48.clone) | copy-start | bytes 484
  374.9 63.4 %copy-start = (f32[10,64,512]{2,1,0:T(8,128)S(1)}, f32[10,64,512]{2,1,0:T(8,128)}, u32[]{:S(2)}) copy-start(f32[10,64,512]{2,1,0:T(8,128)} %refs_1_.1) | copy-start | bytes 3932164
  374.9 63.4 %copy-start.1 = (f32[10,64,512]{2,1,0:T(8,128)S(1)}, f32[10,64,512]{2,1,0:T(8,128)}, u32[]{:S(2)}) copy-start(f32[10,64,512]{2,1,0:T(8,128)} %refs_9_.1) | copy-start | bytes 3932164
  374.9 63.4 %copy-start.2 = (f32[10,64,512]{2,1,0:T(8,128)S(1)}, f32[10,64,512]{2,1,0:T(8,128)}, u32[]{:S(2)}) copy-start(f32[10,64,512]{2,1,0:T(8,128)} %refs_12_.1) | copy-start | bytes 3932164
  438.3 3.9 copy-start.3
  442.1 1.3 copy-start.6
  442.1 1.3 copy-start.7
  442.1 1.3 copy-start.8
  442.1 1.3 copy-start.9
  442.1 1.9 copy-start.5
  442.1 2.6 copy-start.4

commit v6 on v5

--- a/solution.py
+++ b/solution.py
@@ -336,6 +336,45 @@
     def run(self, values):
         self.start(values)
         return self.finish()
+
+
+class Route:
+    PIECES = 2
+
+    def __init__(self, plan, out_index, in_index, full, nets):
+        cols = full.shape[0] // plan.mdl
+        self.size = cols // self.PIECES
+        self.full, self.base = full, lax.axis_index(MDL) * cols
+        self.trades = [Trade(plan, out_index, in_index, net.trade) for net in nets]
+        self.gathers = [
+            Gather(
+                plan, lambda m, i=i: full.at[pl.ds(m * cols + i * self.size, self.size)], net.ring
+            )
+            for i, net in enumerate(nets)
+        ]
+
+    @classmethod
+    def buffers(cls, plan, cols, rows):
+        net = dict(
+            trade=Trade.buffers(plan, cols // cls.PIECES, rows), ring=Gather.semaphores(plan)
+        )
+        return [net] * cls.PIECES
+
+    def start(self, values):
+        for i, trade in enumerate(self.trades):
+            trade.start(values[i * self.size : (i + 1) * self.size])
+
+    def land(self):
+        for i, (trade, gather) in enumerate(zip(self.trades, self.gathers)):
+            self.full[pl.ds(self.base + i * self.size, self.size), :] = trade.finish()
+            gather.start()
+            if i > 0:
+                self.gathers[i - 1].forward()
+        self.gathers[-1].forward()
+
+    def finish(self):
+        for gather in self.gathers:
+            gather.finish()
 
 
 class Reduce:
@@ -786,10 +825,8 @@
         return carry
 
     lax.fori_loop(0, rows // span_size, norms, 0)
-    trade = Trade(
-        plan, r.send_pos, r.arrival, r.trade_net
-    )
-    trade.start(r.normed[pl.ds(plane * cols, cols), :])
+    route = Route(plan, r.send_pos, r.arrival, r.slot_in, r.route_net)
+    route.start(r.normed[pl.ds(plane * cols, cols), :])
     moves(START, r.hidden_move, r.mixed_unit_move, r.one_unit_move, r.stream_move, r.pair_move)
     for group in range(conv_groups, groups):
         complete(group)
@@ -797,11 +834,8 @@
         r.rest[i] = r.blocks[:, TAPS + 2 + i].reshape(C, cols)
     cot_gather.finish()
     moves(START, r.rest_move, r.cot_full_move)
-    r.slot_in[pl.ds(plane * cols, cols), :] = trade.finish()
-    Gather(
-        plan, lambda m: r.slot_in.at[pl.ds(m * cols, cols)],
-        r.slot_net,
-    ).run()
+    route.land()
+    route.finish()
     moves(START, r.slot_in_move)
 
     @pl.when(me < pts - 1)
@@ -836,7 +870,6 @@
         cot_net=ring,
         pair_net=ring,
         hidden_net=ring,
-        slot_net=ring,
         owned=vmem((mdl, plan.slots, share, cols), BF),
         points=vmem((cols, rows), BF),
         spread=vmem((total, share, cols), BF),
@@ -859,7 +892,7 @@
         side_send=dma(groups, plan.width, plan.depth),
         side_recv=dma(groups, pts),
         sum_net=(Sum.buffers(plan, (cols, rows))),
-        trade_net=(Trade.buffers(plan, cols, rows)),
+        route_net=Route.buffers(plan, cols, rows),
     )
     return call(
         functools.partial(front_kernel, plan),
@@ -894,11 +927,6 @@
     )
 
 
-def fetches(plan, srcs, dsts, refs, act):
-    for src, dst, sems in zip(srcs, dsts, refs.fetch_net):
-        fetch_copies(plan, src, dst, sems, act)
-
-
 def head_lanes(ext, cols, head):
     lane = lax.broadcasted_iota(jnp.int32, ext.shape, 1)
     return jnp.where((lane >= cols) | (lane // HD == head), ext, jnp.zeros_like(ext))
@@ -906,224 +934,6 @@
 
 def head_rows(head):
     return pl.ds(pl.multiple_of(head * HD, HD), HD)
-
-
-def attend_kernel(plan, r):
-    plane = lax.axis_index(MDL)
-    rows, cols = r.values.shape
-    heads = cols // HD
-    moves(START, r.left32_move, r.right32_move)
-    greet(everyone(plan))
-    moves(WAIT, r.left32_move, r.right32_move)
-    r.left[...] = r.left32[...].astype(BF)
-    r.right[...] = r.right32[...].astype(BF)
-    fetched = (plan, (r.left, r.right), (r.left_whole, r.right_whole), r)
-    fetches(*fetched, START)
-    group = column(r.group[...])
-    lane = lax.broadcasted_iota(jnp.int32, (rows, cols), 1)
-    same = lane == group
-    slot_in = r.slot_in[...]
-    queries = (dot(slot_in, r.rest[0], TN) + r.vectors[6:7, :]).astype(BF)
-    r.q_ext[:, :cols] = queries * BF(HD ** (-0.5))
-    r.q_ext[:, cols:] = jnp.where(same, 1.0, 0.0).astype(BF)
-    r.k_ext[:, :cols] = dot(slot_in, r.rest[1], TN).astype(BF)
-    r.k_ext[:, cols:] = jnp.where(same | (lane >= plan.groups), 0.0, -1e30).astype(BF)
-    values = dot(slot_in, r.rest[2], TN) + r.vectors[7:8, :]
-    r.values[...] = values.astype(BF)
-    r.v_aug[:, :HD] = values.T.astype(BF).reshape(heads, HD, rows)
-    r.v_aug[:, HD:] = jnp.ones((heads, HD, rows), BF)
-    moves(START, r.q_ext_move, r.k_ext_move, r.values_move)
-
-    def one(head, carry):
-        keys = r.k_ext[...]
-        values_t = r.v_aug[pl.ds(head, 1)][0]
-        for tile in range(rows // TILE):
-            span = slice(tile * TILE, (tile + 1) * TILE)
-            scores = dot(keys, head_lanes(r.q_ext[span, :], cols, head), NT)
-            top = jnp.max(scores, 0, keepdims=True)
-            soft = jnp.exp(scores - top).astype(BF)
-            summed = dot(values_t, soft)
-            total = summed[HD : HD + 1]
-            r.attended[head_rows(head), span] = (summed[:HD] / total).astype(BF)
-            r.lse[pl.ds(head, 1), :, span] = (top + jnp.log(total))[None]
-        return carry
-
-    lax.fori_loop(0, heads, one, 0)
-    moves(START, r.attended_move, r.lse_move)
-    trade = Trade(
-        plan, r.arrival, r.send_pos, r.trade_net
-    )
-    r.attended_rows[pl.ds(plane * cols, cols), :] = trade.run(r.attended[...])
-    Gather(
-        plan, lambda m: r.attended_rows.at[pl.ds(m * cols, cols)],
-        r.rows_net,
-    ).run()
-    fetches(*fetched, WAIT)
-    moves(WAIT, r.q_ext_move, r.k_ext_move, r.values_move, r.attended_move, r.lse_move)
-
-
-def attend(plan, slot_in, rest, vectors, group, send_pos, arrival, left, right):
-    rows, cols = group.shape[1], vectors.shape[1]
-    heads = cols // HD
-    fetched = fetch_shape(plan, left)
-    vmem = pltpu.VMEM
-    return call(
-        functools.partial(attend_kernel, plan),
-        "attend",
-        2,
-        dict(
-            slot_in=slot_in, rest=rest, vectors=vectors, group=group,
-            send_pos=send_pos, arrival=arrival, left32=Late(left), right32=Late(right),
-        ),
-        dict(
-            q_ext=Late((rows, 2 * cols), BF),
-            k_ext=Late((rows, 2 * cols), BF),
-            values=Late((rows, cols), BF),
-            attended=Late((cols, rows), BF),
-            lse=Late((heads, 1, rows), F32),
-            attended_rows=((C, rows), BF),
-            left_whole=(fetched.shape, fetched.dtype),
-            right_whole=(fetched.shape, fetched.dtype),
-        ),
-        dict(
-            left=vmem(left.shape, BF),
-            right=vmem(right.shape, BF),
-            v_aug=vmem((heads, 2 * HD, rows), BF),
-            fetch_net=[fetch_sems(plan), fetch_sems(plan)],
-            trade_net=(Trade.buffers(plan, cols, rows)),
-            rows_net=(Gather.semaphores(plan)),
-        ),
-        4 * heads * rows * rows * cols,
-        free=("left_whole", "right_whole"),
-    )
-
-
-def attend_back_kernel(plan, r):
-    plane = lax.axis_index(MDL)
-    rows, cols = r.values.shape
-    heads = cols // HD
-    greet(everyone(plan))
-    moves(START, r.second32_move, r.slot_in_move, r.rest_move)
-    fetched = (plan, (r.second,), (r.second_whole,), r)
-    mlp_count = r.mlp_grads.shape[0]
-    reduce = Reduce(
-        plan, r.reduce_net
-    )
-    for group in range(reduce.groups):
-        for place in range(MLP_PACK):
-            reduce.store(r.mlp_grads[group * MLP_PACK + place], group, place)
-        reduce.start(group)
-    moves(WAIT, r.second32_move)
-    r.second[...] = r.second32[...].astype(BF)
-    fetches(*fetched, START)
-    grad_slot = r.grad_slot[...]
-    grad_t = dot(r.pair[pl.ds(plane, 1), 1][0], grad_slot, TN).astype(BF).astype(F32)
-    r.grad[...] = grad_t.T.astype(BF)
-    weighed = grad_t * r.attended[...].astype(F32)
-    r.inner[...] = jnp.sum(weighed.reshape(heads, HD, rows), 1, keepdims=True)
-    r.keys_t[...] = r.k_ext[:, :cols].astype(F32).T.astype(BF)
-    r.dk_acc[...] = jnp.zeros_like(r.dk_acc)
-    r.dv_acc[...] = jnp.zeros_like(r.dv_acc)
-
-    def one(head, carry):
-        queries = head_lanes(r.q_ext[...], cols, head)
-        pure = queries[:, :cols]
-        grad = head_lanes(r.grad[...], cols, head)
-        lse = r.lse[pl.ds(head, 1)][0]
-        inner = r.inner[pl.ds(head, 1)][0]
-        keys_t = r.keys_t[head_rows(head), :]
-        dq = jnp.zeros((HD, rows), F32)
-        for tile in range(rows // TILE):
-            span = slice(tile * TILE, (tile + 1) * TILE)
-            scores = dot(r.k_ext[span, :], queries, NT)
-            soft = jnp.exp(scores - lse)
-            grad_soft = dot(r.values[span, :], grad, NT)
-            grad_scores = (soft * (grad_soft - inner)).astype(BF)
-            r.dv_acc[span, :] += dot(soft.astype(BF), grad)
-            r.dk_acc[span, :] += dot(grad_scores, pure)
-            dq = dq + dot(keys_t[:, span], grad_scores)
-        r.dq[head_rows(head), :] = (dq * HD ** (-0.5)).astype(BF)
-        reduce.step(head - delay)
-        return carry
-
-    delay = max(heads - reduce.steps, 0)
-    lax.fori_loop(0, heads, one, 0)
-    for s in range(heads - delay, reduce.steps):
-        reduce.step(s)
-    moves(WAIT, r.slot_in_move, r.rest_move)
-    dk = r.dk_acc[...].astype(BF)
-    dv = r.dv_acc[...].astype(BF)
-    back = dot(r.rest[0], r.dq[...]) + dot(r.rest[1], dk, NT) + dot(r.rest[2], dv, NT)
-    r.parts[...] = back.astype(BF).reshape(plan.mdl, cols, rows)
-    back_sum = Sum(plan, r.parts, r.sum_net)
-    back_sum.start()
-    r.weight_grads[0] = dot(r.slot_in[...], r.dq[...], NT).astype(BF)
-    r.weight_grads[1] = dot(r.slot_in[...], dk).astype(BF)
-    back_sum.middle()
-    r.weight_grads[2] = dot(r.slot_in[...], dv).astype(BF)
-    r.weight_grads[3] = dot(r.grad_slot[...], r.attended[...], NT).astype(BF)
-    trade = Trade(
-        plan, r.arrival, r.send_pos, r.trade_net
-    )
-    trade.start(back_sum.finish().astype(BF))
-    moves(START, r.weight_grads_move)
-    r.sums[...] = jnp.zeros_like(r.sums)
-    r.sums[:, 0:1] = jnp.sum(r.dq[...].astype(F32), 1, keepdims=True)
-    r.sums[:, 1:2] = jnp.sum(dv.astype(F32), 0, keepdims=True).T
-    r.grad_normed[pl.ds(plane * cols, cols), :] = trade.finish()
-    Gather(
-        plan, lambda m: r.grad_normed.at[pl.ds(m * cols, cols)],
-        r.rows_net,
-    ).run()
-    reduce.finish(r.mlp_summed)
-    reduce.end()
-    fetches(*fetched, WAIT)
-    moves(WAIT, r.weight_grads_move)
-
-
-MLP_PACK = 4
-
-
-def attend_back(
-    plan, kept, grad_slot, slot_in, rest, pair, send_pos, arrival, mlp_grads, second
-):
-    rows, cols = kept.values.shape
-    heads = cols // HD
-    vmem = pltpu.VMEM
-    fetched = fetch_shape(plan, second)
-    return call(
-        functools.partial(attend_back_kernel, plan),
-        "attend_back",
-        3,
-        dict(
-            q_ext=kept.q_ext, k_ext=kept.k_ext, values=kept.values, attended=kept.attended, lse=kept.lse, grad_slot=grad_slot, slot_in=Late(slot_in), rest=Late(rest),
-            pair=pair, send_pos=send_pos, arrival=arrival, mlp_grads=mlp_grads, second32=Late(second),
-        ),
-        dict(
-            grad_normed=((C, rows), BF),
-            weight_grads=Late((4, C, cols), BF),
-            sums=((cols, 8), F32),
-            mlp_summed=((mlp_grads.shape[0], C // plan.pts, cols), BF),
-            second_whole=(fetched.shape, fetched.dtype),
-        ),
-        dict(
-            second=vmem(second.shape, BF),
-            grad=vmem((rows, cols), BF),
-            inner=vmem((heads, 1, rows), F32),
-            keys_t=vmem((cols, rows), BF),
-            dk_acc=vmem((rows, cols), F32),
-            dv_acc=vmem((rows, cols), F32),
-            dq=vmem((cols, rows), BF),
-            parts=vmem((plan.mdl, cols, rows), BF),
-            reduce_net=(Reduce.buffers(plan, mlp_grads.shape[0], MLP_PACK, cols)),
-            fetch_net=[fetch_sems(plan)],
-            sum_net=(Sum.buffers(plan, (cols, rows))),
-            trade_net=(Trade.buffers(plan, cols, rows)),
-            rows_net=(Gather.semaphores(plan)),
-        ),
-        10 * heads * rows * rows * cols,
-        free=("second_whole",),
-    )
 
 
 SPAN = 128
@@ -1148,21 +958,15 @@
     return times
 
 
-def mlp_kernel(plan, r):
+def mlp_part(plan, r):
     mdl = plan.mdl
     plane = lax.axis_index(MDL)
     cols, rows = r.cot.shape
     ff_blocks = FF // C
     own = pl.ds(plane * cols, cols)
-    moves(START, r.first32_move, r.stream_move, r.rest_move, r.cot_full_move)
-    r.cot[...] = r.cot_rows[...].astype(F32).T.astype(BF)
-    greet(everyone(plan))
-    moves(WAIT, r.first32_move)
-    r.first[...] = r.first32[...].astype(BF)
-    fetched = (plan, (r.first,), (r.first_whole,), r)
-    fetches(*fetched, START)
+    moves(WAIT, r.pair_move)
     r.acc[...] = beside([r.pair[m, 1] for m in range(mdl)])(r.attended_rows, cols)
-    moves(WAIT, r.stream_move, r.rest_move, r.cot_full_move)
+    moves(WAIT, r.stream_move, r.cot_full_move)
 
     def norms(span):
         branch = (r.acc[:, span] + r.vec[:, 8:9]).astype(BF).astype(F32)
@@ -1223,97 +1027,259 @@
     r.grad_two[...] = grad_two
     branch = grad_two.astype(BF)
     r.branch_full[own, :] = branch
-    trade = Trade(
-        plan, r.send_pos, r.arrival, r.trade_net
-    )
-    trade.start(branch)
+    route = Route(plan, r.send_pos, r.arrival, r.grad_slot, r.in_route)
+    route.start(branch)
+    fetch(plan, r, 2, START)
+    out_sum.middle()
+
+    def along(values):
+        return jnp.sum(values.astype(F32), 1, keepdims=True)
+
+    r.mlp_sums[:, 0:1] = along(branch)
+    r.mlp_sums[:, 1:2] = along(grad_normed * unit)
+    r.mlp_sums[:, 2:3] = along(grad_normed)
+    for k in range(ff_blocks):
+        part = slice(k * cols, (k + 1) * cols)
+        r.mlp_sums[:, 3 + k : 4 + k] = along(r.grad_pre[part, :])
+        r.mlp_grads[k] = dot(r.normed[...], r.grad_pre[part, :], NT).astype(BF)
+        r.mlp_grads[ff_blocks + k] = dot(r.cot_full[...], r.act[part, :], NT).astype(BF)
+    r.mlp_sums[:, 3 + ff_blocks : 4 + ff_blocks] = along(cot)
+    moves(START, r.grad_two_move)
+    route.land()
+    bias = r.vec[own, 11 + ff_blocks : 12 + ff_blocks]
+    r.out[...] = (r.two[own, :] + out_sum.finish() + bias).T.astype(BF)
+    route.finish()
+    for m in others(plane, mdl):
+        stats_copy(m, plane).wait_send()
+
+
+def attend_part(plan, r):
+    plane = lax.axis_index(MDL)
+    rows, cols = r.values.shape
+    heads = cols // HD
+    group = column(r.group[...])
+    lane = lax.broadcasted_iota(jnp.int32, (rows, cols), 1)
+    same = lane == group
+    slot_in = r.slot_in[...]
+    queries = (dot(slot_in, r.rest[0], TN) + r.vectors[6:7, :]).astype(BF)
+    r.q_ext[:, :cols] = queries * BF(HD ** (-0.5))
+    r.q_ext[:, cols:] = jnp.where(same, 1.0, 0.0).astype(BF)
+    r.k_ext[:, :cols] = dot(slot_in, r.rest[1], TN).astype(BF)
+    r.k_ext[:, cols:] = jnp.where(same | (lane >= plan.groups), 0.0, -1e30).astype(BF)
+    values = dot(slot_in, r.rest[2], TN) + r.vectors[7:8, :]
+    r.values[...] = values.astype(BF)
+    r.v_aug[:, :HD] = values.T.astype(BF).reshape(heads, HD, rows)
+    r.v_aug[:, HD:] = jnp.ones((heads, HD, rows), BF)
+
+    def one(head, carry):
+        keys = r.k_ext[...]
+        values_t = r.v_aug[pl.ds(head, 1)][0]
+        for tile in range(rows // TILE):
+            span = slice(tile * TILE, (tile + 1) * TILE)
+            scores = dot(keys, head_lanes(r.q_ext[span, :], cols, head), NT)
+            top = jnp.max(scores, 0, keepdims=True)
+            soft = jnp.exp(scores - top).astype(BF)
+            summed = dot(values_t, soft)
+            total = summed[HD : HD + 1]
+            r.attended[head_rows(head), span] = (summed[:HD] / total).astype(BF)
+            r.lse[pl.ds(head, 1), :, span] = (top + jnp.log(total))[None]
+        return carry
+
+    route = Route(plan, r.arrival, r.send_pos, r.attended_rows, r.out_route)
+    for i, trade in enumerate(route.trades):
+        share = heads // route.PIECES
+        lax.fori_loop(i * share, (i + 1) * share, one, 0)
+        trade.start(r.attended[i * route.size : (i + 1) * route.size, :])
+    fetch(plan, r, 1, START)
+    route.land()
+    route.finish()
+
+
+def attend_back_part(plan, r):
+    plane = lax.axis_index(MDL)
+    rows, cols = r.values.shape
+    heads = cols // HD
+    greet(everyone(plan))
+    mlp_count = r.mlp_grads.shape[0]
+    reduce = Reduce(
+        plan, r.reduce_net
+    )
+    for group in range(reduce.groups):
+        for place in range(MLP_PACK):
+            reduce.store(r.mlp_grads[group * MLP_PACK + place], group, place)
+        reduce.start(group)
     branch_gather = Gather(
         plan, lambda m: r.branch_full.at[pl.ds(m * cols, cols)],
         r.branch_net,
     )
     branch_gather.start()
-    out_sum.middle()
-
-    def along(values):
-        return jnp.sum(values.astype(F32), 1, keepdims=True)
-
-    r.sums[:, 0:1] = along(branch)
-    r.sums[:, 1:2] = along(grad_normed * unit)
-    r.sums[:, 2:3] = along(grad_normed)
-    for k in range(ff_blocks):
-        part = slice(k * cols, (k + 1) * cols)
-        r.sums[:, 3 + k : 4 + k] = along(r.grad_pre[part, :])
-        r.weight_grads[k] = dot(r.normed[...], r.grad_pre[part, :], NT).astype(BF)
-        r.weight_grads[ff_blocks + k] = dot(r.cot_full[...], r.act[part, :], NT).astype(BF)
-    r.sums[:, 3 + ff_blocks : 4 + ff_blocks] = along(cot)
-    r.grad_slot[own, :] = trade.finish()
-    slot_gather = Gather(
-        plan, lambda m: r.grad_slot.at[pl.ds(m * cols, cols)],
-        r.slot_net,
-    )
-    slot_gather.start()
-    moves(START, r.weight_grads_move, r.grad_two_move)
+    fetch(plan, r, 3, START)
+    grad_slot = r.grad_slot[...]
+    grad_t = dot(r.pair[pl.ds(plane, 1), 1][0], grad_slot, TN).astype(BF).astype(F32)
+    r.grad[...] = grad_t.T.astype(BF)
+    weighed = grad_t * r.attended[...].astype(F32)
+    r.inner[...] = jnp.sum(weighed.reshape(heads, HD, rows), 1, keepdims=True)
+    r.keys_t[...] = r.k_ext[:, :cols].astype(F32).T.astype(BF)
+    r.dk_acc[...] = jnp.zeros_like(r.dk_acc)
+    r.dv_acc[...] = jnp.zeros_like(r.dv_acc)
+
+    def one(head, carry):
+        queries = head_lanes(r.q_ext[...], cols, head)
+        pure = queries[:, :cols]
+        grad = head_lanes(r.grad[...], cols, head)
+        lse = r.lse[pl.ds(head, 1)][0]
+        inner = r.inner[pl.ds(head, 1)][0]
+        keys_t = r.keys_t[head_rows(head), :]
+        dq = jnp.zeros((HD, rows), F32)
+        for tile in range(rows // TILE):
+            span = slice(tile * TILE, (tile + 1) * TILE)
+            scores = dot(r.k_ext[span, :], queries, NT)
+            soft = jnp.exp(scores - lse)
+            grad_soft = dot(r.values[span, :], grad, NT)
+            grad_scores = (soft * (grad_soft - inner)).astype(BF)
+            r.dv_acc[span, :] += dot(soft.astype(BF), grad)
+            r.dk_acc[span, :] += dot(grad_scores, pure)
+            dq = dq + dot(keys_t[:, span], grad_scores)
+        r.dq[head_rows(head), :] = (dq * HD ** (-0.5)).astype(BF)
+        reduce.step(head - delay)
+        return carry
+
+    delay = max(heads - reduce.steps, 0)
+    lax.fori_loop(0, heads, one, 0)
+    for s in range(heads - delay, reduce.steps):
+        reduce.step(s)
     branch_gather.forward()
-    bias = r.vec[own, 11 + ff_blocks : 12 + ff_blocks]
-    r.out[...] = (r.two[own, :] + out_sum.finish() + bias).T.astype(BF)
-    slot_gather.forward()
+    dk = r.dk_acc[...].astype(BF)
+    dv = r.dv_acc[...].astype(BF)
+    back = dot(r.rest[0], r.dq[...]) + dot(r.rest[1], dk, NT) + dot(r.rest[2], dv, NT)
+    r.back_parts[...] = back.astype(BF).reshape(plan.mdl, cols, rows)
+    back_sum = Sum(plan, r.back_parts, r.sum_net)
+    back_sum.start()
+    r.attend_grads[0] = dot(r.slot_in[...], r.dq[...], NT).astype(BF)
+    r.attend_grads[1] = dot(r.slot_in[...], dk).astype(BF)
+    back_sum.middle()
+    r.attend_grads[2] = dot(r.slot_in[...], dv).astype(BF)
+    r.attend_grads[3] = dot(r.grad_slot[...], r.attended[...], NT).astype(BF)
+    route = Route(plan, r.arrival, r.send_pos, r.grad_normed, r.back_route)
+    route.start(back_sum.finish().astype(BF))
+    moves(START, r.attend_grads_move)
+    r.attend_sums[...] = jnp.zeros_like(r.attend_sums)
+    r.attend_sums[:, 0:1] = jnp.sum(r.dq[...].astype(F32), 1, keepdims=True)
+    r.attend_sums[:, 1:2] = jnp.sum(dv.astype(F32), 0, keepdims=True).T
+    route.land()
     branch_gather.finish()
     moves(START, r.branch_full_move)
-    slot_gather.finish()
-    fetches(*fetched, WAIT)
-    moves(WAIT, r.weight_grads_move, r.grad_two_move, r.branch_full_move)
-    for m in others(plane, mdl):
-        stats_copy(m, plane).wait_send()
-
-
-def mlp(plan, attended_rows, first, rest, cot, send_pos, arrival, moment):
+    route.finish()
+    reduce.finish(r.mlp_summed)
+    reduce.end()
+
+
+MLP_PACK = 4
+
+
+MLP_PACK = 4
+
+
+def fetch(plan, r, place, act):
+    source = (r.left32, r.right32, r.first32, r.second32)[place]
+    whole = (r.left_whole, r.right_whole, r.first_whole, r.second_whole)[place]
+    if act == START:
+        moves(WAIT, (r.left32_move, r.right32_move, r.first32_move, r.second32_move)[place])
+        r.low[place] = source[...].astype(BF)
+    fetch_copies(plan, r.low.at[place], whole, r.fetch_net[place], act)
+
+
+def middle_kernel(plan, r):
+    moves(START, r.left32_move, r.pair_move, r.stream_move, r.cot_full_move)
+    moves(START, r.right32_move, r.first32_move, r.second32_move)
+    greet(everyone(plan))
+    fetch(plan, r, 0, START)
+    r.cot[...] = r.cot_rows[...].astype(F32).T.astype(BF)
+    attend_part(plan, r)
+    mlp_part(plan, r)
+    attend_back_part(plan, r)
+    for place in range(4):
+        fetch(plan, r, place, WAIT)
+    moves(WAIT, r.grad_two_move, r.attend_grads_move, r.branch_full_move)
+
+
+def middle(plan, first, vectors, cot, left, right, moment, second):
     rows, cols = cot.shape
     ff_blocks = FF // C
+    heads = cols // HD
     vmem = pltpu.VMEM
-    scratch = dict(
-        cot=vmem((cols, rows), BF),
-        first=vmem(moment.shape, BF),
-        acc=vmem((C, rows), F32),
-        two=vmem((C, rows), F32),
-        two_unit=vmem((C, rows), F32),
-        two_std=vmem((1, rows), F32),
-        normed=vmem((C, rows), BF),
-        pre=vmem((cols, rows), F32),
-        grad_act=vmem((cols, rows), F32),
-        act=vmem((ff_blocks * cols, rows), BF),
-        grad_pre=vmem((ff_blocks * cols, rows), BF),
-        stats=vmem((plan.mdl, 8, rows), F32),
-        stats_send=dma(plan.mdl),
-        stats_recv=dma(plan.mdl),
-        parts=vmem((plan.mdl, cols, rows), BF),
-        out_parts=vmem((plan.mdl, cols, rows), BF),
-        grad_net=(Sum.buffers(plan, (cols, rows))),
-        out_net=(Sum.buffers(plan, (cols, rows))),
-        trade_net=(Trade.buffers(plan, cols, rows)),
-        branch_net=(Gather.semaphores(plan)),
-        slot_net=(Gather.semaphores(plan)),
-        fetch_net=[fetch_sems(plan)],
-    )
+    whole = (fetch_shape(plan, left).shape, BF)
+    route = Route.buffers(plan, cols, rows)
+    total = Sum.buffers(plan, (cols, rows))
     return call(
-        functools.partial(mlp_kernel, plan),
-        "mlp",
-        6,
+        functools.partial(middle_kernel, plan),
+        "middle",
+        2,
         dict(
-            attended_rows=attended_rows, pair=first.pair, stream=Late(first.stream), vec=first.vec, cot_full=Late(first.cot_full), rest=Late(rest), cot_rows=cot,
-            send_pos=send_pos, arrival=arrival, first32=Late(moment),
+            slot_in=first.slot_in, rest=first.rest, vectors=vectors, group=first.group,
+            send_pos=first.send_pos, arrival=first.arrival, vec=first.vec, cot_rows=cot,
+            pair=Late(first.pair), stream=Late(first.stream), cot_full=Late(first.cot_full),
+            left32=Late(left), right32=Late(right), first32=Late(moment), second32=Late(second),
         ),
         dict(
-            first_whole=(fetch_shape(plan, moment).shape, BF),
-            grad_slot=((C, rows), BF),
-            branch_full=Late((C, rows), BF),
+            left_whole=whole,
+            right_whole=whole,
+            first_whole=whole,
+            second_whole=whole,
             grad_two=Late((cols, rows), F32),
             out=((rows, cols), BF),
-            weight_grads=Late((2 * ff_blocks, C, cols), BF),
-            sums=((cols, 4 + ff_blocks), F32),
+            mlp_sums=((cols, 4 + ff_blocks), F32),
+            grad_normed=((C, rows), BF),
+            attend_grads=Late((4, C, cols), BF),
+            attend_sums=((cols, 8), F32),
+            branch_full=Late((C, rows), BF),
+            mlp_summed=((2 * ff_blocks, C // plan.pts, cols), BF),
         ),
-        scratch,
-        16 * rows * C * cols * ff_blocks,
-        free=("first_whole",),
+        dict(
+            low=vmem((4,) + left.shape, BF),
+            q_ext=vmem((rows, 2 * cols), BF),
+            k_ext=vmem((rows, 2 * cols), BF),
+            values=vmem((rows, cols), BF),
+            attended=vmem((cols, rows), BF),
+            lse=vmem((heads, 1, rows), F32),
+            attended_rows=vmem((C, rows), BF),
+            v_aug=vmem((heads, 2 * HD, rows), BF),
+            cot=vmem((cols, rows), BF),
+            acc=vmem((C, rows), F32),
+            two=vmem((C, rows), F32),
+            two_unit=vmem((C, rows), F32),
+            two_std=vmem((1, rows), F32),
+            normed=vmem((C, rows), BF),
+            pre=vmem((cols, rows), F32),
+            grad_act=vmem((cols, rows), F32),
+            act=vmem((ff_blocks * cols, rows), BF),
+            grad_pre=vmem((ff_blocks * cols, rows), BF),
+            stats=vmem((plan.mdl, 8, rows), F32),
+            stats_send=dma(plan.mdl),
+            stats_recv=dma(plan.mdl),
+            parts=vmem((plan.mdl, cols, rows), BF),
+            out_parts=vmem((plan.mdl, cols, rows), BF),
+            grad_slot=vmem((C, rows), BF),
+            mlp_grads=vmem((2 * ff_blocks, C, cols), BF),
+            grad=vmem((rows, cols), BF),
+            inner=vmem((heads, 1, rows), F32),
+            keys_t=vmem((cols, rows), BF),
+            dk_acc=vmem((rows, cols), F32),
+            dv_acc=vmem((rows, cols), F32),
+            dq=vmem((cols, rows), BF),
+            back_parts=vmem((plan.mdl, cols, rows), BF),
+            grad_net=total,
+            out_net=total,
+            sum_net=total,
+            out_route=route,
+            in_route=route,
+            back_route=route,
+            branch_net=Gather.semaphores(plan),
+            reduce_net=Reduce.buffers(plan, 2 * ff_blocks, MLP_PACK, cols),
+            fetch_net=[fetch_sems(plan)] * 4,
+        ),
+        14 * heads * rows * rows * cols + 16 * rows * C * cols * ff_blocks,
+        free=("left_whole", "right_whole", "first_whole", "second_whole"),
     )
 
 
@@ -1331,7 +1297,9 @@
     me, plane = lax.axis_index(PTS), lax.axis_index(MDL)
     own_cols = pl.ds(plane * cols, cols)
     middle = slice(HALO, HALO + rows)
-    moves(START, r.grad_normed_move, r.branch_full_move, r.one_unit_move, r.mixed_unit_move, r.pair_move, r.hidden_move, r.taken_move, r.taps_move, r.grad_two_move)
+    first = (r.grad_normed_move, r.one_unit_move, r.branch_full_move, r.mixed_unit_move, r.pair_move)
+    second = (r.hidden_move, r.taken_move, r.grad_two_move, r.taps_move)
+    moves(START, *first, *second)
     greet([{PTS: v} for v in others(me, pts)] + [{MDL: plane + 1 - 2 * lax.rem(plane, 2)}])
     reduce = Reduce(
         plan, r.reduce_net
@@ -1340,7 +1308,7 @@
     for b in range(ready):
         reduce.store(r.attend_grads[b], b // BACK_PACK, b % BACK_PACK)
     reduce.start(0)
-    moves(WAIT, r.grad_normed_move, r.branch_full_move, r.one_unit_move, r.mixed_unit_move, r.pair_move, r.hidden_move, r.taken_move, r.taps_move, r.grad_two_move)
+    moves(WAIT, *first)
 
     def grads(group):
         if group == ready // BACK_PACK:
@@ -1419,6 +1387,7 @@
     def _():
         r.back[:, :HALO] = jnp.zeros((C, HALO), BF)
 
+    moves(WAIT, *second)
     for group in range(1, groups):
         grads(group)
         reduce.start(group)
@@ -1442,10 +1411,7 @@
         r.attend_sums[:, 0:2],
         r.mlp_sums[...],
     ]
-    at = 0
-    for column in columns:
-        r.vectors[pl.ds(me, 1), :, at : at + column.shape[1]] = column[None]
-        at += column.shape[1]
+    r.vectors[pl.ds(me, 1)] = jnp.concatenate(columns, 1).T[None]
 
     def vector_copy(p, slot):
         return push(
@@ -1496,7 +1462,7 @@
     for p in others(me, pts):
         vector_copy(p, p).wait_recv()
         total = total + r.vectors[pl.ds(p, 1)][0]
-    r.vector_grad[...] = total.T
+    r.vector_grad[...] = total
     reduce.end()
     for p in others(me, pts):
         vector_copy(p, me).wait_send()
@@ -1543,7 +1509,7 @@
             delta=vmem((C, rows), F32),
             mixed=vmem((C, rows), BF),
             back=vmem((C, rows + 2 * HALO), BF),
-            vectors=vmem((plan.pts, cols, 12 + FF // C), F32),
+            vectors=vmem((plan.pts, 12 + FF // C, cols), F32),
             halo_send=dma(2),
             halo_recv=dma(2),
             core_send=dma(2),
@@ -1801,43 +1767,19 @@
         from_patch[None],
         scan_lengths,
     )
-    rest, send_pos, arrival = first.rest, first.send_pos, first.arrival
-    kept = attend(
-        plan,
-        first.slot_in,
-        rest,
-        vectors,
-        first.group,
-        send_pos,
-        arrival,
-        row_eigen_basis,
-        right_basis,
-    )
-    middle = mlp(
-        plan, kept.attended_rows, first, rest, cotangent, send_pos, arrival, first_moment
-    )
-    back = attend_back(
-        plan,
-        kept,
-        middle.grad_slot,
-        first.slot_in,
-        rest,
-        first.pair,
-        send_pos,
-        arrival,
-        middle.weight_grads,
-        second_moment,
+    between = middle(
+        plan, first, vectors, cotangent, row_eigen_basis, right_basis, first_moment, second_moment
     )
     last = back_pass(
         plan,
         first,
         ids,
-        back.grad_normed,
-        middle.branch_full,
-        middle.grad_two,
-        back.weight_grads,
-        middle.sums,
-        back.sums,
+        between.grad_normed,
+        between.branch_full,
+        between.grad_two,
+        between.attend_grads,
+        between.mlp_sums,
+        between.attend_sums,
     )
     vector_grad = last.vector_grad
     listed = BACK_ORDER + MLP_ORDER
@@ -1850,11 +1792,11 @@
         plan,
         place_of_slot,
         last.summed,
-        back.mlp_summed,
-        kept.left_whole,
-        kept.right_whole,
-        middle.first_whole,
-        back.second_whole,
+        between.mlp_summed,
+        between.left_whole,
+        between.right_whole,
+        between.first_whole,
+        between.second_whole,
     )
     reduced = ended.rows.transpose(1, 2, 0, 3).reshape(plan.slots, C // pts, C)
     results = ended.results
@@ -1866,7 +1808,7 @@
     )
     new_vectors = vectors - VECTOR_RATE * vector_step
     return (
-        middle.out,
+        between.out,
         last.point_grad,
         reduced.astype(F32),
         new_first,

time: 454 us -> 424 us (0.934)
  Pallas kernels: 434 us -> 405 us
    pallas_call x6 -> x4, Pallas kernels: 434 us -> 405 us  [call(): pl.pallas_call(body, in_specs=[pl.BlockSpec(memory_space=space(*item)) fo...]
where the time goes in v6:
time: 424 us; the launch traced here: 417 us
  Pallas kernels  405 us (96%)
  other arithmetic  8.77 us (2%)
    pallas_call x4, Pallas kernels, call(): pl.pallas_call(body, in_specs=[pl.BlockSpec(memory_space=space(*item)) fo...  405 us

profile of v6, /device:TPU:29, one launch (start us, length us, event | category | flops | bytes accessed | tf_op | source)
XLA Modules:
  0.0 417.0 jit_solution(25827127527911995)
XLA Ops:
  0.6 0.8 reduce-window.4
  1.5 1.6 select_bitcast_fusion.refs_5_.refs_9_
  3.2 118.6 %front.1 = (bf16[8,27,64,128]{3,2,1,0:T(8,128)(2,1)}, bf16[27,128,1024]{2,1,0:T(8,128)(2,1)}, bf16[512,1024]{1,0:T(8,128)(2,1)}, bf16[4,2,512,128]{3,2,1,0:T(8,1...) custom-call(s32[40]{0:T(128)} %refs_0_.1, ...), custom_call_target="tpu_custom_call" | custom-call | flops 18119393280 | bytes 20000000 | tf_op jit(solution)/shard_map/front/pallas_call | solution.py:157
  121.7 154.9 %middle.1 = (bf16[2,8,64,512]{3,2,1,0:T(8,128)(2,1)}, bf16[2,8,64,512]{3,2,1,0:T(8,128)(2,1)}, bf16[2,8,64,512]{3,2,1,0:T(8,128)(2,1)}, bf16[2,8,64,512]{3,2,1,0...) custom-call(bf16[512,1024]{1,0:T(8,128)(2,1)} %get-tuple-element.44., ...), custom_call_target="tpu_custom_call" | custom-call | flops 19327352832 | bytes 20000000 | tf_op jit(solution)/shard_map/middle/pallas_call | solution.py:157
  276.6 0.0 copy-start.10
  276.6 0.0 copy-start.11
  276.7 68.6 %back_pass.1 = (bf16[32,64,128]{2,1,0:T(8,128)(2,1)}, f32[1024,128]{1,0:T(8,128)}, f32[16,128]{1,0:T(8,128)}) custom-call(bf16[27,128,1024]{2,1,0:T(8,128)(2,1)} %get-tuple-element.54.refs_0_, bf16[4,2,512,128]{3,2,1,0:T(8,128)(2,1)} %get-tuple-element.50.refs_8_.refs_1_, f32[512,16]{1,0:T(8,128)} %get-tuple-element.49.refs_6_.refs_2_, ...), custom_call_target="tpu_custom_call" | custom-call | flops 19931332608 | bytes 20000000 | tf_op jit(solution)/shard_map/back_pass/pallas_call | solution.py:157
  345.3 0.0 copy-done.10
  345.3 0.0 copy-done.11
  345.3 0.6 select_reduce_fusion.refs_0_
  345.9 0.0 copy-start
  345.9 0.0 copy-start.1
  345.9 0.0 copy-start.2
  346.0 62.9 %owner_update.1 = (bf16[4,10,64,128]{3,2,1,0:T(8,128)(2,1)}, bf16[10,2,64,512]{3,2,1,0:T(8,128)(2,1)}) custom-call(s32[40]{0:T(128)} %select_reduce_fusion.refs_0_, bf16[32,64,128]{2,1,0:T(8,128)(2,1)} %get-tuple-element.68.refs_1_, bf16[8,64,128]{2,1,0:T(8,128)(2,1)} %get-tuple-element.69.refs_2_, bf16[2,8,64,512]{3,2,1,0:T(8,128)(2,1)} %get-tuple-element.70.refs_3_, ...), custom_call_target="tpu_custom_call" | custom-call | flops 2147483648 | bytes 20000000 | tf_op jit(solution)/shard_map/owner_update/pallas_call | solution.py:157
  408.9 0.0 copy-done
  408.9 0.0 copy-done.1
  408.9 0.0 copy-done.2
  408.9 0.0 copy-start.3
  408.9 3.8 fusion.8
  412.7 0.0 copy-start.6
  412.7 0.0 copy-start.7
  412.7 0.0 copy-start.8
  412.7 0.0 copy-start.9
  412.7 0.0 copy-start.5
  412.7 0.0 copy-start.4
  412.7 0.0 copy-done.3
  412.8 1.2 copy_bitcast_fusion
  414.0 0.0 copy-done.6
  414.0 0.0 copy-done.7
  414.0 0.0 copy-done.8
  414.0 0.0 copy-done.9
  414.0 0.6 multiply_subtract_fusion
  414.6 0.0 copy-done.5
  414.6 0.7 copy.34
  415.3 0.0 copy-done.4
  415.3 0.8 copy.35
  416.1 0.6 copy.36
  (1 shorter events, 0.0 us)
Async XLA Ops:
  276.6 68.7 %copy-start.10 = (s32[40]{0:T(128)S(1)}, s32[40]{0:T(128)}, u32[]{:S(2)}) copy-start(s32[40]{0:T(128)} %refs_0_.1) | copy-start | bytes 484
  276.6 68.7 %copy-start.11 = (s32[40]{0:T(128)S(1)}, s32[40]{0:T(128)}, u32[]{:S(2)}) copy-start(s32[40]{0:T(128)} %constant.48.clone) | copy-start | bytes 484
  345.9 62.9 %copy-start = (f32[10,64,512]{2,1,0:T(8,128)S(1)}, f32[10,64,512]{2,1,0:T(8,128)}, u32[]{:S(2)}) copy-start(f32[10,64,512]{2,1,0:T(8,128)} %refs_1_.1) | copy-start | bytes 3932164
  345.9 62.9 %copy-start.1 = (f32[10,64,512]{2,1,0:T(8,128)S(1)}, f32[10,64,512]{2,1,0:T(8,128)}, u32[]{:S(2)}) copy-start(f32[10,64,512]{2,1,0:T(8,128)} %refs_13_.1) | copy-start | bytes 3932164
  345.9 62.9 %copy-start.2 = (f32[10,64,512]{2,1,0:T(8,128)S(1)}, f32[10,64,512]{2,1,0:T(8,128)}, u32[]{:S(2)}) copy-start(f32[10,64,512]{2,1,0:T(8,128)} %refs_14_.1) | copy-start | bytes 3932164
  408.9 3.9 copy-start.3
  412.7 1.3 copy-start.6
  412.7 1.3 copy-start.7
  412.7 1.3 copy-start.8
  412.7 1.3 copy-start.9
  412.7 1.9 copy-start.5
  412.7 2.6 copy-start.4

commit v7 on v6

--- a/solution.py
+++ b/solution.py
@@ -26,7 +26,7 @@
 WINDOW = TILE + 2 * HALO
 BF = jnp.bfloat16
 F32 = jnp.float32
-VMEM_LIMIT = 56 * 1024 * 1024
+VMEM_LIMIT = 58 * 1024 * 1024
 
 NN = (((1,), (0,)), ((), ()))
 NT = (((1,), (1,)), ((), ()))
@@ -301,11 +301,18 @@
         vmem = pltpu.VMEM((plan.pts, cols, capacity), BF)
         return dict(leave=vmem, land=vmem, send=dma(plan.pts), recv=dma(plan.pts))
 
-    def hot(self, index, part):
+    def leaving(self, values, part):
         capacity = self.bufs.leave.shape[2]
-        row = index[...]
+        row = self.out_index[...]
         places = lax.broadcasted_iota(jnp.int32, (capacity, row.shape[1]), 0) + part * capacity
-        return jnp.where(places == row, 1.0, 0.0).astype(BF)
+        hot = jnp.where(places == row, 1.0, 0.0).astype(BF)
+        return dot(hot, values, NT).T.astype(BF)
+
+    def landing(self, part):
+        capacity = self.bufs.land.shape[2]
+        shape = (self.in_index.shape[1], capacity)
+        places = lax.broadcasted_iota(jnp.int32, shape, 1) + part * capacity
+        return jnp.where(places == self.in_column, 1.0, 0.0).astype(BF)
 
     def copy(self, part, slot):
         b = self.bufs
@@ -317,25 +324,22 @@
     def start(self, values):
         b = self.bufs
         for part in others(self.me, self.size):
-            b.leave[pl.ds(part, 1)] = dot(values, self.hot(self.out_index, part), NT).astype(BF)[None]
+            b.leave[pl.ds(part, 1)] = self.leaving(values, part)[None]
             self.copy(part, self.me).start()
-        b.land[pl.ds(self.me, 1)] = dot(values, self.hot(self.out_index, self.me), NT).astype(BF)[None]
+        b.land[pl.ds(self.me, 1)] = self.leaving(values, self.me)[None]
 
     def finish(self):
         b = self.bufs
-        total = dot(b.land[pl.ds(self.me, 1)][0], self.hot(self.in_index, self.me))
+        self.in_column = column(self.in_index[...])
+        total = dot(self.landing(self.me), b.land[pl.ds(self.me, 1)][0], NT)
         for step in range(1, self.size):
             part = lax.rem(self.me + self.size - step, self.size)
-            hot = self.hot(self.in_index, part)
+            hot = self.landing(part)
             self.copy(part, part).wait_recv()
-            total = total + dot(b.land[pl.ds(part, 1)][0], hot)
+            total = total + dot(hot, b.land[pl.ds(part, 1)][0], NT)
         for part in others(self.me, self.size):
             self.copy(part, self.me).wait_send()
-        return total.astype(BF)
-
-    def run(self, values):
-        self.start(values)
-        return self.finish()
+        return total.T.astype(BF)
 
 
 class Route:
@@ -707,7 +711,7 @@
                     far_copy(group, source, 1).wait_recv()
                 pass_on(group, source, act)
 
-    ahead = 2
+    ahead = groups
     for group in range(ahead):
         pass_on(group, me, START)
 
@@ -971,24 +975,32 @@
     def norms(span):
         branch = (r.acc[:, span] + r.vec[:, 8:9]).astype(BF).astype(F32)
         two = r.stream[:, span] + branch
-        r.two[:, span] = two
+        r.stream[:, span] = two
         unit, inv_std = unit_columns(two)
         r.two_unit[:, span] = unit
         r.two_std[:, span] = inv_std
         r.normed[:, span] = (unit * r.vec[:, 9:10] + r.vec[:, 10:11]).astype(BF)
 
     over_spans(rows, norms)
+    if cols % 128 == 0:
+        first, second = (
+            jnp.concatenate([r.rest[low + k] for k in range(ff_blocks)], 1)
+            for low in (3, 3 + ff_blocks)
+        )
+        r.acc[...] = dot(first, r.normed[...], TN)
+        r.grad_act[...] = dot(second, r.cot_full[...], TN)
     for k in range(ff_blocks):
         part = slice(k * cols, (k + 1) * cols)
-        r.pre[...] = dot(r.rest[3 + k], r.normed[...], TN) + r.vec[own, 11 + k : 12 + k]
-        r.grad_act[...] = dot(r.rest[3 + ff_blocks + k], r.cot_full[...], TN)
+        if cols % 128 != 0:
+            r.acc[part, :] = dot(r.rest[3 + k], r.normed[...], TN)
+            r.grad_act[part, :] = dot(r.rest[3 + ff_blocks + k], r.cot_full[...], TN)
 
         def bend(span):
-            pre = r.pre[:, span]
+            pre = r.acc[part, span] + r.vec[own, 11 + k : 12 + k]
             half = 0.5 * (1.0 + lax.erf(pre * 0.7071067811865476))
             r.act[part, span] = (pre * half).astype(BF)
             slope = half + pre * jnp.exp(-0.5 * pre * pre) * 0.3989422804014327
-            r.grad_pre[part, span] = (r.grad_act[:, span] * slope).astype(BF)
+            r.grad_pre[part, span] = (r.grad_act[part, span] * slope).astype(BF)
 
         over_spans(rows, bend, 256)
     r.acc[...] = beside([r.rest[3 + k] for k in range(ff_blocks)])(r.grad_pre, cols)
@@ -1047,7 +1059,7 @@
     moves(START, r.grad_two_move)
     route.land()
     bias = r.vec[own, 11 + ff_blocks : 12 + ff_blocks]
-    r.out[...] = (r.two[own, :] + out_sum.finish() + bias).T.astype(BF)
+    r.out[...] = (r.stream[own, :] + out_sum.finish() + bias).T.astype(BF)
     route.finish()
     for m in others(plane, mdl):
         stats_copy(m, plane).wait_send()
@@ -1068,28 +1080,37 @@
     r.k_ext[:, cols:] = jnp.where(same | (lane >= plan.groups), 0.0, -1e30).astype(BF)
     values = dot(slot_in, r.rest[2], TN) + r.vectors[7:8, :]
     r.values[...] = values.astype(BF)
-    r.v_aug[:, :HD] = values.T.astype(BF).reshape(heads, HD, rows)
-    r.v_aug[:, HD:] = jnp.ones((heads, HD, rows), BF)
+    r.v_ext[:, :cols] = values.astype(BF)
+    r.v_ext[:, cols:] = jnp.ones((rows, cols), BF)
+    r.heads_out[...] = jnp.zeros_like(r.heads_out)
+    r.heads_lse[...] = jnp.zeros_like(r.heads_lse)
 
     def one(head, carry):
-        keys = r.k_ext[...]
-        values_t = r.v_aug[pl.ds(head, 1)][0]
+        keys, weights = r.k_ext[...], r.v_ext[...]
+        lane = lax.broadcasted_iota(jnp.int32, (TILE, cols), 1)
         for tile in range(rows // TILE):
             span = slice(tile * TILE, (tile + 1) * TILE)
-            scores = dot(keys, head_lanes(r.q_ext[span, :], cols, head), NT)
-            top = jnp.max(scores, 0, keepdims=True)
-            soft = jnp.exp(scores - top).astype(BF)
-            summed = dot(values_t, soft)
-            total = summed[HD : HD + 1]
-            r.attended[head_rows(head), span] = (summed[:HD] / total).astype(BF)
-            r.lse[pl.ds(head, 1), :, span] = (top + jnp.log(total))[None]
+            scores = dot(head_lanes(r.q_ext[span, :], cols, head), keys, NT)
+            top = jnp.max(scores, 1, keepdims=True)
+            summed = dot(jnp.exp(scores - top).astype(BF), weights)
+            total = summed[:, cols : cols + 1]
+            r.heads_out[span, :] = jnp.where(
+                lane // HD == head, summed[:, :cols] / total, r.heads_out[span, :]
+            )
+            r.heads_lse[span, :] = jnp.where(
+                lane == head, top + jnp.log(total), r.heads_lse[span, :]
+            )
         return carry
 
     route = Route(plan, r.arrival, r.send_pos, r.attended_rows, r.out_route)
     for i, trade in enumerate(route.trades):
         share = heads // route.PIECES
-        lax.fori_loop(i * share, (i + 1) * share, one, 0)
-        trade.start(r.attended[i * route.size : (i + 1) * route.size, :])
+        lax.fori_loop(i * share, (i + 1) * share, one, 0, unroll=2)
+        part = slice(i * route.size, (i + 1) * route.size)
+        r.attended[part, :] = r.heads_out[...].T[part].astype(BF)
+        trade.start(r.attended[part, :])
+    r.lse[...] = r.heads_lse[...].T[:heads][:, None]
+    fetch(plan, r, 0, START)
     fetch(plan, r, 1, START)
     route.land()
     route.finish()
@@ -1152,8 +1173,8 @@
     dk = r.dk_acc[...].astype(BF)
     dv = r.dv_acc[...].astype(BF)
     back = dot(r.rest[0], r.dq[...]) + dot(r.rest[1], dk, NT) + dot(r.rest[2], dv, NT)
-    r.back_parts[...] = back.astype(BF).reshape(plan.mdl, cols, rows)
-    back_sum = Sum(plan, r.back_parts, r.sum_net)
+    r.parts[...] = back.astype(BF).reshape(plan.mdl, cols, rows)
+    back_sum = Sum(plan, r.parts, r.sum_net)
     back_sum.start()
     r.attend_grads[0] = dot(r.slot_in[...], r.dq[...], NT).astype(BF)
     r.attend_grads[1] = dot(r.slot_in[...], dk).astype(BF)
@@ -1193,7 +1214,6 @@
     moves(START, r.left32_move, r.pair_move, r.stream_move, r.cot_full_move)
     moves(START, r.right32_move, r.first32_move, r.second32_move)
     greet(everyone(plan))
-    fetch(plan, r, 0, START)
     r.cot[...] = r.cot_rows[...].astype(F32).T.astype(BF)
     attend_part(plan, r)
     mlp_part(plan, r)
@@ -1243,15 +1263,15 @@
             attended=vmem((cols, rows), BF),
             lse=vmem((heads, 1, rows), F32),
             attended_rows=vmem((C, rows), BF),
-            v_aug=vmem((heads, 2 * HD, rows), BF),
+            v_ext=vmem((rows, 2 * cols), BF),
+            heads_out=vmem((rows, cols), F32),
+            heads_lse=vmem((rows, cols), F32),
             cot=vmem((cols, rows), BF),
             acc=vmem((C, rows), F32),
-            two=vmem((C, rows), F32),
             two_unit=vmem((C, rows), F32),
             two_std=vmem((1, rows), F32),
             normed=vmem((C, rows), BF),
-            pre=vmem((cols, rows), F32),
-            grad_act=vmem((cols, rows), F32),
+            grad_act=vmem((ff_blocks * cols, rows), F32),
             act=vmem((ff_blocks * cols, rows), BF),
             grad_pre=vmem((ff_blocks * cols, rows), BF),
             stats=vmem((plan.mdl, 8, rows), F32),
@@ -1267,7 +1287,6 @@
             dk_acc=vmem((rows, cols), F32),
             dv_acc=vmem((rows, cols), F32),
             dq=vmem((cols, rows), BF),
-            back_parts=vmem((plan.mdl, cols, rows), BF),
             grad_net=total,
             out_net=total,
             sum_net=total,
@@ -1478,7 +1497,7 @@
         core_copy(low_end, 0, core).wait_send()
 
 
-LAG = 2
+LAG = 4
 
 
 def back_pass(

time: 424 us -> 415 us (0.979)
  Pallas kernels: 405 us -> 395 us
    pallas_call x4, Pallas kernels: 405 us -> 395 us  [call(): pl.pallas_call(body, in_specs=[pl.BlockSpec(memory_space=space(*item)) fo...]
where the time goes in v7:
time: 415 us; the launch traced here: 407 us
  Pallas kernels  395 us (95%)
  other arithmetic  8.77 us (2%)
    pallas_call x4, Pallas kernels, call(): pl.pallas_call(body, in_specs=[pl.BlockSpec(memory_space=space(*item)) fo...  395 us

profile of v7, /device:TPU:29, one launch (start us, length us, event | category | flops | bytes accessed | tf_op | source)
XLA Modules:
  0.0 406.6 jit_solution(12686455370888096847)
XLA Ops:
  0.6 0.8 reduce-window.4
  1.5 1.6 select_bitcast_fusion.refs_5_.refs_9_
  3.2 113.4 %front.1 = (bf16[8,27,64,128]{3,2,1,0:T(8,128)(2,1)}, bf16[27,128,1024]{2,1,0:T(8,128)(2,1)}, bf16[512,1024]{1,0:T(8,128)(2,1)}, bf16[4,2,512,128]{3,2,1,0:T(8,1...) custom-call(s32[40]{0:T(128)} %refs_0_.1, ...), custom_call_target="tpu_custom_call" | custom-call | flops 18119393280 | bytes 20000000 | tf_op jit(solution)/shard_map/front/pallas_call | solution.py:157
  116.5 151.6 %middle.1 = (bf16[2,8,64,512]{3,2,1,0:T(8,128)(2,1)}, bf16[2,8,64,512]{3,2,1,0:T(8,128)(2,1)}, bf16[2,8,64,512]{3,2,1,0:T(8,128)(2,1)}, bf16[2,8,64,512]{3,2,1,0...) custom-call(bf16[512,1024]{1,0:T(8,128)(2,1)} %get-tuple-element.44., ...), custom_call_target="tpu_custom_call" | custom-call | flops 19327352832 | bytes 20000000 | tf_op jit(solution)/shard_map/middle/pallas_call | solution.py:157
  268.2 0.0 copy-start.10
  268.2 0.0 copy-start.11
  268.2 68.6 %back_pass.1 = (bf16[32,64,128]{2,1,0:T(8,128)(2,1)}, f32[1024,128]{1,0:T(8,128)}, f32[16,128]{1,0:T(8,128)}) custom-call(bf16[27,128,1024]{2,1,0:T(8,128)(2,1)} %get-tuple-element.54.refs_0_, bf16[4,2,512,128]{3,2,1,0:T(8,128)(2,1)} %get-tuple-element.50.refs_8_.refs_1_, f32[512,16]{1,0:T(8,128)} %get-tuple-element.49.refs_6_.refs_2_, ...), custom_call_target="tpu_custom_call" | custom-call | flops 19931332608 | bytes 20000000 | tf_op jit(solution)/shard_map/back_pass/pallas_call | solution.py:157
  336.8 0.0 copy-done.10
  336.8 0.0 copy-done.11
  336.9 0.6 select_reduce_fusion.refs_0_
  337.5 0.0 copy-start
  337.5 0.0 copy-start.1
  337.5 0.0 copy-start.2
  337.5 61.1 %owner_update.1 = (bf16[4,10,64,128]{3,2,1,0:T(8,128)(2,1)}, bf16[10,2,64,512]{3,2,1,0:T(8,128)(2,1)}) custom-call(s32[40]{0:T(128)} %select_reduce_fusion.refs_0_, bf16[32,64,128]{2,1,0:T(8,128)(2,1)} %get-tuple-element.68.refs_1_, bf16[8,64,128]{2,1,0:T(8,128)(2,1)} %get-tuple-element.69.refs_2_, bf16[2,8,64,512]{3,2,1,0:T(8,128)(2,1)} %get-tuple-element.70.refs_3_, ...), custom_call_target="tpu_custom_call" | custom-call | flops 2147483648 | bytes 20000000 | tf_op jit(solution)/shard_map/owner_update/pallas_call | solution.py:157
  398.6 0.0 copy-done
  398.6 0.0 copy-done.1
  398.6 0.0 copy-done.2
  398.6 0.0 copy-start.3
  398.6 3.8 fusion.8
  402.4 0.0 copy-start.6
  402.4 0.0 copy-start.7
  402.4 0.0 copy-start.8
  402.4 0.0 copy-start.9
  402.4 0.0 copy-start.5
  402.4 0.0 copy-start.4
  402.4 0.0 copy-done.3
  402.4 1.2 copy_bitcast_fusion
  403.7 0.0 copy-done.6
  403.7 0.0 copy-done.7
  403.7 0.0 copy-done.8
  403.7 0.0 copy-done.9
  403.7 0.6 multiply_subtract_fusion
  404.3 0.0 copy-done.5
  404.3 0.7 copy.34
  405.0 0.0 copy-done.4
  405.0 0.8 copy.35
  405.8 0.6 copy.36
  (1 shorter events, 0.0 us)
Async XLA Ops:
  268.2 68.7 %copy-start.10 = (s32[40]{0:T(128)S(1)}, s32[40]{0:T(128)}, u32[]{:S(2)}) copy-start(s32[40]{0:T(128)} %refs_0_.1) | copy-start | bytes 484
  268.2 68.7 %copy-start.11 = (s32[40]{0:T(128)S(1)}, s32[40]{0:T(128)}, u32[]{:S(2)}) copy-start(s32[40]{0:T(128)} %constant.48.clone) | copy-start | bytes 484
  337.5 61.1 %copy-start = (f32[10,64,512]{2,1,0:T(8,128)S(1)}, f32[10,64,512]{2,1,0:T(8,128)}, u32[]{:S(2)}) copy-start(f32[10,64,512]{2,1,0:T(8,128)} %refs_1_.1) | copy-start | bytes 3932164
  337.5 61.1 %copy-start.1 = (f32[10,64,512]{2,1,0:T(8,128)S(1)}, f32[10,64,512]{2,1,0:T(8,128)}, u32[]{:S(2)}) copy-start(f32[10,64,512]{2,1,0:T(8,128)} %refs_13_.1) | copy-start | bytes 3932164
  337.5 61.1 %copy-start.2 = (f32[10,64,512]{2,1,0:T(8,128)S(1)}, f32[10,64,512]{2,1,0:T(8,128)}, u32[]{:S(2)}) copy-start(f32[10,64,512]{2,1,0:T(8,128)} %refs_14_.1) | copy-start | bytes 3932164
  398.6 3.9 copy-start.3
  402.4 1.3 copy-start.6
  402.4 1.3 copy-start.7
  402.4 1.3 copy-start.8
  402.4 1.3 copy-start.9
  402.4 1.9 copy-start.5
  402.4 2.6 copy-start.4

commit v8 on v7

--- a/solution.py
+++ b/solution.py
@@ -1166,7 +1166,7 @@
         return carry
 
     delay = max(heads - reduce.steps, 0)
-    lax.fori_loop(0, heads, one, 0)
+    lax.fori_loop(0, heads, one, 0, unroll=2)
     for s in range(heads - delay, reduce.steps):
         reduce.step(s)
     branch_gather.forward()
@@ -1497,7 +1497,7 @@
         core_copy(low_end, 0, core).wait_send()
 
 
-LAG = 4
+LAG = 5
 
 
 def back_pass(

time: 415 us -> 415 us (level)
  no operation moved by 1% of the time
where the time goes in v8:
time: 415 us; the launch traced here: 407 us
  Pallas kernels  395 us (95%)
  other arithmetic  8.77 us (2%)
    pallas_call x4, Pallas kernels, call(): pl.pallas_call(body, in_specs=[pl.BlockSpec(memory_space=space(*item)) fo...  395 us

profile of v8, /device:TPU:29, one launch (start us, length us, event | category | flops | bytes accessed | tf_op | source)
XLA Modules:
  0.0 407.1 jit_solution(17843103859068829601)
XLA Ops:
  0.6 0.8 reduce-window.4
  1.5 1.6 select_bitcast_fusion.refs_5_.refs_9_
  3.2 113.4 %front.1 = (bf16[8,27,64,128]{3,2,1,0:T(8,128)(2,1)}, bf16[27,128,1024]{2,1,0:T(8,128)(2,1)}, bf16[512,1024]{1,0:T(8,128)(2,1)}, bf16[4,2,512,128]{3,2,1,0:T(8,1...) custom-call(s32[40]{0:T(128)} %refs_0_.1, ...), custom_call_target="tpu_custom_call" | custom-call | flops 18119393280 | bytes 20000000 | tf_op jit(solution)/shard_map/front/pallas_call | solution.py:157
  116.5 151.8 %middle.1 = (bf16[2,8,64,512]{3,2,1,0:T(8,128)(2,1)}, bf16[2,8,64,512]{3,2,1,0:T(8,128)(2,1)}, bf16[2,8,64,512]{3,2,1,0:T(8,128)(2,1)}, bf16[2,8,64,512]{3,2,1,0...) custom-call(bf16[512,1024]{1,0:T(8,128)(2,1)} %get-tuple-element.44., ...), custom_call_target="tpu_custom_call" | custom-call | flops 19327352832 | bytes 20000000 | tf_op jit(solution)/shard_map/middle/pallas_call | solution.py:157
  268.3 0.0 copy-start.10
  268.4 0.0 copy-start.11
  268.4 68.6 %back_pass.1 = (bf16[32,64,128]{2,1,0:T(8,128)(2,1)}, f32[1024,128]{1,0:T(8,128)}, f32[16,128]{1,0:T(8,128)}) custom-call(bf16[27,128,1024]{2,1,0:T(8,128)(2,1)} %get-tuple-element.54.refs_0_, bf16[4,2,512,128]{3,2,1,0:T(8,128)(2,1)} %get-tuple-element.50.refs_8_.refs_1_, f32[512,16]{1,0:T(8,128)} %get-tuple-element.49.refs_6_.refs_2_, ...), custom_call_target="tpu_custom_call" | custom-call | flops 19931332608 | bytes 20000000 | tf_op jit(solution)/shard_map/back_pass/pallas_call | solution.py:157
  337.0 0.0 copy-done.10
  337.0 0.0 copy-done.11
  337.0 0.6 select_reduce_fusion.refs_0_
  337.6 0.0 copy-start
  337.6 0.0 copy-start.1
  337.6 0.0 copy-start.2
  337.7 61.2 %owner_update.1 = (bf16[4,10,64,128]{3,2,1,0:T(8,128)(2,1)}, bf16[10,2,64,512]{3,2,1,0:T(8,128)(2,1)}) custom-call(s32[40]{0:T(128)} %select_reduce_fusion.refs_0_, bf16[32,64,128]{2,1,0:T(8,128)(2,1)} %get-tuple-element.68.refs_1_, bf16[8,64,128]{2,1,0:T(8,128)(2,1)} %get-tuple-element.69.refs_2_, bf16[2,8,64,512]{3,2,1,0:T(8,128)(2,1)} %get-tuple-element.70.refs_3_, ...), custom_call_target="tpu_custom_call" | custom-call | flops 2147483648 | bytes 20000000 | tf_op jit(solution)/shard_map/owner_update/pallas_call | solution.py:157
  398.9 0.0 copy-done
  398.9 0.0 copy-done.1
  398.9 0.0 copy-done.2
  398.9 0.0 copy-start.3
  398.9 3.8 fusion.8
  402.7 0.0 copy-start.6
  402.7 0.0 copy-start.7
  402.7 0.0 copy-start.8
  402.7 0.0 copy-start.9
  402.7 0.0 copy-start.5
  402.7 0.0 copy-start.4
  402.7 0.0 copy-done.3
  402.7 1.2 copy_bitcast_fusion
  404.0 0.0 copy-done.6
  404.0 0.0 copy-done.7
  404.0 0.0 copy-done.8
  404.0 0.0 copy-done.9
  404.0 0.6 multiply_subtract_fusion
  404.6 0.0 copy-done.5
  404.6 0.7 copy.34
  405.3 0.0 copy-done.4
  405.3 0.8 copy.35
  406.1 0.6 copy.36
  (1 shorter events, 0.0 us)
Async XLA Ops:
  268.3 68.7 %copy-start.10 = (s32[40]{0:T(128)S(1)}, s32[40]{0:T(128)}, u32[]{:S(2)}) copy-start(s32[40]{0:T(128)} %refs_0_.1) | copy-start | bytes 484
  268.4 68.7 %copy-start.11 = (s32[40]{0:T(128)S(1)}, s32[40]{0:T(128)}, u32[]{:S(2)}) copy-start(s32[40]{0:T(128)} %constant.48.clone) | copy-start | bytes 484
  337.6 61.2 %copy-start = (f32[10,64,512]{2,1,0:T(8,128)S(1)}, f32[10,64,512]{2,1,0:T(8,128)}, u32[]{:S(2)}) copy-start(f32[10,64,512]{2,1,0:T(8,128)} %refs_1_.1) | copy-start | bytes 3932164
  337.6 61.2 %copy-start.1 = (f32[10,64,512]{2,1,0:T(8,128)S(1)}, f32[10,64,512]{2,1,0:T(8,128)}, u32[]{:S(2)}) copy-start(f32[10,64,512]{2,1,0:T(8,128)} %refs_13_.1) | copy-start | bytes 3932164
  337.6 61.2 %copy-start.2 = (f32[10,64,512]{2,1,0:T(8,128)S(1)}, f32[10,64,512]{2,1,0:T(8,128)}, u32[]{:S(2)}) copy-start(f32[10,64,512]{2,1,0:T(8,128)} %refs_14_.1) | copy-start | bytes 3932164
  398.9 3.9 copy-start.3
  402.7 1.3 copy-start.6
  402.7 1.3 copy-start.7
  402.7 1.3 copy-start.8
  402.7 1.3 copy-start.9
  402.7 1.9 copy-start.5
  402.7 2.6 copy-start.4
